TPU v7x, 32 devices: a whole 2x2x4 slice. The times are simulated.
32 devices in a mesh: dp: 4 (over y, x), vocab: 8 (over z, core).
Axes of the slice: x: 2, y: 2, z: 4, core: 2. Of those that a mesh axis runs over, the one named last changes fastest.
Arguments:
- src_ids: int32 [4, 1024], P('dp'), may hold values from 0 to 37887
- src_seg: int32 [4, 1024], P('dp'), may hold values from 0 to 30, as said below
- tgt_ids: int32 [4, 1024], P('dp'), may hold values from 0 to 37887
- tgt_seg: int32 [4, 1024], P('dp'), may hold values from 0 to 30, as said below
- pick_pos: int32 [4, 256], P('dp'), may hold values from 0 to 1023
- pick_label: int32 [4, 256], P('dp'), may hold values from 0 to 37887
- attn_w: float32 [12, 512, 512], P(None, 'dp')
- attn_m: float32 [12, 512, 512], P(None, 'dp'), may hold values from -0.00012207031 to 0.00012207031
- attn_v: float32 [12, 512, 512], P(None, 'dp'), may hold values from 1.8694485e-11 to 2.9911176e-10
- ffn_w: float32 [4, 2048, 512], P(None, 'dp'), may hold values from -0.25 to 0.25
- ffn_m: float32 [4, 2048, 512], P(None, 'dp'), may hold values from -0.00012207031 to 0.00012207031
- ffn_v: float32 [4, 2048, 512], P(None, 'dp'), may hold values from 1.8694485e-11 to 2.9911176e-10
- soap_basis: float32 [4, 512, 512], replicated, as said below
- soap_stats: float32 [4, 512, 512], replicated, as said below
- norm_p: float32 [14, 512], P(None, 'dp')
- norm_m: float32 [14, 512], P(None, 'dp'), may hold values from -0.00061035156 to 0.00061035156
- norm_v: float32 [14, 512], P(None, 'dp'), may hold values from 3.738897e-10 to 5.982235e-09
- embedding: float32 [37888, 512], P('vocab', 'dp')
- embed_m: float32 [37888, 512], P('vocab', 'dp'), may hold values from -0.00012207031 to 0.00012207031
- embed_v: float32 [37888, 512], P('vocab', 'dp'), may hold values from 1.8694485e-11 to 2.9911176e-10
Outputs:
- loss_sum: float32 [], replicated
- sentences: float32 [], replicated
- grad_norm: float32 [], replicated
- attn_w_new: float32 [12, 512, 512], P(None, 'dp')
- attn_m_new: float32 [12, 512, 512], P(None, 'dp')
- attn_v_new: float32 [12, 512, 512], P(None, 'dp')
- ffn_w_new: float32 [4, 2048, 512], P(None, 'dp')
- ffn_m_new: float32 [4, 2048, 512], P(None, 'dp')
- ffn_v_new: float32 [4, 2048, 512], P(None, 'dp')
- basis_new: float32 [4, 512, 512], replicated
- stats_new: float32 [4, 512, 512], replicated
- norm_p_new: float32 [14, 512], P(None, 'dp')
- norm_m_new: float32 [14, 512], P(None, 'dp')
- norm_v_new: float32 [14, 512], P(None, 'dp')
- embedding_new: float32 [37888, 512], P('vocab', 'dp')
- embed_m_new: float32 [37888, 512], P('vocab', 'dp')
- embed_v_new: float32 [37888, 512], P('vocab', 'dp')
Inputs may be any that keep to these rules, and one draw needn't show every extreme that they name: Sentence numbers of a row start at 0 and rise by one at the first token of each sentence; row r of src_seg and row r of tgt_seg hold the same number of sentences; the last row holds 31 sentences. `tgt_seg`: same law as src_seg, with the same number of sentences in each row. `soap_basis`: orthogonal matrices. `soap_stats`: symmetric positive definite.
All inputs are finite; a program needn't handle non-finite values.
Results may differ from a plain program's by a relative error of at most 0.012.
Values may be sent and summed in bfloat16 or wider, within the bound.
A program may use at most 384 MiB of HBM per device.

v0:
```python
from functools import partial
import math

import jax
import jax.numpy as jnp
from jax import lax
from jax.sharding import PartitionSpec as P

HEADS = 8
STEP = 10


highest = lax.Precision.HIGHEST
beta_one = 0.9
beta_two = 0.999
adam_eps = 1e-08
decay_rate = 0.01
rate_matrix = 0.03
rate_vector = 0.3
clip_limit = 1.0
stat_decay = 0.95
norm_eps = 1e-06


def combined_all(value, axis, combine):
    everything = jax.tree.map(lambda part: lax.all_gather(part, axis), value)
    leading = jax.tree.map(lambda part: part[0], everything)

    def lap(k, so_far):
        return combine(so_far, jax.tree.map(lambda part: part[k], everything))

    return lax.fori_loop(1, lax.axis_size(axis), lap, leading)


def dot_plain(left, right):
    return jnp.dot(left, right, preferred_element_type=jnp.float32)


def dot_last(left, right):
    return lax.dot_general(
        left, right, (((1,), (1,)), ((), ())), preferred_element_type=jnp.float32
    )


def dot_first(left, right):
    return lax.dot_general(
        left, right, (((0,), (0,)), ((), ())), preferred_element_type=jnp.float32
    )


def layer_norm(values, gain_row, bias_row):
    centre = values - jnp.mean(values, axis=-1, keepdims=True)
    spread = jnp.mean(centre * centre, axis=-1, keepdims=True)
    return centre * lax.rsqrt(spread + norm_eps) * gain_row + bias_row


def sinusoid(length, model_width):
    places = jnp.arange(length, dtype=jnp.float32)[:, None]
    halves = jnp.arange(model_width // 2, dtype=jnp.float32)[None, :]
    angles = places * jnp.exp(halves * (-2.0 * math.log(10000.0) / model_width))
    return jnp.stack([jnp.sin(angles), jnp.cos(angles)], axis=-1).reshape(length, model_width)


def allowed_bias(seg_query, seg_keys, place_query, causal):
    allowed = seg_query[:, None] == seg_keys[None, :]
    if causal:
        allowed = allowed & (jnp.arange(seg_keys.shape[0])[None, :] <= place_query[:, None])
    return jnp.where(allowed, 0.0, -1000000000.0).astype(jnp.float32)


def pick_weights(target_seg, pick_rows):
    sentence = jnp.take(target_seg, pick_rows, axis=0)
    return jnp.sum((sentence[:, None] == sentence[None, :]).astype(jnp.float32), axis=1)


def block_scores(query_part, key_heads, seg_part, seg_keys, place_part, causal, score_scale):
    scores = (
        jnp.einsum("qhd,khd->hqk", query_part, key_heads, preferred_element_type=jnp.float32)
        * score_scale
    )
    return scores + allowed_bias(seg_part, seg_keys, place_part, causal)[None]


def attn_forward(query_in, key_in, weights, seg_query, seg_keys, causal, start):
    length = query_in.shape[0]
    block_rows = min(512, length)
    queries = dot_plain(query_in, weights[0]).astype(jnp.bfloat16)
    key_local = dot_plain(key_in, weights[1]).astype(jnp.bfloat16)
    value_local = dot_plain(key_in, weights[2]).astype(jnp.bfloat16)
    key_heads = key_local.reshape(seg_keys.shape[0], HEADS, -1)
    value_heads = value_local.reshape(seg_keys.shape[0], HEADS, -1)
    head_size = key_heads.shape[-1]
    score_scale = 1.0 / math.sqrt(head_size)
    places = (start + jnp.arange(length)).reshape(-1, block_rows)

    def one_block(inputs):
        query_part, seg_part, place_part = inputs
        scores = block_scores(
            query_part, key_heads, seg_part, seg_keys, place_part, causal, score_scale
        )
        row_top = jnp.max(scores, axis=-1, keepdims=True)
        exponent = jnp.exp(scores - row_top)
        row_total = jnp.sum(exponent, axis=-1, keepdims=True)
        softmax_low = (exponent / row_total).astype(jnp.bfloat16)
        mixed_part = jnp.einsum(
            "hqk,khd->qhd", softmax_low, value_heads, preferred_element_type=jnp.float32
        )
        return (mixed_part, row_top, row_total)

    mixed, tops, totals = lax.map(
        one_block,
        (
            queries.reshape(-1, block_rows, HEADS, head_size),
            seg_query.reshape(-1, block_rows),
            places,
        ),
    )
    mixed = mixed.reshape(length, -1).astype(jnp.bfloat16)
    stored = (
        query_in,
        key_in,
        queries,
        key_heads,
        value_heads,
        mixed,
        tops,
        totals,
        weights,
        seg_query,
        seg_keys,
        causal,
        start,
    )
    return (dot_plain(mixed, weights[3]), stored)


def attn_backward(grad_out, stored):
    (
        query_in,
        key_in,
        queries,
        key_heads,
        value_heads,
        mixed,
        tops,
        totals,
        weights,
        seg_query,
        seg_keys,
        causal,
        start,
    ) = stored
    length = query_in.shape[0]
    block_rows = min(512, length)
    head_size = key_heads.shape[-1]
    score_scale = 1.0 / math.sqrt(head_size)
    places = (start + jnp.arange(length)).reshape(-1, block_rows)
    grad_low = grad_out.astype(jnp.bfloat16)
    grad_wo = dot_first(mixed, grad_low)
    grad_mixed = dot_last(grad_low, weights[3]).astype(jnp.bfloat16)

    def one_block(running, inputs):
        query_part, grad_part, seg_part, place_part, row_top, row_total = inputs
        scores = block_scores(
            query_part, key_heads, seg_part, seg_keys, place_part, causal, score_scale
        )
        softmax_rows = jnp.exp(scores - row_top) / row_total
        grad_softmax = jnp.einsum(
            "qhd,khd->hqk", grad_part, value_heads, preferred_element_type=jnp.float32
        )
        row_inner = jnp.sum(softmax_rows * grad_softmax, axis=-1, keepdims=True)
        grad_scores = (softmax_rows * (grad_softmax - row_inner)).astype(jnp.bfloat16)
        grad_query = (
            jnp.einsum("hqk,khd->qhd", grad_scores, key_heads, preferred_element_type=jnp.float32)
            * score_scale
        )
        grad_keys = (
            running[0]
            + jnp.einsum(
                "hqk,qhd->khd", grad_scores, query_part, preferred_element_type=jnp.float32
            )
            * score_scale
        )
        grad_values = running[1] + jnp.einsum(
            "hqk,qhd->khd",
            softmax_rows.astype(jnp.bfloat16),
            grad_part,
            preferred_element_type=jnp.float32,
        )
        return ((grad_keys, grad_values), grad_query)

    zero_keys = jnp.zeros(key_heads.shape, jnp.float32)
    (grad_keys, grad_values), grad_query = lax.scan(
        one_block,
        (zero_keys, zero_keys),
        (
            queries.reshape(-1, block_rows, HEADS, head_size),
            grad_mixed.reshape(-1, block_rows, HEADS, head_size),
            seg_query.reshape(-1, block_rows),
            places,
            tops,
            totals,
        ),
    )
    grad_query = grad_query.reshape(length, -1).astype(jnp.bfloat16)
    grad_keys = grad_keys.reshape(seg_keys.shape[0], -1)
    grad_values = grad_values.reshape(seg_keys.shape[0], -1)
    grad_keys = grad_keys.astype(jnp.bfloat16)
    grad_values = grad_values.astype(jnp.bfloat16)
    grad_weights = jnp.stack(
        [
            dot_first(query_in, grad_query),
            dot_first(key_in, grad_keys),
            dot_first(key_in, grad_values),
            grad_wo,
        ]
    )
    grad_query_in = dot_last(grad_query, weights[0])
    grad_key_in = dot_last(grad_keys, weights[1]) + dot_last(grad_values, weights[2])
    return (grad_weights, grad_query_in, grad_key_in)


def ffn_forward(inputs, w_in, w_out):
    hidden = dot_last(inputs, w_in)
    active, gelu_back = jax.vjp(partial(jax.nn.gelu, approximate=True), hidden)
    active = active.astype(jnp.bfloat16)
    return (dot_plain(active, w_out), (inputs, active, gelu_back, w_in, w_out))


def ffn_backward(grad_out, stored):
    inputs, active, gelu_back, w_in, w_out = stored
    grad_low = grad_out.astype(jnp.bfloat16)
    grad_w_out = dot_first(active, grad_low)
    grad_hidden = gelu_back(dot_last(grad_low, w_out))[0].astype(jnp.bfloat16)
    grad_w_in = dot_first(grad_hidden, inputs)
    return (grad_w_in, grad_w_out, dot_plain(grad_hidden, w_in))


def lookup(token_ids, table_low, offset):
    block_rows = min(512, token_ids.shape[0])
    columns = offset + jnp.arange(table_low.shape[0])

    def one_block(id_block):
        one_hot = (id_block[:, None] == columns[None, :]).astype(jnp.bfloat16)
        return dot_plain(one_hot, table_low)

    return lax.map(one_block, token_ids.reshape(-1, block_rows)).reshape(token_ids.shape[0], -1)


def lookup_back(token_ids, grad_rows, vocab_count, offset):
    block_rows = min(512, token_ids.shape[0])
    columns = offset + jnp.arange(vocab_count)

    def one_block(running, inputs):
        id_block, grad_block = inputs
        one_hot = (id_block[:, None] == columns[None, :]).astype(jnp.bfloat16)
        return (running + dot_first(one_hot, grad_block), None)

    initial = jnp.zeros((vocab_count, grad_rows.shape[1]), jnp.float32)
    summed, _ = lax.scan(
        one_block,
        initial,
        (token_ids.reshape(-1, block_rows), grad_rows.reshape(-1, block_rows, grad_rows.shape[1])),
    )
    return summed


def combine_stats(earlier, later):
    row_top = jnp.maximum(earlier[0], later[0])
    row_total = earlier[1] * jnp.exp(earlier[0] - row_top) + later[1] * jnp.exp(later[0] - row_top)
    return (row_top, row_total, earlier[2] + later[2])


def adam_direction(moment, second):
    return moment / (1.0 - beta_one**STEP) / (jnp.sqrt(second / (1.0 - beta_two**STEP)) + adam_eps)


def adam_update(weight, grad_item, moment, second, step_rate, decay_weight):
    moment = beta_one * moment + (1.0 - beta_one) * grad_item
    second = beta_two * second + (1.0 - beta_two) * grad_item * grad_item
    return (
        weight - step_rate * (adam_direction(moment, second) + decay_weight * weight),
        moment,
        second,
    )


def renew_basis(statistic, soap_basis):
    product = jnp.einsum("mde,mef->mdf", statistic, soap_basis, precision=highest)
    gram_matrix = jnp.einsum("mdf,mdg->mfg", product, product, precision=highest)
    factor = jnp.linalg.cholesky(gram_matrix)

    def solve_one(lower_factor, product_one):
        return jax.scipy.linalg.solve_triangular(lower_factor, product_one.T, lower=True)

    return jnp.swapaxes(jax.vmap(solve_one)(factor, product), 1, 2)


def body(
    src_ids,
    src_seg,
    tgt_ids,
    tgt_seg,
    pick_pos,
    pick_label,
    attn_w,
    attn_m,
    attn_v,
    ffn_w,
    ffn_m,
    ffn_v,
    soap_basis,
    soap_stats,
    norm_p,
    norm_m,
    norm_v,
    embedding,
    embed_m,
    embed_v,
):
    w_attn, w_ffn, norm_low, table_low = (
        lax.all_gather(attn_w.astype(jnp.bfloat16), "dp", axis=1, tiled=True),
        lax.all_gather(ffn_w.astype(jnp.bfloat16), "dp", axis=1, tiled=True),
        lax.all_gather(norm_p.astype(jnp.bfloat16), "dp", axis=1, tiled=True),
        lax.all_gather(embedding.astype(jnp.bfloat16), "dp", axis=1, tiled=True),
    )
    norm_rows = norm_low.astype(jnp.float32)
    vocab_count, model_width = table_low.shape
    offset = lax.axis_index("vocab") * vocab_count
    source, source_seg, target, target_seg = (src_ids[0], src_seg[0], tgt_ids[0], tgt_seg[0])
    pick_rows, labels = (pick_pos[0], pick_label[0])
    length = source.shape[0]
    embed_scale = math.sqrt(model_width)
    start = 0
    source_sum, target_sum = (
        lax.psum(lookup(source, table_low, offset).astype(jnp.bfloat16), "vocab").astype(
            jnp.float32
        ),
        lax.psum(lookup(target, table_low, offset).astype(jnp.bfloat16), "vocab").astype(
            jnp.float32
        ),
    )
    positional = sinusoid(length, model_width)
    pullbacks = [None] * 7
    gain_grads = [None] * 7
    bias_grads = [None] * 7

    def normalize(values, index):
        normed, pullbacks[index] = jax.vjp(
            layer_norm, values, norm_rows[index], norm_rows[7 + index]
        )
        return normed

    def normalize_back(grad_out, index):
        grad_in, gain_grads[index], bias_grads[index] = pullbacks[index](grad_out)
        return grad_in

    residual = source_sum * embed_scale + positional
    normed = normalize(residual, 0).astype(jnp.bfloat16)
    branch, enc_attn = attn_forward(
        normed, normed, w_attn[0:4], source_seg, source_seg, False, start
    )
    residual = residual + branch
    normed = normalize(residual, 1).astype(jnp.bfloat16)
    branch, enc_ffn = ffn_forward(normed, w_ffn[0], w_ffn[1])
    residual = residual + branch
    encoded = normalize(residual, 2).astype(jnp.bfloat16)
    residual = target_sum * embed_scale + positional
    normed = normalize(residual, 3).astype(jnp.bfloat16)
    branch, dec_self = attn_forward(
        normed, normed, w_attn[4:8], target_seg, target_seg, True, start
    )
    residual = residual + branch
    normed = normalize(residual, 4).astype(jnp.bfloat16)
    branch, dec_cross = attn_forward(
        normed, encoded, w_attn[8:12], target_seg, source_seg, False, start
    )
    residual = residual + branch
    normed = normalize(residual, 5).astype(jnp.bfloat16)
    branch, dec_ffn = ffn_forward(normed, w_ffn[2], w_ffn[3])
    residual = residual + branch
    final_out = normalize(residual, 6)
    inside = (pick_rows >= start) & (pick_rows < start + length)
    local_rows = jnp.where(inside, pick_rows - start, 0)
    picked = jnp.take(final_out, pick_rows, axis=0).astype(jnp.bfloat16)
    logits = dot_last(picked, table_low)
    row_top = jnp.max(logits, axis=-1)
    row_total = jnp.sum(jnp.exp(logits - row_top[:, None]), axis=-1)
    label_hit = labels[:, None] == offset + jnp.arange(vocab_count)[None, :]
    chosen = jnp.sum(jnp.where(label_hit, logits, 0.0), axis=-1)
    row_top, row_total, chosen = combined_all((row_top, row_total, chosen), "vocab", combine_stats)
    log_total = row_top + jnp.log(row_total)
    weight = 1.0 / pick_weights(target_seg, pick_rows)
    loss_part = jnp.sum((log_total - chosen) * weight)
    count_part = (target_seg[-1] + 1).astype(jnp.float32)
    grad_logits = (
        weight[:, None] * (jnp.exp(logits - log_total[:, None]) - label_hit.astype(jnp.float32))
    ).astype(jnp.bfloat16)
    grad_picked = lax.psum(dot_plain(grad_logits, table_low), "vocab")
    grad_table = dot_first(grad_logits, picked)
    scatter_rows = jnp.where(inside, local_rows, length)
    grad_final = (
        jnp.zeros((length, model_width), jnp.float32).at[scatter_rows].add(grad_picked, mode="drop")
    )
    grad_res = normalize_back(grad_final, 6)
    dec_in, dec_out, grad_normed = ffn_backward(grad_res, dec_ffn)
    grad_res = grad_res + normalize_back(grad_normed, 5)
    cross_grads, grad_query_in, grad_encoded = attn_backward(grad_res, dec_cross)
    grad_res = grad_res + normalize_back(grad_query_in, 4)
    self_grads, grad_query_in, grad_key_in = attn_backward(grad_res, dec_self)
    grad_res = grad_res + normalize_back(grad_query_in + grad_key_in, 3)
    grad_target = (grad_res * embed_scale).astype(jnp.bfloat16)
    grad_res = normalize_back(grad_encoded, 2)
    enc_in, enc_out, grad_normed = ffn_backward(grad_res, enc_ffn)
    grad_res = grad_res + normalize_back(grad_normed, 1)
    enc_grads, grad_query_in, grad_key_in = attn_backward(grad_res, enc_attn)
    grad_res = grad_res + normalize_back(grad_query_in + grad_key_in, 0)
    grad_source = (grad_res * embed_scale).astype(jnp.bfloat16)
    grad_table = (
        grad_table
        + lookup_back(source, grad_source, vocab_count, offset)
        + lookup_back(target, grad_target, vocab_count, offset)
    )
    attn_grad = jnp.concatenate([enc_grads, self_grads, cross_grads], axis=0)
    ffn_grad = jnp.stack([enc_in, enc_out, dec_in, dec_out])
    norm_grad = jnp.concatenate([jnp.stack(gain_grads), jnp.stack(bias_grads)], axis=0)
    g_attn, g_ffn, g_norm, g_embed = (
        lax.psum_scatter(attn_grad, "dp", scatter_dimension=1, tiled=True),
        lax.psum_scatter(ffn_grad, "dp", scatter_dimension=1, tiled=True),
        lax.psum_scatter(norm_grad, "dp", scatter_dimension=1, tiled=True),
        lax.psum_scatter(grad_table, "dp", scatter_dimension=1, tiled=True),
    )
    first_copy = (lax.axis_index("vocab") == 0).astype(jnp.float32)
    layer_sq = jnp.sum(g_attn * g_attn) + jnp.sum(g_ffn * g_ffn) + jnp.sum(g_norm * g_norm)
    raw_squares = jnp.sum(g_embed * g_embed) + first_copy * layer_sq
    loss_sum, sentences, squares = lax.psum(
        (first_copy * loss_part, first_copy * count_part, raw_squares), ("dp", "vocab")
    )
    g_attn, g_ffn, g_norm, g_embed = (
        g_attn / sentences,
        g_ffn / sentences,
        g_norm / sentences,
        g_embed / sentences,
    )
    grad_norm = jnp.sqrt(squares) / sentences
    clip_factor = jnp.minimum(1.0, clip_limit / (grad_norm + norm_eps))
    g_attn, g_ffn, g_norm, g_embed = (
        g_attn * clip_factor,
        g_ffn * clip_factor,
        g_norm * clip_factor,
        g_embed * clip_factor,
    )
    new_attn, m_attn, v_attn = adam_update(attn_w, g_attn, attn_m, attn_v, rate_matrix, decay_rate)
    new_norm, m_norm, v_norm = adam_update(norm_p, g_norm, norm_m, norm_v, rate_vector, 0.0)
    new_embed, m_embed, v_embed = adam_update(
        embedding, g_embed, embed_m, embed_v, rate_matrix, decay_rate
    )
    rotated = jnp.einsum("mfd,mde->mfe", g_ffn, soap_basis, precision=highest)
    m_ffn = beta_one * ffn_m + (1.0 - beta_one) * rotated
    v_ffn = beta_two * ffn_v + (1.0 - beta_two) * rotated * rotated
    back_rotated = jnp.einsum(
        "mfe,mde->mfd", adam_direction(m_ffn, v_ffn), soap_basis, precision=highest
    )
    new_ffn = ffn_w - rate_matrix * (back_rotated + decay_rate * ffn_w)
    stat_part = jnp.einsum("mfd,mfe->mde", g_ffn, g_ffn, precision=highest)
    new_stats = stat_decay * soap_stats + (1.0 - stat_decay) * lax.psum(stat_part, "dp")
    new_basis = renew_basis(new_stats, soap_basis)
    return (
        loss_sum,
        sentences,
        grad_norm,
        new_attn,
        m_attn,
        v_attn,
        new_ffn,
        m_ffn,
        v_ffn,
        new_basis,
        new_stats,
        new_norm,
        m_norm,
        v_norm,
        new_embed,
        m_embed,
        v_embed,
    )


def solution(mesh):
    placed = (
        P("dp", None),
        P("dp", None),
        P("dp", None),
        P("dp", None),
        P("dp", None),
        P("dp", None),
        P(None, "dp", None),
        P(None, "dp", None),
        P(None, "dp", None),
        P(None, "dp", None),
        P(None, "dp", None),
        P(None, "dp", None),
        P(),
        P(),
        P(None, "dp"),
        P(None, "dp"),
        P(None, "dp"),
        P("vocab", "dp"),
        P("vocab", "dp"),
        P("vocab", "dp"),
    )
    return jax.shard_map(
        body,
        mesh=mesh,
        in_specs=placed,
        out_specs=(
            P(),
            P(),
            P(),
            P(None, "dp", None),
            P(None, "dp", None),
            P(None, "dp", None),
            P(None, "dp", None),
            P(None, "dp", None),
            P(None, "dp", None),
            P(),
            P(),
            P(None, "dp"),
            P(None, "dp"),
            P(None, "dp"),
            P("vocab", "dp"),
            P("vocab", "dp"),
            P("vocab", "dp"),
        ),
        check_vma=False,
    )
```

profile of v0, /device:TPU:0, one launch (start us, length us, event | category | flops | bytes accessed | tf_op | source)
XLA Modules:
  0.0 2090.9 jit_solution(11112402972196352083)
XLA Ops:
  12.1 59.1 %all-gather.10.cloned.1.call-done = bf16[4736,512]{1,0:T(8,128)(2,1)} async-done(((bf16[4736,128]{1,0:T(8,128)(2,1)}), bf16[4736,512]{1,0:T(8,128)(2,1)}) %all-gather.10.cloned.1.call-update) | async-done | bytes 4849680 | tf_op jit(solution)/shard_map/all_gather | solution.py:325
  127.1 32.9 %all-reduce.11.cloned.1.call-done = (bf16[1024,512]{1,0:T(8,128)(2,1)}, bf16[1024,512]{1,0:T(8,128)(2,1)}) async-done(((bf16[1024,512]{1,0:T(8,128)(2,1)}, bf16[1024,512]{1,0:T(8,128)(2,1)}), (bf16[1024,512]{1,0:T(8,128)(2,1)}, bf16[1024,512]{1,0:T(8,128)(2,1)})) %all-reduce.11.cloned.1.call-update) | async-done | bytes 2097168 | tf_op jit(solution)/shard_map/psum | solution.py:339
  166.0 66.3 %all-gather.12.cloned.1.call-done = bf16[12,512,512]{2,1,0:T(8,128)(2,1)} async-done(((bf16[12,128,512]{2,1,0:T(8,128)(2,1)}), bf16[12,512,512]{2,1,0:T(8,128)(2,1)}) %all-gather.12.cloned.1.call-update) | async-done | bytes 6291472 | tf_op jit(solution)/shard_map/all_gather | solution.py:322
  242.0 27.9 %while.151 = (s32[]{:T(128)}, bf16[2,512,8,64]{1,3,2,0:T(8,128)(2,1)}, f32[2,8,512,1]{2,1,3,0:T(8,128)S(1)}, f32[2,8,512,1]{2,1,3,0:T(8,128)S(1)}, bf16[2,512,8,...) while((s32[]{:T(128)}, ...), condition=%wide.region_8.9_spmd, body=%wide.region_5.0_spmd.sunk | while | flops 1126162432 | bytes 70942912 | solution.py:110
  288.9 26.9 %while.152 = (s32[]{:T(128)}, bf16[2,512,8,64]{1,3,2,0:T(8,128)(2,1)}, f32[2,8,512,1]{2,1,3,0:T(8,128)S(1)}, f32[2,8,512,1]{2,1,3,0:T(8,128)S(1)}, bf16[2,512,8,...) while((s32[]{:T(128)}, ...), condition=%wide.region_19.20_spmd, body=%wide.region_16.19_spmd.sunk | while | flops 1125113856 | bytes 70936760 | solution.py:110
  357.1 27.2 %while.153 = (s32[]{:T(128)}, bf16[2,512,8,64]{1,3,2,0:T(8,128)(2,1)}, f32[2,8,512,1]{2,1,3,0:T(8,128)S(1)}, f32[2,8,512,1]{2,1,3,0:T(8,128)S(1)}, bf16[2,512,8,...) while((s32[]{:T(128)}, ...), condition=%wide.region_27.28_spmd, body=%wide.region_24.27_spmd.sunk | while | flops 1125113856 | bytes 70936760 | solution.py:110
  450.3 53.4 %all-reduce.7.cloned.1.call-done = f32[256,512]{1,0:T(8,128)} async-done(((f32[256,512]{1,0:T(8,128)}), f32[256,512]{1,0:T(8,128)}) %all-reduce.7.cloned.1.call-update) | async-done | bytes 524304 | tf_op jit(solution)/shard_map/psum | solution.py:399
  543.0 98.2 %while.158 = (s32[]{:T(128)}, f32[1024,8,64]{0,2,1:T(8,128)S(1)}, f32[1024,8,64]{0,2,1:T(8,128)}, bf16[2,512,8,64]{1,3,2,0:T(8,128)(2,1)}, bf16[2,512,8,64]{1,3,...) while((s32[]{:T(128)}, f32[1024,8,64]{0,2,1:T(8,128)S(1)}, ...), condition=%wide.region_49.50_spmd.clone, body=%wide.region_47.49_spmd.clone.sunk | while | flops 2730225664 | bytes 182593920 | solution.py:193
  553.8 14.4 multiply_reduce_fusion.32
  602.6 14.4 multiply_reduce_fusion.32
  671.9 98.0 %while.161 = (s32[]{:T(128)}, f32[1024,8,64]{0,2,1:T(8,128)S(1)}, f32[1024,8,64]{0,2,1:T(8,128)}, bf16[2,512,8,64]{1,3,2,0:T(8,128)(2,1)}, bf16[2,512,8,64]{1,3,...) while((s32[]{:T(128)}, f32[1024,8,64]{0,2,1:T(8,128)S(1)}, ...), condition=%wide.region_65.66_spmd.clone, body=%wide.region_63.65_spmd.clone.sunk | while | flops 2731274240 | bytes 182600080 | solution.py:193
  682.7 14.4 multiply_reduce_fusion.34
  731.5 14.4 multiply_reduce_fusion.34
  810.9 98.0 %while.159 = (s32[]{:T(128)}, f32[1024,8,64]{0,2,1:T(8,128)S(1)}, f32[1024,8,64]{0,2,1:T(8,128)}, bf16[2,512,8,64]{1,3,2,0:T(8,128)(2,1)}, bf16[2,512,8,64]{1,3,...) while((s32[]{:T(128)}, f32[1024,8,64]{0,2,1:T(8,128)S(1)}, ...), condition=%wide.region_56.57_spmd.clone, body=%wide.region_54.56_spmd.clone.sunk | while | flops 2730225664 | bytes 182593920 | solution.py:193
  821.8 14.4 multiply_reduce_fusion.33
  870.5 14.4 multiply_reduce_fusion.33
  927.5 18.5 while.162
  947.9 18.6 while.160
  1032.0 43.2 %reduce-scatter.5.cloned.1.call-done = f32[4736,128]{1,0:T(8,128)} async-done(((f32[4736,512]{1,0:T(8,128)}), f32[4736,128]{1,0:T(8,128)}) %reduce-scatter.5.cloned.1.call-update) | async-done | bytes 2424848 | tf_op jit(solution)/shard_map/reduce_scatter | solution.py:431
  1078.2 121.2 %reduce-scatter.7.cloned.1.call-done = f32[12,128,512]{2,1,0:T(8,128)} async-done(((f32[12,512,512]{2,1,0:T(8,128)}), f32[12,128,512]{2,1,0:T(8,128)}) %reduce-scatter.7.cloned.1.call-update) | async-done | bytes 3145744 | tf_op jit(solution)/shard_map/reduce_scatter | solution.py:428
  1202.7 153.9 %reduce-scatter.9.cloned.1.call-done = f32[4,512,512]{2,1,0:T(8,128)} async-done(((f32[4,2048,512]{2,1,0:T(8,128)}), f32[4,512,512]{2,1,0:T(8,128)}) %reduce-scatter.9.cloned.1.call-update) | async-done | bytes 4194320 | tf_op jit(solution)/shard_map/reduce_scatter | solution.py:429
  1363.1 39.4 %all-reduce.1 = (f32[]{:T(128)}, f32[]{:T(128)}, f32[]{:T(128)}) all-reduce(f32[]{:T(128)S(6)} %mul.898, f32[]{:T(128)S(6)} %mul.899, f32[]{:T(128)S(6)} %add.642), channel_id=1, replica_groups=mesh['dp'=4,'vocab'=8] {'dp','vocab'}, use_global_device_ids=true, to_apply=%region_39.40 | all-reduce | flops 3 | bytes 24 | tf_op jit(solution)/shard_map/psum | solution.py:436
  1417.0 16.6 multiply_add_fusion.5
  1460.9 60.8 %all-reduce.9.cloned.1.call-done = f32[4,512,512]{2,1,0:T(8,128)} async-done(((f32[4,512,512]{2,1,0:T(8,128)}), f32[4,512,512]{2,1,0:T(8,128)}) %all-reduce.9.cloned.1.call-update) | async-done | bytes 4194320 | tf_op jit(solution)/shard_map/psum | solution.py:466
  1555.9 46.9 %custom-call.35 = f32[4,128,128]{2,1,0:T(8,128)S(1)} custom-call(f32[4,128,128]{2,1,0:T(8,128)S(1)} %cholesky.274), custom_call_target="Cholesky" | custom-call | tf_op jit(solution)/shard_map/jit(cholesky)/cholesky | solution.py:291
  1602.8 39.5 %custom-call.36 = f32[4,1,128,128]{2,3,1,0:T(8,128)S(1)} custom-call(f32[4,1,128,128]{3,2,1,0:T(8,128)S(1)} %select_bitcast_fusion.2), custom_call_target="InvertDiagBlocksLowerTriangular" | custom-call | tf_op jit(solution)/shard_map/jit(cholesky)/cholesky | solution.py:291
  1649.9 46.9 %custom-call.37 = f32[4,128,128]{2,1,0:T(8,128)S(1)} custom-call(f32[4,128,128]{2,1,0:T(8,128)S(1)} %cholesky.278), custom_call_target="Cholesky" | custom-call | tf_op jit(solution)/shard_map/jit(cholesky)/cholesky | solution.py:291
  1697.6 39.3 %custom-call.38 = f32[4,1,128,128]{2,3,1,0:T(8,128)S(1)} custom-call(f32[4,1,128,128]{3,2,1,0:T(8,128)S(1)} %get-tuple-element.1578), custom_call_target="InvertDiagBlocksLowerTriangular" | custom-call | tf_op jit(solution)/shard_map/jit(cholesky)/cholesky | solution.py:291
  1741.0 47.3 %custom-call.39 = f32[4,128,128]{2,1,0:T(8,128)S(1)} custom-call(f32[4,128,128]{2,1,0:T(8,128)S(1)} %cholesky.283), custom_call_target="Cholesky" | custom-call | tf_op jit(solution)/shard_map/jit(cholesky)/cholesky | solution.py:291
  1789.0 39.3 %custom-call.40 = f32[4,1,128,128]{2,3,1,0:T(8,128)S(1)} custom-call(f32[4,1,128,128]{3,2,1,0:T(8,128)S(1)} %get-tuple-element.1576), custom_call_target="InvertDiagBlocksLowerTriangular" | custom-call | tf_op jit(solution)/shard_map/jit(cholesky)/cholesky | solution.py:291
  1832.1 46.9 %custom-call.41 = f32[4,128,128]{2,1,0:T(8,128)S(1)} custom-call(f32[4,128,128]{2,1,0:T(8,128)S(1)} %convolution_subtract_fusion.3), custom_call_target="Cholesky" | custom-call | tf_op jit(solution)/shard_map/jit(cholesky)/cholesky | solution.py:291
  1897.6 157.4 %custom-call.42 = f32[4,4,128,128]{2,3,1,0:T(8,128)S(1)} custom-call(f32[4,4,128,128]{3,2,1,0:T(8,128)S(1)} %bitcast.837), custom_call_target="InvertDiagBlocksLowerTriangular" | custom-call | tf_op jit(solution)/shard_map/vmap(jit(_solve_triangular))/triangular_solve | solution.py:294
  (1000 shorter events, 900.5 us)
Async XLA Ops:
  7.2 64.0 %all-gather.10.cloned.1.call-start = ((), (), s32[]{:S(2)}) async-start(), calls=%async_computation.4 | async-start | bytes 6062080 | tf_op jit(solution)/shard_map/all_gather | solution.py:325
  10.1 149.9 %all-reduce.11.cloned.1.call-start = ((), (), s32[]{:S(2)}) async-start(), calls=%async_computation.13 | async-start | bytes 4194304 | tf_op jit(solution)/shard_map/psum | solution.py:339
  83.0 12.2 copy-start.67
  95.1 137.2 %all-gather.12.cloned.1.call-start = ((), (), s32[]{:S(2)}) async-start(), calls=%async_computation.5 | async-start | bytes 7864320 | tf_op jit(solution)/shard_map/all_gather | solution.py:322
  96.6 242.0 %all-gather.14.cloned.1.call-start = ((), (), s32[]{:S(2)}) async-start(), calls=%async_computation.6 | async-start | bytes 10485760 | tf_op jit(solution)/shard_map/all_gather | solution.py:323
  100.4 403.3 %all-reduce.7.cloned.1.call-start = ((), (), s32[]{:S(2)}) async-start(), calls=%async_computation.7 | async-start | bytes 1048576 | tf_op jit(solution)/shard_map/psum | solution.py:399
  114.2 49.9 %copy-start.192 = (f32[1,512]{1,0:T(1,128)}, f32[1,512]{1,0:T(1,128)S(1)}, u32[]{:S(2)}) copy-start(f32[1,512]{1,0:T(1,128)S(1)} %get-tuple-element.1588) | copy-start | bytes 6148
  114.2 51.3 %copy-start.194 = (f32[1,512]{1,0:T(1,128)}, f32[1,512]{1,0:T(1,128)S(1)}, u32[]{:S(2)}) copy-start(f32[1,512]{1,0:T(1,128)S(1)} %get-tuple-element.1592) | copy-start | bytes 6148
  166.0 66.3 %copy-start.126 = (bf16[1024,512]{1,0:T(8,128)(2,1)}, bf16[1024,512]{1,0:T(8,128)(2,1)S(1)}, u32[]{:S(2)}) copy-start(bf16[1024,512]{1,0:T(8,128)(2,1)S(1)} %add_convert_fusion.5) | copy-start | bytes 3145732
  389.8 139.6 %copy-start.184 = (f32[1024]{0:T(1024)}, f32[1024]{0:T(1024)S(1)}, u32[]{:S(2)}) copy-start(f32[1024]{0:T(1024)S(1)} %broadcast_multiply_fusion.1) | copy-start | bytes 12292
  390.2 139.1 %copy-start.210 = (f32[1024]{0:T(1024)}, f32[1024]{0:T(1024)S(1)}, u32[]{:S(2)}) copy-start(f32[1024]{0:T(1024)S(1)} %fusion.249) | copy-start | bytes 12292
  404.6 35.1 %copy-start.235 = (f32[256]{0:T(256)S(1)}, f32[256]{0:T(256)}, u32[]{:S(2)}) copy-start(f32[256]{0:T(256)} %convert_reduce_fusion) | copy-start | bytes 3076
  450.1 580.6 %reduce-scatter.11.cloned.1.call-start = ((), (), s32[]{:S(2)}) async-start(), calls=%async_computation.11 | async-start | bytes 40960 | tf_op jit(solution)/shard_map/reduce_scatter | solution.py:430
  512.4 17.9 copy-start.80
  512.4 17.9 copy-start.200
  925.5 149.7 %reduce-scatter.5.cloned.1.call-start = ((), (), s32[]{:S(2)}) async-start(), calls=%async_computation.8 | async-start | bytes 12124160 | tf_op jit(solution)/shard_map/reduce_scatter | solution.py:431
  927.5 18.5 copy-start.46
  947.9 18.6 copy-start.121
  947.9 18.6 copy-start.198
  979.0 220.4 %reduce-scatter.7.cloned.1.call-start = ((), (), s32[]{:S(2)}) async-start(), calls=%async_computation.9 | async-start | bytes 15728640 | tf_op jit(solution)/shard_map/reduce_scatter | solution.py:428
  1002.4 354.2 %reduce-scatter.9.cloned.1.call-start = ((), (), s32[]{:S(2)}) async-start(), calls=%async_computation.10 | async-start | bytes 20971520 | tf_op jit(solution)/shard_map/reduce_scatter | solution.py:429
  1027.7 493.9 %all-reduce.9.cloned.1.call-start = ((), (), s32[]{:S(2)}) async-start(), calls=%async_computation.12 | async-start | bytes 8388608 | tf_op jit(solution)/shard_map/psum | solution.py:466
  1416.9 16.6 copy-start.190
  1416.9 16.6 copy-start.191
  1416.9 16.6 copy-start.228
  1416.9 16.6 copy-start.229
  1417.0 18.6 copy-start.85
  1417.0 18.6 copy-start.98
  1435.6 13.2 copy-start.68
  1435.6 13.2 copy-start.69
  1435.6 13.2 copy-start.116
  1435.6 13.2 copy-start.117
  (264 other events, 1227.5 us)
Sparse Core Ops, SparseCore 0:
  10.4 60.7 all-gather.9
  95.2 64.7 all-reduce.10
  162.5 69.7 all-gather.11
  234.6 87.6 all-gather.13
  450.3 53.4 all-reduce.6
  925.7 21.4 reduce-scatter.10
  979.1 96.0 reduce-scatter.4
  1078.6 120.6 reduce-scatter.6
  1202.8 153.8 reduce-scatter.8
  1417.0 104.6 all-reduce.8
where the time goes:
time: 2100 us; the launch traced here: 2090 us
  other arithmetic  665 us (32%)
  waiting for transfers between devices  591 us (28%)
  matrix products  580 us (28%)
  local copies, waits for them, and re-layouts  146 us (7%)
  blocking collectives  77.8 us (4%)
  between operations  24.3 us (1%)
    another operation x18, other arithmetic, renew_basis(): factor = jnp.linalg.cholesky(gram_matrix)  309 us
    another operation x4, other arithmetic, solve_one(): jax.scipy.linalg.solve_triangular(lower_factor, product_one.T, lower=True)  162 us
    reduce_scatter x1, waiting for transfers between devices, body(): lax.psum_scatter(ffn_grad, 'dp', scatter_dimension=1, tiled=True)  154 us
    reduce_scatter x1, waiting for transfers between devices, body(): lax.psum_scatter(attn_grad, 'dp', scatter_dimension=1, tiled=True)  121 us
    dot_general x12, matrix products, block_scores(): jnp.einsum('qhd,khd->hqk', query_part, key_heads, preferred_element_type=...  103 us
    dot_general x21, matrix products, dot_first(): lax.dot_general(left, right, (((0,), (0,)), ((), ())), preferred_element_...  90.2 us
    dot_general x21, matrix products, dot_plain(): return jnp.dot(left, right, preferred_element_type=jnp.float32)  71.7 us
    convert_element_type x6, other arithmetic, one_block(): (softmax_rows * (grad_softmax - row_inner)).astype(jnp.bfloat16)  68.9 us
  transfers between devices with their start and end apart: 10, of which 8 were waited for; matrix products, arithmetic and copies ran while one was open for 13% of the time, Pallas kernels for 0%

commit v1 on v0

v1 whole, which is shorter than its diff:
```python
from functools import partial
import math

import jax
import jax.numpy as jnp
import numpy as np
from jax import lax
from jax.experimental import pallas as pl
from jax.experimental.pallas import tpu as pltpu
from jax.sharding import PartitionSpec as P

HEADS = 8
STEP = 10
TILE = 128

highest = lax.Precision.HIGHEST
beta_one = 0.9
beta_two = 0.999
adam_eps = 1e-08
decay_rate = 0.01
rate_matrix = 0.03
rate_vector = 0.3
clip_limit = 1.0
stat_decay = 0.95
norm_eps = 1e-06
masked = -1e30
log_two_e = math.log2(math.e)
vmem = pl.BlockSpec(memory_space=pltpu.VMEM)
smem = pl.BlockSpec(memory_space=pltpu.SMEM)


def dot_dims(left, right, left_dim, right_dim):
    return lax.dot_general(
        left, right, (((left_dim,), (right_dim,)), ((), ())), preferred_element_type=jnp.float32
    )


def dot_exact(left, right, left_dim, right_dim):
    return lax.dot_general(
        left,
        right,
        (((left_dim,), (right_dim,)), ((), ())),
        precision=highest,
        preferred_element_type=jnp.float32,
    )


def call(kernel, outs, *args, scratch=(), smem_args=0):
    return pl.pallas_call(
        kernel,
        out_shape=outs,
        in_specs=[vmem] * (len(args) - smem_args) + [smem] * smem_args,
        out_specs=jax.tree.map(lambda _: vmem, outs),
        scratch_shapes=list(scratch),
        compiler_params=pltpu.CompilerParams(vmem_limit_bytes=56 * 2**20),
    )(*args)


def low(*shape):
    return jax.ShapeDtypeStruct(shape, jnp.bfloat16)


def full(*shape):
    return jax.ShapeDtypeStruct(shape, jnp.float32)


def norm_parts(values):
    centre = values - jnp.mean(values, axis=-1, keepdims=True)
    spread = jnp.mean(centre * centre, axis=-1, keepdims=True)
    root = lax.rsqrt(spread + norm_eps)
    return centre * root, root


def norm_forward(values, ln_ref):
    return norm_parts(values)[0] * ln_ref[0:1, :] + ln_ref[1:2, :]


def norm_backward(grad, values, ln_ref, ln_grad_ref):
    normed, root = norm_parts(values)
    ln_grad_ref[0:1, :] = jnp.sum(grad * normed, axis=0, keepdims=True)
    ln_grad_ref[1:2, :] = jnp.sum(grad, axis=0, keepdims=True)
    inner = grad * ln_ref[0:1, :]
    return root * (
        inner
        - jnp.mean(inner, axis=-1, keepdims=True)
        - normed * jnp.mean(inner * normed, axis=-1, keepdims=True)
    )


def at_tile(index):
    return pl.ds(pl.multiple_of(index * TILE, TILE), TILE)


def tile_mask(segq_ref, segk_ref, qi, ki, causal):
    allowed = segk_ref[at_tile(ki), :] == segq_ref[:, at_tile(qi)]
    if causal:
        ahead = lax.broadcasted_iota(jnp.int32, (TILE, TILE), 0) - lax.broadcasted_iota(
            jnp.int32, (TILE, TILE), 1
        )
        allowed = allowed & (ahead <= (qi - ki) * TILE)
    return allowed


def for_tiles(count, edge_ref, causal, step):
    def one(pair, carry):
        qi, ki = pair // count, lax.rem(pair, count)
        live = (edge_ref[0, qi] <= edge_ref[3, ki]) & (edge_ref[2, ki] <= edge_ref[1, qi])
        if causal:
            live = live & (ki <= qi)

        @pl.when(live)
        def _():
            step(qi, ki)

        return carry

    lax.fori_loop(0, count * count, one, 0)


def tile_edges(seg_q, seg_k):
    last = TILE - 1
    return jnp.stack([seg_q[::TILE], seg_q[last::TILE], seg_k[::TILE], seg_k[last::TILE]])


def attn_forward_kernel(causal, cross, *refs):
    refs = list(refs)
    x_ref, ln_ref, w_ref, segq_ref, segk_ref = refs[:5]
    refs = refs[5:]
    key_ref = refs.pop(0) if cross else None
    (edge_ref, out_ref, a_ref, qt_ref, kt_ref, vt_ref, ot_ref, lse_ref, top_ref, sum_ref, acc_ref) = refs
    length, width = x_ref.shape
    head_size = width // HEADS
    a_ref[...] = norm_forward(x_ref[...], ln_ref).astype(jnp.bfloat16)
    key_in = key_ref if cross else a_ref
    qt_ref[...] = dot_dims(a_ref[...], w_ref[0], 1, 0).astype(jnp.bfloat16).T
    kt_ref[...] = dot_dims(key_in[...], w_ref[1], 1, 0).astype(jnp.bfloat16).T
    vt_ref[...] = dot_dims(key_in[...], w_ref[2], 1, 0).astype(jnp.bfloat16).T
    top_ref[...] = jnp.full(top_ref.shape, masked, jnp.float32)
    sum_ref[...] = jnp.zeros(sum_ref.shape, jnp.float32)
    acc_ref[...] = jnp.zeros(acc_ref.shape, jnp.float32)
    scale = log_two_e / math.sqrt(head_size)
    bands = [slice(h * head_size, (h + 1) * head_size) for h in range(HEADS)]

    def step(qi, ki):
        q_at, k_at = at_tile(qi), at_tile(ki)
        allowed = tile_mask(segq_ref, segk_ref, qi, ki, causal)
        scores = [dot_dims(kt_ref[band, k_at], qt_ref[band, q_at], 0, 0) * scale for band in bands]
        scores = [jnp.where(allowed, part, masked) for part in scores]
        top = top_ref[:, q_at]
        new_top = jnp.maximum(
            top,
            jnp.concatenate([jnp.max(part, axis=0, keepdims=True) for part in scores], axis=0),
        )
        fade = jnp.exp2(top - new_top)
        parts = [jnp.exp2(scores[h] - new_top[h : h + 1]) for h in range(HEADS)]
        top_ref[:, q_at] = new_top
        sum_ref[:, q_at] = sum_ref[:, q_at] * fade + jnp.concatenate(
            [jnp.sum(part, axis=0, keepdims=True) for part in parts], axis=0
        )
        mixed = [
            dot_dims(vt_ref[bands[h], k_at], parts[h].astype(jnp.bfloat16), 1, 0)
            for h in range(HEADS)
        ]
        acc = acc_ref[:, q_at]
        acc_ref[:, q_at] = jnp.concatenate(
            [acc[bands[h]] * fade[h : h + 1] + mixed[h] for h in range(HEADS)], axis=0
        )

    for_tiles(length // TILE, edge_ref, causal, step)
    lse_ref[...] = top_ref[...] + jnp.log2(sum_ref[...])
    for h in range(HEADS):
        ot_ref[bands[h], :] = (acc_ref[bands[h], :] / sum_ref[h : h + 1, :]).astype(jnp.bfloat16)
    out_ref[...] = x_ref[...] + dot_dims(ot_ref[...], w_ref[3], 0, 0)


def attn_forward(x, ln, weights, seg_q, seg_k, key_in, causal):
    length, width = x.shape
    cross = key_in is not None
    segs = (seg_q[None, :], jnp.broadcast_to(seg_k[:, None], (length, TILE)))
    edges = tile_edges(seg_q, seg_k)
    args = (x, ln, weights, *segs) + ((key_in,) if cross else ()) + (edges,)
    outs = (full(length, width), low(length, width)) + (low(width, length),) * 4
    out, normed, *stored = call(
        partial(attn_forward_kernel, causal, cross),
        outs + (full(HEADS, length),),
        *args,
        scratch=[
            pltpu.VMEM((HEADS, length), jnp.float32),
            pltpu.VMEM((HEADS, length), jnp.float32),
            pltpu.VMEM((width, length), jnp.float32),
        ],
        smem_args=1,
    )
    return out, (x, ln, weights, segs, edges, causal, cross, normed, stored)


def attn_backward_kernel(causal, cross, *refs):
    (g_ref, x_ref, ln_ref, w_ref, segq_ref, segk_ref, qt_ref, kt_ref, vt_ref, ot_ref, lse_ref) = refs[:11]
    refs = list(refs[11:])
    edge_ref, out_ref, ln_grad_ref, low_ref, gq_ref, gk_ref, gv_ref = refs[:7]
    refs = refs[7:]
    key_grad_ref = refs.pop(0) if cross else None
    got_ref, delta_ref, gqt_ref, gkt_ref, gvt_ref = refs
    length, width = x_ref.shape
    head_size = width // HEADS
    low_ref[...] = g_ref[...].astype(jnp.bfloat16)
    got_ref[...] = dot_dims(low_ref[...], w_ref[3], 1, 1).astype(jnp.bfloat16).T
    bands = [slice(h * head_size, (h + 1) * head_size) for h in range(HEADS)]
    for h in range(HEADS):
        delta_ref[h : h + 1, :] = jnp.sum(
            got_ref[bands[h], :].astype(jnp.float32) * ot_ref[bands[h], :].astype(jnp.float32),
            axis=0,
            keepdims=True,
        )
    for ref in (gqt_ref, gkt_ref, gvt_ref):
        ref[...] = jnp.zeros(ref.shape, jnp.float32)
    scale = log_two_e / math.sqrt(head_size)
    back = 1.0 / math.sqrt(head_size)

    def step(qi, ki):
        q_at, k_at = at_tile(qi), at_tile(ki)
        allowed = tile_mask(segq_ref, segk_ref, qi, ki, causal)
        scores = [dot_dims(kt_ref[band, k_at], qt_ref[band, q_at], 0, 0) for band in bands]
        grads = [dot_dims(vt_ref[band, k_at], got_ref[band, q_at], 0, 0) for band in bands]
        parts = [
            jnp.where(allowed, jnp.exp2(scores[h] * scale - lse_ref[h : h + 1, q_at]), 0.0)
            for h in range(HEADS)
        ]
        grads = [parts[h] * (grads[h] - delta_ref[h : h + 1, q_at]) for h in range(HEADS)]
        parts_t = [part.T.astype(jnp.bfloat16) for part in parts]
        grads_t = [part.T.astype(jnp.bfloat16) for part in grads]
        grads = [part.astype(jnp.bfloat16) for part in grads]
        for ref, place, terms in (
            (gvt_ref, k_at, [dot_dims(got_ref[bands[h], q_at], parts_t[h], 1, 0) for h in range(HEADS)]),
            (gkt_ref, k_at, [dot_dims(qt_ref[bands[h], q_at], grads_t[h], 1, 0) for h in range(HEADS)]),
            (gqt_ref, q_at, [dot_dims(kt_ref[bands[h], k_at], grads[h], 1, 0) for h in range(HEADS)]),
        ):
            ref[:, place] += jnp.concatenate(terms, axis=0)

    for_tiles(length // TILE, edge_ref, causal, step)
    gq_ref[...] = (gqt_ref[...] * back).astype(jnp.bfloat16).T
    gk_ref[...] = (gkt_ref[...] * back).astype(jnp.bfloat16).T
    gv_ref[...] = gvt_ref[...].astype(jnp.bfloat16).T
    from_query = dot_dims(gq_ref[...], w_ref[0], 1, 1)
    from_keys = dot_dims(gk_ref[...], w_ref[1], 1, 1) + dot_dims(gv_ref[...], w_ref[2], 1, 1)
    if cross:
        key_grad_ref[...] = from_keys
    else:
        from_query = from_query + from_keys
    out_ref[...] = g_ref[...] + norm_backward(from_query, x_ref[...], ln_ref, ln_grad_ref)


def attn_backward(grad, stored):
    x, ln, weights, segs, edges, causal, cross, _, kept = stored
    length, width = x.shape
    outs = (full(length, width), full(2, width)) + (low(length, width),) * 4
    if cross:
        outs = outs + (full(length, width),)
    out, ln_grad, *rest = call(
        partial(attn_backward_kernel, causal, cross),
        outs,
        grad,
        x,
        ln,
        weights,
        *segs,
        *kept,
        edges,
        scratch=[pltpu.VMEM((width, length), jnp.bfloat16), pltpu.VMEM((HEADS, length), jnp.float32)]
        + [pltpu.VMEM((width, length), jnp.float32)] * 3,
        smem_args=1,
    )
    return out, ln_grad, rest[:4], rest[4] if cross else None


def gelu_parts(hidden):
    root = math.sqrt(2.0 / math.pi)
    square = hidden * hidden
    bend = jnp.tanh(root * hidden * (1.0 + 0.044715 * square))
    value = 0.5 * hidden * (1.0 + bend)
    slope = 0.5 * (1.0 + bend) + 0.5 * hidden * (1.0 - bend * bend) * root * (
        1.0 + 3.0 * 0.044715 * square
    )
    return value, slope


def ffn_forward_kernel(chunk, x_ref, ln_ref, next_ref, w_in_ref, w_out_ref, out_ref, a_ref, after_ref):
    a_ref[...] = norm_forward(x_ref[...], ln_ref).astype(jnp.bfloat16)
    total = x_ref[...]
    for start in range(0, w_in_ref.shape[0], chunk):
        part = slice(start, start + chunk)
        hidden = dot_dims(a_ref[...], w_in_ref[part, :], 1, 1)
        active = gelu_parts(hidden)[0].astype(jnp.bfloat16)
        total = total + dot_dims(active, w_out_ref[part, :], 1, 0)
    out_ref[...] = total
    after_ref[...] = norm_forward(total, next_ref).astype(after_ref.dtype)


def ffn_forward(x, ln, ln_next, w_in, w_out):
    length, width = x.shape
    out, normed, after = call(
        partial(ffn_forward_kernel, 512),
        (full(length, width), low(length, width), low(length, width)),
        x,
        ln,
        ln_next,
        w_in,
        w_out,
    )
    return out, after, (x, ln, w_in, w_out, normed)


def ffn_backward_kernel(
    chunk, g_ref, x_ref, ln_ref, a_ref, w_in_ref, w_out_ref, out_ref, ln_grad_ref, low_ref, ut_ref, ht_ref
):
    low_ref[...] = g_ref[...].astype(jnp.bfloat16)
    total = jnp.zeros(g_ref.shape, jnp.float32)
    for start in range(0, w_in_ref.shape[0], chunk):
        part = slice(start, start + chunk)
        hidden = dot_dims(a_ref[...], w_in_ref[part, :], 1, 1)
        value, slope = gelu_parts(hidden)
        ut_ref[part, :] = value.astype(jnp.bfloat16).T
        grad = (dot_dims(low_ref[...], w_out_ref[part, :], 1, 1) * slope).astype(jnp.bfloat16)
        ht_ref[part, :] = grad.T
        total = total + dot_dims(grad, w_in_ref[part, :], 1, 0)
    out_ref[...] = g_ref[...] + norm_backward(total, x_ref[...], ln_ref, ln_grad_ref)


def ffn_backward(grad, stored):
    x, ln, w_in, w_out, normed = stored
    length, width = x.shape
    hidden = w_in.shape[0]
    out, ln_grad, *rest = call(
        partial(ffn_backward_kernel, 512),
        (full(length, width), full(2, width), low(length, width), low(hidden, length), low(hidden, length)),
        grad,
        x,
        ln,
        normed,
        w_in,
        w_out,
    )
    return out, ln_grad, rest


def norm_backward_kernel(g_ref, x_ref, ln_ref, out_ref, ln_grad_ref):
    out_ref[...] = norm_backward(g_ref[...], x_ref[...], ln_ref, ln_grad_ref)


def plain_norm_backward(grad, x, ln):
    return call(norm_backward_kernel, (full(*x.shape), full(2, x.shape[1])), grad, x, ln)


def small_factor(block):
    size = block.shape[0]
    eye = (
        lax.broadcasted_iota(jnp.int32, (size, size), 0)
        == lax.broadcasted_iota(jnp.int32, (size, size), 1)
    ).astype(jnp.float32)
    whole = jnp.concatenate([block, eye], axis=1)
    rows = [whole[8 * u : 8 * u + 8] for u in range(size // 8)]
    shape = rows[0].shape
    sub = lax.broadcasted_iota(jnp.int32, shape, 0)

    def lane_splat(value, lane):
        return jnp.broadcast_to(value[:, lane : lane + 1], shape)

    def row_splat(value, row):
        return jnp.broadcast_to(value[row : row + 1, :], shape)

    for g in range(len(rows)):
        first = 8 * g
        lanes = {
            u: [lane_splat(rows[u], first + s) for s in range(8)] for u in range(g, len(rows))
        }
        scale = jnp.zeros(shape, jnp.float32)
        for t in range(8):
            pivot = row_splat(lanes[g][t], t)
            root = lax.rsqrt(pivot)
            inverse = root * root
            scale = jnp.where(sub == t, root, scale)
            row_t = row_splat(rows[g], t) * inverse
            splats = {s: row_splat(lanes[g][s], t) * inverse for s in range(t + 1, 8)}
            for u in range(g, len(rows)):
                factor = lanes[u][t]
                if u == g:
                    factor = jnp.where(sub > t, factor, 0.0)
                rows[u] = rows[u] - factor * row_t
                for s in range(t + 1, 8):
                    lanes[u][s] = lanes[u][s] - factor * splats[s]
        rows[g] = rows[g] * scale
    return jnp.concatenate(rows, axis=0)[:, size:]


def renew_kernel(stat_ref, basis_ref, out_ref, gram_ref, rest_ref):
    size = stat_ref.shape[0]
    product = dot_exact(stat_ref[...], basis_ref[...], 1, 0)
    rest_ref[...] = product
    gram_ref[...] = dot_exact(product, product, 0, 0)
    for low in range(0, size, 128):
        high = low + 128
        block = gram_ref[low:high, low:high]
        corner = small_factor(block[:64, :64])
        across = dot_exact(corner, block[:64, 64:], 1, 0)
        second = small_factor(block[64:, 64:] - dot_exact(across, across, 0, 0))
        below = dot_exact(second, dot_exact(across, corner, 0, 0), 1, 0)
        inverse = jnp.concatenate(
            [
                jnp.concatenate([corner, jnp.zeros_like(corner)], axis=1),
                jnp.concatenate([-below, second], axis=1),
            ],
            axis=0,
        )
        columns = dot_exact(rest_ref[:, low:high], inverse, 1, 1)
        out_ref[:, low:high] = columns
        if high < size:
            panel = dot_exact(inverse, gram_ref[low:high, high:], 1, 0)
            gram_ref[high:, high:] -= dot_exact(panel, panel, 0, 0)
            rest_ref[:, high:] -= dot_exact(columns, panel, 1, 0)


def renew_basis(statistic, basis):
    shape = statistic.shape
    return call(
        renew_kernel,
        full(*shape),
        statistic,
        basis,
        scratch=[pltpu.VMEM(shape, jnp.float32), pltpu.VMEM(shape, jnp.float32)],
    )


def sinusoid(length, model_width):
    places = np.arange(length, dtype=np.float32)[:, None]
    halves = np.arange(model_width // 2, dtype=np.float32)[None, :]
    angles = places * np.exp(halves * np.float32(-2.0 * math.log(10000.0) / model_width))
    angles = angles.astype(np.float64)
    return (
        np.stack([np.sin(angles), np.cos(angles)], axis=-1)
        .reshape(length, model_width)
        .astype(np.float32)
    )


def one_hot(ids, columns):
    return (ids[:, None] == columns[None, :]).astype(jnp.bfloat16)


def pick_weights(target_seg, pick_rows):
    sentence = jnp.take(target_seg, pick_rows, axis=0)
    return jnp.sum((sentence[:, None] == sentence[None, :]).astype(jnp.float32), axis=1)


def combine_stats(tops, totals, chosen):
    top = jnp.max(tops, axis=0)
    return top, jnp.sum(totals * jnp.exp(tops - top), axis=0), jnp.sum(chosen, axis=0)


def adam_direction(moment, second):
    return moment / (1.0 - beta_one**STEP) / (jnp.sqrt(second / (1.0 - beta_two**STEP)) + adam_eps)


def adam_update(weight, grad_item, moment, second, step_rate, decay_weight):
    moment = beta_one * moment + (1.0 - beta_one) * grad_item
    second = beta_two * second + (1.0 - beta_two) * grad_item * grad_item
    return (
        weight - step_rate * (adam_direction(moment, second) + decay_weight * weight),
        moment,
        second,
    )


def share_rows(array, owners, shares, share):
    rows, columns = array.shape
    blocks = array.reshape(owners, shares, rows // (owners * shares), columns)
    return lax.dynamic_index_in_dim(blocks, share, 1, keepdims=False)


def body(
    src_ids,
    src_seg,
    tgt_ids,
    tgt_seg,
    pick_pos,
    pick_label,
    attn_w,
    attn_m,
    attn_v,
    ffn_w,
    ffn_m,
    ffn_v,
    soap_basis,
    soap_stats,
    norm_p,
    norm_m,
    norm_v,
    embedding,
    embed_m,
    embed_v,
):
    owners, replicas = lax.axis_size("dp"), lax.axis_size("vocab")
    replica = lax.axis_index("vocab")
    w_attn, w_ffn, norm_low, table_low = (
        lax.all_gather(attn_w.astype(jnp.bfloat16), "dp", axis=1, tiled=True),
        lax.all_gather(ffn_w.astype(jnp.bfloat16), "dp", axis=1, tiled=True),
        lax.all_gather(norm_p.astype(jnp.bfloat16), "dp", axis=1, tiled=True),
        lax.all_gather(embedding.astype(jnp.bfloat16), "dp", axis=1, tiled=True),
    )
    norm_rows = norm_low.astype(jnp.float32)
    norms = [jnp.stack([norm_rows[k], norm_rows[7 + k]]) for k in range(7)]
    vocab_count, width = table_low.shape
    columns = replica * vocab_count + jnp.arange(vocab_count)
    source, source_seg, target, target_seg = (src_ids[0], src_seg[0], tgt_ids[0], tgt_seg[0])
    pick_rows, labels = (pick_pos[0], pick_label[0])
    length = source.shape[0]
    embed_scale = math.sqrt(width)
    looked_up = [
        lax.psum(
            dot_dims(one_hot(ids, columns), table_low, 1, 0).astype(jnp.bfloat16), "vocab"
        ).astype(jnp.float32)
        for ids in (source, target)
    ]
    positional = sinusoid(length, width)

    enc_in = looked_up[0] * embed_scale + positional
    enc_mid, enc_attn = attn_forward(
        enc_in, norms[0], w_attn[0:4], source_seg, source_seg, None, False
    )
    enc_out, encoded, enc_ffn = ffn_forward(enc_mid, norms[1], norms[2], w_ffn[0], w_ffn[1])
    dec_in = looked_up[1] * embed_scale + positional
    dec_mid, dec_self = attn_forward(
        dec_in, norms[3], w_attn[4:8], target_seg, target_seg, None, True
    )
    dec_late, dec_cross = attn_forward(
        dec_mid, norms[4], w_attn[8:12], target_seg, source_seg, encoded, False
    )
    dec_out, final_low, dec_ffn = ffn_forward(dec_late, norms[5], norms[6], w_ffn[2], w_ffn[3])

    chosen_rows = one_hot(pick_rows, jnp.arange(length))
    picked = dot_dims(chosen_rows, final_low, 1, 0).astype(jnp.bfloat16)
    logits = dot_dims(picked, table_low, 1, 1)
    row_top = jnp.max(logits, axis=-1)
    row_total = jnp.sum(jnp.exp(logits - row_top[:, None]), axis=-1)
    label_hit = labels[:, None] == columns[None, :]
    chosen = jnp.sum(jnp.where(label_hit, logits, 0.0), axis=-1)
    row_top, row_total, chosen = combine_stats(
        *jnp.moveaxis(lax.all_gather(jnp.stack([row_top, row_total, chosen]), "vocab"), 1, 0)
    )
    log_total = row_top + jnp.log(row_total)
    weight = 1.0 / pick_weights(target_seg, pick_rows)
    loss_part = jnp.sum((log_total - chosen) * weight)
    count_part = (target_seg[-1] + 1).astype(jnp.float32)
    grad_logits = (
        weight[:, None] * (jnp.exp(logits - log_total[:, None]) - label_hit.astype(jnp.float32))
    ).astype(jnp.bfloat16)
    grad_picked = lax.psum(dot_dims(grad_logits, table_low, 1, 0), "vocab")
    grad_table = dot_dims(grad_logits, picked, 0, 0)
    picked_high = grad_picked.astype(jnp.bfloat16)
    picked_rest = (grad_picked - picked_high.astype(jnp.float32)).astype(jnp.bfloat16)
    grad_final = dot_dims(chosen_rows, picked_high, 0, 0) + dot_dims(chosen_rows, picked_rest, 0, 0)

    norm_grads = [None] * 7
    grad, norm_grads[6] = plain_norm_backward(grad_final, dec_out, norms[6])
    grad, norm_grads[5], dec_ffn_parts = ffn_backward(grad, dec_ffn)
    grad, norm_grads[4], cross_parts, grad_encoded = attn_backward(grad, dec_cross)
    grad, norm_grads[3], self_parts, _ = attn_backward(grad, dec_self)
    grad_target = (grad * embed_scale).astype(jnp.bfloat16)
    grad, norm_grads[2] = plain_norm_backward(grad_encoded, enc_out, norms[2])
    grad, norm_grads[1], enc_ffn_parts = ffn_backward(grad, enc_ffn)
    grad, norm_grads[0], enc_parts, _ = attn_backward(grad, enc_attn)
    grad_source = (grad * embed_scale).astype(jnp.bfloat16)
    for ids, rows in ((source, grad_source), (target, grad_target)):
        grad_table = grad_table + dot_dims(one_hot(ids, columns), rows, 0, 0)

    chosen_columns = share_rows(jnp.eye(width, dtype=jnp.bfloat16), owners, replicas, replica)
    chosen_columns = chosen_columns.reshape(-1, width)

    def weight_grads(stored, parts):
        normed, kept, cross = stored[7], stored[8], stored[6]
        grad_low, gq, gk, gv = parts
        key_in = encoded if cross else normed
        share = [dot_dims(chosen_columns, rows, 1, 1).astype(jnp.bfloat16) for rows in (normed, key_in)]
        mixed = share_rows(kept[3], owners, replicas, replica).reshape(-1, length)
        return [
            dot_dims(share[0], gq, 1, 0),
            dot_dims(share[1], gk, 1, 0),
            dot_dims(share[1], gv, 1, 0),
            dot_dims(mixed, grad_low, 1, 0),
        ]

    def hidden_grads(stored, parts):
        grad_low, values, grads = parts
        return [
            dot_dims(share_rows(rows, owners, replicas, replica).reshape(-1, length), right, 1, 0)
            for rows, right in ((grads, stored[4]), (values, grad_low))
        ]

    pieces = (
        weight_grads(enc_attn, enc_parts)
        + weight_grads(dec_self, self_parts)
        + weight_grads(dec_cross, cross_parts)
        + hidden_grads(enc_ffn, enc_ffn_parts)
        + hidden_grads(dec_ffn, dec_ffn_parts)
    )
    pieces = [piece.astype(jnp.bfloat16).reshape(owners, -1, width) for piece in pieces]
    summed = lax.psum_scatter(
        jnp.concatenate(pieces, axis=1), "dp", scatter_dimension=0, tiled=False
    )
    shared = lax.all_gather(summed, "vocab")
    attn_rows = 12 * (width // (owners * replicas))
    g_attn = jnp.moveaxis(shared[:, :attn_rows].reshape(replicas, 12, -1, width), 0, 1)
    g_attn = g_attn.reshape(12, -1, width).astype(jnp.float32)
    g_ffn = jnp.moveaxis(shared[:, attn_rows:].reshape(replicas, 4, -1, width), 0, 1)
    g_ffn = g_ffn.reshape(4, -1, width).astype(jnp.float32)
    norm_grad = jnp.stack(norm_grads)
    norm_grad = jnp.concatenate([norm_grad[:, 0], norm_grad[:, 1]], axis=0)
    g_norm = lax.psum_scatter(norm_grad, "dp", scatter_dimension=1, tiled=True)
    g_embed = lax.psum_scatter(
        grad_table.astype(jnp.bfloat16), "dp", scatter_dimension=1, tiled=True
    ).astype(jnp.float32)

    first_copy = (replica == 0).astype(jnp.float32)
    layer_sq = jnp.sum(g_attn * g_attn) + jnp.sum(g_ffn * g_ffn) + jnp.sum(g_norm * g_norm)
    raw_squares = jnp.sum(g_embed * g_embed) + first_copy * layer_sq
    loss_sum, sentences, squares = lax.psum(
        jnp.stack([first_copy * loss_part, first_copy * count_part, raw_squares]), ("dp", "vocab")
    )
    grad_norm = jnp.sqrt(squares) / sentences
    factor = jnp.minimum(1.0, clip_limit / (grad_norm + norm_eps)) / sentences
    g_attn, g_ffn, g_norm, g_embed = (
        g_attn * factor,
        g_ffn * factor,
        g_norm * factor,
        g_embed * factor,
    )
    matrix = replica % 4
    own_grad = lax.dynamic_index_in_dim(g_ffn, matrix, 0, keepdims=False)
    own_stat = stat_decay * lax.dynamic_index_in_dim(soap_stats, matrix, 0, keepdims=False) + (
        1.0 - stat_decay
    ) * lax.psum(dot_exact(own_grad, own_grad, 0, 0), "dp")
    own_basis = renew_basis(own_stat, lax.dynamic_index_in_dim(soap_basis, matrix, 0, keepdims=False))
    renewed = lax.all_gather(jnp.stack([own_stat, own_basis]).astype(jnp.bfloat16), "vocab")[:4]
    new_stats, new_basis = (renewed[:, k].astype(jnp.float32) for k in (0, 1))

    new_attn, m_attn, v_attn = adam_update(attn_w, g_attn, attn_m, attn_v, rate_matrix, decay_rate)
    new_norm, m_norm, v_norm = adam_update(norm_p, g_norm, norm_m, norm_v, rate_vector, 0.0)
    new_embed, m_embed, v_embed = adam_update(
        embedding, g_embed, embed_m, embed_v, rate_matrix, decay_rate
    )
    rotated = jnp.einsum("mfd,mde->mfe", g_ffn, soap_basis, precision=highest)
    m_ffn = beta_one * ffn_m + (1.0 - beta_one) * rotated
    v_ffn = beta_two * ffn_v + (1.0 - beta_two) * rotated * rotated
    back_rotated = jnp.einsum(
        "mfe,mde->mfd", adam_direction(m_ffn, v_ffn), soap_basis, precision=highest
    )
    new_ffn = ffn_w - rate_matrix * (back_rotated + decay_rate * ffn_w)
    return (
        loss_sum,
        sentences,
        grad_norm,
        new_attn,
        m_attn,
        v_attn,
        new_ffn,
        m_ffn,
        v_ffn,
        new_basis,
        new_stats,
        new_norm,
        m_norm,
        v_norm,
        new_embed,
        m_embed,
        v_embed,
    )


def solution(mesh):
    placed = (
        P("dp", None),
        P("dp", None),
        P("dp", None),
        P("dp", None),
        P("dp", None),
        P("dp", None),
        P(None, "dp", None),
        P(None, "dp", None),
        P(None, "dp", None),
        P(None, "dp", None),
        P(None, "dp", None),
        P(None, "dp", None),
        P(),
        P(),
        P(None, "dp"),
        P(None, "dp"),
        P(None, "dp"),
        P("vocab", "dp"),
        P("vocab", "dp"),
        P("vocab", "dp"),
    )
    return jax.shard_map(
        body,
        mesh=mesh,
        in_specs=placed,
        out_specs=(
            P(),
            P(),
            P(),
            P(None, "dp", None),
            P(None, "dp", None),
            P(None, "dp", None),
            P(None, "dp", None),
            P(None, "dp", None),
            P(None, "dp", None),
            P(),
            P(),
            P(None, "dp"),
            P(None, "dp"),
            P(None, "dp"),
            P("vocab", "dp"),
            P("vocab", "dp"),
            P("vocab", "dp"),
        ),
        check_vma=False,
    )
```

time: 2100 us -> 1020 us (0.49)
  other arithmetic: 665 us -> 63.7 us
  matrix products: 580 us -> 108 us
  Pallas kernels: 0 us -> 209 us
  waiting for transfers between devices: 591 us -> 469 us
  local copies, waits for them, and re-layouts: 146 us -> 78.8 us
    another operation x24 -> x10, other arithmetic: 478 us -> 8.78 us  [the longest x3 5.13 us: body(): jnp.stack([own_stat, own_basis]).astype(jnp.bfloat16)]
    dot_general x104 -> x30, matrix products: 518 us -> 87.2 us  [the longest x29 84.4 us: dot_dims(): lax.dot_general(left, right, (((left_dim,), (right_dim,)), ((), ())), pre...]
    reduce_scatter x4 -> x1, waiting for transfers between devices: 318 us -> 15.5 us  [body(): g_norm = lax.psum_scatter(norm_grad, 'dp', scatter_dimension=1, tiled=True)]
    pallas_call x0 -> x12, Pallas kernels: none -> 209 us  [call(): pl.pallas_call(kernel, out_shape=outs, in_specs=[vmem] * (len(args) - sme...]
    all_gather x0 -> x2, waiting for transfers between devices: none -> 80.3 us  [the longest x1 40.9 us: body(): lax.all_gather(jnp.stack([own_stat, own_basis]).astype(jnp.bfloat16), 'vo...]
    convert_element_type x17 -> x1, other arithmetic: 75.8 us -> 6.78 us  [body(): new_stats, new_basis = (renewed[:, k].astype(jnp.float32) for k in (0, 1))]
    unnamed x10 -> x13, waiting for transfers between devices: 0.16 us -> 61.1 us
    reduce_sum x22 -> x3, other arithmetic: 43.6 us -> 1.34 us  [the longest x1 1.29 us: body(): row_total = jnp.sum(jnp.exp(logits - row_top[:, None]), axis=-1)]
  transfers between devices with their start and end apart: 10 -> 11, of which waited for: 8 -> 10; matrix products, arithmetic and copies ran while one was open for 13% -> 12% of each run, Pallas kernels for 0% -> 4%
where the time goes in v1:
time: 1020 us; the launch traced here: 1010 us
  waiting for transfers between devices  469 us (46%)
  Pallas kernels  209 us (20%)
  matrix products  108 us (11%)
  local copies, waits for them, and re-layouts  78.8 us (8%)
  other arithmetic  63.7 us (6%)
  blocking collectives  61.1 us (6%)
  between operations  22.2 us (2%)
    pallas_call x12, Pallas kernels, call(): pl.pallas_call(kernel, out_shape=outs, in_specs=[vmem] * (len(args) - sme...  209 us
    dot_general x29, matrix products, dot_dims(): lax.dot_general(left, right, (((left_dim,), (right_dim,)), ((), ())), pre...  84.4 us
    all_gather x1, waiting for transfers between devices, body(): lax.all_gather(attn_w.astype(jnp.bfloat16), 'dp', axis=1, tiled=True)  67.4 us
    unnamed x13, waiting for transfers between devices  61.1 us
    all_gather x1, waiting for transfers between devices, body(): lax.all_gather(embedding.astype(jnp.bfloat16), 'dp', axis=1, tiled=True)  61 us
    psum x1, waiting for transfers between devices, body(): grad_picked = lax.psum(dot_dims(grad_logits, table_low, 1, 0), 'vocab')  51.8 us
    psum x1, waiting for transfers between devices, body(): lax.psum(dot_exact(own_grad, own_grad, 0, 0), 'dp')  49.9 us
    psum x1, waiting for transfers between devices, body(): lax.psum(dot_dims(one_hot(ids, columns), table_low, 1, 0).astype(jnp.bflo...  45 us
  transfers between devices with their start and end apart: 11, of which 10 were waited for; matrix products, arithmetic and copies ran while one was open for 12% of the time, Pallas kernels for 4%

profile of v1, /device:TPU:0, one launch (start us, length us, event | category | flops | bytes accessed | tf_op | source)
XLA Modules:
  0.0 1014.0 jit_solution(10911725796901003266)
XLA Ops:
  10.2 61.0 %all-gather.8.cloned.1.call-done = bf16[4736,512]{1,0:T(8,128)(2,1)} async-done(((bf16[4736,128]{1,0:T(8,128)(2,1)}), bf16[4736,512]{1,0:T(8,128)(2,1)}) %all-gather.8.cloned.1.call-update) | async-done | bytes 4849680 | tf_op jit(solution)/shard_map/all_gather | solution.py:507
  71.2 8.8 fusion.45
  93.9 8.0 all_gather.26
  106.4 45.0 %all-reduce.10.cloned.1.call-done = (bf16[1024,512]{1,0:T(8,128)(2,1)}, bf16[1024,512]{1,0:T(8,128)(2,1)}) async-done(((bf16[1024,512]{1,0:T(8,128)(2,1)}, bf16[1024,512]{1,0:T(8,128)(2,1)}), (bf16[1024,512]{1,0:T(8,128)(2,1)}, bf16[1024,512]{1,0:T(8,128)(2,1)})) %all-reduce.10.cloned.1.call-update) | async-done | bytes 2097168 | tf_op jit(solution)/shard_map/psum | solution.py:518
  156.2 67.4 %all-gather.10.cloned.1.call-done = bf16[12,512,512]{2,1,0:T(8,128)(2,1)} async-done(((bf16[12,128,512]{2,1,0:T(8,128)(2,1)}), bf16[12,512,512]{2,1,0:T(8,128)(2,1)}) %all-gather.10.cloned.1.call-update) | async-done | bytes 6291472 | tf_op jit(solution)/shard_map/all_gather | solution.py:504
  230.3 22.5 %shard_map.333 = (f32[1024,512]{1,0:T(8,128)}, bf16[1024,512]{1,0:T(8,128)(2,1)}, bf16[512,1024]{1,0:T(8,128)(2,1)}, bf16[512,1024]{1,0:T(8,128)(2,1)}, bf16[512...) custom-call(f32[1024,512]{1,0:T(8,128)} %get-tuple-element.180.refs_0_.refs_1_, ...), custom_call_target="tpu_custom_call" | custom-call | tf_op jit(solution)/shard_map/pallas_call | solution.py:49
  253.8 17.3 %shard_map.332 = (f32[1024,512]{1,0:T(8,128)}, bf16[1024,512]{1,0:T(8,128)(2,1)}, bf16[512,1024]{1,0:T(8,128)(2,1)}, bf16[512,1024]{1,0:T(8,128)(2,1)}, bf16[512...) custom-call(f32[1024,512]{1,0:T(8,128)} %get-tuple-element.181.refs_0_, ...), custom_call_target="tpu_custom_call" | custom-call | tf_op jit(solution)/shard_map/pallas_call | solution.py:49
  276.4 37.2 %all-gather.12.cloned.1.call-done = bf16[4,2048,512]{2,1,0:T(8,128)(2,1)} async-done(((bf16[4,512,512]{2,1,0:T(8,128)(2,1)}), bf16[4,2048,512]{2,1,0:T(8,128)(2,1)}) %all-gather.12.cloned.1.call-update) | async-done | bytes 8388624 | tf_op jit(solution)/shard_map/all_gather | solution.py:505
  320.1 10.9 %shard_map.334 = (f32[1024,512]{1,0:T(8,128)}, bf16[1024,512]{1,0:T(8,128)(2,1)}, bf16[1024,512]{1,0:T(8,128)(2,1)}) custom-call(f32[1024,512]{1,0:T(8,128)} %get-tuple-element.78.x_ref, f32[2,512]{1,0:T(2,128)} %get-tuple-element.209.ln_ref, f32[2,512]{1,0:T(2,128)} %get-tuple-element.210.next_ref.ln_ref, bf16[2048,512]{1,0:T(8,128)(2,1)} %get-tuple-element.174.w_in_ref, ...), custom_call_target="tpu_custom_call" | custom-call | tf_op jit(solution)/shard_map/pallas_call | solution.py:49
  331.0 19.2 %shard_map.335 = (f32[1024,512]{1,0:T(8,128)}, bf16[1024,512]{1,0:T(8,128)(2,1)}, bf16[512,1024]{1,0:T(8,128)(2,1)}, bf16[512,1024]{1,0:T(8,128)(2,1)}, bf16[512...) custom-call(f32[1024,512]{1,0:T(8,128)} %get-tuple-element.77.refs_0_.refs_1_, ...), custom_call_target="tpu_custom_call" | custom-call | tf_op jit(solution)/shard_map/pallas_call | solution.py:49
  350.2 11.0 %shard_map.336 = (f32[1024,512]{1,0:T(8,128)}, bf16[1024,512]{1,0:T(8,128)(2,1)}, bf16[1024,512]{1,0:T(8,128)(2,1)}) custom-call(f32[1024,512]{1,0:T(8,128)} %get-tuple-element.80.x_ref, f32[2,512]{1,0:T(2,128)} %get-tuple-element.211.ln_ref, f32[2,512]{1,0:T(2,128)} %get-tuple-element.212.next_ref.ln_ref, bf16[2048,512]{1,0:T(8,128)(2,1)} %get-tuple-element.172.w_in_ref, ...), custom_call_target="tpu_custom_call" | custom-call | tf_op jit(solution)/shard_map/pallas_call | solution.py:49
  365.9 14.1 %all-gather.1 = f32[8,3,256]{2,1,0:T(4,128)S(1)} all-gather(f32[1,3,256]{2,1,0:T(4,128)S(1)} %maximum_bitcast_fusion), channel_id=2, replica_groups=mesh['dp'=4,'vocab'=8] {'vocab'}, dimensions={0}, use_global_device_ids=true | all-gather | bytes 27648 | tf_op jit(solution)/shard_map/all_gather | solution.py:547
  390.3 51.8 %all-reduce.6.cloned.1.call-done = f32[256,512]{1,0:T(8,128)} async-done(((f32[256,512]{1,0:T(8,128)}), f32[256,512]{1,0:T(8,128)}) %all-reduce.6.cloned.1.call-update) | async-done | bytes 524304 | tf_op jit(solution)/shard_map/psum | solution.py:556
  451.7 17.4 %shard_map.338 = (f32[1024,512]{1,0:T(8,128)}, f32[2,512]{1,0:T(2,128)}, bf16[1024,512]{1,0:T(8,128)(2,1)}, bf16[2048,1024]{1,0:T(8,128)(2,1)}, bf16[2048,1024]{1,0:T(8,128)(2,1)}) custom-call(f32[1024,512]{1,0:T(8,128)} %get-tuple-element.83.g_ref, f32[1024,512]{1,0:T(8,128)} %get-tuple-element.80.x_ref, f32[2,512]{1,0:T(2,128)} %get-tuple-element.211.ln_ref, ...), custom_call_target="tpu_custom_call" | custom-call | tf_op jit(solution)/shard_map/pallas_call | solution.py:49
  471.3 25.0 %shard_map.339 = (f32[1024,512]{1,0:T(8,128)}, f32[2,512]{1,0:T(2,128)}, bf16[1024,512]{1,0:T(8,128)(2,1)}, bf16[1024,512]{1,0:T(8,128)(2,1)}, bf16[1024,512]{1,...) custom-call(f32[1024,512]{1,0:T(8,128)} %get-tuple-element.85.refs_0_, ...), custom_call_target="tpu_custom_call" | custom-call | tf_op jit(solution)/shard_map/pallas_call | solution.py:49
  507.4 17.7 %shard_map.341 = (f32[1024,512]{1,0:T(8,128)}, f32[2,512]{1,0:T(2,128)}, bf16[1024,512]{1,0:T(8,128)(2,1)}, bf16[2048,1024]{1,0:T(8,128)(2,1)}, bf16[2048,1024]{1,0:T(8,128)(2,1)}) custom-call(f32[1024,512]{1,0:T(8,128)} %get-tuple-element.93.g_ref, f32[1024,512]{1,0:T(8,128)} %get-tuple-element.78.x_ref, f32[2,512]{1,0:T(2,128)} %get-tuple-element.209.ln_ref, ...), custom_call_target="tpu_custom_call" | custom-call | tf_op jit(solution)/shard_map/pallas_call | solution.py:49
  529.2 29.1 %shard_map.342 = (f32[1024,512]{1,0:T(8,128)}, f32[2,512]{1,0:T(2,128)}, bf16[1024,512]{1,0:T(8,128)(2,1)}, bf16[1024,512]{1,0:T(8,128)(2,1)}, bf16[1024,512]{1,0:T(8,128)(2,1)}, /*index=5*/bf16[1024,512]{1,0:T(8,128)(2,1)}) custom-call(f32[1024,512]{1,0:T(8,128)} %get-tuple-element.95.refs_0_, f32[1024,512]{1,0:T(8,128)} %get-tuple-element.180.refs_0_.refs_1_, ...), custom_call_target="tpu_custom_call" | custom-call | tf_op jit(solution)/shard_map/pallas_call | solution.py:49
  559.1 21.6 %shard_map.344 = (f32[7,2,512]{2,1,0:T(2,128)S(1)}, f32[1024,512]{1,0:T(8,128)}, bf16[1024,512]{1,0:T(8,128)(2,1)}, bf16[1024,512]{1,0:T(8,128)(2,1)}, bf16[1024,512]{1,0:T(8,128)(2,1)}, /*index=5*/bf16[1024,512]{1,0:T(8,128)(2,1)}) fusion(f32[7,2,512]{2,1,0:T(2,128)S(1)} %constant_dynamic-update-slice_fusion.20, f32[1024,512]{1,0:T(8,128)} %get-tuple-element.102, ...), kind=kCustom, calls=%fused_computation.133 | custom fusion | bytes 17348608 | tf_op jit(solution)/shard_map/pallas_call | solution.py:49
  610.5 10.1 fusion
  620.6 8.5 fusion.4
  629.3 11.2 %add_convert_fusion = bf16[4736,512]{1,0:T(8,128)(2,1)} fusion(f32[4736,512]{1,0:T(8,128)} %fusion.4, f32[4736,512]{1,0:T(8,128)} %fusion, bf16[256,4736]{1,0:T(8,128)(2,1)} %copy-done.9, bf16[256,512]{1,0:T(8,128)(2,1)S(1)} %copy-done.23), kind=kOutput, calls=%fused_computation.9 | convolution fusion | flops 1248788480 | bytes 26935296 | tf_op jit(solution)/shard_map/dot_general | solution.py:33
  640.5 7.4 copy.54
  650.6 15.5 %reduce-scatter.8.cloned.1.call-done = f32[14,128]{1,0:T(8,128)} async-done(((f32[14,512]{1,0:T(8,128)}), f32[14,128]{1,0:T(8,128)}) %reduce-scatter.8.cloned.1.call-update) | async-done | bytes 7184 | tf_op jit(solution)/shard_map/reduce_scatter | solution.py:617
  667.4 60.3 %reduce-scatter.10.cloned.1.call-done = bf16[128,4736]{1,0:T(8,128)(2,1)} async-done(((bf16[512,4736]{1,0:T(8,128)(2,1)}), bf16[128,4736]{1,0:T(8,128)(2,1)}) %reduce-scatter.10.cloned.1.call-update) | async-done | bytes 1212432
  732.5 39.5 %all-gather.14.cloned.1.call-done = bf16[8,448,512]{2,1,0:T(8,128)(2,1)} async-done(((bf16[1,448,512]{2,1,0:T(8,128)(2,1)}), bf16[8,448,512]{2,1,0:T(8,128)(2,1)}) %all-gather.14.cloned.1.call-update) | async-done | bytes 3670032 | tf_op jit(solution)/shard_map/all_gather | solution.py:609
  780.8 39.1 %psum.38 = f32[3]{0:T(128)S(1)} all-reduce(f32[3]{0:T(128)S(1)} %pad_maximum_fusion.9), channel_id=1, replica_groups=mesh['dp'=4,'vocab'=8] {'dp','vocab'}, use_global_device_ids=true, to_apply=%region_18.19 | all-reduce | flops 3 | bytes 24 | tf_op jit(solution)/shard_map/psum | solution.py:625
  832.9 49.9 %all-reduce.8.cloned.1.call-done = f32[512,512]{1,0:T(8,128)} async-done(((f32[512,512]{1,0:T(8,128)}), f32[512,512]{1,0:T(8,128)}) %all-reduce.8.cloned.1.call-update) | async-done | bytes 1048592 | tf_op jit(solution)/shard_map/psum | solution.py:640
  885.6 29.1 %shard_map.343 = f32[512,512]{1,0:T(8,128)} custom-call(f32[512,512]{1,0:T(8,128)} %get-tuple-element.162.stat_ref, f32[512,512]{1,0:T(8,128)} %dynamic-slice_bitcast_fusion.basis_ref), custom_call_target="tpu_custom_call" | custom-call | tf_op jit(solution)/shard_map/pallas_call | solution.py:49
  921.6 10.2 %multiply_add_fusion = (f32[4,512,512]{2,1,0:T(8,128)S(1)}, f32[4,512,512]{2,1,0:T(8,128)S(1)}) fusion(f32[4,512,512]{2,1,0:T(8,128)} %param.31, f32[4,512,512]{2,1,0:T(8,128)} %param.32, f32[4,512,512]{2,1,0:T(8,128)S(1)} %bitcast.194, f32[4,512,512]{2,1,0:T(8,128)S(1)} %copy-done.10), kind=kOutput, calls=%fused_computation.38 | convolution fusion | flops 6449790976 | bytes 25165824 | tf_op jit(solution)/shard_map/mfd,mde->mfe/dot_general | solution.py:650
  931.8 9.5 multiply_subtract_fusion.1
  941.4 11.1 %multiply_subtract_fusion = f32[4,512,512]{2,1,0:T(8,128)} fusion(f32[4,512,512]{2,1,0:T(8,128)S(1)} %copy-done.16, f32[4,512,512]{2,1,0:T(8,128)S(1)} %copy-done.10, f32[4,512,512]{2,1,0:T(8,128)S(1)} %get-tuple-element.179, f32[4,512,512]{2,1,0:T(8,128)S(1)} %get-tuple-element.178), kind=kOutput, calls=%fused_computation.31 | convolution fusion | flops 6450839552 | bytes 20971520 | tf_op jit(solution)/shard_map/mfe,mde->mfd/dot_general | solution.py:653
  958.5 40.9 %all-gather.16.cloned.1.call-done = bf16[8,2,512,512]{3,2,1,0:T(8,128)(2,1)} async-done(((bf16[1,2,512,512]{3,2,1,0:T(8,128)(2,1)}), bf16[8,2,512,512]{3,2,1,0:T(8,128)(2,1)}) %all-gather.16.cloned.1.call-update) | async-done | bytes 8388624 | tf_op jit(solution)/shard_map/all_gather | solution.py:642
  (276 shorter events, 164.8 us)
Async XLA Ops:
  7.2 64.0 %copy-start.62 = (s32[1,1024]{1,0:T(1,128)S(1)}, s32[1,1024]{1,0:T(1,128)}, u32[]{:S(2)}) copy-start(s32[1,1024]{1,0:T(1,128)} %param.21) | copy-start | bytes 12292
  7.2 64.0 %all-gather.8.cloned.1.call-start = ((), (), s32[]{:S(2)}) async-start(), calls=%async_computation.3 | async-start | bytes 6062080 | tf_op jit(solution)/shard_map/all_gather | solution.py:507
  10.1 141.2 %all-reduce.10.cloned.1.call-start = ((), (), s32[]{:S(2)}) async-start(), calls=%async_computation.13 | async-start | bytes 4194304 | tf_op jit(solution)/shard_map/psum | solution.py:518
  86.4 137.2 %all-gather.10.cloned.1.call-start = ((), (), s32[]{:S(2)}) async-start(), calls=%async_computation.4 | async-start | bytes 7864320 | tf_op jit(solution)/shard_map/all_gather | solution.py:504
  87.9 225.7 %all-gather.12.cloned.1.call-start = ((), (), s32[]{:S(2)}) async-start(), calls=%async_computation.5 | async-start | bytes 10485760 | tf_op jit(solution)/shard_map/all_gather | solution.py:505
  91.7 350.4 %all-reduce.6.cloned.1.call-start = ((), (), s32[]{:S(2)}) async-start(), calls=%async_computation.6 | async-start | bytes 1048576 | tf_op jit(solution)/shard_map/psum | solution.py:556
  252.8 21.5 %copy-start.30 = (bf16[1024,512]{1,0:T(8,128)(2,1)S(1)}, bf16[1024,512]{1,0:T(8,128)(2,1)}, u32[]{:S(2)}) copy-start(bf16[1024,512]{1,0:T(8,128)(2,1)} %get-tuple-element.109) | copy-start | bytes 3145732
  331.0 31.9 %slice-start = ((s8[4849664]{0:T(1024)(128)(4,1)}), s8[4194304]{0:T(1024)(128)(4,1)S(1)}, s32[]{:S(2)}) async-start(s8[4849664]{0:T(1024)(128)(4,1)} %bitcast.198), calls=%async_computation.14 | async-start | bytes 8388608
  350.2 12.7 %slice-start.1 = ((s8[4849664]{0:T(1024)(128)(4,1)}), s8[655360]{0:T(1024)(128)(4,1)S(1)}, s32[]{:S(2)}) async-start(s8[4849664]{0:T(1024)(128)(4,1)} %bitcast.198), calls=%async_computation.15 | async-start | bytes 1310720
  364.6 15.4 %copy-start.61 = (f32[256]{0:T(256)S(1)}, f32[256]{0:T(256)}, u32[]{:S(2)}) copy-start(f32[256]{0:T(256)} %convert_reduce_fusion) | copy-start | bytes 3076
  385.9 262.0 %reduce-scatter.12.cloned.1.call-start = ((), (), s32[]{:S(2)}) async-start(), calls=%async_computation.12 | async-start | bytes 2293760
  451.7 18.5 %copy-start.14 = (bf16[1024,512]{1,0:T(8,128)(2,1)S(1)}, bf16[1024,512]{1,0:T(8,128)(2,1)}, u32[]{:S(2)}) copy-start(bf16[1024,512]{1,0:T(8,128)(2,1)} %get-tuple-element.84.a_ref) | copy-start | bytes 3145732
  471.3 25.0 %copy-start.21 = (bf16[64,1024]{1,0:T(8,128)(2,1)S(1)}, bf16[64,1024]{1,0:T(8,128)(2,1)}, u32[]{:S(2)}) copy-start(bf16[64,1024]{1,0:T(8,128)(2,1)} %convolution_convert_fusion.5) | copy-start | bytes 393220
  507.4 20.6 %copy-start.13 = (bf16[1024,512]{1,0:T(8,128)(2,1)S(1)}, bf16[1024,512]{1,0:T(8,128)(2,1)}, u32[]{:S(2)}) copy-start(bf16[1024,512]{1,0:T(8,128)(2,1)} %get-tuple-element.94.a_ref) | copy-start | bytes 3145732
  529.2 29.8 %copy-start.60 = (f32[2,512]{1,0:T(2,128)S(1)}, f32[2,512]{1,0:T(2,128)}, u32[]{:S(2)}) copy-start(f32[2,512]{1,0:T(2,128)} %get-tuple-element.131) | copy-start | bytes 12292
  529.2 29.8 %copy-start.59 = (f32[2,512]{1,0:T(2,128)S(1)}, f32[2,512]{1,0:T(2,128)}, u32[]{:S(2)}) copy-start(f32[2,512]{1,0:T(2,128)} %get-tuple-element.132) | copy-start | bytes 12292
  529.2 29.8 %copy-start.1 = (s32[1,1024]{1,0:T(1,128)S(1)}, s32[1,1024]{1,0:T(1,128)}, u32[]{:S(2)}) copy-start(s32[1,1024]{1,0:T(1,128)} %refs_4_.3) | copy-start | bytes 12292
  529.2 29.8 %copy-start.4 = (f32[1024,512]{1,0:T(8,128)S(1)}, f32[1024,512]{1,0:T(8,128)}, u32[]{:S(2)}) copy-start(f32[1024,512]{1,0:T(8,128)} %get-tuple-element.181.refs_0_) | copy-start | bytes 6291460
  529.2 29.9 %copy-start.5 = (bf16[4,512,512]{2,1,0:T(8,128)(2,1)S(1)}, bf16[4,512,512]{2,1,0:T(8,128)(2,1)}, u32[]{:S(2)}) copy-start(bf16[4,512,512]{2,1,0:T(8,128)(2,1)} %get-tuple-element.177.refs_2_) | copy-start | bytes 6291460
  529.2 29.9 %copy-start.12 = (s32[1024,128]{1,0:T(8,128)S(1)}, s32[1024,128]{1,0:T(8,128)}, u32[]{:S(2)}) copy-start(s32[1024,128]{1,0:T(8,128)} %broadcast_in_dim.21.refs_4_) | copy-start | bytes 1572868
  529.2 29.9 %copy-start.46 = (f32[2,512]{1,0:T(2,128)S(1)}, f32[2,512]{1,0:T(2,128)}, u32[]{:S(2)}) copy-start(f32[2,512]{1,0:T(2,128)} %get-tuple-element.207.refs_1_) | copy-start | bytes 12292
  529.2 29.9 %copy-start.47 = (f32[8,1024]{1,0:T(8,128)S(1)}, f32[8,1024]{1,0:T(8,128)}, u32[]{:S(2)}) copy-start(f32[8,1024]{1,0:T(8,128)} %get-tuple-element.107) | copy-start | bytes 98308
  529.2 29.9 %copy-start.52 = (s32[4,8]{1,0:T(4,128)S(1)}, s32[4,8]{1,0:T(4,128)}, u32[]{:S(2)}) copy-start(s32[4,8]{1,0:T(4,128)} %get-tuple-element.201.refs_5_) | copy-start | bytes 388
  596.0 12.3 %copy-start.24 = (bf16[256,512]{1,0:T(8,128)(2,1)S(1)}, bf16[256,512]{1,0:T(8,128)(2,1)}, u32[]{:S(2)}) copy-start(bf16[256,512]{1,0:T(8,128)(2,1)} %convolution_convert_fusion.1) | copy-start | bytes 786436
  609.7 56.3 %reduce-scatter.8.cloned.1.call-start = ((), (), s32[]{:S(2)}) async-start(), calls=%async_computation.8 | async-start | bytes 40960 | tf_op jit(solution)/shard_map/reduce_scatter | solution.py:617
  629.1 98.5 %reduce-scatter.10.cloned.1.call-start = ((), (), s32[]{:S(2)}) async-start(), calls=%async_computation.11 | async-start | bytes 6062080
  647.9 124.1 %all-gather.14.cloned.1.call-start = ((), (), s32[]{:S(2)}) async-start(), calls=%async_computation.7 | async-start | bytes 4128768 | tf_op jit(solution)/shard_map/all_gather | solution.py:609
  648.6 234.2 %all-reduce.8.cloned.1.call-start = ((), (), s32[]{:S(2)}) async-start(), calls=%async_computation.9 | async-start | bytes 2097152 | tf_op jit(solution)/shard_map/psum | solution.py:640
  830.4 169.0 %all-gather.16.cloned.1.call-start = ((), (), s32[]{:S(2)}) async-start(), calls=%async_computation.10 | async-start | bytes 9437184 | tf_op jit(solution)/shard_map/all_gather | solution.py:642
  941.3 11.1 %copy-start.7 = (bf16[4736,128]{1,0:T(8,128)(2,1)S(1)}, bf16[4736,128]{1,0:T(8,128)(2,1)}, u32[]{:S(2)}) copy-start(bf16[4736,128]{1,0:T(8,128)(2,1)} %copy.55) | copy-start | bytes 3637252
  941.3 11.1 %copy-start.8 = (f32[4736,128]{1,0:T(8,128)S(1)}, f32[4736,128]{1,0:T(8,128)}, u32[]{:S(2)}) copy-start(f32[4736,128]{1,0:T(8,128)} %param.38) | copy-start | bytes 7274500
  941.3 11.1 %copy-start.19 = (f32[4736,128]{1,0:T(8,128)S(1)}, f32[4736,128]{1,0:T(8,128)}, u32[]{:S(2)}) copy-start(f32[4736,128]{1,0:T(8,128)} %param.39) | copy-start | bytes 7274500
  (47 other events, 318.1 us)
Sparse Core Ops, SparseCore 0:
  10.4 60.7 all-gather.7
  86.5 64.7 all-reduce.9
  153.8 69.7 all-gather.9
  225.9 87.6 all-gather.11
  386.1 56.0 all-reduce.5
  609.8 30.2 reduce-scatter.11
  643.6 22.4 reduce-scatter.7
  669.4 58.2 reduce-scatter.9
  729.4 42.5 all-gather.13
  830.5 52.2 all-reduce.7
  917.2 82.0 all-gather.15

commit v2 on v1

--- a/solution.py
+++ b/solution.py
@@ -27,6 +27,7 @@
 log_two_e = math.log2(math.e)
 vmem = pl.BlockSpec(memory_space=pltpu.VMEM)
 smem = pl.BlockSpec(memory_space=pltpu.SMEM)
+mesh_ids = pl.DeviceIdType.MESH
 
 
 def dot_dims(left, right, left_dim, right_dim):
@@ -430,6 +431,294 @@
     )
 
 
+def peers_of(axis):
+    size, me = lax.axis_size(axis), lax.axis_index(axis)
+    return [
+        (step, lax.rem(me + step, size), lax.rem(me + size - step, size)) for step in range(1, size)
+    ]
+
+
+def greet(*places):
+    barrier = pltpu.get_barrier_semaphore()
+    for axis, index in places:
+        pl.semaphore_signal(barrier, inc=1, device_id={axis: index}, device_id_type=mesh_ids)
+    pl.semaphore_wait(barrier, len(places))
+
+
+def push(source, target, sems, slot, axis, index):
+    copy = pltpu.make_async_remote_copy(
+        src_ref=source,
+        dst_ref=target,
+        send_sem=sems[0].at[slot],
+        recv_sem=sems[1].at[slot],
+        device_id={axis: index},
+        device_id_type=mesh_ids,
+    )
+    copy.start()
+    return copy
+
+
+def sem_pair(count):
+    return [pltpu.SemaphoreType.DMA((count,)), pltpu.SemaphoreType.DMA((count,))]
+
+
+def talk(kernel, outs, collective_id, *args, scratch=()):
+    return pl.pallas_call(
+        kernel,
+        out_shape=outs,
+        in_specs=[vmem] * len(args),
+        out_specs=jax.tree.map(lambda _: vmem, outs),
+        scratch_shapes=list(scratch),
+        compiler_params=pltpu.CompilerParams(
+            collective_id=collective_id, has_side_effects=True, vmem_limit_bytes=56 * 2**20
+        ),
+    )(*args)
+
+
+def gather_kernel(axis, x_ref, out_ref, send_sems, recv_sems):
+    others = peers_of(axis)
+    greet(*[(axis, to) for _, to, _ in others])
+    me = lax.axis_index(axis)
+    sems = (send_sems, recv_sems)
+    copies = [push(x_ref, out_ref.at[me], sems, step - 1, axis, to) for step, to, _ in others]
+    out_ref[me] = x_ref[...]
+    for copy in copies:
+        copy.wait()
+
+
+def gather_small(x, axis, collective_id):
+    size = lax.axis_size(axis)
+    out = jax.ShapeDtypeStruct((size, *x.shape), x.dtype)
+    return talk(partial(gather_kernel, axis), out, collective_id, x, scratch=sem_pair(size - 1))
+
+
+def sum_kernel(x_ref, out_ref, parts_ref, mine_ref, s0, r0, s1, r1):
+    others = peers_of("vocab")
+    greet(*[("vocab", to) for _, to, _ in others])
+    size, me = lax.axis_size("vocab"), lax.axis_index("vocab")
+    rows = mine_ref.shape[0]
+
+    def rows_of(index):
+        return pl.ds(pl.multiple_of(index * rows, rows), rows)
+
+    copies = [
+        push(x_ref.at[rows_of(to)], parts_ref.at[me], (s0, r0), step - 1, "vocab", to)
+        for step, to, _ in others
+    ]
+    parts_ref[me] = x_ref[rows_of(me), :]
+    for copy in copies:
+        copy.wait()
+    total = parts_ref[0].astype(jnp.float32)
+    for index in range(1, size):
+        total = total + parts_ref[index].astype(jnp.float32)
+    mine_ref[...] = total.astype(mine_ref.dtype)
+    copies = [
+        push(mine_ref, out_ref.at[rows_of(me)], (s1, r1), step - 1, "vocab", to)
+        for step, to, _ in others
+    ]
+    out_ref[rows_of(me), :] = mine_ref[...]
+    for copy in copies:
+        copy.wait()
+
+
+def sum_vocab(x, collective_id):
+    replicas = lax.axis_size("vocab")
+    rows, columns = x.shape
+    share = rows // replicas
+    return talk(
+        sum_kernel,
+        jax.ShapeDtypeStruct(x.shape, x.dtype),
+        collective_id,
+        x,
+        scratch=[
+            pltpu.VMEM((replicas, share, columns), x.dtype),
+            pltpu.VMEM((share, columns), x.dtype),
+        ]
+        + sem_pair(replicas - 1)
+        + sem_pair(replicas - 1),
+    )
+
+
+def tail_kernel(
+    x_ref, few_ref, out_ref, sum_ref, parts_ref, mine_ref, seen_ref, line_ref, lines_ref,
+    s0, r0, s1, r1, s2, r2, s3, r3,
+):
+    owners, replicas = peers_of("dp"), peers_of("vocab")
+    greet(*[("dp", to) for _, to, _ in owners], *[("vocab", to) for _, to, _ in replicas])
+    me, here = lax.axis_index("dp"), lax.axis_index("vocab")
+    rows = mine_ref.shape[0]
+
+    def rows_of(index):
+        return pl.ds(pl.multiple_of(index * rows, rows), rows)
+
+    few = [
+        push(few_ref, seen_ref.at[here], (s2, r2), step - 1, "vocab", to) for step, to, _ in replicas
+    ]
+    wide = [
+        push(x_ref.at[rows_of(to)], parts_ref.at[me], (s0, r0), step - 1, "dp", to)
+        for step, to, _ in owners
+    ]
+    seen_ref[here] = few_ref[...]
+    parts_ref[me] = x_ref[rows_of(me), :]
+    for copy in few:
+        copy.wait()
+    line_ref[...] = jnp.sum(seen_ref[...], axis=0)
+    few = [
+        push(line_ref, lines_ref.at[me], (s3, r3), step - 1, "dp", to) for step, to, _ in owners
+    ]
+    lines_ref[me] = line_ref[...]
+    for copy in wide:
+        copy.wait()
+    mine_ref[...] = jnp.sum(parts_ref[...].astype(jnp.float32), axis=0).astype(mine_ref.dtype)
+    wide = [
+        push(mine_ref, out_ref.at[rows_of(me)], (s1, r1), step - 1, "dp", to)
+        for step, to, _ in owners
+    ]
+    out_ref[rows_of(me), :] = mine_ref[...]
+    for copy in few:
+        copy.wait()
+    sum_ref[...] = jnp.sum(lines_ref[...], axis=0)
+    for copy in wide:
+        copy.wait()
+
+
+def sum_tail(x, few, collective_id):
+    owners, replicas = lax.axis_size("dp"), lax.axis_size("vocab")
+    rows, columns = x.shape
+    share = rows // owners
+    return talk(
+        tail_kernel,
+        (jax.ShapeDtypeStruct(x.shape, x.dtype), full(*few.shape)),
+        collective_id,
+        x,
+        few,
+        scratch=[
+            pltpu.VMEM((owners, share, columns), x.dtype),
+            pltpu.VMEM((share, columns), x.dtype),
+            pltpu.VMEM((replicas, *few.shape), jnp.float32),
+            pltpu.VMEM(few.shape, jnp.float32),
+            pltpu.VMEM((owners, *few.shape), jnp.float32),
+        ]
+        + sem_pair(owners - 1)
+        + sem_pair(owners - 1)
+        + sem_pair(replicas - 1)
+        + sem_pair(owners - 1),
+    )
+
+
+def flip(index, bit):
+    return index + bit - 2 * bit * lax.rem(index // bit, 2)
+
+
+def quad_kernel(x_ref, out_ref, send_sems, recv_sems):
+    here = lax.axis_index("vocab")
+    far, near = flip(here, 2), flip(here, 1)
+    greet(("vocab", far), ("vocab", near))
+    sems = (send_sems, recv_sems)
+    mine, theirs = lax.rem(here, 4), lax.rem(far, 4)
+    copies = [
+        push(x_ref, out_ref.at[mine], sems, 0, "vocab", far),
+        push(x_ref, out_ref.at[mine], sems, 1, "vocab", near),
+    ]
+    out_ref[mine] = x_ref[...]
+    copies[0].wait()
+    relay = push(out_ref.at[theirs], out_ref.at[theirs], sems, 2, "vocab", near)
+    copies[1].wait()
+    relay.wait()
+
+
+def gather_quad(x, collective_id):
+    out = jax.ShapeDtypeStruct((4, *x.shape), x.dtype)
+    return talk(quad_kernel, out, collective_id, x, scratch=sem_pair(3))
+
+
+def gradient_kernel(x_ref, out_ref, parts_ref, s0, r0, s1, r1, s2, r2):
+    owners = peers_of("dp")
+    here, me = lax.axis_index("vocab"), lax.axis_index("dp")
+    near = flip(here, 1)
+    size = lax.axis_size("vocab")
+    steps = range(2, size, 2)
+    chunks = x_ref.shape[1]
+    greet(
+        *[("dp", to) for _, to, _ in owners],
+        *[("vocab", lax.rem(here + step, size)) for step in steps],
+        ("vocab", near),
+    )
+
+    def spread(c, origin, sems, slot, to):
+        place = out_ref.at[origin, c]
+        return push(place, place, sems, slot, "vocab", to)
+
+    arriving = [
+        [
+            push(x_ref.at[to, c], parts_ref.at[me, c], (s0, r0), (step - 1) * chunks + c, "dp", to)
+            for step, to, _ in owners
+        ]
+        for c in range(chunks)
+    ]
+    far, close = [], []
+    for c in range(chunks):
+        parts_ref[me, c] = x_ref[me, c]
+        for copy in arriving[c]:
+            copy.wait()
+        total = jnp.sum(parts_ref[:, c].astype(jnp.float32), axis=0)
+        out_ref[here, c] = total.astype(out_ref.dtype)
+        far.append(
+            [
+                spread(c, here, (s1, r1), k * chunks + c, lax.rem(here + step, size))
+                for k, step in enumerate(steps)
+            ]
+        )
+        close.append(spread(c, here, (s2, r2), c, near))
+    for c in range(chunks):
+        for k, step in enumerate(steps):
+            far[c][k].wait()
+            origin = lax.rem(here + size - step, size)
+            close.append(spread(c, origin, (s2, r2), (k + 1) * chunks + c, near))
+    for copy in close:
+        copy.wait()
+
+
+def share_gradients(x, collective_id):
+    owners, replicas = lax.axis_size("dp"), lax.axis_size("vocab")
+    chunks = x.shape[1]
+    others = (replicas // 2 - 1) * chunks
+    return talk(
+        gradient_kernel,
+        jax.ShapeDtypeStruct((replicas, *x.shape[1:]), x.dtype),
+        collective_id,
+        x,
+        scratch=[pltpu.VMEM(x.shape, x.dtype)]
+        + sem_pair((owners - 1) * chunks)
+        + sem_pair(others)
+        + sem_pair(others + chunks),
+    )
+
+
+def swap_kernel(x_ref, out_ref, send_sems, recv_sems):
+    others = peers_of("dp")
+    greet(*[("dp", to) for _, to, _ in others])
+    me = lax.axis_index("dp")
+    copies = [
+        push(x_ref.at[to], out_ref.at[me], (send_sems, recv_sems), step - 1, "dp", to)
+        for step, to, _ in others
+    ]
+    out_ref[me] = x_ref[me]
+    for copy in copies:
+        copy.wait()
+
+
+def swap_owners(x, collective_id):
+    owners = lax.axis_size("dp")
+    return talk(
+        swap_kernel,
+        jax.ShapeDtypeStruct(x.shape, x.dtype),
+        collective_id,
+        x,
+        scratch=sem_pair(owners - 1),
+    )
+
+
 def sinusoid(length, model_width):
     places = np.arange(length, dtype=np.float32)[:, None]
     halves = np.arange(model_width // 2, dtype=np.float32)[None, :]
@@ -500,11 +789,12 @@
 ):
     owners, replicas = lax.axis_size("dp"), lax.axis_size("vocab")
     replica = lax.axis_index("vocab")
+    own_table = embedding.astype(jnp.bfloat16)
     w_attn, w_ffn, norm_low, table_low = (
         lax.all_gather(attn_w.astype(jnp.bfloat16), "dp", axis=1, tiled=True),
         lax.all_gather(ffn_w.astype(jnp.bfloat16), "dp", axis=1, tiled=True),
         lax.all_gather(norm_p.astype(jnp.bfloat16), "dp", axis=1, tiled=True),
-        lax.all_gather(embedding.astype(jnp.bfloat16), "dp", axis=1, tiled=True),
+        lax.all_gather(own_table, "dp", axis=1, tiled=True),
     )
     norm_rows = norm_low.astype(jnp.float32)
     norms = [jnp.stack([norm_rows[k], norm_rows[7 + k]]) for k in range(7)]
@@ -514,12 +804,25 @@
     pick_rows, labels = (pick_pos[0], pick_label[0])
     length = source.shape[0]
     embed_scale = math.sqrt(width)
-    looked_up = [
-        lax.psum(
-            dot_dims(one_hot(ids, columns), table_low, 1, 0).astype(jnp.bfloat16), "vocab"
-        ).astype(jnp.float32)
-        for ids in (source, target)
-    ]
+    all_ids = gather_small(jnp.concatenate([src_ids, tgt_ids]), "dp", 1)
+    halves = replica * (vocab_count // 2) + jnp.arange(vocab_count // 2)
+    paired = own_table.reshape(vocab_count // 2, -1)
+
+    def look_up(ids):
+        wide = lax.dot_general(one_hot(ids // 2, halves), paired, (((1,), (0,)), ((), ())))
+        left, right = jnp.split(wide, 2, axis=1)
+        return jnp.where((ids % 2 == 0)[:, None], left, right)
+
+    source_part, target_part = (look_up(all_ids[:, k].reshape(-1)) for k in (0, 1))
+    source_sum = lax.psum(source_part, "vocab")
+    source_sum, target_part = lax.optimization_barrier((source_sum, target_part))
+    target_sum = lax.psum(target_part, "vocab")
+
+    def own_row(summed, collective_id):
+        blocks = swap_owners(summed.reshape(owners, length, -1), collective_id)
+        return jnp.swapaxes(blocks, 0, 1).reshape(length, -1).astype(jnp.float32)
+
+    looked_up = [own_row(source_sum, 2), own_row(target_sum, 3)]
     positional = sinusoid(length, width)
 
     enc_in = looked_up[0] * embed_scale + positional
@@ -543,9 +846,10 @@
     row_total = jnp.sum(jnp.exp(logits - row_top[:, None]), axis=-1)
     label_hit = labels[:, None] == columns[None, :]
     chosen = jnp.sum(jnp.where(label_hit, logits, 0.0), axis=-1)
-    row_top, row_total, chosen = combine_stats(
-        *jnp.moveaxis(lax.all_gather(jnp.stack([row_top, row_total, chosen]), "vocab"), 1, 0)
-    )
+    seen = gather_small(
+        jnp.pad(jnp.stack([row_top, row_total, chosen]), ((0, 5), (0, 0))), "vocab", 4
+    )
+    row_top, row_total, chosen = combine_stats(seen[:, 0], seen[:, 1], seen[:, 2])
     log_total = row_top + jnp.log(row_total)
     weight = 1.0 / pick_weights(target_seg, pick_rows)
     loss_part = jnp.sum((log_total - chosen) * weight)
@@ -553,11 +857,14 @@
     grad_logits = (
         weight[:, None] * (jnp.exp(logits - log_total[:, None]) - label_hit.astype(jnp.float32))
     ).astype(jnp.bfloat16)
-    grad_picked = lax.psum(dot_dims(grad_logits, table_low, 1, 0), "vocab")
-    grad_table = dot_dims(grad_logits, picked, 0, 0)
-    picked_high = grad_picked.astype(jnp.bfloat16)
-    picked_rest = (grad_picked - picked_high.astype(jnp.float32)).astype(jnp.bfloat16)
-    grad_final = dot_dims(chosen_rows, picked_high, 0, 0) + dot_dims(chosen_rows, picked_rest, 0, 0)
+    grad_picked = sum_vocab(dot_dims(grad_logits, table_low, 1, 0).astype(jnp.bfloat16), 5)
+    grad_table = lax.psum_scatter(
+        dot_dims(grad_logits, picked, 0, 0).astype(jnp.bfloat16),
+        "dp",
+        scatter_dimension=1,
+        tiled=True,
+    )
+    grad_final = dot_dims(chosen_rows, grad_picked, 0, 0)
 
     norm_grads = [None] * 7
     grad, norm_grads[6] = plain_norm_backward(grad_final, dec_out, norms[6])
@@ -569,8 +876,16 @@
     grad, norm_grads[1], enc_ffn_parts = ffn_backward(grad, enc_ffn)
     grad, norm_grads[0], enc_parts, _ = attn_backward(grad, enc_attn)
     grad_source = (grad * embed_scale).astype(jnp.bfloat16)
-    for ids, rows in ((source, grad_source), (target, grad_target)):
-        grad_table = grad_table + dot_dims(one_hot(ids, columns), rows, 0, 0)
+    token_grads = jnp.concatenate([grad_source, grad_target]).reshape(2 * length, owners, -1)
+    token_grads = swap_owners(jnp.swapaxes(token_grads, 0, 1), 6).reshape(owners * 2 * length, -1)
+    flat_ids = all_ids.reshape(-1)
+    even = (flat_ids % 2 == 0)[:, None]
+    token_grads = jnp.concatenate(
+        [jnp.where(even, token_grads, 0), jnp.where(even, 0, token_grads)], axis=1
+    )
+    g_embed = grad_table.astype(jnp.float32) + dot_dims(
+        one_hot(flat_ids // 2, halves), token_grads, 0, 0
+    ).reshape(vocab_count, -1)
 
     chosen_columns = share_rows(jnp.eye(width, dtype=jnp.bfloat16), owners, replicas, replica)
     chosen_columns = chosen_columns.reshape(-1, width)
@@ -602,29 +917,27 @@
         + hidden_grads(enc_ffn, enc_ffn_parts)
         + hidden_grads(dec_ffn, dec_ffn_parts)
     )
-    pieces = [piece.astype(jnp.bfloat16).reshape(owners, -1, width) for piece in pieces]
-    summed = lax.psum_scatter(
-        jnp.concatenate(pieces, axis=1), "dp", scatter_dimension=0, tiled=False
-    )
-    shared = lax.all_gather(summed, "vocab")
-    attn_rows = 12 * (width // (owners * replicas))
-    g_attn = jnp.moveaxis(shared[:, :attn_rows].reshape(replicas, 12, -1, width), 0, 1)
-    g_attn = g_attn.reshape(12, -1, width).astype(jnp.float32)
-    g_ffn = jnp.moveaxis(shared[:, attn_rows:].reshape(replicas, 4, -1, width), 0, 1)
-    g_ffn = g_ffn.reshape(4, -1, width).astype(jnp.float32)
+    blocks = [piece.astype(jnp.bfloat16).reshape(owners, -1, width) for piece in pieces]
+    blocks = [jnp.concatenate(blocks[k : k + 4], axis=1) for k in (0, 4, 8)] + blocks[12:]
+    shared = share_gradients(jnp.stack(blocks, axis=1), 7)
+    g_attn = shared[:, :3].reshape(replicas, 12, -1, width)
+    g_attn = jnp.swapaxes(g_attn, 0, 1).reshape(12, -1, width).astype(jnp.float32)
+    g_ffn = jnp.swapaxes(shared[:, 3:], 0, 1).reshape(4, -1, width)
     norm_grad = jnp.stack(norm_grads)
     norm_grad = jnp.concatenate([norm_grad[:, 0], norm_grad[:, 1]], axis=0)
     g_norm = lax.psum_scatter(norm_grad, "dp", scatter_dimension=1, tiled=True)
-    g_embed = lax.psum_scatter(
-        grad_table.astype(jnp.bfloat16), "dp", scatter_dimension=1, tiled=True
-    ).astype(jnp.float32)
-
+
+    matrix = replica % 4
+    own_grad = lax.dynamic_index_in_dim(g_ffn, matrix, 0, keepdims=False)
+    own_products = dot_dims(own_grad, own_grad, 0, 0)
+    g_ffn = g_ffn.astype(jnp.float32)
     first_copy = (replica == 0).astype(jnp.float32)
     layer_sq = jnp.sum(g_attn * g_attn) + jnp.sum(g_ffn * g_ffn) + jnp.sum(g_norm * g_norm)
     raw_squares = jnp.sum(g_embed * g_embed) + first_copy * layer_sq
-    loss_sum, sentences, squares = lax.psum(
-        jnp.stack([first_copy * loss_part, first_copy * count_part, raw_squares]), ("dp", "vocab")
-    )
+    few = jnp.stack([first_copy * loss_part, first_copy * count_part, raw_squares])
+    few = jnp.broadcast_to(jnp.pad(few, (0, 5))[:, None], (8, 128))
+    own_products, few = sum_tail(own_products, few, 8)
+    loss_sum, sentences, squares = few[0, 0], few[1, 0], few[2, 0]
     grad_norm = jnp.sqrt(squares) / sentences
     factor = jnp.minimum(1.0, clip_limit / (grad_norm + norm_eps)) / sentences
     g_attn, g_ffn, g_norm, g_embed = (
@@ -633,14 +946,15 @@
         g_norm * factor,
         g_embed * factor,
     )
-    matrix = replica % 4
-    own_grad = lax.dynamic_index_in_dim(g_ffn, matrix, 0, keepdims=False)
+    all_products = lax.all_gather(own_products.astype(jnp.bfloat16), "vocab")[:4]
+    new_stats = stat_decay * soap_stats + (1.0 - stat_decay) * (factor * factor) * (
+        all_products.astype(jnp.float32)
+    )
     own_stat = stat_decay * lax.dynamic_index_in_dim(soap_stats, matrix, 0, keepdims=False) + (
         1.0 - stat_decay
-    ) * lax.psum(dot_exact(own_grad, own_grad, 0, 0), "dp")
+    ) * (factor * factor) * own_products
     own_basis = renew_basis(own_stat, lax.dynamic_index_in_dim(soap_basis, matrix, 0, keepdims=False))
-    renewed = lax.all_gather(jnp.stack([own_stat, own_basis]).astype(jnp.bfloat16), "vocab")[:4]
-    new_stats, new_basis = (renewed[:, k].astype(jnp.float32) for k in (0, 1))
+    new_basis = gather_quad(own_basis.astype(jnp.bfloat16), 9).astype(jnp.float32)
 
     new_attn, m_attn, v_attn = adam_update(attn_w, g_attn, attn_m, attn_v, rate_matrix, decay_rate)
     new_norm, m_norm, v_norm = adam_update(norm_p, g_norm, norm_m, norm_v, rate_vector, 0.0)

time: 1020 us -> 826 us (0.81)
  waiting for transfers between devices: 469 us -> 118 us
  Pallas kernels: 209 us -> 427 us
  blocking collectives: 61.1 us -> 8.35 us
  matrix products: 108 us -> 85.5 us
    pallas_call x0 -> x9, Pallas kernels: none -> 220 us  [talk(): pl.pallas_call(kernel, out_shape=outs, in_specs=[vmem] * len(args), out_s...]
    all_gather x3 -> x2, waiting for transfers between devices: 141 us -> 11 us  [the longest x1 11 us: body(): lax.all_gather(own_table, 'dp', axis=1, tiled=True)]
    psum x3 -> x2, waiting for transfers between devices: 147 us -> 69 us  [the longest x1 50.3 us: body(): source_sum = lax.psum(source_part, 'vocab')]
    all_gather x1, waiting for transfers between devices: 67.4 us -> 0.57 us  [body(): lax.all_gather(attn_w.astype(jnp.bfloat16), 'dp', axis=1, tiled=True)]
    unnamed x13 -> x9, waiting for transfers between devices: 61.1 us -> 0.66 us
    psum x1 -> x0, blocking collectives: 39.1 us -> none  [body(): lax.psum(jnp.stack([first_copy * loss_part, first_copy * count_part, raw_...]
    dot_general x29 -> x26, matrix products: 84.4 us -> 47 us  [dot_dims(): lax.dot_general(left, right, (((left_dim,), (right_dim,)), ((), ())), pre...]
    reduce_scatter x1, waiting for transfers between devices: 15.5 us -> 0.01 us  [body(): g_norm = lax.psum_scatter(norm_grad, 'dp', scatter_dimension=1, tiled=True)]
  transfers between devices with their start and end apart: 11 -> 8, of which waited for: 10 -> 5; matrix products, arithmetic and copies ran while one was open for 12% -> 20% of each run, Pallas kernels for 4% -> 33%
where the time goes in v2:
time: 826 us; the launch traced here: 816 us
  Pallas kernels  427 us (52%)
  waiting for transfers between devices  118 us (14%)
  matrix products  85.5 us (10%)
  local copies, waits for them, and re-layouts  82.3 us (10%)
  other arithmetic  70.6 us (9%)
  between operations  24 us (3%)
  blocking collectives  8.35 us (1%)
    pallas_call x9, Pallas kernels, talk(): pl.pallas_call(kernel, out_shape=outs, in_specs=[vmem] * len(args), out_s...  220 us
    pallas_call x12, Pallas kernels, call(): pl.pallas_call(kernel, out_shape=outs, in_specs=[vmem] * (len(args) - sme...  207 us
    psum x1, waiting for transfers between devices, body(): source_sum = lax.psum(source_part, 'vocab')  50.3 us
    dot_general x26, matrix products, dot_dims(): lax.dot_general(left, right, (((left_dim,), (right_dim,)), ((), ())), pre...  47 us
    all_gather x1, waiting for transfers between devices, body(): lax.all_gather(ffn_w.astype(jnp.bfloat16), 'dp', axis=1, tiled=True)  37 us
    pallas_call x1, local copies, waits for them, and re-layouts, call(): pl.pallas_call(kernel, out_shape=outs, in_specs=[vmem] * (len(args) - sme...  20.6 us
    psum x1, waiting for transfers between devices, body(): target_sum = lax.psum(target_part, 'vocab')  18.7 us
  transfers between devices with their start and end apart: 8, of which 5 were waited for; matrix products, arithmetic and copies ran while one was open for 20% of the time, Pallas kernels for 33%

profile of v2, /device:TPU:0, one launch (start us, length us, event | category | flops | bytes accessed | tf_op | source)
XLA Modules:
  0.0 816.3 jit_solution(14985323643990673357)
XLA Ops:
  9.4 7.5 shard_map.332
  20.1 6.9 fusion.4
  30.0 6.9 fusion.2
  39.8 50.3 %all-reduce.5.cloned.1.call-done = bf16[4096,128]{1,0:T(8,128)(2,1)} async-done(((bf16[4096,128]{1,0:T(8,128)(2,1)}), bf16[4096,128]{1,0:T(8,128)(2,1)}) %all-reduce.5.cloned.1.call-update) | async-done | bytes 1048592 | tf_op jit(solution)/shard_map/psum | solution.py:817
  99.1 8.3 %all_gather.18 = bf16[14,512]{1,0:T(8,128)(2,1)S(1)} all-gather(bf16[14,128]{1,0:T(8,128)(2,1)S(1)} %convert_element_type.163), channel_id=1, replica_groups=mesh['dp'=4,'vocab'=8] {'dp'}, dimensions={1}, use_global_device_ids=true | all-gather | bytes 17920 | tf_op jit(solution)/shard_map/all_gather | solution.py:796
  111.5 20.9 %shard_map.333 = bf16[4,1024,128]{2,1,0:T(8,128)(2,1)} custom-call(bf16[4,1024,128]{2,1,0:T(8,128)(2,1)} %bitcast.229), custom_call_target="tpu_custom_call" | custom-call | tf_op jit(solution)/shard_map/pallas_call | solution.py:466
  132.5 18.7 %all-reduce.7.cloned.1.call-done.x_ref = bf16[4,1024,128]{2,1,0:T(8,128)(2,1)} async-done(((bf16[4,1024,128]{2,1,0:T(8,128)(2,1)}), bf16[4,1024,128]{2,1,0:T(8,128)(2,1)}) %all-reduce.7.cloned.1.call-update) | async-done | bytes 1048592 | tf_op jit(solution)/shard_map/psum | solution.py:819
  151.2 28.1 %shard_map.335 = bf16[4,1024,128]{2,1,0:T(8,128)(2,1)} custom-call(bf16[4,1024,128]{2,1,0:T(8,128)(2,1)} %all-reduce.7.cloned.1.call-done.x_ref), custom_call_target="tpu_custom_call" | custom-call | tf_op jit(solution)/shard_map/pallas_call | solution.py:466
  191.1 18.6 %shard_map.336 = (f32[1024,512]{1,0:T(8,128)}, bf16[1024,512]{1,0:T(8,128)(2,1)}, bf16[512,1024]{1,0:T(8,128)(2,1)}, bf16[512,1024]{1,0:T(8,128)(2,1)}, bf16[512...) custom-call(f32[1024,512]{1,0:T(8,128)} %get-tuple-element.215.refs_0_, ...), custom_call_target="tpu_custom_call" | custom-call | tf_op jit(solution)/shard_map/pallas_call | solution.py:50
  210.7 21.3 %shard_map.334 = (f32[1024,512]{1,0:T(8,128)}, bf16[1024,512]{1,0:T(8,128)(2,1)}, bf16[512,1024]{1,0:T(8,128)(2,1)}, bf16[512,1024]{1,0:T(8,128)(2,1)}, bf16[512...) custom-call(f32[1024,512]{1,0:T(8,128)} %get-tuple-element.216.refs_0_.refs_1_, ...), custom_call_target="tpu_custom_call" | custom-call | tf_op jit(solution)/shard_map/pallas_call | solution.py:50
  237.2 37.0 %all-gather.8.cloned.1.call-done = bf16[4,2048,512]{2,1,0:T(8,128)(2,1)} async-done(((bf16[4,512,512]{2,1,0:T(8,128)(2,1)}), bf16[4,2048,512]{2,1,0:T(8,128)(2,1)}) %all-gather.8.cloned.1.call-update) | async-done | bytes 8388624 | tf_op jit(solution)/shard_map/all_gather | solution.py:795
  280.7 11.2 %shard_map.337 = (f32[1024,512]{1,0:T(8,128)}, bf16[1024,512]{1,0:T(8,128)(2,1)}, bf16[1024,512]{1,0:T(8,128)(2,1)}) custom-call(f32[1024,512]{1,0:T(8,128)} %get-tuple-element.85.x_ref, f32[2,512]{1,0:T(2,128)} %get-tuple-element.219.ln_ref, f32[2,512]{1,0:T(2,128)} %get-tuple-element.220.next_ref.ln_ref, bf16[2048,512]{1,0:T(8,128)(2,1)} %get-tuple-element.176.w_in_ref, ...), custom_call_target="tpu_custom_call" | custom-call | tf_op jit(solution)/shard_map/pallas_call | solution.py:50
  291.9 18.7 %shard_map.338 = (f32[1024,512]{1,0:T(8,128)}, bf16[1024,512]{1,0:T(8,128)(2,1)}, bf16[512,1024]{1,0:T(8,128)(2,1)}, bf16[512,1024]{1,0:T(8,128)(2,1)}, bf16[512...) custom-call(f32[1024,512]{1,0:T(8,128)} %get-tuple-element.84.refs_0_.refs_1_, ...), custom_call_target="tpu_custom_call" | custom-call | tf_op jit(solution)/shard_map/pallas_call | solution.py:50
  310.6 11.1 %shard_map.339 = (f32[1024,512]{1,0:T(8,128)}, bf16[1024,512]{1,0:T(8,128)(2,1)}, bf16[1024,512]{1,0:T(8,128)(2,1)}) custom-call(f32[1024,512]{1,0:T(8,128)} %get-tuple-element.87.x_ref, f32[2,512]{1,0:T(2,128)} %get-tuple-element.221.ln_ref, f32[2,512]{1,0:T(2,128)} %get-tuple-element.222.next_ref.ln_ref, bf16[2048,512]{1,0:T(8,128)(2,1)} %get-tuple-element.174.w_in_ref, ...), custom_call_target="tpu_custom_call" | custom-call | tf_op jit(solution)/shard_map/pallas_call | solution.py:50
  323.4 11.0 %all-gather.10.cloned.1.call-done = bf16[4736,512]{1,0:T(8,128)(2,1)} async-done(((bf16[4736,128]{1,0:T(8,128)(2,1)}), bf16[4736,512]{1,0:T(8,128)(2,1)}) %all-gather.10.cloned.1.call-update) | async-done | bytes 4849680 | tf_op jit(solution)/shard_map/all_gather | solution.py:797
  340.3 7.4 shard_map.340
  357.0 16.6 %shard_map.341 = bf16[256,512]{1,0:T(8,128)(2,1)} custom-call(bf16[256,512]{1,0:T(8,128)(2,1)} %convolution_convert_fusion.5.x_ref), custom_call_target="tpu_custom_call" | custom-call | tf_op jit(solution)/shard_map/pallas_call | solution.py:466
  381.4 17.3 %shard_map.343 = (f32[1024,512]{1,0:T(8,128)}, f32[2,512]{1,0:T(2,128)}, bf16[1024,512]{1,0:T(8,128)(2,1)}, bf16[2048,1024]{1,0:T(8,128)(2,1)}, bf16[2048,1024]{1,0:T(8,128)(2,1)}) custom-call(f32[1024,512]{1,0:T(8,128)} %get-tuple-element.90.g_ref, f32[1024,512]{1,0:T(8,128)} %get-tuple-element.87.x_ref, f32[2,512]{1,0:T(2,128)} %get-tuple-element.221.ln_ref, ...), custom_call_target="tpu_custom_call" | custom-call | tf_op jit(solution)/shard_map/pallas_call | solution.py:50
  398.7 24.3 %shard_map.344 = (f32[1024,512]{1,0:T(8,128)}, f32[2,512]{1,0:T(2,128)}, bf16[1024,512]{1,0:T(8,128)(2,1)}, bf16[1024,512]{1,0:T(8,128)(2,1)}, bf16[1024,512]{1,...) custom-call(f32[1024,512]{1,0:T(8,128)} %get-tuple-element.92.refs_0_, ...), custom_call_target="tpu_custom_call" | custom-call | tf_op jit(solution)/shard_map/pallas_call | solution.py:50
  427.8 17.7 %shard_map.346 = (f32[1024,512]{1,0:T(8,128)}, f32[2,512]{1,0:T(2,128)}, bf16[1024,512]{1,0:T(8,128)(2,1)}, bf16[2048,1024]{1,0:T(8,128)(2,1)}, bf16[2048,1024]{1,0:T(8,128)(2,1)}) custom-call(f32[1024,512]{1,0:T(8,128)} %get-tuple-element.100.g_ref, f32[1024,512]{1,0:T(8,128)} %get-tuple-element.85.x_ref, f32[2,512]{1,0:T(2,128)} %get-tuple-element.219.ln_ref, ...), custom_call_target="tpu_custom_call" | custom-call | tf_op jit(solution)/shard_map/pallas_call | solution.py:50
  445.7 27.7 %shard_map.347 = (f32[1024,512]{1,0:T(8,128)}, f32[2,512]{1,0:T(2,128)}, bf16[1024,512]{1,0:T(8,128)(2,1)}, bf16[1024,512]{1,0:T(8,128)(2,1)}, bf16[1024,512]{1,0:T(8,128)(2,1)}, /*index=5*/bf16[1024,512]{1,0:T(8,128)(2,1)}) custom-call(f32[1024,512]{1,0:T(8,128)} %get-tuple-element.102.refs_0_, f32[1024,512]{1,0:T(8,128)} %get-tuple-element.216.refs_0_.refs_1_, ...), custom_call_target="tpu_custom_call" | custom-call | tf_op jit(solution)/shard_map/pallas_call | solution.py:50
  474.1 20.6 %shard_map.353 = (f32[7,2,512]{2,1,0:T(2,128)S(1)}, bf16[1024,512]{1,0:T(8,128)(2,1)}, bf16[1024,512]{1,0:T(8,128)(2,1)}, bf16[1024,512]{1,0:T(8,128)(2,1)}, bf1...) fusion(f32[7,2,512]{2,1,0:T(2,128)S(1)} %constant_dynamic-update-slice_fusion.8, ...), kind=kCustom, calls=%fused_computation.130 | custom fusion | bytes 17348608 | tf_op jit(solution)/shard_map/pallas_call | solution.py:50
  505.8 7.4 copy.67
  519.5 28.6 %shard_map.349 = bf16[4,2048,128]{2,1,0:T(8,128)(2,1)} custom-call(bf16[4,2048,128]{2,1,0:T(8,128)(2,1)} %bitcast.213), custom_call_target="tpu_custom_call" | custom-call | tf_op jit(solution)/shard_map/pallas_call | solution.py:466
  567.4 56.8 %shard_map.348 = bf16[8,7,64,512]{3,2,1,0:T(8,128)(2,1)} custom-call(bf16[4,7,64,512]{3,2,1,0:T(8,128)(2,1)} %constant_dynamic-update-slice_fusion.x_ref), custom_call_target="tpu_custom_call" | custom-call | tf_op jit(solution)/shard_map/pallas_call | solution.py:466
  628.6 12.0 %fusion = f32[2368,256]{1,0:T(8,128)} fusion(s32[8192]{0:T(1024)S(1)} %add_select_fusion.1, s32[2368]{0:T(1024)S(1)} %copy-done.45, bf16[8192,128]{1,0:T(8,128)(2,1)S(1)} %get-tuple-element.183, bf16[8192,128]{1,0:T(8,128)(2,1)S(1)} %get-tuple-element.182), kind=kOutput, calls=%fused_computation.1 | convolution fusion | flops 9959899136 | bytes 6661376 | tf_op jit(solution)/shard_map/dot_general | solution.py:34
  663.2 32.0 %shard_map.350 = (f32[512,512]{1,0:T(8,128)}, f32[8,128]{1,0:T(8,128)}) custom-call(f32[512,512]{1,0:T(8,128)} %fusion.42.x_ref, f32[8,128]{1,0:T(8,128)} %broadcast_in_dim.93.few_ref), custom_call_target="tpu_custom_call" | custom-call | tf_op jit(solution)/shard_map/pallas_call | solution.py:466
  706.4 29.2 %shard_map.351 = f32[512,512]{1,0:T(8,128)} custom-call(f32[512,512]{1,0:T(8,128)} %get-tuple-element.187.stat_ref, f32[512,512]{1,0:T(8,128)} %dynamic-slice_bitcast_fusion.basis_ref), custom_call_target="tpu_custom_call" | custom-call | tf_op jit(solution)/shard_map/pallas_call | solution.py:50
  737.7 22.1 %shard_map.352 = bf16[4,512,512]{2,1,0:T(8,128)(2,1)} custom-call(bf16[512,512]{1,0:T(8,128)(2,1)} %convert_element_type.202.x_ref), custom_call_target="tpu_custom_call" | custom-call | tf_op jit(solution)/shard_map/pallas_call | solution.py:466
  764.9 11.7 %multiply_add_fusion.1 = (f32[4,512,512]{2,1,0:T(8,128)S(1)}, f32[4,512,512]{2,1,0:T(8,128)}) fusion(f32[4,512,512]{2,1,0:T(8,128)} %param.31, f32[4,512,512]{2,1,0:T(8,128)} %param.32, f32[4,512,512]{2,1,0:T(8,128)S(1)} %copy-done.12, bf16[4,512,512]{2,1,0:T(8,128)(2,1)S(1)} %bitcast.211, f32[]{:T(128)S(6)} %div.120), kind=kOutput, calls=%fused_computation.36 | convolution fusion | flops 6451888128 | bytes 23068676 | tf_op jit(solution)/shard_map/mfd,mde->mfe/dot_general | solution.py:964
  776.6 7.5 multiply_subtract_fusion.1
  784.1 13.1 %multiply_subtract_fusion = f32[4,512,512]{2,1,0:T(8,128)} fusion(f32[4,512,512]{2,1,0:T(8,128)} %param.30, f32[4,512,512]{2,1,0:T(8,128)S(1)} %copy-done.12, f32[4,512,512]{2,1,0:T(8,128)} %get-tuple-element.181, f32[4,512,512]{2,1,0:T(8,128)S(1)} %get-tuple-element.180), kind=kOutput, calls=%fused_computation.29 | convolution fusion | flops 6450839552 | bytes 20971520 | tf_op jit(solution)/shard_map/mfe,mde->mfd/dot_general | solution.py:967
  (262 shorter events, 163.9 us)
Async XLA Ops:
  8.0 82.0 %all-reduce.5.cloned.1.call-start = ((), (), s32[]{:S(2)}) async-start(), calls=%async_computation.2 | async-start | bytes 2097152 | tf_op jit(solution)/shard_map/psum | solution.py:817
  29.9 121.3 %all-reduce.7.cloned.1.call-start = ((), (), s32[]{:S(2)}) async-start(), calls=%async_computation.4 | async-start | bytes 2097152 | tf_op jit(solution)/shard_map/psum | solution.py:819
  36.9 53.3 %copy-start.5 = (f32[12,128,512]{2,1,0:T(8,128)S(1)}, f32[12,128,512]{2,1,0:T(8,128)}, u32[]{:S(2)}) copy-start(f32[12,128,512]{2,1,0:T(8,128)} %param.27) | copy-start | bytes 9437188
  90.1 94.4 %all-gather.6.cloned.1.call-start = ((), (), s32[]{:S(2)}) async-start(), calls=%async_computation.3 | async-start | bytes 7864320 | tf_op jit(solution)/shard_map/all_gather | solution.py:794
  91.5 182.7 %all-gather.8.cloned.1.call-start = ((), (), s32[]{:S(2)}) async-start(), calls=%async_computation.5 | async-start | bytes 10485760 | tf_op jit(solution)/shard_map/all_gather | solution.py:795
  95.4 239.0 %all-gather.10.cloned.1.call-start = ((), (), s32[]{:S(2)}) async-start(), calls=%async_computation.6 | async-start | bytes 6062080 | tf_op jit(solution)/shard_map/all_gather | solution.py:797
  96.0 83.3 %copy-start.24 = (f32[4,1024,128]{2,1,0:T(8,128)S(1)}, f32[4,1024,128]{2,1,0:T(8,128)}, u32[]{:S(2)}) copy-start(f32[4,1024,128]{2,1,0:T(8,128)} %constant.224) | copy-start | bytes 6291460
  96.0 558.7 %reduce-scatter.5.cloned.1.call-start = ((), (), s32[]{:S(2)}) async-start(), calls=%async_computation.7 | async-start | bytes 40960 | tf_op jit(solution)/shard_map/reduce_scatter | solution.py:928
  209.7 25.4 %copy-start.32 = (bf16[1024,512]{1,0:T(8,128)(2,1)S(1)}, bf16[1024,512]{1,0:T(8,128)(2,1)}, u32[]{:S(2)}) copy-start(bf16[1024,512]{1,0:T(8,128)(2,1)} %get-tuple-element.112) | copy-start | bytes 3145732
  323.4 14.9 %copy-start.48 = (s32[1,256]{1,0:T(1,128)S(1)}, s32[1,256]{1,0:T(1,128)}, u32[]{:S(2)}) copy-start(s32[1,256]{1,0:T(1,128)} %param.26) | copy-start | bytes 3076
  445.6 28.4 %copy-start.53 = (f32[2,512]{1,0:T(2,128)S(1)}, f32[2,512]{1,0:T(2,128)}, u32[]{:S(2)}) copy-start(f32[2,512]{1,0:T(2,128)} %get-tuple-element.137) | copy-start | bytes 12292
  445.6 28.4 %copy-start.52 = (f32[2,512]{1,0:T(2,128)S(1)}, f32[2,512]{1,0:T(2,128)}, u32[]{:S(2)}) copy-start(f32[2,512]{1,0:T(2,128)} %get-tuple-element.138) | copy-start | bytes 12292
  445.6 28.4 %copy-start.1 = (s32[1,1024]{1,0:T(1,128)S(1)}, s32[1,1024]{1,0:T(1,128)}, u32[]{:S(2)}) copy-start(s32[1,1024]{1,0:T(1,128)} %refs_4_.3) | copy-start | bytes 12292
  445.6 28.4 %copy-start.3 = (f32[1024,512]{1,0:T(8,128)S(1)}, f32[1024,512]{1,0:T(8,128)}, u32[]{:S(2)}) copy-start(f32[1024,512]{1,0:T(8,128)} %get-tuple-element.215.refs_0_) | copy-start | bytes 6291460
  445.6 28.4 %copy-start.4 = (bf16[4,512,512]{2,1,0:T(8,128)(2,1)S(1)}, bf16[4,512,512]{2,1,0:T(8,128)(2,1)}, u32[]{:S(2)}) copy-start(bf16[4,512,512]{2,1,0:T(8,128)(2,1)} %get-tuple-element.178.refs_2_) | copy-start | bytes 6291460
  445.6 28.4 %copy-start.14 = (s32[1024,128]{1,0:T(8,128)S(1)}, s32[1024,128]{1,0:T(8,128)}, u32[]{:S(2)}) copy-start(s32[1024,128]{1,0:T(8,128)} %broadcast_in_dim.89.refs_4_) | copy-start | bytes 1572868
  445.6 28.4 %copy-start.38 = (f32[2,512]{1,0:T(2,128)S(1)}, f32[2,512]{1,0:T(2,128)}, u32[]{:S(2)}) copy-start(f32[2,512]{1,0:T(2,128)} %get-tuple-element.218.refs_1_) | copy-start | bytes 12292
  445.6 28.4 %copy-start.39 = (f32[8,1024]{1,0:T(8,128)S(1)}, f32[8,1024]{1,0:T(8,128)}, u32[]{:S(2)}) copy-start(f32[8,1024]{1,0:T(8,128)} %get-tuple-element.118) | copy-start | bytes 98308
  445.6 28.4 %copy-start.42 = (s32[4,8]{1,0:T(4,128)S(1)}, s32[4,8]{1,0:T(4,128)}, u32[]{:S(2)}) copy-start(s32[4,8]{1,0:T(4,128)} %get-tuple-element.212.refs_5_) | copy-start | bytes 388
  474.1 20.6 %copy-start.51 = (f32[2,512]{1,0:T(2,128)S(1)}, f32[2,512]{1,0:T(2,128)}, u32[]{:S(2)}) copy-start(f32[2,512]{1,0:T(2,128)} %get-tuple-element.140) | copy-start | bytes 12292
  474.1 20.6 %copy-start.50 = (f32[2,512]{1,0:T(2,128)S(1)}, f32[2,512]{1,0:T(2,128)}, u32[]{:S(2)}) copy-start(f32[2,512]{1,0:T(2,128)} %get-tuple-element.141) | copy-start | bytes 12292
  474.1 20.6 %copy-start.49 = (f32[2,512]{1,0:T(2,128)S(1)}, f32[2,512]{1,0:T(2,128)}, u32[]{:S(2)}) copy-start(f32[2,512]{1,0:T(2,128)} %get-tuple-element.142) | copy-start | bytes 12292
  495.5 161.2 %reduce-scatter.7.cloned.1.call-start = ((), (), s32[]{:S(2)}) async-start(), calls=%async_computation.9 | async-start | bytes 6062080
  548.1 253.6 %all-gather.12.cloned.1.call-start = ((), (), s32[]{:S(2)}) async-start(), calls=%async_computation.8 | async-start | bytes 4718592 | tf_op jit(solution)/shard_map/all_gather | solution.py:949
  566.7 57.6 %copy-start.11 = (bf16[4,2048,128]{2,1,0:T(8,128)(2,1)S(1)}, bf16[4,2048,128]{2,1,0:T(8,128)(2,1)}, u32[]{:S(2)}) copy-start(bf16[4,2048,128]{2,1,0:T(8,128)(2,1)} %shard_map.349) | copy-start | bytes 6291460
  737.7 26.5 %copy-start.41 = (f32[14,128]{1,0:T(8,128)S(1)}, f32[14,128]{1,0:T(8,128)}, u32[]{:S(2)}) copy-start(f32[14,128]{1,0:T(8,128)} %reduce-scatter.5.cloned.1.call-done) | copy-start | bytes 21508
  737.7 26.5 %copy-start.46 = (f32[14,128]{1,0:T(8,128)S(1)}, f32[14,128]{1,0:T(8,128)}, u32[]{:S(2)}) copy-start(f32[14,128]{1,0:T(8,128)} %param.36) | copy-start | bytes 21508
  737.7 26.5 %copy-start.47 = (f32[14,128]{1,0:T(8,128)S(1)}, f32[14,128]{1,0:T(8,128)}, u32[]{:S(2)}) copy-start(f32[14,128]{1,0:T(8,128)} %param.37) | copy-start | bytes 21508
  784.1 13.2 %copy-start.8 = (bf16[4736,128]{1,0:T(8,128)(2,1)S(1)}, bf16[4736,128]{1,0:T(8,128)(2,1)}, u32[]{:S(2)}) copy-start(bf16[4736,128]{1,0:T(8,128)(2,1)} %copy.68) | copy-start | bytes 3637252
  784.1 13.2 %copy-start.10 = (f32[4736,128]{1,0:T(8,128)S(1)}, f32[4736,128]{1,0:T(8,128)}, u32[]{:S(2)}) copy-start(f32[4736,128]{1,0:T(8,128)} %param.38) | copy-start | bytes 7274500
  784.1 13.2 %copy-start.21 = (f32[4736,128]{1,0:T(8,128)S(1)}, f32[4736,128]{1,0:T(8,128)}, u32[]{:S(2)}) copy-start(f32[4736,128]{1,0:T(8,128)} %param.39) | copy-start | bytes 7274500
  784.1 13.2 %copy-start.22 = (f32[4736,128]{1,0:T(8,128)S(1)}, f32[4736,128]{1,0:T(8,128)}, u32[]{:S(2)}) copy-start(f32[4736,128]{1,0:T(8,128)} %param.40) | copy-start | bytes 7274500
  (32 other events, 160.3 us)
Sparse Core Ops, SparseCore 0:
  30.0 59.9 all-reduce.4
  93.0 58.1 all-reduce.6
  702.1 46.6 all-gather.11
Sparse Core Ops, SparseCore 1:
  93.0 91.4 all-gather.5
  186.8 87.4 all-gather.7
  276.5 57.8 all-gather.9
  495.5 22.7 reduce-scatter.4
  548.2 77.6 reduce-scatter.6

commit v3 on v2

--- a/solution.py
+++ b/solution.py
@@ -123,12 +123,49 @@
     return jnp.stack([seg_q[::TILE], seg_q[last::TILE], seg_k[::TILE], seg_k[last::TILE]])
 
 
-def attn_forward_kernel(causal, cross, *refs):
+def lay_weights(w_ref, piece_refs):
+    own = piece_refs[0]
+    w_ref_rows = own.shape[1]
+    me, side = lax.axis_index("dp"), lax.rem(lax.axis_index("vocab"), 2)
+    half = own.shape[0] // 2
+
+    def rows_of(index):
+        return pl.ds(pl.multiple_of(index * w_ref_rows, w_ref_rows), w_ref_rows)
+
+    w_ref[:, rows_of(me), :] = own[...]
+    for k in range(1, 4):
+        rows = rows_of(me ^ k)
+        w_ref[pl.ds(side * half, half), rows, :] = piece_refs[k][...]
+        w_ref[pl.ds((1 - side) * half, half), rows, :] = piece_refs[k + 3][...]
+
+
+def gather_weights(own, after):
+    if after is not None:
+        own, _ = lax.optimization_barrier((own, after))
+    owners, replicas = lax.axis_size("dp"), lax.axis_size("vocab")
+    if owners != 4:
+        whole = lax.all_gather(own, "dp", axis=1, tiled=True)
+        return (whole,), whole[0, 0]
+    half = own.shape[0] // 2
+    mine = lax.dynamic_slice_in_dim(own, lax.axis_index("vocab") % 2 * half, half, 0)
+    got = [lax.ppermute(mine, "dp", [(s, s ^ k) for s in range(owners)]) for k in range(1, 4)]
+    swapped = [lax.ppermute(part, "vocab", [(s, s ^ 1) for s in range(replicas)]) for part in got]
+    return (own, *got, *swapped), swapped[-1][0, 0]
+
+
+def attn_forward_kernel(causal, cross, pieces, *refs):
     refs = list(refs)
-    x_ref, ln_ref, w_ref, segq_ref, segk_ref = refs[:5]
-    refs = refs[5:]
+    x_ref, ln_ref, segq_ref, segk_ref = refs[:4]
+    refs = refs[4:]
     key_ref = refs.pop(0) if cross else None
-    (edge_ref, out_ref, a_ref, qt_ref, kt_ref, vt_ref, ot_ref, lse_ref, top_ref, sum_ref, acc_ref) = refs
+    piece_refs, refs = refs[:pieces], refs[pieces:]
+    edge_ref, out_ref, a_ref, qt_ref, kt_ref, vt_ref, ot_ref, lse_ref = refs[:8]
+    refs = refs[8:]
+    w_ref = piece_refs[0]
+    if pieces > 1:
+        w_ref = refs.pop(0)
+        lay_weights(w_ref, piece_refs)
+    top_ref, sum_ref, acc_ref = refs
     length, width = x_ref.shape
     head_size = width // HEADS
     a_ref[...] = norm_forward(x_ref[...], ln_ref).astype(jnp.bfloat16)
@@ -179,11 +216,14 @@
     cross = key_in is not None
     segs = (seg_q[None, :], jnp.broadcast_to(seg_k[:, None], (length, TILE)))
     edges = tile_edges(seg_q, seg_k)
-    args = (x, ln, weights, *segs) + ((key_in,) if cross else ()) + (edges,)
+    args = (x, ln, *segs) + ((key_in,) if cross else ()) + (*weights, edges)
     outs = (full(length, width), low(length, width)) + (low(width, length),) * 4
+    outs = outs + (full(HEADS, length),)
+    if len(weights) > 1:
+        outs = outs + (low(4, width, width),)
     out, normed, *stored = call(
-        partial(attn_forward_kernel, causal, cross),
-        outs + (full(HEADS, length),),
+        partial(attn_forward_kernel, causal, cross, len(weights)),
+        outs,
         *args,
         scratch=[
             pltpu.VMEM((HEADS, length), jnp.float32),
@@ -192,7 +232,8 @@
         ],
         smem_args=1,
     )
-    return out, (x, ln, weights, segs, edges, causal, cross, normed, stored)
+    whole = stored.pop() if len(weights) > 1 else weights[0]
+    return out, (x, ln, whole, segs, edges, causal, cross, normed, stored)
 
 
 def attn_backward_kernel(causal, cross, *refs):
@@ -285,7 +326,13 @@
     return value, slope
 
 
-def ffn_forward_kernel(chunk, x_ref, ln_ref, next_ref, w_in_ref, w_out_ref, out_ref, a_ref, after_ref):
+def ffn_forward_kernel(chunk, pieces, x_ref, ln_ref, next_ref, *refs):
+    piece_refs, (out_ref, a_ref, after_ref, *refs) = refs[:pieces], refs[pieces:]
+    w_ref = piece_refs[0]
+    if pieces > 1:
+        (w_ref,) = refs
+        lay_weights(w_ref, piece_refs)
+    w_in_ref, w_out_ref = w_ref.at[0], w_ref.at[1]
     a_ref[...] = norm_forward(x_ref[...], ln_ref).astype(jnp.bfloat16)
     total = x_ref[...]
     for start in range(0, w_in_ref.shape[0], chunk):
@@ -297,23 +344,21 @@
     after_ref[...] = norm_forward(total, next_ref).astype(after_ref.dtype)
 
 
-def ffn_forward(x, ln, ln_next, w_in, w_out):
+def ffn_forward(x, ln, ln_next, weights):
     length, width = x.shape
-    out, normed, after = call(
-        partial(ffn_forward_kernel, 512),
-        (full(length, width), low(length, width), low(length, width)),
-        x,
-        ln,
-        ln_next,
-        w_in,
-        w_out,
-    )
-    return out, after, (x, ln, w_in, w_out, normed)
+    outs = (full(length, width), low(length, width), low(length, width))
+    if len(weights) > 1:
+        outs = outs + (low(2, 4 * weights[0].shape[1], width),)
+    out, normed, after, *whole = call(
+        partial(ffn_forward_kernel, 512, len(weights)), outs, x, ln, ln_next, *weights
+    )
+    return out, after, (x, ln, whole[0] if whole else weights[0], normed)
 
 
 def ffn_backward_kernel(
-    chunk, g_ref, x_ref, ln_ref, a_ref, w_in_ref, w_out_ref, out_ref, ln_grad_ref, low_ref, ut_ref, ht_ref
+    chunk, g_ref, x_ref, ln_ref, a_ref, w_ref, out_ref, ln_grad_ref, low_ref, ut_ref, ht_ref
 ):
+    w_in_ref, w_out_ref = w_ref.at[0], w_ref.at[1]
     low_ref[...] = g_ref[...].astype(jnp.bfloat16)
     total = jnp.zeros(g_ref.shape, jnp.float32)
     for start in range(0, w_in_ref.shape[0], chunk):
@@ -328,9 +373,9 @@
 
 
 def ffn_backward(grad, stored):
-    x, ln, w_in, w_out, normed = stored
+    x, ln, weights, normed = stored
     length, width = x.shape
-    hidden = w_in.shape[0]
+    hidden = weights.shape[1]
     out, ln_grad, *rest = call(
         partial(ffn_backward_kernel, 512),
         (full(length, width), full(2, width), low(length, width), low(hidden, length), low(hidden, length)),
@@ -338,8 +383,7 @@
         x,
         ln,
         normed,
-        w_in,
-        w_out,
+        weights,
     )
     return out, ln_grad, rest
 
@@ -475,21 +519,27 @@
     )(*args)
 
 
-def gather_kernel(axis, x_ref, out_ref, send_sems, recv_sems):
+def gather_kernel(axis, *refs):
+    count = (len(refs) - 2) // 2
     others = peers_of(axis)
     greet(*[(axis, to) for _, to, _ in others])
     me = lax.axis_index(axis)
-    sems = (send_sems, recv_sems)
-    copies = [push(x_ref, out_ref.at[me], sems, step - 1, axis, to) for step, to, _ in others]
-    out_ref[me] = x_ref[...]
+    copies = [
+        push(refs[k], refs[count + k].at[me], refs[-2:], k * len(others) + step - 1, axis, to)
+        for k in range(count)
+        for step, to, _ in others
+    ]
+    for k in range(count):
+        refs[count + k][me] = refs[k][...]
     for copy in copies:
         copy.wait()
 
 
-def gather_small(x, axis, collective_id):
+def gather_small(axis, collective_id, *arrays):
     size = lax.axis_size(axis)
-    out = jax.ShapeDtypeStruct((size, *x.shape), x.dtype)
-    return talk(partial(gather_kernel, axis), out, collective_id, x, scratch=sem_pair(size - 1))
+    outs = tuple(jax.ShapeDtypeStruct((size, *x.shape), x.dtype) for x in arrays)
+    sems = sem_pair((size - 1) * len(arrays))
+    return talk(partial(gather_kernel, axis), outs, collective_id, *arrays, scratch=sems)
 
 
 def sum_kernel(x_ref, out_ref, parts_ref, mine_ref, s0, r0, s1, r1):
@@ -539,17 +589,22 @@
     )
 
 
+def flip(index, bit):
+    return index + bit - 2 * bit * lax.rem(index // bit, 2)
+
+
 def tail_kernel(
-    x_ref, few_ref, out_ref, sum_ref, parts_ref, mine_ref, seen_ref, line_ref, lines_ref,
-    s0, r0, s1, r1, s2, r2, s3, r3,
+    x_ref, few_ref, out_ref, sum_ref, parts_ref, seen_ref, line_ref, lines_ref,
+    s0, r0, s1, r1, s2, r2, s3, r3, s4, r4,
 ):
     owners, replicas = peers_of("dp"), peers_of("vocab")
     greet(*[("dp", to) for _, to, _ in owners], *[("vocab", to) for _, to, _ in replicas])
-    me, here = lax.axis_index("dp"), lax.axis_index("vocab")
-    rows = mine_ref.shape[0]
+    size, me, here = lax.axis_size("dp"), lax.axis_index("dp"), lax.axis_index("vocab")
+    near, side = flip(here, 1), lax.rem(here, 2)
+    rows = parts_ref.shape[1]
 
     def rows_of(index):
-        return pl.ds(pl.multiple_of(index * rows, rows), rows)
+        return pl.ds(pl.multiple_of((side * size + index) * rows, rows), rows)
 
     few = [
         push(few_ref, seen_ref.at[here], (s2, r2), step - 1, "vocab", to) for step, to, _ in replicas
@@ -569,32 +624,33 @@
     lines_ref[me] = line_ref[...]
     for copy in wide:
         copy.wait()
-    mine_ref[...] = jnp.sum(parts_ref[...].astype(jnp.float32), axis=0).astype(mine_ref.dtype)
-    wide = [
-        push(mine_ref, out_ref.at[rows_of(me)], (s1, r1), step - 1, "dp", to)
-        for step, to, _ in owners
-    ]
-    out_ref[rows_of(me), :] = mine_ref[...]
+    out_ref[rows_of(me), :] = jnp.sum(parts_ref[...], axis=0)
+    mine = out_ref.at[rows_of(me)]
+    wide = [push(mine, mine, (s1, r1), step - 1, "dp", to) for step, to, _ in owners]
+    close = [push(mine, mine, (s4, r4), 0, "vocab", near)]
     for copy in few:
         copy.wait()
     sum_ref[...] = jnp.sum(lines_ref[...], axis=0)
-    for copy in wide:
+    for copy, (step, _, origin) in zip(wide, owners):
+        copy.wait()
+        theirs = out_ref.at[rows_of(origin)]
+        close.append(push(theirs, theirs, (s4, r4), step, "vocab", near))
+    for copy in close:
         copy.wait()
 
 
 def sum_tail(x, few, collective_id):
     owners, replicas = lax.axis_size("dp"), lax.axis_size("vocab")
     rows, columns = x.shape
-    share = rows // owners
+    share = rows // (2 * owners)
     return talk(
         tail_kernel,
-        (jax.ShapeDtypeStruct(x.shape, x.dtype), full(*few.shape)),
+        (full(*x.shape), full(*few.shape)),
         collective_id,
         x,
         few,
         scratch=[
-            pltpu.VMEM((owners, share, columns), x.dtype),
-            pltpu.VMEM((share, columns), x.dtype),
+            pltpu.VMEM((owners, share, columns), jnp.float32),
             pltpu.VMEM((replicas, *few.shape), jnp.float32),
             pltpu.VMEM(few.shape, jnp.float32),
             pltpu.VMEM((owners, *few.shape), jnp.float32),
@@ -602,34 +658,45 @@
         + sem_pair(owners - 1)
         + sem_pair(owners - 1)
         + sem_pair(replicas - 1)
-        + sem_pair(owners - 1),
-    )
-
-
-def flip(index, bit):
-    return index + bit - 2 * bit * lax.rem(index // bit, 2)
-
-
-def quad_kernel(x_ref, out_ref, send_sems, recv_sems):
+        + sem_pair(owners - 1)
+        + sem_pair(owners),
+    )
+
+
+def far_replicas():
+    here, size = lax.axis_index("vocab"), lax.axis_size("vocab")
+    return [
+        (step // 2 - 1, lax.rem(here + step, size), lax.rem(here + size - step, size))
+        for step in range(2, size, 2)
+    ]
+
+
+def basis_kernel(x_ref, out_ref, s0, r0, s1, r1):
     here = lax.axis_index("vocab")
-    far, near = flip(here, 2), flip(here, 1)
-    greet(("vocab", far), ("vocab", near))
-    sems = (send_sems, recv_sems)
-    mine, theirs = lax.rem(here, 4), lax.rem(far, 4)
+    near, side = flip(here, 1), lax.rem(here, 2)
+    others = far_replicas()
+    greet(*[("vocab", to) for _, to, _ in others], ("vocab", near))
+    rows = x_ref.shape[0] // 2
+    half = pl.ds(pl.multiple_of(side * rows, rows), rows)
     copies = [
-        push(x_ref, out_ref.at[mine], sems, 0, "vocab", far),
-        push(x_ref, out_ref.at[mine], sems, 1, "vocab", near),
+        push(x_ref.at[half], out_ref.at[here // 2, half], (s0, r0), slot, "vocab", to)
+        for slot, to, _ in others
     ]
-    out_ref[mine] = x_ref[...]
-    copies[0].wait()
-    relay = push(out_ref.at[theirs], out_ref.at[theirs], sems, 2, "vocab", near)
-    copies[1].wait()
-    relay.wait()
-
-
-def gather_quad(x, collective_id):
-    out = jax.ShapeDtypeStruct((4, *x.shape), x.dtype)
-    return talk(quad_kernel, out, collective_id, x, scratch=sem_pair(3))
+    out_ref[here // 2] = x_ref[...]
+    close = []
+    for copy, (slot, _, origin) in zip(copies, others):
+        copy.wait()
+        place = out_ref.at[origin // 2, half]
+        close.append(push(place, place, (s1, r1), slot, "vocab", near))
+    for copy in close:
+        copy.wait()
+
+
+def gather_basis(x, collective_id):
+    pairs = lax.axis_size("vocab") // 2
+    out = jax.ShapeDtypeStruct((pairs, *x.shape), x.dtype)
+    sems = sem_pair(pairs - 1) + sem_pair(pairs - 1)
+    return talk(basis_kernel, out, collective_id, x, scratch=sems)
 
 
 def gradient_kernel(x_ref, out_ref, parts_ref, s0, r0, s1, r1, s2, r2):
@@ -695,16 +762,24 @@
     )
 
 
-def swap_kernel(x_ref, out_ref, send_sems, recv_sems):
+def swap_kernel(x_ref, out_ref, s0, r0, s1, r1):
     others = peers_of("dp")
-    greet(*[("dp", to) for _, to, _ in others])
-    me = lax.axis_index("dp")
+    me, here = lax.axis_index("dp"), lax.axis_index("vocab")
+    near, side = flip(here, 1), lax.rem(here, 2)
+    greet(*[("dp", to) for _, to, _ in others], ("vocab", near))
+    rows = x_ref.shape[1] // 2
+    half = pl.ds(pl.multiple_of(side * rows, rows), rows)
     copies = [
-        push(x_ref.at[to], out_ref.at[me], (send_sems, recv_sems), step - 1, "dp", to)
+        push(x_ref.at[to, half], out_ref.at[me, half], (s0, r0), step - 1, "dp", to)
         for step, to, _ in others
     ]
     out_ref[me] = x_ref[me]
-    for copy in copies:
+    close = []
+    for copy, (step, _, origin) in zip(copies, others):
+        copy.wait()
+        place = out_ref.at[origin, half]
+        close.append(push(place, place, (s1, r1), step - 1, "vocab", near))
+    for copy in close:
         copy.wait()
 
 
@@ -715,7 +790,95 @@
         jax.ShapeDtypeStruct(x.shape, x.dtype),
         collective_id,
         x,
-        scratch=sem_pair(owners - 1),
+        scratch=sem_pair(owners - 1) + sem_pair(owners - 1),
+    )
+
+
+def token_kernel(
+    scale, x_ref, place_ref, out_ref, near_ref, parts_ref, blocks_ref, row_ref,
+    s0, r0, s1, r1, s2, r2, s3, r3, s4, r4,
+):
+    owners, others = peers_of("dp"), far_replicas()
+    me, here = lax.axis_index("dp"), lax.axis_index("vocab")
+    near, side = flip(here, 1), lax.rem(here, 2)
+    greet(
+        *[("dp", to) for _, to, _ in owners], *[("vocab", to) for _, to, _ in others], ("vocab", near)
+    )
+    count, length, columns = x_ref.shape
+    half, pairs = length // 2, lax.axis_size("vocab") // 2
+    share = half // pairs
+
+    def half_of(which):
+        return pl.ds(pl.multiple_of(which * half, half), half)
+
+    def share_of(index):
+        return pl.ds(pl.multiple_of(index // 2 * share, share), share)
+
+    def place_of(index):
+        return pl.ds(pl.multiple_of(side * half + index // 2 * share, share), share)
+
+    first = push(x_ref.at[:, half_of(1 - side)], near_ref, (s0, r0), 0, "vocab", near)
+    first.wait()
+    near_ref[...] += x_ref[:, half_of(side)]
+    copies = [
+        push(near_ref.at[:, share_of(to)], parts_ref.at[slot], (s1, r1), slot, "vocab", to)
+        for slot, to, _ in others
+    ]
+    for copy in copies:
+        copy.wait()
+    total = near_ref[:, share_of(here)]
+    for slot, _, _ in others:
+        total = total + parts_ref[slot]
+    blocks_ref[...] = total
+    copies = [
+        push(
+            blocks_ref.at[to],
+            row_ref.at[me, place_of(here)],
+            (s2, r2),
+            step - 1,
+            "dp",
+            to,
+        )
+        for step, to, _ in owners
+    ]
+    row_ref[me, place_of(here)] = blocks_ref[me]
+    for copy in copies:
+        copy.wait()
+    mine = row_ref.at[:, place_of(here)]
+    copies = [push(mine, mine, (s3, r3), slot, "vocab", to) for slot, to, _ in others]
+    close = [push(mine, mine, (s4, r4), 0, "vocab", near)]
+    for copy, (slot, _, origin) in zip(copies, others):
+        copy.wait()
+        theirs = row_ref.at[:, place_of(origin)]
+        close.append(push(theirs, theirs, (s4, r4), slot + 1, "vocab", near))
+    for copy in close:
+        copy.wait()
+    for owner in range(count):
+        band = slice(owner * columns, (owner + 1) * columns)
+        out_ref[:, band] = row_ref[owner].astype(jnp.float32) * scale + place_ref[:, band]
+
+
+def gather_tokens(x, places, scale, collective_id):
+    owners, pairs = lax.axis_size("dp"), lax.axis_size("vocab") // 2
+    _, length, columns = x.shape
+    half = length // 2
+    return talk(
+        partial(token_kernel, scale),
+        full(length, owners * columns),
+        collective_id,
+        x,
+        places,
+        scratch=[
+            pltpu.VMEM((owners, half, columns), x.dtype),
+            pltpu.VMEM((pairs - 1, owners, half // pairs, columns), x.dtype),
+            pltpu.VMEM((owners, half // pairs, columns), x.dtype),
+            pltpu.VMEM((owners, length, columns), x.dtype),
+        ]
+        + sem_pair(1)
+        + sem_pair(pairs - 1)
+        + sem_pair(owners - 1)
+        + sem_pair(pairs - 1)
+        + sem_pair(pairs),
     )
 
 
@@ -757,6 +920,16 @@
         moment,
         second,
     )
+
+
+def rotate(values, basis):
+    high = basis.astype(jnp.bfloat16)
+    rest = (basis - high.astype(jnp.float32)).astype(jnp.bfloat16)
+
+    def product(part):
+        return jnp.einsum("mfd,mde->mfe", values, part, preferred_element_type=jnp.float32)
+
+    return product(high) + product(rest)
 
 
 def share_rows(array, owners, shares, share):
@@ -790,13 +963,18 @@
     owners, replicas = lax.axis_size("dp"), lax.axis_size("vocab")
     replica = lax.axis_index("vocab")
     own_table = embedding.astype(jnp.bfloat16)
-    w_attn, w_ffn, norm_low, table_low = (
-        lax.all_gather(attn_w.astype(jnp.bfloat16), "dp", axis=1, tiled=True),
-        lax.all_gather(ffn_w.astype(jnp.bfloat16), "dp", axis=1, tiled=True),
-        lax.all_gather(norm_p.astype(jnp.bfloat16), "dp", axis=1, tiled=True),
-        lax.all_gather(own_table, "dp", axis=1, tiled=True),
-    )
-    norm_rows = norm_low.astype(jnp.float32)
+    own_norms = jnp.pad(norm_p.astype(jnp.bfloat16).astype(jnp.float32), ((0, 2), (0, 0)))
+    all_ids, norm_rows = gather_small("dp", 1, jnp.concatenate([src_ids, tgt_ids]), own_norms)
+    norm_rows = jnp.swapaxes(norm_rows, 0, 1).reshape(16, -1)
+    w_attn = [None] * 3
+    w_ffn = [None] * 2
+    w_attn[0], ready = gather_weights(attn_w[0:4].astype(jnp.bfloat16), None)
+    w_ffn[0], ready = gather_weights(ffn_w[0:2].astype(jnp.bfloat16), ready)
+    w_attn[1], ready = gather_weights(attn_w[4:8].astype(jnp.bfloat16), ready)
+    w_attn[2], ready = gather_weights(attn_w[8:12].astype(jnp.bfloat16), ready)
+    w_ffn[1], ready = gather_weights(ffn_w[2:4].astype(jnp.bfloat16), ready)
+    late_table, _ = lax.optimization_barrier((own_table, ready))
+    table_low = lax.all_gather(late_table, "dp", axis=1, tiled=True)
     norms = [jnp.stack([norm_rows[k], norm_rows[7 + k]]) for k in range(7)]
     vocab_count, width = table_low.shape
     columns = replica * vocab_count + jnp.arange(vocab_count)
@@ -804,7 +982,6 @@
     pick_rows, labels = (pick_pos[0], pick_label[0])
     length = source.shape[0]
     embed_scale = math.sqrt(width)
-    all_ids = gather_small(jnp.concatenate([src_ids, tgt_ids]), "dp", 1)
     halves = replica * (vocab_count // 2) + jnp.arange(vocab_count // 2)
     paired = own_table.reshape(vocab_count // 2, -1)
 
@@ -814,30 +991,24 @@
         return jnp.where((ids % 2 == 0)[:, None], left, right)
 
     source_part, target_part = (look_up(all_ids[:, k].reshape(-1)) for k in (0, 1))
-    source_sum = lax.psum(source_part, "vocab")
-    source_sum, target_part = lax.optimization_barrier((source_sum, target_part))
     target_sum = lax.psum(target_part, "vocab")
-
-    def own_row(summed, collective_id):
-        blocks = swap_owners(summed.reshape(owners, length, -1), collective_id)
-        return jnp.swapaxes(blocks, 0, 1).reshape(length, -1).astype(jnp.float32)
-
-    looked_up = [own_row(source_sum, 2), own_row(target_sum, 3)]
     positional = sinusoid(length, width)
-
-    enc_in = looked_up[0] * embed_scale + positional
+    source_part = source_part.reshape(owners, length, -1)
+    enc_in = gather_tokens(source_part, positional, embed_scale, 2)
     enc_mid, enc_attn = attn_forward(
-        enc_in, norms[0], w_attn[0:4], source_seg, source_seg, None, False
-    )
-    enc_out, encoded, enc_ffn = ffn_forward(enc_mid, norms[1], norms[2], w_ffn[0], w_ffn[1])
-    dec_in = looked_up[1] * embed_scale + positional
+        enc_in, norms[0], w_attn[0], source_seg, source_seg, None, False
+    )
+    enc_out, encoded, enc_ffn = ffn_forward(enc_mid, norms[1], norms[2], w_ffn[0])
+    target_rows = swap_owners(target_sum.reshape(owners, length, -1), 3)
+    target_rows = jnp.swapaxes(target_rows, 0, 1).reshape(length, -1).astype(jnp.float32)
+    dec_in = target_rows * embed_scale + positional
     dec_mid, dec_self = attn_forward(
-        dec_in, norms[3], w_attn[4:8], target_seg, target_seg, None, True
+        dec_in, norms[3], w_attn[1], target_seg, target_seg, None, True
     )
     dec_late, dec_cross = attn_forward(
-        dec_mid, norms[4], w_attn[8:12], target_seg, source_seg, encoded, False
-    )
-    dec_out, final_low, dec_ffn = ffn_forward(dec_late, norms[5], norms[6], w_ffn[2], w_ffn[3])
+        dec_mid, norms[4], w_attn[2], target_seg, source_seg, encoded, False
+    )
+    dec_out, final_low, dec_ffn = ffn_forward(dec_late, norms[5], norms[6], w_ffn[1])
 
     chosen_rows = one_hot(pick_rows, jnp.arange(length))
     picked = dot_dims(chosen_rows, final_low, 1, 0).astype(jnp.bfloat16)
@@ -846,9 +1017,8 @@
     row_total = jnp.sum(jnp.exp(logits - row_top[:, None]), axis=-1)
     label_hit = labels[:, None] == columns[None, :]
     chosen = jnp.sum(jnp.where(label_hit, logits, 0.0), axis=-1)
-    seen = gather_small(
-        jnp.pad(jnp.stack([row_top, row_total, chosen]), ((0, 5), (0, 0))), "vocab", 4
-    )
+    seen = jnp.pad(jnp.stack([row_top, row_total, chosen]), ((0, 5), (0, 0)))
+    (seen,) = gather_small("vocab", 4, seen)
     row_top, row_total, chosen = combine_stats(seen[:, 0], seen[:, 1], seen[:, 2])
     log_total = row_top + jnp.log(row_total)
     weight = 1.0 / pick_weights(target_seg, pick_rows)
@@ -907,7 +1077,7 @@
         grad_low, values, grads = parts
         return [
             dot_dims(share_rows(rows, owners, replicas, replica).reshape(-1, length), right, 1, 0)
-            for rows, right in ((grads, stored[4]), (values, grad_low))
+            for rows, right in ((grads, stored[3]), (values, grad_low))
         ]
 
     pieces = (
@@ -927,10 +1097,10 @@
     norm_grad = jnp.concatenate([norm_grad[:, 0], norm_grad[:, 1]], axis=0)
     g_norm = lax.psum_scatter(norm_grad, "dp", scatter_dimension=1, tiled=True)
 
-    matrix = replica % 4
+    matrix = replica // 2
     own_grad = lax.dynamic_index_in_dim(g_ffn, matrix, 0, keepdims=False)
     own_products = dot_dims(own_grad, own_grad, 0, 0)
-    g_ffn = g_ffn.astype(jnp.float32)
+    g_ffn_low, g_ffn = g_ffn, g_ffn.astype(jnp.float32)
     first_copy = (replica == 0).astype(jnp.float32)
     layer_sq = jnp.sum(g_attn * g_attn) + jnp.sum(g_ffn * g_ffn) + jnp.sum(g_norm * g_norm)
     raw_squares = jnp.sum(g_embed * g_embed) + first_copy * layer_sq
@@ -940,13 +1110,12 @@
     loss_sum, sentences, squares = few[0, 0], few[1, 0], few[2, 0]
     grad_norm = jnp.sqrt(squares) / sentences
     factor = jnp.minimum(1.0, clip_limit / (grad_norm + norm_eps)) / sentences
-    g_attn, g_ffn, g_norm, g_embed = (
+    g_attn, g_norm, g_embed = (
         g_attn * factor,
-        g_ffn * factor,
         g_norm * factor,
         g_embed * factor,
     )
-    all_products = lax.all_gather(own_products.astype(jnp.bfloat16), "vocab")[:4]
+    all_products = lax.all_gather(own_products.astype(jnp.bfloat16), "vocab")[::2]
     new_stats = stat_decay * soap_stats + (1.0 - stat_decay) * (factor * factor) * (
         all_products.astype(jnp.float32)
     )
@@ -954,18 +1123,18 @@
         1.0 - stat_decay
     ) * (factor * factor) * own_products
     own_basis = renew_basis(own_stat, lax.dynamic_index_in_dim(soap_basis, matrix, 0, keepdims=False))
-    new_basis = gather_quad(own_basis.astype(jnp.bfloat16), 9).astype(jnp.float32)
+    new_basis = gather_basis(own_basis.astype(jnp.bfloat16), 9).astype(jnp.float32)
 
     new_attn, m_attn, v_attn = adam_update(attn_w, g_attn, attn_m, attn_v, rate_matrix, decay_rate)
     new_norm, m_norm, v_norm = adam_update(norm_p, g_norm, norm_m, norm_v, rate_vector, 0.0)
     new_embed, m_embed, v_embed = adam_update(
         embedding, g_embed, embed_m, embed_v, rate_matrix, decay_rate
     )
-    rotated = jnp.einsum("mfd,mde->mfe", g_ffn, soap_basis, precision=highest)
+    rotated = factor * rotate(g_ffn_low, soap_basis)
     m_ffn = beta_one * ffn_m + (1.0 - beta_one) * rotated
     v_ffn = beta_two * ffn_v + (1.0 - beta_two) * rotated * rotated
     back_rotated = jnp.einsum(
-        "mfe,mde->mfd", adam_direction(m_ffn, v_ffn), soap_basis, precision=highest
+        "mfe,mde->mfd", adam_direction(m_ffn, v_ffn), soap_basis, precision=lax.Precision.HIGH
     )
     new_ffn = ffn_w - rate_matrix * (back_rotated + decay_rate * ffn_w)
     return (

time: 826 us -> 772 us (0.935)
  waiting for transfers between devices: 118 us -> 53.2 us
  starting transfers between devices: 0.51 us -> 22.2 us
  blocking collectives: 8.35 us -> 0 us
    ppermute x0 -> x30, waiting for transfers between devices: none -> 53 us  [the longest x15 52.8 us: gather_weights(): lax.ppermute(mine, 'dp', [(s, s ^ k) for s in range(owners)])]
    psum x1 -> x0, waiting for transfers between devices: 50.3 us -> none  [body(): source_sum = lax.psum(source_part, 'vocab')]
    all_gather x4 -> x2, waiting for transfers between devices: 48.5 us -> 0.03 us  [the longest x1 0.03 us: body(): table_low = lax.all_gather(late_table, 'dp', axis=1, tiled=True)]
    ppermute x0 -> x30, starting transfers between devices: none -> 21.3 us  [the longest x15 18.7 us: gather_weights(): lax.ppermute(mine, 'dp', [(s, s ^ k) for s in range(owners)])]
    psum x1, waiting for transfers between devices: 18.7 us -> 0.01 us  [body(): target_sum = lax.psum(target_part, 'vocab')]
    all_gather x1 -> x0, blocking collectives: 8.35 us -> none  [body(): lax.all_gather(norm_p.astype(jnp.bfloat16), 'dp', axis=1, tiled=True)]
    unnamed x125 -> x181, local copies, waits for them, and re-layouts: 15.6 us -> 22.1 us
  transfers between devices with their start and end apart: 8 -> 35, of which waited for: 5 -> 7; matrix products, arithmetic and copies ran while one was open for 20% -> 21% of each run, Pallas kernels for 33% -> 36%
where the time goes in v3:
time: 772 us; the launch traced here: 763 us
  Pallas kernels  426 us (55%)
  matrix products  84.2 us (11%)
  local copies, waits for them, and re-layouts  78.2 us (10%)
  other arithmetic  75.1 us (10%)
  waiting for transfers between devices  53.2 us (7%)
  between operations  24.5 us (3%)
  starting transfers between devices  22.2 us (3%)
    pallas_call x9, Pallas kernels, talk(): pl.pallas_call(kernel, out_shape=outs, in_specs=[vmem] * len(args), out_s...  216 us
    pallas_call x12, Pallas kernels, call(): pl.pallas_call(kernel, out_shape=outs, in_specs=[vmem] * (len(args) - sme...  210 us
    ppermute x15, waiting for transfers between devices, gather_weights(): lax.ppermute(mine, 'dp', [(s, s ^ k) for s in range(owners)])  52.8 us
    dot_general x26, matrix products, dot_dims(): lax.dot_general(left, right, (((left_dim,), (right_dim,)), ((), ())), pre...  44.4 us
    unnamed x181, local copies, waits for them, and re-layouts  22.1 us
    ppermute x15, starting transfers between devices, gather_weights(): lax.ppermute(mine, 'dp', [(s, s ^ k) for s in range(owners)])  18.7 us
    pallas_call x1, local copies, waits for them, and re-layouts, call(): pl.pallas_call(kernel, out_shape=outs, in_specs=[vmem] * (len(args) - sme...  18.7 us
    dot_general x2, matrix products, look_up(): lax.dot_general(one_hot(ids // 2, halves), paired, (((1,), (0,)), ((), ())))  15.5 us
  transfers between devices with their start and end apart: 35, of which 7 were waited for; matrix products, arithmetic and copies ran while one was open for 21% of the time, Pallas kernels for 36%

profile of v3, /device:TPU:0, one launch (start us, length us, event | category | flops | bytes accessed | tf_op | source)
XLA Modules:
  0.0 763.3 jit_solution(4317945847039840450)
XLA Ops:
  10.7 7.8 %shard_map.332 = (s32[4,2,1024]{2,1,0:T(2,128)}, f32[4,16,128]{2,1,0:T(8,128)}) custom-call(s32[2,1024]{1,0:T(2,128)} %pad_add_fusion.refs_0_, f32[16,128]{1,0:T(8,128)} %pad_convert_fusion.refs_1_), custom_call_target="tpu_custom_call" | custom-call | tf_op jit(solution)/shard_map/pallas_call | solution.py:510
  23.3 6.8 fusion.2
  51.3 8.6 %fusion.4 = bf16[4096,256]{1,0:T(8,128)(2,1)S(1)} fusion(bf16[2368,256]{1,0:T(8,128)(2,1)} %copy-done.29, s32[2368]{0:T(1024)S(1)} %iota_add_fusion.1, s32[4096]{0:T(1024)S(1)} %add_select_fusion.4), kind=kOutput, calls=%fused_computation.5 | convolution fusion | flops 4975755264 | bytes 3335424 | tf_op jit(solution)/shard_map/dot_general | solution.py:989
  70.7 7.1 collective-permute-done.18.refs_6_
  97.3 16.7 %collective-permute-done.26.refs_3_ = bf16[1,512,512]{2,1,0:T(8,128)(2,1)S(1)} collective-permute-done((bf16[1,512,512]{2,1,0:T(8,128)(2,1)}, bf16[1,512,512]{2,1,0:T(8,128)(2,1)S(1)}, u32[]{:S(2)}, u32[]{:S(2)}) %collective-permute-start.26) | collective-permute-done | bytes 524320 | tf_op jit(solution)/shard_map/ppermute | solution.py:151
  115.9 20.5 %collective-permute-done.14.refs_3_ = bf16[1,512,512]{2,1,0:T(8,128)(2,1)S(1)} collective-permute-done((bf16[1,512,512]{2,1,0:T(8,128)(2,1)}, bf16[1,512,512]{2,1,0:T(8,128)(2,1)S(1)}, u32[]{:S(2)}, u32[]{:S(2)}) %collective-permute-start.14) | collective-permute-done | bytes 524320 | tf_op jit(solution)/shard_map/ppermute | solution.py:151
  138.4 43.1 %shard_map.333.refs_0_.refs_1_ = f32[1024,512]{1,0:T(8,128)} custom-call(bf16[4,1024,128]{2,1,0:T(8,128)(2,1)} %bitcast.234, f32[1024,512]{1,0:T(8,128)} %constant.225.clone.place_ref), custom_call_target="tpu_custom_call" | custom-call | tf_op jit(solution)/shard_map/pallas_call | solution.py:510
  182.3 12.7 %shard_map.335 = bf16[4,1024,128]{2,1,0:T(8,128)(2,1)} custom-call(bf16[4,1024,128]{2,1,0:T(8,128)(2,1)} %all-reduce.5.cloned.1.call-done.x_ref), custom_call_target="tpu_custom_call" | custom-call | tf_op jit(solution)/shard_map/pallas_call | solution.py:510
  199.5 17.5 %shard_map.336 = (f32[1024,512]{1,0:T(8,128)}, bf16[1024,512]{1,0:T(8,128)(2,1)}, bf16[512,1024]{1,0:T(8,128)(2,1)}, bf16[512,1024]{1,0:T(8,128)(2,1)}, bf16[512...) custom-call(f32[1024,512]{1,0:T(8,128)} %copy_bitcast_fusion.refs_0_, ...), custom_call_target="tpu_custom_call" | custom-call | tf_op jit(solution)/shard_map/pallas_call | solution.py:50
  218.0 20.9 %shard_map.334 = (f32[1024,512]{1,0:T(8,128)}, bf16[1024,512]{1,0:T(8,128)(2,1)}, bf16[512,1024]{1,0:T(8,128)(2,1)}, bf16[512,1024]{1,0:T(8,128)(2,1)}, bf16[512...) custom-call(f32[1024,512]{1,0:T(8,128)} %shard_map.333.refs_0_.refs_1_, ...), custom_call_target="tpu_custom_call" | custom-call | tf_op jit(solution)/shard_map/pallas_call | solution.py:50
  244.3 12.5 %shard_map.337 = (f32[1024,512]{1,0:T(8,128)}, bf16[1024,512]{1,0:T(8,128)(2,1)}, bf16[1024,512]{1,0:T(8,128)(2,1)}, bf16[2,2048,512]{2,1,0:T(8,128)(2,1)}) custom-call(f32[1024,512]{1,0:T(8,128)} %get-tuple-element.90.x_ref, f32[2,512]{1,0:T(2,128)} %get-tuple-element.221.ln_ref, f32[2,512]{1,0:T(2,128)} %get-tuple-element.222.next_ref.ln_ref, ...), custom_call_target="tpu_custom_call" | custom-call | tf_op jit(solution)/shard_map/pallas_call | solution.py:50
  257.6 20.2 %shard_map.338 = (f32[1024,512]{1,0:T(8,128)}, bf16[1024,512]{1,0:T(8,128)(2,1)}, bf16[512,1024]{1,0:T(8,128)(2,1)}, bf16[512,1024]{1,0:T(8,128)(2,1)}, bf16[512...) custom-call(f32[1024,512]{1,0:T(8,128)} %get-tuple-element.89.refs_0_.refs_1_, ...), custom_call_target="tpu_custom_call" | custom-call | tf_op jit(solution)/shard_map/pallas_call | solution.py:50
  278.9 12.5 %shard_map.339 = (f32[1024,512]{1,0:T(8,128)}, bf16[1024,512]{1,0:T(8,128)(2,1)}, bf16[1024,512]{1,0:T(8,128)(2,1)}, bf16[2,2048,512]{2,1,0:T(8,128)(2,1)}) custom-call(f32[1024,512]{1,0:T(8,128)} %get-tuple-element.92.x_ref, f32[2,512]{1,0:T(2,128)} %get-tuple-element.223.ln_ref, f32[2,512]{1,0:T(2,128)} %get-tuple-element.224.next_ref.ln_ref, ...), custom_call_target="tpu_custom_call" | custom-call | tf_op jit(solution)/shard_map/pallas_call | solution.py:50
  301.1 7.5 shard_map.340
  318.2 16.1 %shard_map.341 = bf16[256,512]{1,0:T(8,128)(2,1)} custom-call(bf16[256,512]{1,0:T(8,128)(2,1)} %convolution_convert_fusion.5.x_ref), custom_call_target="tpu_custom_call" | custom-call | tf_op jit(solution)/shard_map/pallas_call | solution.py:510
  342.1 17.5 %shard_map.343 = (f32[1024,512]{1,0:T(8,128)}, f32[2,512]{1,0:T(2,128)}, bf16[1024,512]{1,0:T(8,128)(2,1)}, bf16[2048,1024]{1,0:T(8,128)(2,1)}, bf16[2048,1024]{1,0:T(8,128)(2,1)}) custom-call(f32[1024,512]{1,0:T(8,128)} %get-tuple-element.95.g_ref, f32[1024,512]{1,0:T(8,128)} %get-tuple-element.92.x_ref, f32[2,512]{1,0:T(2,128)} %get-tuple-element.223.ln_ref, ...), custom_call_target="tpu_custom_call" | custom-call | tf_op jit(solution)/shard_map/pallas_call | solution.py:50
  359.6 25.6 %shard_map.344 = (f32[1024,512]{1,0:T(8,128)}, f32[2,512]{1,0:T(2,128)}, bf16[1024,512]{1,0:T(8,128)(2,1)}, bf16[1024,512]{1,0:T(8,128)(2,1)}, bf16[1024,512]{1,...) custom-call(f32[1024,512]{1,0:T(8,128)} %get-tuple-element.98.refs_0_, ...), custom_call_target="tpu_custom_call" | custom-call | tf_op jit(solution)/shard_map/pallas_call | solution.py:50
  390.2 17.8 %shard_map.346 = (f32[1024,512]{1,0:T(8,128)}, f32[2,512]{1,0:T(2,128)}, bf16[1024,512]{1,0:T(8,128)(2,1)}, bf16[2048,1024]{1,0:T(8,128)(2,1)}, bf16[2048,1024]{1,0:T(8,128)(2,1)}) custom-call(f32[1024,512]{1,0:T(8,128)} %get-tuple-element.107.g_ref, f32[1024,512]{1,0:T(8,128)} %get-tuple-element.90.x_ref, f32[2,512]{1,0:T(2,128)} %get-tuple-element.221.ln_ref, ...), custom_call_target="tpu_custom_call" | custom-call | tf_op jit(solution)/shard_map/pallas_call | solution.py:50
  408.0 26.3 %shard_map.347 = (f32[1024,512]{1,0:T(8,128)}, f32[2,512]{1,0:T(2,128)}, bf16[1024,512]{1,0:T(8,128)(2,1)}, bf16[1024,512]{1,0:T(8,128)(2,1)}, bf16[1024,512]{1,0:T(8,128)(2,1)}, /*index=5*/bf16[1024,512]{1,0:T(8,128)(2,1)}) custom-call(f32[1024,512]{1,0:T(8,128)} %get-tuple-element.110.refs_0_, f32[1024,512]{1,0:T(8,128)} %shard_map.333.refs_0_.refs_1_, ...), custom_call_target="tpu_custom_call" | custom-call | tf_op jit(solution)/shard_map/pallas_call | solution.py:50
  435.1 18.7 %shard_map.353 = (f32[7,2,512]{2,1,0:T(2,128)S(1)}, bf16[1024,512]{1,0:T(8,128)(2,1)}, bf16[1024,512]{1,0:T(8,128)(2,1)}, bf16[1024,512]{1,0:T(8,128)(2,1)}, bf1...) fusion(f32[7,2,512]{2,1,0:T(2,128)S(1)} %constant_dynamic-update-slice_fusion.8, ...), kind=kCustom, calls=%fused_computation.124 | custom fusion | bytes 17348608 | tf_op jit(solution)/shard_map/pallas_call | solution.py:50
  462.3 7.4 copy.63
  476.0 24.4 %shard_map.349 = bf16[4,2048,128]{2,1,0:T(8,128)(2,1)} custom-call(bf16[4,2048,128]{2,1,0:T(8,128)(2,1)} %bitcast.231), custom_call_target="tpu_custom_call" | custom-call | tf_op jit(solution)/shard_map/pallas_call | solution.py:510
  520.9 57.3 %shard_map.348 = bf16[8,7,64,512]{3,2,1,0:T(8,128)(2,1)} custom-call(bf16[4,7,64,512]{3,2,1,0:T(8,128)(2,1)} %constant_dynamic-update-slice_fusion.x_ref), custom_call_target="tpu_custom_call" | custom-call | tf_op jit(solution)/shard_map/pallas_call | solution.py:510
  582.6 11.2 %fusion = f32[2368,256]{1,0:T(8,128)S(1)} fusion(s32[8192]{0:T(1024)S(1)} %copy-done.67, s32[2368]{0:T(1024)S(1)} %copy-done.72, bf16[8192,128]{1,0:T(8,128)(2,1)S(1)} %get-tuple-element.186, bf16[8192,128]{1,0:T(8,128)(2,1)S(1)} %get-tuple-element.185), kind=kOutput, calls=%fused_computation.1 | convolution fusion | flops 9959899136 | bytes 6661376 | tf_op jit(solution)/shard_map/dot_general | solution.py:34
  613.8 22.1 %shard_map.350 = (f32[512,512]{1,0:T(8,128)}, f32[8,128]{1,0:T(8,128)}) custom-call(f32[512,512]{1,0:T(8,128)} %fusion.41.x_ref, f32[8,128]{1,0:T(8,128)} %broadcast_in_dim.93.few_ref), custom_call_target="tpu_custom_call" | custom-call | tf_op jit(solution)/shard_map/pallas_call | solution.py:510
  652.2 29.1 %shard_map.351 = f32[512,512]{1,0:T(8,128)} custom-call(f32[512,512]{1,0:T(8,128)} %get-tuple-element.193.stat_ref, f32[512,512]{1,0:T(8,128)} %dynamic-slice_bitcast_fusion.basis_ref), custom_call_target="tpu_custom_call" | custom-call | tf_op jit(solution)/shard_map/pallas_call | solution.py:50
  683.4 25.3 %shard_map.352 = bf16[4,512,512]{2,1,0:T(8,128)(2,1)} custom-call(bf16[512,512]{1,0:T(8,128)(2,1)} %convert_element_type.201.x_ref), custom_call_target="tpu_custom_call" | custom-call | tf_op jit(solution)/shard_map/pallas_call | solution.py:510
  713.8 7.7 %multiply_add_fusion.1 = (f32[4,512,512]{2,1,0:T(8,128)}, f32[4,512,512]{2,1,0:T(8,128)}) fusion(f32[4,512,512]{2,1,0:T(8,128)} %param.31, f32[4,512,512]{2,1,0:T(8,128)} %param.32, f32[4,512,512]{2,1,0:T(8,128)S(1)} %fusion.38, bf16[4,512,512]{2,1,0:T(8,128)(2,1)S(1)} %bitcast.227, f32[4,512,512]{2,1,0:T(8,128)S(1)} %copy-done.4, f32[]{:T(128)S(6)} %div.131), kind=kOutput, calls=%fused_computation.35 | convolution fusion | flops 1087373312 | bytes 27262980 | tf_op jit(solution)/shard_map/mfd,mde->mfe/dot_general | solution.py:930
  722.9 6.4 multiply_subtract_fusion.1
  729.3 13.3 %multiply_subtract_fusion = f32[4,512,512]{2,1,0:T(8,128)} fusion(f32[4,512,512]{2,1,0:T(8,128)S(1)} %copy-done.19, f32[4,512,512]{2,1,0:T(8,128)S(1)} %copy-done.4, f32[4,512,512]{2,1,0:T(8,128)} %get-tuple-element.184, f32[4,512,512]{2,1,0:T(8,128)} %get-tuple-element.183), kind=kOutput, calls=%fused_computation.28 | convolution fusion | flops 3229614080 | bytes 20971520 | tf_op jit(solution)/shard_map/mfe,mde->mfd/dot_general | solution.py:1136
  742.6 6.2 multiply_subtract_fusion.2
  748.8 5.6 multiply_add_fusion
  (373 shorter events, 186.4 us)
Async XLA Ops:
  8.0 174.3 %all-reduce.5.cloned.1.call-start = ((), (), s32[]{:S(2)}) async-start(), calls=%async_computation.2 | async-start | bytes 2097152 | tf_op jit(solution)/shard_map/psum | solution.py:994
  33.0 262.2 %all-gather.4.cloned.1.call-start = ((), (), s32[]{:S(2)}) async-start(), calls=%async_computation.3 | async-start | bytes 6062080 | tf_op jit(solution)/shard_map/all_gather | solution.py:977
  38.3 26.5 %collective-permute-start.2 = (bf16[2,128,512]{2,1,0:T(8,128)(2,1)}, bf16[2,128,512]{2,1,0:T(8,128)(2,1)}, u32[]{:S(2)}, u32[]{:S(2)}) collective-permute-start(bf16[2,128,512]{2,1,0:T(8,128)(2,1)} %constant_dynamic-slice_fusion.11), channel_id=1, source_target_pairs={{0,24},{8,16},{16,8},{24,0},{1,25},{9,17},{17,9},{25,1},{2,26},{10... | collective-permute-start | bytes 786440 | tf_op jit(solution)/shard_map/ppermute | solution.py:151
  40.6 24.6 %collective-permute-start.1 = (bf16[2,128,512]{2,1,0:T(8,128)(2,1)}, bf16[2,128,512]{2,1,0:T(8,128)(2,1)}, u32[]{:S(2)}, u32[]{:S(2)}) collective-permute-start(bf16[2,128,512]{2,1,0:T(8,128)(2,1)} %constant_dynamic-slice_fusion.11), channel_id=1, source_target_pairs={{0,16},{8,24},{16,0},{24,8},{1,17},{9,25},{17,1},{25,9},{2,18},{10... | collective-permute-start | bytes 786440 | tf_op jit(solution)/shard_map/ppermute | solution.py:151
  41.2 27.9 %collective-permute-start = (bf16[2,128,512]{2,1,0:T(8,128)(2,1)}, bf16[2,128,512]{2,1,0:T(8,128)(2,1)}, u32[]{:S(2)}, u32[]{:S(2)}) collective-permute-start(bf16[2,128,512]{2,1,0:T(8,128)(2,1)} %constant_dynamic-slice_fusion.11), channel_id=1, source_target_pairs={{0,8},{8,0},{16,24},{24,16},{1,9},{9,1},{17,25},{25,17},{2,10},{10... | collective-permute-start | bytes 786440 | tf_op jit(solution)/shard_map/ppermute | solution.py:151
  42.5 27.2 %collective-permute-start.20 = (bf16[2,128,512]{2,1,0:T(8,128)(2,1)}, bf16[2,128,512]{2,1,0:T(8,128)(2,1)}, u32[]{:S(2)}, u32[]{:S(2)}) collective-permute-start(bf16[2,128,512]{2,1,0:T(8,128)(2,1)} %constant_dynamic-slice_fusion.8), channel_id=1, source_target_pairs={{0,24},{8,16},{16,8},{24,0},{1,25},{9,17},{17,9},{25,1},{2,26},{10... | collective-permute-start | bytes 786440 | tf_op jit(solution)/shard_map/ppermute | solution.py:151
  44.8 25.3 %collective-permute-start.19 = (bf16[2,128,512]{2,1,0:T(8,128)(2,1)}, bf16[2,128,512]{2,1,0:T(8,128)(2,1)}, u32[]{:S(2)}, u32[]{:S(2)}) collective-permute-start(bf16[2,128,512]{2,1,0:T(8,128)(2,1)} %constant_dynamic-slice_fusion.8), channel_id=1, source_target_pairs={{0,16},{8,24},{16,0},{24,8},{1,17},{9,25},{17,1},{25,9},{2,18},{10... | collective-permute-start | bytes 786440 | tf_op jit(solution)/shard_map/ppermute | solution.py:151
  45.4 559.6 %reduce-scatter.5.cloned.1.call-start = ((), (), s32[]{:S(2)}) async-start(), calls=%async_computation.4 | async-start | bytes 40960 | tf_op jit(solution)/shard_map/reduce_scatter | solution.py:1098
  64.8 13.0 %collective-permute-start.18 = (bf16[2,128,512]{2,1,0:T(8,128)(2,1)}, bf16[2,128,512]{2,1,0:T(8,128)(2,1)}, u32[]{:S(2)}, u32[]{:S(2)}) collective-permute-start(bf16[2,128,512]{2,1,0:T(8,128)(2,1)} %constant_dynamic-slice_fusion.8), channel_id=1, source_target_pairs={{0,8},{8,0},{16,24},{24,16},{1,9},{9,1},{17,25},{25,17},{2,10},{10... | collective-permute-start | bytes 786440 | tf_op jit(solution)/shard_map/ppermute | solution.py:151
  65.2 17.9 %collective-permute-start.8 = (bf16[2,128,512]{2,1,0:T(8,128)(2,1)}, bf16[2,128,512]{2,1,0:T(8,128)(2,1)S(1)}, u32[]{:S(2)}, u32[]{:S(2)}) collective-permute-start(bf16[2,128,512]{2,1,0:T(8,128)(2,1)} %constant_dynamic-slice_fusion.10), channel_id=1, source_target_pairs={{0,24},{8,16},{16,8},{24,0},{1,25},{9,17},{17,9},{25,1},{2,26},{10... | collective-permute-start | bytes 786440 | tf_op jit(solution)/shard_map/ppermute | solution.py:151
  69.1 18.2 %collective-permute-start.7 = (bf16[2,128,512]{2,1,0:T(8,128)(2,1)}, bf16[2,128,512]{2,1,0:T(8,128)(2,1)S(1)}, u32[]{:S(2)}, u32[]{:S(2)}) collective-permute-start(bf16[2,128,512]{2,1,0:T(8,128)(2,1)} %constant_dynamic-slice_fusion.10), channel_id=1, source_target_pairs={{0,16},{8,24},{16,0},{24,8},{1,17},{9,25},{17,1},{25,9},{2,18},{10... | collective-permute-start | bytes 786440 | tf_op jit(solution)/shard_map/ppermute | solution.py:151
  69.7 18.1 %collective-permute-start.6 = (bf16[2,128,512]{2,1,0:T(8,128)(2,1)}, bf16[2,128,512]{2,1,0:T(8,128)(2,1)S(1)}, u32[]{:S(2)}, u32[]{:S(2)}) collective-permute-start(bf16[2,128,512]{2,1,0:T(8,128)(2,1)} %constant_dynamic-slice_fusion.10), channel_id=1, source_target_pairs={{0,8},{8,0},{16,24},{24,16},{1,9},{9,1},{17,25},{25,17},{2,10},{10... | collective-permute-start | bytes 786440 | tf_op jit(solution)/shard_map/ppermute | solution.py:151
  70.1 17.7 %collective-permute-start.5 = (bf16[2,128,512]{2,1,0:T(8,128)(2,1)}, bf16[2,128,512]{2,1,0:T(8,128)(2,1)S(1)}, u32[]{:S(2)}, u32[]{:S(2)}) collective-permute-start(bf16[2,128,512]{2,1,0:T(8,128)(2,1)} %collective-permute-done.2.refs_7_), channel_id=1, source_target_pairs={{0,1},{1,0},{2,3},{3,2},{4,5},{5,4},{6,7},{7,6},{8,9},{9,8},{10,11... | collective-permute-start | bytes 786440 | tf_op jit(solution)/shard_map/ppermute | solution.py:152
  77.8 11.5 %collective-permute-start.4 = (bf16[2,128,512]{2,1,0:T(8,128)(2,1)}, bf16[2,128,512]{2,1,0:T(8,128)(2,1)S(1)}, u32[]{:S(2)}, u32[]{:S(2)}) collective-permute-start(bf16[2,128,512]{2,1,0:T(8,128)(2,1)} %collective-permute-done.1.refs_6_), channel_id=1, source_target_pairs={{0,1},{1,0},{2,3},{3,2},{4,5},{5,4},{6,7},{7,6},{8,9},{9,8},{10,11... | collective-permute-start | bytes 786440 | tf_op jit(solution)/shard_map/ppermute | solution.py:152
  83.1 7.6 collective-permute-start.3
  87.9 6.4 collective-permute-start.10
  89.3 24.7 %collective-permute-start.26 = (bf16[1,512,512]{2,1,0:T(8,128)(2,1)}, bf16[1,512,512]{2,1,0:T(8,128)(2,1)S(1)}, u32[]{:S(2)}, u32[]{:S(2)}) collective-permute-start(bf16[1,512,512]{2,1,0:T(8,128)(2,1)} %constant_dynamic-slice_fusion.7), channel_id=1, source_target_pairs={{0,24},{8,16},{16,8},{24,0},{1,25},{9,17},{17,9},{25,1},{2,26},{10... | collective-permute-start | bytes 1572872 | tf_op jit(solution)/shard_map/ppermute | solution.py:151
  90.7 45.7 %collective-permute-start.14 = (bf16[1,512,512]{2,1,0:T(8,128)(2,1)}, bf16[1,512,512]{2,1,0:T(8,128)(2,1)S(1)}, u32[]{:S(2)}, u32[]{:S(2)}) collective-permute-start(bf16[1,512,512]{2,1,0:T(8,128)(2,1)} %constant_dynamic-slice_fusion.9), channel_id=1, source_target_pairs={{0,24},{8,16},{16,8},{24,0},{1,25},{9,17},{17,9},{25,1},{2,26},{10... | collective-permute-start | bytes 1572872 | tf_op jit(solution)/shard_map/ppermute | solution.py:151
  92.3 102.7 %collective-permute-start.13 = (bf16[1,512,512]{2,1,0:T(8,128)(2,1)}, bf16[1,512,512]{2,1,0:T(8,128)(2,1)}, u32[]{:S(2)}, u32[]{:S(2)}) collective-permute-start(bf16[1,512,512]{2,1,0:T(8,128)(2,1)} %constant_dynamic-slice_fusion.9), channel_id=1, source_target_pairs={{0,16},{8,24},{16,0},{24,8},{1,17},{9,25},{17,1},{25,9},{2,18},{10... | collective-permute-start | bytes 1572872 | tf_op jit(solution)/shard_map/ppermute | solution.py:151
  93.8 101.7 %collective-permute-start.12 = (bf16[1,512,512]{2,1,0:T(8,128)(2,1)}, bf16[1,512,512]{2,1,0:T(8,128)(2,1)}, u32[]{:S(2)}, u32[]{:S(2)}) collective-permute-start(bf16[1,512,512]{2,1,0:T(8,128)(2,1)} %constant_dynamic-slice_fusion.9), channel_id=1, source_target_pairs={{0,8},{8,0},{16,24},{24,16},{1,9},{9,1},{17,25},{25,17},{2,10},{10... | collective-permute-start | bytes 1572872 | tf_op jit(solution)/shard_map/ppermute | solution.py:151
  95.8 143.1 %collective-permute-start.25 = (bf16[1,512,512]{2,1,0:T(8,128)(2,1)}, bf16[1,512,512]{2,1,0:T(8,128)(2,1)}, u32[]{:S(2)}, u32[]{:S(2)}) collective-permute-start(bf16[1,512,512]{2,1,0:T(8,128)(2,1)} %constant_dynamic-slice_fusion.7), channel_id=1, source_target_pairs={{0,16},{8,24},{16,0},{24,8},{1,17},{9,25},{17,1},{25,9},{2,18},{10... | collective-permute-start | bytes 1572872 | tf_op jit(solution)/shard_map/ppermute | solution.py:151
  114.0 125.4 %collective-permute-start.24 = (bf16[1,512,512]{2,1,0:T(8,128)(2,1)}, bf16[1,512,512]{2,1,0:T(8,128)(2,1)}, u32[]{:S(2)}, u32[]{:S(2)}) collective-permute-start(bf16[1,512,512]{2,1,0:T(8,128)(2,1)} %constant_dynamic-slice_fusion.7), channel_id=1, source_target_pairs={{0,8},{8,0},{16,24},{24,16},{1,9},{9,1},{17,25},{25,17},{2,10},{10... | collective-permute-start | bytes 1572872 | tf_op jit(solution)/shard_map/ppermute | solution.py:151
  136.4 103.0 %collective-permute-start.17 = (bf16[1,512,512]{2,1,0:T(8,128)(2,1)S(1)}, bf16[1,512,512]{2,1,0:T(8,128)(2,1)}, u32[]{:S(2)}, u32[]{:S(2)}) collective-permute-start(bf16[1,512,512]{2,1,0:T(8,128)(2,1)S(1)} %collective-permute-done.14.refs_3_), channel_id=1, source_target_pairs={{0,1},{1,0},{2,3},{3,2},{4,5},{5,4},{6,7},{7,6},{8,9},{9,8},{10,11... | collective-permute-start | bytes 1572872 | tf_op jit(solution)/shard_map/ppermute | solution.py:152
  195.0 45.3 %collective-permute-start.16 = (bf16[1,512,512]{2,1,0:T(8,128)(2,1)}, bf16[1,512,512]{2,1,0:T(8,128)(2,1)S(1)}, u32[]{:S(2)}, u32[]{:S(2)}) collective-permute-start(bf16[1,512,512]{2,1,0:T(8,128)(2,1)} %collective-permute-done.13.refs_2_), channel_id=1, source_target_pairs={{0,1},{1,0},{2,3},{3,2},{4,5},{5,4},{6,7},{7,6},{8,9},{9,8},{10,11... | collective-permute-start | bytes 1572872 | tf_op jit(solution)/shard_map/ppermute | solution.py:152
  195.5 45.1 %collective-permute-start.15 = (bf16[1,512,512]{2,1,0:T(8,128)(2,1)}, bf16[1,512,512]{2,1,0:T(8,128)(2,1)S(1)}, u32[]{:S(2)}, u32[]{:S(2)}) collective-permute-start(bf16[1,512,512]{2,1,0:T(8,128)(2,1)} %collective-permute-done.12.refs_1_), channel_id=1, source_target_pairs={{0,1},{1,0},{2,3},{3,2},{4,5},{5,4},{6,7},{7,6},{8,9},{9,8},{10,11... | collective-permute-start | bytes 1572872 | tf_op jit(solution)/shard_map/ppermute | solution.py:152
  238.9 38.9 %collective-permute-start.29 = (bf16[1,512,512]{2,1,0:T(8,128)(2,1)S(1)}, bf16[1,512,512]{2,1,0:T(8,128)(2,1)S(1)}, u32[]{:S(2)}, u32[]{:S(2)}) collective-permute-start(bf16[1,512,512]{2,1,0:T(8,128)(2,1)S(1)} %collective-permute-done.26.refs_3_), channel_id=1, source_target_pairs={{0,1},{1,0},{2,3},{3,2},{4,5},{5,4},{6,7},{7,6},{8,9},{9,8},{10,11... | collective-permute-start | bytes 1572872 | tf_op jit(solution)/shard_map/ppermute | solution.py:152
  239.4 38.4 %collective-permute-start.28 = (bf16[1,512,512]{2,1,0:T(8,128)(2,1)}, bf16[1,512,512]{2,1,0:T(8,128)(2,1)S(1)}, u32[]{:S(2)}, u32[]{:S(2)}) collective-permute-start(bf16[1,512,512]{2,1,0:T(8,128)(2,1)} %collective-permute-done.25.refs_2_), channel_id=1, source_target_pairs={{0,1},{1,0},{2,3},{3,2},{4,5},{5,4},{6,7},{7,6},{8,9},{9,8},{10,11... | collective-permute-start | bytes 1572872 | tf_op jit(solution)/shard_map/ppermute | solution.py:152
  239.5 38.3 %collective-permute-start.27 = (bf16[1,512,512]{2,1,0:T(8,128)(2,1)}, bf16[1,512,512]{2,1,0:T(8,128)(2,1)S(1)}, u32[]{:S(2)}, u32[]{:S(2)}) collective-permute-start(bf16[1,512,512]{2,1,0:T(8,128)(2,1)} %collective-permute-done.24.refs_1_), channel_id=1, source_target_pairs={{0,1},{1,0},{2,3},{3,2},{4,5},{5,4},{6,7},{7,6},{8,9},{9,8},{10,11... | collective-permute-start | bytes 1572872 | tf_op jit(solution)/shard_map/ppermute | solution.py:152
  240.3 16.4 %collective-permute-start.22 = (bf16[2,128,512]{2,1,0:T(8,128)(2,1)}, bf16[2,128,512]{2,1,0:T(8,128)(2,1)S(1)}, u32[]{:S(2)}, u32[]{:S(2)}) collective-permute-start(bf16[2,128,512]{2,1,0:T(8,128)(2,1)} %collective-permute-done.19.refs_7_), channel_id=1, source_target_pairs={{0,1},{1,0},{2,3},{3,2},{4,5},{5,4},{6,7},{7,6},{8,9},{9,8},{10,11... | collective-permute-start | bytes 786440 | tf_op jit(solution)/shard_map/ppermute | solution.py:152
  240.5 16.3 %collective-permute-start.21 = (bf16[2,128,512]{2,1,0:T(8,128)(2,1)}, bf16[2,128,512]{2,1,0:T(8,128)(2,1)S(1)}, u32[]{:S(2)}, u32[]{:S(2)}) collective-permute-start(bf16[2,128,512]{2,1,0:T(8,128)(2,1)} %collective-permute-done.18.refs_6_), channel_id=1, source_target_pairs={{0,1},{1,0},{2,3},{3,2},{4,5},{5,4},{6,7},{7,6},{8,9},{9,8},{10,11... | collective-permute-start | bytes 786440 | tf_op jit(solution)/shard_map/ppermute | solution.py:152
  454.5 152.5 %reduce-scatter.7.cloned.1.call-start = ((), (), s32[]{:S(2)}) async-start(), calls=%async_computation.6 | async-start | bytes 6062080
  500.5 248.3 %all-gather.6.cloned.1.call-start = ((), (), s32[]{:S(2)}) async-start(), calls=%async_computation.5 | async-start | bytes 4718592 | tf_op jit(solution)/shard_map/all_gather | solution.py:1118
  (87 other events, 1612.0 us)
Sparse Core Ops, SparseCore 0:
  33.2 60.0 all-reduce.4
  642.7 45.6 all-gather.5
Sparse Core Ops, SparseCore 1:
  45.5 120.1 all-gather.3
  454.6 28.2 reduce-scatter.4
  500.5 76.3 reduce-scatter.6

commit v4 on v3

--- a/solution.py
+++ b/solution.py
@@ -123,37 +123,55 @@
     return jnp.stack([seg_q[::TILE], seg_q[last::TILE], seg_k[::TILE], seg_k[last::TILE]])
 
 
-def lay_weights(w_ref, piece_refs):
+def lay_weights(w_ref, piece_refs, part, first):
     own = piece_refs[0]
-    w_ref_rows = own.shape[1]
+    matrices, rows = w_ref.shape[0], w_ref.shape[1] // 4
+    half = own.shape[0] // 2
     me, side = lax.axis_index("dp"), lax.rem(lax.axis_index("vocab"), 2)
-    half = own.shape[0] // 2
-
-    def rows_of(index):
-        return pl.ds(pl.multiple_of(index * w_ref_rows, w_ref_rows), w_ref_rows)
-
-    w_ref[:, rows_of(me), :] = own[...]
-    for k in range(1, 4):
-        rows = rows_of(me ^ k)
-        w_ref[pl.ds(side * half, half), rows, :] = piece_refs[k][...]
-        w_ref[pl.ds((1 - side) * half, half), rows, :] = piece_refs[k + 3][...]
-
-
-def gather_weights(own, after):
-    if after is not None:
-        own, _ = lax.optimization_barrier((own, after))
-    owners, replicas = lax.axis_size("dp"), lax.axis_size("vocab")
+    for m in range(matrices):
+        span = slice(first + m * rows, first + (m + 1) * rows)
+        w_ref[m, pl.ds(pl.multiple_of(me * rows, rows), rows), :] = own[
+            part * half + span.start : part * half + span.stop, :
+        ]
+        for k in range(1, 4):
+            place = pl.ds(pl.multiple_of((me ^ k) * rows, rows), rows)
+
+            @pl.when(side == part)
+            def _():
+                w_ref[m, place, :] = piece_refs[k][span, :]
+
+            @pl.when(side != part)
+            def _():
+                w_ref[m, place, :] = piece_refs[k + 3][span, :]
+
+
+def flip_sites(part, axis, bit):
+    return lax.ppermute(part, axis, [(s, s ^ bit) for s in range(lax.axis_size(axis))])
+
+
+def late_weights(attn, ffn, after, later):
+    owners = lax.axis_size("dp")
+    width = attn.shape[-1]
+    attn, ffn = attn.astype(jnp.bfloat16), ffn.astype(jnp.bfloat16)
     if owners != 4:
-        whole = lax.all_gather(own, "dp", axis=1, tiled=True)
-        return (whole,), whole[0, 0]
-    half = own.shape[0] // 2
-    mine = lax.dynamic_slice_in_dim(own, lax.axis_index("vocab") % 2 * half, half, 0)
-    got = [lax.ppermute(mine, "dp", [(s, s ^ k) for s in range(owners)]) for k in range(1, 4)]
-    swapped = [lax.ppermute(part, "vocab", [(s, s ^ 1) for s in range(replicas)]) for part in got]
-    return (own, *got, *swapped), swapped[-1][0, 0]
-
-
-def attn_forward_kernel(causal, cross, pieces, *refs):
+        attn, ffn = (lax.all_gather(part, "dp", axis=1, tiled=True) for part in (attn, ffn))
+        return ((attn[:4],), 0, 0), ((attn[4:],), 0, 0), ((ffn,), 0, 0), ffn[0, 0]
+    halves = [
+        jnp.concatenate([attn[4 * k : 4 * k + 4].reshape(-1, width), ffn[k]]) for k in range(2)
+    ]
+    own = jnp.concatenate(halves)
+    side = lax.axis_index("vocab") % 2
+    mine = jnp.where(side == 0, halves[0], halves[1])
+    mine, _ = lax.optimization_barrier((mine, after))
+    got = [flip_sites(mine, "dp", k) for k in range(1, 4)]
+    *got, _ = lax.optimization_barrier((*got, later))
+    swapped = [flip_sites(part, "vocab", 1) for part in got]
+    pieces = (own, *got, *swapped)
+    rows = 4 * attn.shape[1]
+    return (pieces, 0, 0), (pieces, 1, 0), (pieces, None, rows), swapped[-1][0]
+
+
+def attn_forward_kernel(causal, cross, pieces, part, first, *refs):
     refs = list(refs)
     x_ref, ln_ref, segq_ref, segk_ref = refs[:4]
     refs = refs[4:]
@@ -164,7 +182,7 @@
     w_ref = piece_refs[0]
     if pieces > 1:
         w_ref = refs.pop(0)
-        lay_weights(w_ref, piece_refs)
+        lay_weights(w_ref, piece_refs, part, first)
     top_ref, sum_ref, acc_ref = refs
     length, width = x_ref.shape
     head_size = width // HEADS
@@ -213,6 +231,7 @@
 
 def attn_forward(x, ln, weights, seg_q, seg_k, key_in, causal):
     length, width = x.shape
+    weights, part, first = weights
     cross = key_in is not None
     segs = (seg_q[None, :], jnp.broadcast_to(seg_k[:, None], (length, TILE)))
     edges = tile_edges(seg_q, seg_k)
@@ -222,7 +241,7 @@
     if len(weights) > 1:
         outs = outs + (low(4, width, width),)
     out, normed, *stored = call(
-        partial(attn_forward_kernel, causal, cross, len(weights)),
+        partial(attn_forward_kernel, causal, cross, len(weights), part, first),
         outs,
         *args,
         scratch=[
@@ -326,12 +345,13 @@
     return value, slope
 
 
-def ffn_forward_kernel(chunk, pieces, x_ref, ln_ref, next_ref, *refs):
+def ffn_forward_kernel(chunk, pieces, first, x_ref, ln_ref, next_ref, *refs):
     piece_refs, (out_ref, a_ref, after_ref, *refs) = refs[:pieces], refs[pieces:]
     w_ref = piece_refs[0]
     if pieces > 1:
         (w_ref,) = refs
-        lay_weights(w_ref, piece_refs)
+        for part in range(2):
+            lay_weights(w_ref.at[part : part + 1], piece_refs, part, first)
     w_in_ref, w_out_ref = w_ref.at[0], w_ref.at[1]
     a_ref[...] = norm_forward(x_ref[...], ln_ref).astype(jnp.bfloat16)
     total = x_ref[...]
@@ -346,19 +366,22 @@
 
 def ffn_forward(x, ln, ln_next, weights):
     length, width = x.shape
+    weights, _, first = weights
     outs = (full(length, width), low(length, width), low(length, width))
     if len(weights) > 1:
-        outs = outs + (low(2, 4 * weights[0].shape[1], width),)
+        outs = outs + (low(2, 4 * (weights[0].shape[0] // 2 - first), width),)
     out, normed, after, *whole = call(
-        partial(ffn_forward_kernel, 512, len(weights)), outs, x, ln, ln_next, *weights
-    )
-    return out, after, (x, ln, whole[0] if whole else weights[0], normed)
+        partial(ffn_forward_kernel, 512, len(weights), first), outs, x, ln, ln_next, *weights
+    )
+    return out, after, (x, ln, whole[0] if whole else weights[0], normed, out, ln_next)
 
 
 def ffn_backward_kernel(
-    chunk, g_ref, x_ref, ln_ref, a_ref, w_ref, out_ref, ln_grad_ref, low_ref, ut_ref, ht_ref
+    chunk, after_ref, y_ref, next_ref, x_ref, ln_ref, a_ref, w_ref,
+    out_ref, next_grad_ref, ln_grad_ref, low_ref, ut_ref, ht_ref, g_ref,
 ):
     w_in_ref, w_out_ref = w_ref.at[0], w_ref.at[1]
+    g_ref[...] = norm_backward(after_ref[...], y_ref[...], next_ref, next_grad_ref)
     low_ref[...] = g_ref[...].astype(jnp.bfloat16)
     total = jnp.zeros(g_ref.shape, jnp.float32)
     for start in range(0, w_in_ref.shape[0], chunk):
@@ -372,28 +395,25 @@
     out_ref[...] = g_ref[...] + norm_backward(total, x_ref[...], ln_ref, ln_grad_ref)
 
 
-def ffn_backward(grad, stored):
-    x, ln, weights, normed = stored
+def ffn_backward(grad_after, stored):
+    x, ln, weights, normed, out, ln_next = stored
     length, width = x.shape
     hidden = weights.shape[1]
-    out, ln_grad, *rest = call(
+    outs = (full(length, width), full(2, width), full(2, width))
+    outs = outs + (low(length, width), low(hidden, length), low(hidden, length))
+    out, next_grad, ln_grad, *rest = call(
         partial(ffn_backward_kernel, 512),
-        (full(length, width), full(2, width), low(length, width), low(hidden, length), low(hidden, length)),
-        grad,
+        outs,
+        grad_after,
+        out,
+        ln_next,
         x,
         ln,
         normed,
         weights,
-    )
-    return out, ln_grad, rest
-
-
-def norm_backward_kernel(g_ref, x_ref, ln_ref, out_ref, ln_grad_ref):
-    out_ref[...] = norm_backward(g_ref[...], x_ref[...], ln_ref, ln_grad_ref)
-
-
-def plain_norm_backward(grad, x, ln):
-    return call(norm_backward_kernel, (full(*x.shape), full(2, x.shape[1])), grad, x, ln)
+        scratch=[pltpu.VMEM((length, width), jnp.float32)],
+    )
+    return out, next_grad, ln_grad, rest
 
 
 def small_factor(block):
@@ -671,35 +691,9 @@
     ]
 
 
-def basis_kernel(x_ref, out_ref, s0, r0, s1, r1):
-    here = lax.axis_index("vocab")
-    near, side = flip(here, 1), lax.rem(here, 2)
-    others = far_replicas()
-    greet(*[("vocab", to) for _, to, _ in others], ("vocab", near))
-    rows = x_ref.shape[0] // 2
-    half = pl.ds(pl.multiple_of(side * rows, rows), rows)
-    copies = [
-        push(x_ref.at[half], out_ref.at[here // 2, half], (s0, r0), slot, "vocab", to)
-        for slot, to, _ in others
-    ]
-    out_ref[here // 2] = x_ref[...]
-    close = []
-    for copy, (slot, _, origin) in zip(copies, others):
-        copy.wait()
-        place = out_ref.at[origin // 2, half]
-        close.append(push(place, place, (s1, r1), slot, "vocab", near))
-    for copy in close:
-        copy.wait()
-
-
-def gather_basis(x, collective_id):
-    pairs = lax.axis_size("vocab") // 2
-    out = jax.ShapeDtypeStruct((pairs, *x.shape), x.dtype)
-    sems = sem_pair(pairs - 1) + sem_pair(pairs - 1)
-    return talk(basis_kernel, out, collective_id, x, scratch=sems)
-
-
-def gradient_kernel(x_ref, out_ref, parts_ref, s0, r0, s1, r1, s2, r2):
+def gradient_kernel(
+    x_ref, rows_ref, out_ref, swapped_ref, parts_ref, s0, r0, s1, r1, s2, r2, s3, r3, s4, r4
+):
     owners = peers_of("dp")
     here, me = lax.axis_index("vocab"), lax.axis_index("dp")
     near = flip(here, 1)
@@ -723,6 +717,13 @@
         ]
         for c in range(chunks)
     ]
+    half_rows = rows_ref.shape[1] // 2
+    half = pl.ds(pl.multiple_of(lax.rem(here, 2) * half_rows, half_rows), half_rows)
+    swaps = [
+        push(rows_ref.at[to, half], swapped_ref.at[me, half], (s3, r3), step - 1, "dp", to)
+        for step, to, _ in owners
+    ]
+    swapped_ref[me] = rows_ref[me]
     far, close = [], []
     for c in range(chunks):
         parts_ref[me, c] = x_ref[me, c]
@@ -742,23 +743,33 @@
             far[c][k].wait()
             origin = lax.rem(here + size - step, size)
             close.append(spread(c, origin, (s2, r2), (k + 1) * chunks + c, near))
+    for copy, (step, _, origin) in zip(swaps, owners):
+        copy.wait()
+        place = swapped_ref.at[origin, half]
+        close.append(push(place, place, (s4, r4), step - 1, "vocab", near))
     for copy in close:
         copy.wait()
 
 
-def share_gradients(x, collective_id):
+def share_gradients(x, rows, collective_id):
     owners, replicas = lax.axis_size("dp"), lax.axis_size("vocab")
     chunks = x.shape[1]
     others = (replicas // 2 - 1) * chunks
     return talk(
         gradient_kernel,
-        jax.ShapeDtypeStruct((replicas, *x.shape[1:]), x.dtype),
+        (
+            jax.ShapeDtypeStruct((replicas, *x.shape[1:]), x.dtype),
+            jax.ShapeDtypeStruct(rows.shape, rows.dtype),
+        ),
         collective_id,
         x,
+        rows,
         scratch=[pltpu.VMEM(x.shape, x.dtype)]
         + sem_pair((owners - 1) * chunks)
         + sem_pair(others)
-        + sem_pair(others + chunks),
+        + sem_pair(others + chunks)
+        + sem_pair(owners - 1)
+        + sem_pair(owners - 1),
     )
 
 
@@ -795,8 +806,9 @@
 
 
 def token_kernel(
-    scale, x_ref, place_ref, out_ref, near_ref, parts_ref, blocks_ref, row_ref,
-    s0, r0, s1, r1, s2, r2, s3, r3, s4, r4,
+    scale, x_ref, place_ref, attn_ref, ffn_ref, out_ref, attn_out_ref, ffn_out_ref,
+    near_ref, parts_ref, blocks_ref, row_ref,
+    s0, r0, s1, r1, s2, r2, s3, r3, s4, r4, s5, r5, s6, r6,
 ):
     owners, others = peers_of("dp"), far_replicas()
     me, here = lax.axis_index("dp"), lax.axis_index("vocab")
@@ -817,7 +829,30 @@
     def place_of(index):
         return pl.ds(pl.multiple_of(side * half + index // 2 * share, share), share)
 
+    def weight_place(ref, own_ref, origin):
+        count, rows = own_ref.shape[0] // 2, own_ref.shape[1]
+        return ref.at[pl.ds(side * count, count), pl.ds(pl.multiple_of(origin * rows, rows), rows)]
+
+    def send_weights(ref, own_ref, slot):
+        mine = own_ref.at[pl.ds(side * (own_ref.shape[0] // 2), own_ref.shape[0] // 2)]
+        return [
+            push(mine, weight_place(ref, own_ref, me), (s5, r5), slot + step - 1, "dp", to)
+            for step, to, _ in owners
+        ]
+
+    def relay_weights(ref, own_ref, copies, slot):
+        relays = []
+        for copy, (step, _, origin) in zip(copies, owners):
+            copy.wait()
+            place = weight_place(ref, own_ref, origin)
+            relays.append(push(place, place, (s6, r6), slot + step - 1, "vocab", near))
+        return relays
+
     first = push(x_ref.at[:, half_of(1 - side)], near_ref, (s0, r0), 0, "vocab", near)
+    attn_copies = send_weights(attn_out_ref, attn_ref, 0)
+    for ref, own_ref in ((attn_out_ref, attn_ref), (ffn_out_ref, ffn_ref)):
+        rows = own_ref.shape[1]
+        ref[:, pl.ds(pl.multiple_of(me * rows, rows), rows), :] = own_ref[...]
     first.wait()
     near_ref[...] += x_ref[:, half_of(side)]
     copies = [
@@ -844,6 +879,7 @@
     row_ref[me, place_of(here)] = blocks_ref[me]
     for copy in copies:
         copy.wait()
+    ffn_copies = send_weights(ffn_out_ref, ffn_ref, len(owners))
     mine = row_ref.at[:, place_of(here)]
     copies = [push(mine, mine, (s3, r3), slot, "vocab", to) for slot, to, _ in others]
     close = [push(mine, mine, (s4, r4), 0, "vocab", near)]
@@ -851,23 +887,31 @@
         copy.wait()
         theirs = row_ref.at[:, place_of(origin)]
         close.append(push(theirs, theirs, (s4, r4), slot + 1, "vocab", near))
-    for copy in close:
+    close += relay_weights(attn_out_ref, attn_ref, attn_copies, 0)
+    for copy in close[: pairs]:
         copy.wait()
     for owner in range(count):
         band = slice(owner * columns, (owner + 1) * columns)
         out_ref[:, band] = row_ref[owner].astype(jnp.float32) * scale + place_ref[:, band]
-
-
-def gather_tokens(x, places, scale, collective_id):
+    close += relay_weights(ffn_out_ref, ffn_ref, ffn_copies, len(owners))
+    for copy in close[pairs:]:
+        copy.wait()
+
+
+def gather_tokens(x, places, attn, ffn, scale, collective_id):
     owners, pairs = lax.axis_size("dp"), lax.axis_size("vocab") // 2
     _, length, columns = x.shape
     half = length // 2
+    width = owners * columns
+    whole = [low(w.shape[0], owners * w.shape[1], width) for w in (attn, ffn)]
     return talk(
         partial(token_kernel, scale),
-        full(length, owners * columns),
+        (full(length, width), *whole),
         collective_id,
         x,
         places,
+        attn,
+        ffn,
         scratch=[
             pltpu.VMEM((owners, half, columns), x.dtype),
             pltpu.VMEM((pairs - 1, owners, half // pairs, columns), x.dtype),
@@ -878,7 +922,9 @@
         + sem_pair(pairs - 1)
         + sem_pair(owners - 1)
         + sem_pair(pairs - 1)
-        + sem_pair(pairs),
+        + sem_pair(pairs)
+        + sem_pair(2 * owners - 2)
+        + sem_pair(2 * owners - 2),
     )
 
 
@@ -966,17 +1012,8 @@
     own_norms = jnp.pad(norm_p.astype(jnp.bfloat16).astype(jnp.float32), ((0, 2), (0, 0)))
     all_ids, norm_rows = gather_small("dp", 1, jnp.concatenate([src_ids, tgt_ids]), own_norms)
     norm_rows = jnp.swapaxes(norm_rows, 0, 1).reshape(16, -1)
-    w_attn = [None] * 3
-    w_ffn = [None] * 2
-    w_attn[0], ready = gather_weights(attn_w[0:4].astype(jnp.bfloat16), None)
-    w_ffn[0], ready = gather_weights(ffn_w[0:2].astype(jnp.bfloat16), ready)
-    w_attn[1], ready = gather_weights(attn_w[4:8].astype(jnp.bfloat16), ready)
-    w_attn[2], ready = gather_weights(attn_w[8:12].astype(jnp.bfloat16), ready)
-    w_ffn[1], ready = gather_weights(ffn_w[2:4].astype(jnp.bfloat16), ready)
-    late_table, _ = lax.optimization_barrier((own_table, ready))
-    table_low = lax.all_gather(late_table, "dp", axis=1, tiled=True)
     norms = [jnp.stack([norm_rows[k], norm_rows[7 + k]]) for k in range(7)]
-    vocab_count, width = table_low.shape
+    vocab_count, width = embedding.shape[0], attn_w.shape[2]
     columns = replica * vocab_count + jnp.arange(vocab_count)
     source, source_seg, target, target_seg = (src_ids[0], src_seg[0], tgt_ids[0], tgt_seg[0])
     pick_rows, labels = (pick_pos[0], pick_label[0])
@@ -991,24 +1028,34 @@
         return jnp.where((ids % 2 == 0)[:, None], left, right)
 
     source_part, target_part = (look_up(all_ids[:, k].reshape(-1)) for k in (0, 1))
+    positional = sinusoid(length, width)
+    enc_in, enc_attn_w, enc_ffn_w = gather_tokens(
+        source_part.reshape(owners, length, -1),
+        positional,
+        attn_w[0:4].astype(jnp.bfloat16),
+        ffn_w[0:2].astype(jnp.bfloat16),
+        embed_scale,
+        2,
+    )
+    target_part, _ = lax.optimization_barrier((target_part, enc_in))
     target_sum = lax.psum(target_part, "vocab")
-    positional = sinusoid(length, width)
-    source_part = source_part.reshape(owners, length, -1)
-    enc_in = gather_tokens(source_part, positional, embed_scale, 2)
     enc_mid, enc_attn = attn_forward(
-        enc_in, norms[0], w_attn[0], source_seg, source_seg, None, False
-    )
-    enc_out, encoded, enc_ffn = ffn_forward(enc_mid, norms[1], norms[2], w_ffn[0])
+        enc_in, norms[0], ((enc_attn_w,), 0, 0), source_seg, source_seg, None, False
+    )
+    self_w, cross_w, dec_ffn_w, ready = late_weights(attn_w[4:], ffn_w[2:], enc_in, enc_mid)
+    late_table, _ = lax.optimization_barrier((own_table, ready))
+    table_low = lax.all_gather(late_table, "dp", axis=1, tiled=True)
+    enc_out, encoded, enc_ffn = ffn_forward(enc_mid, norms[1], norms[2], ((enc_ffn_w,), 0, 0))
     target_rows = swap_owners(target_sum.reshape(owners, length, -1), 3)
     target_rows = jnp.swapaxes(target_rows, 0, 1).reshape(length, -1).astype(jnp.float32)
     dec_in = target_rows * embed_scale + positional
     dec_mid, dec_self = attn_forward(
-        dec_in, norms[3], w_attn[1], target_seg, target_seg, None, True
+        dec_in, norms[3], self_w, target_seg, target_seg, None, True
     )
     dec_late, dec_cross = attn_forward(
-        dec_mid, norms[4], w_attn[2], target_seg, source_seg, encoded, False
-    )
-    dec_out, final_low, dec_ffn = ffn_forward(dec_late, norms[5], norms[6], w_ffn[1])
+        dec_mid, norms[4], cross_w, target_seg, source_seg, encoded, False
+    )
+    dec_out, final_low, dec_ffn = ffn_forward(dec_late, norms[5], norms[6], dec_ffn_w)
 
     chosen_rows = one_hot(pick_rows, jnp.arange(length))
     picked = dot_dims(chosen_rows, final_low, 1, 0).astype(jnp.bfloat16)
@@ -1036,27 +1083,6 @@
     )
     grad_final = dot_dims(chosen_rows, grad_picked, 0, 0)
 
-    norm_grads = [None] * 7
-    grad, norm_grads[6] = plain_norm_backward(grad_final, dec_out, norms[6])
-    grad, norm_grads[5], dec_ffn_parts = ffn_backward(grad, dec_ffn)
-    grad, norm_grads[4], cross_parts, grad_encoded = attn_backward(grad, dec_cross)
-    grad, norm_grads[3], self_parts, _ = attn_backward(grad, dec_self)
-    grad_target = (grad * embed_scale).astype(jnp.bfloat16)
-    grad, norm_grads[2] = plain_norm_backward(grad_encoded, enc_out, norms[2])
-    grad, norm_grads[1], enc_ffn_parts = ffn_backward(grad, enc_ffn)
-    grad, norm_grads[0], enc_parts, _ = attn_backward(grad, enc_attn)
-    grad_source = (grad * embed_scale).astype(jnp.bfloat16)
-    token_grads = jnp.concatenate([grad_source, grad_target]).reshape(2 * length, owners, -1)
-    token_grads = swap_owners(jnp.swapaxes(token_grads, 0, 1), 6).reshape(owners * 2 * length, -1)
-    flat_ids = all_ids.reshape(-1)
-    even = (flat_ids % 2 == 0)[:, None]
-    token_grads = jnp.concatenate(
-        [jnp.where(even, token_grads, 0), jnp.where(even, 0, token_grads)], axis=1
-    )
-    g_embed = grad_table.astype(jnp.float32) + dot_dims(
-        one_hot(flat_ids // 2, halves), token_grads, 0, 0
-    ).reshape(vocab_count, -1)
-
     chosen_columns = share_rows(jnp.eye(width, dtype=jnp.bfloat16), owners, replicas, replica)
     chosen_columns = chosen_columns.reshape(-1, width)
 
@@ -1080,19 +1106,52 @@
             for rows, right in ((grads, stored[3]), (values, grad_low))
         ]
 
-    pieces = (
-        weight_grads(enc_attn, enc_parts)
-        + weight_grads(dec_self, self_parts)
-        + weight_grads(dec_cross, cross_parts)
-        + hidden_grads(enc_ffn, enc_ffn_parts)
-        + hidden_grads(dec_ffn, dec_ffn_parts)
-    )
-    blocks = [piece.astype(jnp.bfloat16).reshape(owners, -1, width) for piece in pieces]
-    blocks = [jnp.concatenate(blocks[k : k + 4], axis=1) for k in (0, 4, 8)] + blocks[12:]
-    shared = share_gradients(jnp.stack(blocks, axis=1), 7)
-    g_attn = shared[:, :3].reshape(replicas, 12, -1, width)
-    g_attn = jnp.swapaxes(g_attn, 0, 1).reshape(12, -1, width).astype(jnp.float32)
-    g_ffn = jnp.swapaxes(shared[:, 3:], 0, 1).reshape(4, -1, width)
+    def gradient_blocks(pieces):
+        blocks = [piece.astype(jnp.bfloat16).reshape(owners, -1, width) for piece in pieces]
+        return blocks if len(blocks) == 2 else [jnp.concatenate(blocks, axis=1)]
+
+    norm_grads = [None] * 7
+    grad, norm_grads[6], norm_grads[5], dec_ffn_parts = ffn_backward(grad_final, dec_ffn)
+    grad, norm_grads[4], cross_parts, grad_encoded = attn_backward(grad, dec_cross)
+    grad, norm_grads[3], self_parts, _ = attn_backward(grad, dec_self)
+    grad_target = (grad * embed_scale).astype(jnp.bfloat16)
+    early = (
+        gradient_blocks(weight_grads(dec_self, self_parts))
+        + gradient_blocks(weight_grads(dec_cross, cross_parts))
+        + gradient_blocks(hidden_grads(dec_ffn, dec_ffn_parts))
+    )
+    early = jnp.concatenate(early, axis=1)
+    early, grad_encoded = lax.optimization_barrier((early, grad_encoded))
+    early = lax.psum_scatter(early, "dp", scatter_dimension=0, tiled=False)
+    early = lax.all_gather(early, "vocab")
+    grad, norm_grads[2], norm_grads[1], enc_ffn_parts = ffn_backward(grad_encoded, enc_ffn)
+    grad, norm_grads[0], enc_parts, _ = attn_backward(grad, enc_attn)
+    grad_source = (grad * embed_scale).astype(jnp.bfloat16)
+    token_grads = jnp.concatenate([grad_source, grad_target]).reshape(2 * length, owners, -1)
+    late = gradient_blocks(weight_grads(enc_attn, enc_parts)) + gradient_blocks(
+        hidden_grads(enc_ffn, enc_ffn_parts)
+    )
+    late, token_grads = share_gradients(
+        jnp.stack(late, axis=1), jnp.swapaxes(token_grads, 0, 1), 7
+    )
+    token_grads = token_grads.reshape(owners * 2 * length, -1)
+    flat_ids = all_ids.reshape(-1)
+    even = (flat_ids % 2 == 0)[:, None]
+    token_grads = jnp.concatenate(
+        [jnp.where(even, token_grads, 0), jnp.where(even, 0, token_grads)], axis=1
+    )
+    g_embed = grad_table.astype(jnp.float32) + dot_dims(
+        one_hot(flat_ids // 2, halves), token_grads, 0, 0
+    ).reshape(vocab_count, -1)
+
+    def by_matrix(shared, count):
+        blocks = jnp.swapaxes(shared.reshape(replicas, count, -1, width), 0, 1)
+        return blocks.reshape(count, -1, width)
+
+    early, late = by_matrix(early, 4), by_matrix(late, 3)
+    g_attn = [by_matrix(part, 4) for part in (late[0], early[0], early[1])]
+    g_attn = jnp.concatenate(g_attn).astype(jnp.float32)
+    g_ffn = jnp.concatenate([late[1:], early[2:]])
     norm_grad = jnp.stack(norm_grads)
     norm_grad = jnp.concatenate([norm_grad[:, 0], norm_grad[:, 1]], axis=0)
     g_norm = lax.psum_scatter(norm_grad, "dp", scatter_dimension=1, tiled=True)
@@ -1115,15 +1174,21 @@
         g_norm * factor,
         g_embed * factor,
     )
-    all_products = lax.all_gather(own_products.astype(jnp.bfloat16), "vocab")[::2]
+
+    def all_matrices(own):
+        rows = own.shape[0] // 2
+        half = lax.dynamic_slice_in_dim(own.astype(jnp.bfloat16), replica % 2 * rows, rows, 0)
+        return lax.all_gather(half, "vocab").reshape(4, 2 * rows, -1).astype(jnp.float32)
+
+    all_products = all_matrices(own_products)
     new_stats = stat_decay * soap_stats + (1.0 - stat_decay) * (factor * factor) * (
-        all_products.astype(jnp.float32)
+        all_products
     )
     own_stat = stat_decay * lax.dynamic_index_in_dim(soap_stats, matrix, 0, keepdims=False) + (
         1.0 - stat_decay
     ) * (factor * factor) * own_products
     own_basis = renew_basis(own_stat, lax.dynamic_index_in_dim(soap_basis, matrix, 0, keepdims=False))
-    new_basis = gather_basis(own_basis.astype(jnp.bfloat16), 9).astype(jnp.float32)
+    new_basis = all_matrices(own_basis)
 
     new_attn, m_attn, v_attn = adam_update(attn_w, g_attn, attn_m, attn_v, rate_matrix, decay_rate)
     new_norm, m_norm, v_norm = adam_update(norm_p, g_norm, norm_m, norm_v, rate_vector, 0.0)

time: 772 us -> 708 us (0.917)
  waiting for transfers between devices: 53.2 us -> 27.5 us
  starting transfers between devices: 22.2 us -> 5.04 us
  local copies, waits for them, and re-layouts: 78.2 us -> 62.2 us
  Pallas kernels: 426 us -> 416 us
  matrix products: 84.2 us -> 93.3 us
    pallas_call x9 -> x7, Pallas kernels: 216 us -> 175 us  [talk(): pl.pallas_call(kernel, out_shape=outs, in_specs=[vmem] * len(args), out_s...]
    pallas_call x12 -> x11, Pallas kernels: 210 us -> 242 us  [call(): pl.pallas_call(kernel, out_shape=outs, in_specs=[vmem] * (len(args) - sme...]
    ppermute x30 -> x6, waiting for transfers between devices: 53 us -> 26.1 us  [flip_sites(): lax.ppermute(part, axis, [(s, s ^ bit) for s in range(lax.axis_size(axis))])]
    pallas_call x1 -> x0, local copies, waits for them, and re-layouts: 18.7 us -> none  [call(): pl.pallas_call(kernel, out_shape=outs, in_specs=[vmem] * (len(args) - sme...]
    ppermute x30 -> x6, starting transfers between devices: 21.3 us -> 4.15 us  [flip_sites(): lax.ppermute(part, axis, [(s, s ^ bit) for s in range(lax.axis_size(axis))])]
    unnamed x181 -> x152, local copies, waits for them, and re-layouts: 22.1 us -> 20.6 us
  transfers between devices with their start and end apart: 35 -> 14, of which waited for: 7 -> 2; matrix products, arithmetic and copies ran while one was open for 21% -> 20% of each run, Pallas kernels for 36% -> 34%
where the time goes in v4:
time: 708 us; the launch traced here: 701 us
  Pallas kernels  416 us (59%)
  matrix products  93.3 us (13%)
  other arithmetic  71.9 us (10%)
  local copies, waits for them, and re-layouts  62.2 us (9%)
  waiting for transfers between devices  27.5 us (4%)
  between operations  24.2 us (3%)
    pallas_call x11, Pallas kernels, call(): pl.pallas_call(kernel, out_shape=outs, in_specs=[vmem] * (len(args) - sme...  242 us
    pallas_call x7, Pallas kernels, talk(): pl.pallas_call(kernel, out_shape=outs, in_specs=[vmem] * len(args), out_s...  175 us
    dot_general x26, matrix products, dot_dims(): lax.dot_general(left, right, (((left_dim,), (right_dim,)), ((), ())), pre...  49.4 us
    ppermute x6, waiting for transfers between devices, flip_sites(): lax.ppermute(part, axis, [(s, s ^ bit) for s in range(lax.axis_size(axis))])  26.1 us
    unnamed x152, local copies, waits for them, and re-layouts  20.6 us
    dot_general x2, matrix products, product(): jnp.einsum('mfd,mde->mfe', values, part, preferred_element_type=jnp.float32)  17.1 us
  transfers between devices with their start and end apart: 14, of which 2 were waited for; matrix products, arithmetic and copies ran while one was open for 20% of the time, Pallas kernels for 34%

profile of v4, /device:TPU:0, one launch (start us, length us, event | category | flops | bytes accessed | tf_op | source)
XLA Modules:
  0.0 700.6 jit_solution(7853234268594061801)
XLA Ops:
  10.8 7.8 %shard_map.332 = (s32[4,2,1024]{2,1,0:T(2,128)}, f32[4,16,128]{2,1,0:T(8,128)}) custom-call(s32[2,1024]{1,0:T(2,128)} %pad_add_fusion.refs_0_, f32[16,128]{1,0:T(8,128)} %pad_convert_fusion.refs_1_), custom_call_target="tpu_custom_call" | custom-call | tf_op jit(solution)/shard_map/pallas_call | solution.py:530
  26.8 6.8 fusion.2
  33.7 6.8 fusion.4
  47.6 52.1 %shard_map.333 = (f32[1024,512]{1,0:T(8,128)}, bf16[4,512,512]{2,1,0:T(8,128)(2,1)}, bf16[2,2048,512]{2,1,0:T(8,128)(2,1)}) custom-call(bf16[4,1024,128]{2,1,0:T(8,128)(2,1)} %bitcast.249, f32[1024,512]{1,0:T(8,128)} %constant.224.clone.place_ref, bf16[4,128,512]{2,1,0:T(8,128)(2,1)} %get-tuple-element.197.attn_ref, bf16[2,512,512]{2,1,0:T(8,128)(2,1)} %slice.250.ffn_ref), custom_call_target="tpu_custom_call" | custom-call | tf_op jit(solution)/shard_map/pallas_call | solution.py:530
  111.8 24.6 %shard_map.334 = (f32[1024,512]{1,0:T(8,128)}, bf16[1024,512]{1,0:T(8,128)(2,1)}, bf16[512,1024]{1,0:T(8,128)(2,1)}, bf16[512,1024]{1,0:T(8,128)(2,1)}, bf16[512...) custom-call(f32[1024,512]{1,0:T(8,128)} %get-tuple-element.95.refs_0_.refs_1_, ...), custom_call_target="tpu_custom_call" | custom-call | tf_op jit(solution)/shard_map/pallas_call | solution.py:50
  142.1 22.4 %collective-permute-done.1.refs_6_.refs_7_.refs_2_ = bf16[1024,512]{1,0:T(8,128)(2,1)S(1)} collective-permute-done((bf16[1024,512]{1,0:T(8,128)(2,1)}, bf16[1024,512]{1,0:T(8,128)(2,1)S(1)}, u32[]{:S(2)}, u32[]{:S(2)}) %collective-permute-start.1) | collective-permute-done | bytes 1048608 | tf_op jit(solution)/shard_map/ppermute | solution.py:149
  165.8 11.1 %shard_map.337 = (f32[1024,512]{1,0:T(8,128)}, bf16[1024,512]{1,0:T(8,128)(2,1)}, bf16[1024,512]{1,0:T(8,128)(2,1)}) custom-call(f32[1024,512]{1,0:T(8,128)} %get-tuple-element.101.x_ref, f32[2,512]{1,0:T(2,128)} %pad_maximum_fusion.11.ln_ref, f32[2,512]{1,0:T(2,128)} %pad_maximum_fusion.12.next_ref, bf16[2,2048,512]{2,1,0:T(8,128)(2,1)} %get-tuple-element.107.refs_0_.w_ref), custom_call_target="tpu_custom_call" | custom-call | tf_op jit(solution)/shard_map/pallas_call | solution.py:50
  180.3 16.7 %shard_map.335 = bf16[4,1024,128]{2,1,0:T(8,128)(2,1)} custom-call(bf16[4,1024,128]{2,1,0:T(8,128)(2,1)} %all-reduce.6.cloned.1.call-done.x_ref), custom_call_target="tpu_custom_call" | custom-call | tf_op jit(solution)/shard_map/pallas_call | solution.py:530
  200.9 21.4 %shard_map.336 = (f32[1024,512]{1,0:T(8,128)}, bf16[1024,512]{1,0:T(8,128)(2,1)}, bf16[512,1024]{1,0:T(8,128)(2,1)}, bf16[512,1024]{1,0:T(8,128)(2,1)}, bf16[512...) custom-call(f32[1024,512]{1,0:T(8,128)} %copy_bitcast_fusion.refs_0_.refs_1_, ...), custom_call_target="tpu_custom_call" | custom-call | tf_op jit(solution)/shard_map/pallas_call | solution.py:50
  222.3 22.8 %shard_map.338 = (f32[1024,512]{1,0:T(8,128)}, bf16[1024,512]{1,0:T(8,128)(2,1)}, bf16[512,1024]{1,0:T(8,128)(2,1)}, bf16[512,1024]{1,0:T(8,128)(2,1)}, bf16[512...) custom-call(f32[1024,512]{1,0:T(8,128)} %get-tuple-element.106.refs_0_.refs_1_,, ...), custom_call_target="tpu_custom_call" | custom-call | tf_op jit(solution)/shard_map/pallas_call | solution.py:50
  245.2 14.0 %shard_map.339 = (f32[1024,512]{1,0:T(8,128)}, bf16[1024,512]{1,0:T(8,128)(2,1)}, bf16[1024,512]{1,0:T(8,128)(2,1)}, bf16[2,2048,512]{2,1,0:T(8,128)(2,1)}) custom-call(f32[1024,512]{1,0:T(8,128)} %get-tuple-element.109.x_ref, f32[2,512]{1,0:T(2,128)} %pad_maximum_fusion.13.ln_ref, f32[2,512]{1,0:T(2,128)} %pad_maximum_fusion.14.next_ref, ...), custom_call_target="tpu_custom_call" | custom-call | tf_op jit(solution)/shard_map/pallas_call | solution.py:50
  264.5 4.0 fusion.79
  270.4 9.3 %shard_map.340 = f32[8,8,256]{2,1,0:T(8,128)} custom-call(f32[8,256]{1,0:T(8,128)} %select_maximum_fusion.refs_0_), custom_call_target="tpu_custom_call" | custom-call | tf_op jit(solution)/shard_map/pallas_call | solution.py:530
  285.9 16.2 %shard_map.341 = bf16[256,512]{1,0:T(8,128)(2,1)} custom-call(bf16[256,512]{1,0:T(8,128)(2,1)} %convolution_convert_fusion.5.x_ref), custom_call_target="tpu_custom_call" | custom-call | tf_op jit(solution)/shard_map/pallas_call | solution.py:530
  305.1 18.5 %shard_map.342 = (f32[1024,512]{1,0:T(8,128)}, f32[2,512]{1,0:T(2,128)}, f32[2,512]{1,0:T(2,128)}, bf16[1024,512]{1,0:T(8,128)(2,1)}, bf16[2048,1024]{1,0:T(8,128)(2,1)}, /*index=5*/bf16[2048,1024]{1,0:T(8,128)(2,1)}) custom-call(f32[1024,512]{1,0:T(8,128)} %fusion.41.after_ref, f32[1024,512]{1,0:T(8,128)} %get-tuple-element.111.y_ref, ...), custom_call_target="tpu_custom_call" | custom-call | tf_op jit(solution)/shard_map/pallas_call | solution.py:50
  326.3 26.3 %shard_map.343 = (f32[1024,512]{1,0:T(8,128)}, f32[2,512]{1,0:T(2,128)}, bf16[1024,512]{1,0:T(8,128)(2,1)}, bf16[1024,512]{1,0:T(8,128)(2,1)}, bf16[1024,512]{1,...) custom-call(f32[1024,512]{1,0:T(8,128)} %get-tuple-element.114.refs_0_, ...), custom_call_target="tpu_custom_call" | custom-call | tf_op jit(solution)/shard_map/pallas_call | solution.py:50
  352.5 23.5 %shard_map.344 = (f32[1024,512]{1,0:T(8,128)}, f32[2,512]{1,0:T(2,128)}, bf16[1024,512]{1,0:T(8,128)(2,1)}, bf16[1024,512]{1,0:T(8,128)(2,1)}, bf16[1024,512]{1,0:T(8,128)(2,1)}, /*index=5*/bf16[1024,512]{1,0:T(8,128)(2,1)}) custom-call(f32[1024,512]{1,0:T(8,128)} %get-tuple-element.121.refs_0_, f32[1024,512]{1,0:T(8,128)} %copy_bitcast_fusion.refs_0_.refs_1_, ...), custom_call_target="tpu_custom_call" | custom-call | tf_op jit(solution)/shard_map/pallas_call | solution.py:50
  400.3 18.5 %shard_map.345 = (f32[1024,512]{1,0:T(8,128)}, f32[2,512]{1,0:T(2,128)}, f32[2,512]{1,0:T(2,128)}, bf16[1024,512]{1,0:T(8,128)(2,1)}, bf16[2048,1024]{1,0:T(8,128)(2,1)}, /*index=5*/bf16[2048,1024]{1,0:T(8,128)(2,1)}) custom-call(f32[1024,512]{1,0:T(8,128)} %get-tuple-element.141.after_ref, f32[1024,512]{1,0:T(8,128)} %get-tuple-element.142.y_ref, ...), custom_call_target="tpu_custom_call" | custom-call | tf_op jit(solution)/shard_map/pallas_call | solution.py:50
  418.8 32.2 %shard_map.346 = (f32[1024,512]{1,0:T(8,128)}, f32[2,512]{1,0:T(2,128)}, bf16[1024,512]{1,0:T(8,128)(2,1)}, bf16[1024,512]{1,0:T(8,128)(2,1)}, bf16[1024,512]{1,0:T(8,128)(2,1)}, /*index=5*/bf16[1024,512]{1,0:T(8,128)(2,1)}) custom-call(f32[1024,512]{1,0:T(8,128)} %get-tuple-element.144.refs_0_, f32[1024,512]{1,0:T(8,128)} %get-tuple-element.95.refs_0_.refs_1_, ...), custom_call_target="tpu_custom_call" | custom-call | tf_op jit(solution)/shard_map/pallas_call | solution.py:50
  457.0 7.4 %copy.75 = bf16[4736,512]{0,1:T(8,128)(2,1)} copy(bf16[4736,512]{1,0:T(8,128)(2,1)} %convolution_convert_fusion) | data formatting | bytes 9699328
  472.8 4.1 copy.68
  482.6 50.2 %shard_map.347 = (bf16[8,3,64,512]{3,2,1,0:T(8,128)(2,1)}, bf16[4,2048,128]{2,1,0:T(8,128)(2,1)}) custom-call(bf16[4,3,64,512]{3,2,1,0:T(8,128)(2,1)} %pad_maximum_fusion.4.x_ref, bf16[4,2048,128]{2,1,0:T(8,128)(2,1)} %bitcast.234), custom_call_target="tpu_custom_call" | custom-call | tf_op jit(solution)/shard_map/pallas_call | solution.py:530
  536.1 6.1 bitcast_select_fusion.1
  542.2 12.1 %fusion = f32[2368,256]{1,0:T(8,128)} fusion(s32[8192]{0:T(1024)S(1)} %add_select_fusion.1, s32[2368]{0:T(1024)S(1)} %copy-done.57, bf16[8192,128]{1,0:T(8,128)(2,1)S(1)} %get-tuple-element.190, bf16[8192,128]{1,0:T(8,128)(2,1)S(1)} %get-tuple-element.189), kind=kOutput, calls=%fused_computation.1 | convolution fusion | flops 9959899136 | bytes 6661376 | tf_op jit(solution)/shard_map/dot_general | solution.py:34
  574.3 22.3 %shard_map.348 = (f32[512,512]{1,0:T(8,128)}, f32[8,128]{1,0:T(8,128)}) custom-call(f32[512,512]{1,0:T(8,128)} %fusion.44.x_ref, f32[8,128]{1,0:T(8,128)} %broadcast_in_dim.96.few_ref), custom_call_target="tpu_custom_call" | custom-call | tf_op jit(solution)/shard_map/pallas_call | solution.py:530
  600.9 5.5 fusion.39
  612.5 29.0 %shard_map.349 = f32[512,512]{1,0:T(8,128)} custom-call(f32[512,512]{1,0:T(8,128)} %bitcast_add_fusion.stat_ref, f32[512,512]{1,0:T(8,128)} %dynamic-slice_bitcast_fusion.basis_ref), custom_call_target="tpu_custom_call" | custom-call | tf_op jit(solution)/shard_map/pallas_call | solution.py:50
  643.3 11.6 %multiply_add_fusion.1 = (f32[4,512,512]{2,1,0:T(8,128)}, f32[4,512,512]{2,1,0:T(8,128)}) fusion(f32[4,512,512]{2,1,0:T(8,128)} %param.31, f32[4,512,512]{2,1,0:T(8,128)} %param.32, f32[4,512,512]{2,1,0:T(8,128)} %fusion.39, f32[4,512,512]{2,1,0:T(8,128)} %param.33, bf16[2,512,512]{2,1,0:T(8,128)(2,1)S(1)} %bitcast.231, ...), kind=kOutput, calls=%fused_computation.36 | convolution fusion | flops 1088421888 | bytes 27262980 | tf_op jit(solution)/shard_map/mfd,mde->mfe/dot_general | solution.py:976
  655.0 13.2 %multiply_subtract_fusion = f32[4,512,512]{2,1,0:T(8,128)} fusion(f32[4,512,512]{2,1,0:T(8,128)S(1)} %copy-done.28, f32[4,512,512]{2,1,0:T(8,128)S(1)} %copy-done.2, f32[4,512,512]{2,1,0:T(8,128)} %get-tuple-element.188, f32[4,512,512]{2,1,0:T(8,128)} %get-tuple-element.187), kind=kOutput, calls=%fused_computation.29 | convolution fusion | flops 3229614080 | bytes 20971520 | tf_op jit(solution)/shard_map/mfe,mde->mfd/dot_general | solution.py:1201
  669.0 6.5 multiply_subtract_fusion.1
  675.5 6.2 multiply_subtract_fusion.2
  687.5 4.2 convert.13
  (306 shorter events, 143.1 us)
Async XLA Ops:
  8.0 172.2 %all-reduce.6.cloned.1.call-start = ((), (), s32[]{:S(2)}) async-start(), calls=%async_computation.3 | async-start | bytes 2097152 | tf_op jit(solution)/shard_map/psum | solution.py:1041
  9.4 16.1 %copy-start.3 = (f32[12,128,512]{2,1,0:T(8,128)S(1)}, f32[12,128,512]{2,1,0:T(8,128)}, u32[]{:S(2)}) copy-start(f32[12,128,512]{2,1,0:T(8,128)} %param.27) | copy-start | bytes 9437188
  19.6 14.1 %copy-start.56 = (s32[2368]{0:T(1024)}, s32[2368]{0:T(1024)S(1)}, u32[]{:S(2)}) copy-start(s32[2368]{0:T(1024)S(1)} %iota_add_fusion.1) | copy-start | bytes 28420
  26.8 73.9 %copy-start.17 = (bf16[4,128,512]{2,1,0:T(8,128)(2,1)}, bf16[4,128,512]{2,1,0:T(8,128)(2,1)S(1)}, u32[]{:S(2)}) copy-start(bf16[4,128,512]{2,1,0:T(8,128)(2,1)S(1)} %get-tuple-element.195) | copy-start | bytes 1572868
  26.8 73.9 %copy-start.19 = (bf16[4,128,512]{2,1,0:T(8,128)(2,1)}, bf16[4,128,512]{2,1,0:T(8,128)(2,1)S(1)}, u32[]{:S(2)}) copy-start(bf16[4,128,512]{2,1,0:T(8,128)(2,1)S(1)} %get-tuple-element.196) | copy-start | bytes 1572868
  99.7 164.8 %all-gather.7.cloned.1.call-start = ((), (), s32[]{:S(2)}) async-start(), calls=%async_computation.4 | async-start | bytes 6062080 | tf_op jit(solution)/shard_map/all_gather | solution.py:1047
  100.3 352.2 %reduce-scatter.12.cloned.1.call-start = ((), (), s32[]{:S(2)}) async-start(), calls=%async_computation.10 | async-start | bytes 1310720
  102.0 40.1 %collective-permute-start.2 = (bf16[1024,512]{1,0:T(8,128)(2,1)}, bf16[1024,512]{1,0:T(8,128)(2,1)S(1)}, u32[]{:S(2)}, u32[]{:S(2)}) collective-permute-start(bf16[1024,512]{1,0:T(8,128)(2,1)} %maximum_select_fusion), channel_id=1, source_target_pairs={{0,24},{8,16},{16,8},{24,0},{1,25},{9,17},{17,9},{25,1},{2,26},{10... | collective-permute-start | bytes 3145736 | tf_op jit(solution)/shard_map/ppermute | solution.py:149
  102.9 61.6 %collective-permute-start.1 = (bf16[1024,512]{1,0:T(8,128)(2,1)}, bf16[1024,512]{1,0:T(8,128)(2,1)S(1)}, u32[]{:S(2)}, u32[]{:S(2)}) collective-permute-start(bf16[1024,512]{1,0:T(8,128)(2,1)} %maximum_select_fusion), channel_id=1, source_target_pairs={{0,16},{8,24},{16,0},{24,8},{1,17},{9,25},{17,1},{25,9},{2,18},{10... | collective-permute-start | bytes 3145736 | tf_op jit(solution)/shard_map/ppermute | solution.py:149
  104.2 60.3 %collective-permute-start = (bf16[1024,512]{1,0:T(8,128)(2,1)}, bf16[1024,512]{1,0:T(8,128)(2,1)S(1)}, u32[]{:S(2)}, u32[]{:S(2)}) collective-permute-start(bf16[1024,512]{1,0:T(8,128)(2,1)} %maximum_select_fusion), channel_id=1, source_target_pairs={{0,8},{8,0},{16,24},{24,16},{1,9},{9,1},{17,25},{25,17},{2,10},{10... | collective-permute-start | bytes 3145736 | tf_op jit(solution)/shard_map/ppermute | solution.py:149
  138.3 124.0 %copy-start.43 = (pred[4,1,16,512]{3,2,1,0:T(8,128)(4,1)}, pred[4,1,16,512]{3,2,1,0:T(8,128)(4,1)S(1)}, u32[]{:S(2)}) copy-start(pred[4,1,16,512]{3,2,1,0:T(8,128)(4,1)S(1)} %iota_compare_fusion.3) | copy-start | bytes 98308
  142.1 34.8 %copy-start.6 = (bf16[1024,512]{1,0:T(8,128)(2,1)}, bf16[1024,512]{1,0:T(8,128)(2,1)S(1)}, u32[]{:S(2)}) copy-start(bf16[1024,512]{1,0:T(8,128)(2,1)S(1)} %collective-permute-done.2.refs_7_.refs_8_.refs_3_) | copy-start | bytes 3145732
  164.5 35.4 %collective-permute-start.3 = (bf16[1024,512]{1,0:T(8,128)(2,1)S(1)}, bf16[1024,512]{1,0:T(8,128)(2,1)}, u32[]{:S(2)}, u32[]{:S(2)}) collective-permute-start(bf16[1024,512]{1,0:T(8,128)(2,1)S(1)} %collective-permute-done.refs_5_.refs_6_.refs_1_), channel_id=1, source_target_pairs={{0,1},{1,0},{2,3},{3,2},{4,5},{5,4},{6,7},{7,6},{8,9},{9,8},{10,11... | collective-permute-start | bytes 3145736 | tf_op jit(solution)/shard_map/ppermute | solution.py:149
  164.6 35.3 %collective-permute-start.4 = (bf16[1024,512]{1,0:T(8,128)(2,1)S(1)}, bf16[1024,512]{1,0:T(8,128)(2,1)}, u32[]{:S(2)}, u32[]{:S(2)}) collective-permute-start(bf16[1024,512]{1,0:T(8,128)(2,1)S(1)} %collective-permute-done.1.refs_6_.refs_7_.refs_2_), channel_id=1, source_target_pairs={{0,1},{1,0},{2,3},{3,2},{4,5},{5,4},{6,7},{7,6},{8,9},{9,8},{10,11... | collective-permute-start | bytes 3145736 | tf_op jit(solution)/shard_map/ppermute | solution.py:149
  165.1 34.8 %collective-permute-start.5 = (bf16[1024,512]{1,0:T(8,128)(2,1)S(1)}, bf16[1024,512]{1,0:T(8,128)(2,1)}, u32[]{:S(2)}, u32[]{:S(2)}) collective-permute-start(bf16[1024,512]{1,0:T(8,128)(2,1)S(1)} %collective-permute-done.2.refs_7_.refs_8_.refs_3_), channel_id=1, source_target_pairs={{0,1},{1,0},{2,3},{3,2},{4,5},{5,4},{6,7},{7,6},{8,9},{9,8},{10,11... | collective-permute-start | bytes 3145736 | tf_op jit(solution)/shard_map/ppermute | solution.py:149
  180.3 16.7 %copy-start.32 = (f32[4,1024,128]{2,1,0:T(8,128)S(1)}, f32[4,1024,128]{2,1,0:T(8,128)}, u32[]{:S(2)}) copy-start(f32[4,1024,128]{2,1,0:T(8,128)} %constant.238) | copy-start | bytes 6291460
  245.1 17.2 %copy-start.42 = (bf16[1024,512]{1,0:T(8,128)(2,1)S(1)}, bf16[1024,512]{1,0:T(8,128)(2,1)}, u32[]{:S(2)}) copy-start(bf16[1024,512]{1,0:T(8,128)(2,1)} %get-tuple-element.105) | copy-start | bytes 3145732
  305.1 19.6 %copy-start.26 = (bf16[1024,512]{1,0:T(8,128)(2,1)S(1)}, bf16[1024,512]{1,0:T(8,128)(2,1)}, u32[]{:S(2)}) copy-start(bf16[1024,512]{1,0:T(8,128)(2,1)} %get-tuple-element.112.a_ref) | copy-start | bytes 3145732
  400.0 157.6 %reduce-scatter.8.cloned.1.call-start = ((), (), s32[]{:S(2)}) async-start(), calls=%async_computation.6 | async-start | bytes 40960 | tf_op jit(solution)/shard_map/reduce_scatter | solution.py:1157
  418.7 33.0 %copy-start.66 = (f32[2,512]{1,0:T(2,128)S(1)}, f32[2,512]{1,0:T(2,128)}, u32[]{:S(2)}) copy-start(f32[2,512]{1,0:T(2,128)} %get-tuple-element.163) | copy-start | bytes 12292
  418.7 33.0 %copy-start.65 = (f32[2,512]{1,0:T(2,128)S(1)}, f32[2,512]{1,0:T(2,128)}, u32[]{:S(2)}) copy-start(f32[2,512]{1,0:T(2,128)} %get-tuple-element.164) | copy-start | bytes 12292
  418.7 33.0 %copy-start.64 = (f32[2,512]{1,0:T(2,128)S(1)}, f32[2,512]{1,0:T(2,128)}, u32[]{:S(2)}) copy-start(f32[2,512]{1,0:T(2,128)} %get-tuple-element.165) | copy-start | bytes 12292
  418.7 33.0 %copy-start.63 = (f32[2,512]{1,0:T(2,128)S(1)}, f32[2,512]{1,0:T(2,128)}, u32[]{:S(2)}) copy-start(f32[2,512]{1,0:T(2,128)} %get-tuple-element.166) | copy-start | bytes 12292
  418.7 33.0 %copy-start.62 = (f32[2,512]{1,0:T(2,128)S(1)}, f32[2,512]{1,0:T(2,128)}, u32[]{:S(2)}) copy-start(f32[2,512]{1,0:T(2,128)} %get-tuple-element.167) | copy-start | bytes 12292
  418.8 33.0 %copy-start.61 = (f32[2,512]{1,0:T(2,128)S(1)}, f32[2,512]{1,0:T(2,128)}, u32[]{:S(2)}) copy-start(f32[2,512]{1,0:T(2,128)} %get-tuple-element.168) | copy-start | bytes 12292
  452.5 106.4 %all-gather.9.cloned.1.call-start = ((), (), s32[]{:S(2)}) async-start(), calls=%async_computation.5 | async-start | bytes 2359296 | tf_op jit(solution)/shard_map/all_gather | solution.py:1126
  453.2 114.5 %reduce-scatter.10.cloned.1.call-start = ((), (), s32[]{:S(2)}) async-start(), calls=%async_computation.9 | async-start | bytes 6062080
  464.4 217.2 %all-gather.13.cloned.1.call-start = ((), (), s32[]{:S(2)}) async-start(), calls=%async_computation.8 | async-start | bytes 2359296 | tf_op jit(solution)/shard_map/all_gather | solution.py:1181
  536.1 26.6 %copy-start.11 = (bf16[4,8,16,512]{3,2,1,0:T(8,128)(2,1)}, bf16[4,8,16,512]{3,2,1,0:T(8,128)(2,1)S(1)}, u32[]{:S(2)}) copy-start(bf16[4,8,16,512]{3,2,1,0:T(8,128)(2,1)S(1)} %copy.71) | copy-start | bytes 1572868
  598.4 89.1 %all-gather.11.cloned.1.call-start = ((), (), s32[]{:S(2)}) async-start(), calls=%async_computation.7 | async-start | bytes 2359296 | tf_op jit(solution)/shard_map/all_gather | solution.py:1181
  655.0 13.9 %copy-start.4 = (f32[12,128,512]{2,1,0:T(8,128)S(1)}, f32[12,128,512]{2,1,0:T(8,128)}, u32[]{:S(2)}) copy-start(f32[12,128,512]{2,1,0:T(8,128)} %param.27) | copy-start | bytes 9437188
  655.0 13.9 %copy-start.12 = (bf16[4,8,16,512]{3,2,1,0:T(8,128)(2,1)S(1)}, bf16[4,8,16,512]{3,2,1,0:T(8,128)(2,1)}, u32[]{:S(2)}) copy-start(bf16[4,8,16,512]{3,2,1,0:T(8,128)(2,1)} %copy-done.11) | copy-start | bytes 1572868
  (49 other events, 362.3 us)
Sparse Core Ops, SparseCore 0:
  99.8 59.8 all-reduce.5
  455.0 29.4 all-gather.8
  598.5 27.8 all-gather.12
  643.4 27.8 all-gather.10
Sparse Core Ops, SparseCore 1:
  102.6 92.8 all-gather.6
  400.1 28.0 reduce-scatter.11
  452.6 22.8 reduce-scatter.7
  478.8 77.6 reduce-scatter.9

commit v5 on v4

--- a/solution.py
+++ b/solution.py
@@ -46,15 +46,25 @@
     )
 
 
-def call(kernel, outs, *args, scratch=(), smem_args=0):
+def cost_of(microseconds):
+    return pl.CostEstimate(flops=microseconds * 10**9, bytes_accessed=0, transcendentals=0)
+
+
+def call(kernel, outs, *args, scratch=(), smem_args=0, microseconds=5, before=()):
+    def body(*refs):
+        kernel(*refs[: len(args)], *refs[len(args) + len(before) :])
+
     return pl.pallas_call(
-        kernel,
+        body,
         out_shape=outs,
-        in_specs=[vmem] * (len(args) - smem_args) + [smem] * smem_args,
+        in_specs=[vmem] * (len(args) - smem_args)
+        + [smem] * smem_args
+        + [pl.BlockSpec(memory_space=pl.ANY)] * len(before),
         out_specs=jax.tree.map(lambda _: vmem, outs),
         scratch_shapes=list(scratch),
         compiler_params=pltpu.CompilerParams(vmem_limit_bytes=56 * 2**20),
-    )(*args)
+        cost_estimate=cost_of(microseconds),
+    )(*args, *before)
 
 
 def low(*shape):
@@ -88,26 +98,34 @@
     )
 
 
-def at_tile(index):
-    return pl.ds(pl.multiple_of(index * TILE, TILE), TILE)
-
-
-def tile_mask(segq_ref, segk_ref, qi, ki, causal):
-    allowed = segk_ref[at_tile(ki), :] == segq_ref[:, at_tile(qi)]
+def at_tile(index, size):
+    return pl.ds(pl.multiple_of(index * size, size), size)
+
+
+def tile_mask(segq_ref, segk_ref, qi, ki, tile_q, tile_k, causal):
+    seg_k = segk_ref[at_tile(ki, tile_k), :]
+    seg_k = jnp.concatenate([seg_k] * (tile_q // TILE), axis=1)
+    allowed = seg_k == segq_ref[:, at_tile(qi, tile_q)]
     if causal:
-        ahead = lax.broadcasted_iota(jnp.int32, (TILE, TILE), 0) - lax.broadcasted_iota(
-            jnp.int32, (TILE, TILE), 1
+        shape = (tile_k, tile_q)
+        ahead = lax.broadcasted_iota(jnp.int32, shape, 0) - lax.broadcasted_iota(
+            jnp.int32, shape, 1
         )
-        allowed = allowed & (ahead <= (qi - ki) * TILE)
+        allowed = allowed & (ahead <= qi * tile_q - ki * tile_k)
     return allowed
 
 
-def for_tiles(count, edge_ref, causal, step):
+def for_tiles(length, tile_q, tile_k, edge_ref, causal, step):
+    count_q, count_k = length // tile_q, length // tile_k
+    per_q, per_k = tile_q // TILE, tile_k // TILE
+
     def one(pair, carry):
-        qi, ki = pair // count, lax.rem(pair, count)
-        live = (edge_ref[0, qi] <= edge_ref[3, ki]) & (edge_ref[2, ki] <= edge_ref[1, qi])
+        qi, ki = pair // count_k, lax.rem(pair, count_k)
+        live = (edge_ref[0, qi * per_q] <= edge_ref[3, (ki + 1) * per_k - 1]) & (
+            edge_ref[2, ki * per_k] <= edge_ref[1, (qi + 1) * per_q - 1]
+        )
         if causal:
-            live = live & (ki <= qi)
+            live = live & (ki * tile_k < (qi + 1) * tile_q)
 
         @pl.when(live)
         def _():
@@ -115,12 +133,19 @@
 
         return carry
 
-    lax.fori_loop(0, count * count, one, 0)
+    lax.fori_loop(0, count_q * count_k, one, 0)
 
 
 def tile_edges(seg_q, seg_k):
     last = TILE - 1
     return jnp.stack([seg_q[::TILE], seg_q[last::TILE], seg_k[::TILE], seg_k[last::TILE]])
+
+
+def share_selector(rows, owners, shares, share, count):
+    size = rows // (owners * shares)
+    index = jnp.arange(count // shares)
+    picked = index // size * (rows // owners) + share * size + index % size
+    return (picked[:, None] == jnp.arange(count)[None, :]).astype(jnp.bfloat16)
 
 
 def lay_weights(w_ref, piece_refs, part, first):
@@ -155,7 +180,7 @@
     attn, ffn = attn.astype(jnp.bfloat16), ffn.astype(jnp.bfloat16)
     if owners != 4:
         attn, ffn = (lax.all_gather(part, "dp", axis=1, tiled=True) for part in (attn, ffn))
-        return ((attn[:4],), 0, 0), ((attn[4:],), 0, 0), ((ffn,), 0, 0), ffn[0, 0]
+        return ((attn[:4],), 0, 0), ((attn[4:],), 0, 0), ((ffn,), 0, 0), ffn[0, 0, 0]
     halves = [
         jnp.concatenate([attn[4 * k : 4 * k + 4].reshape(-1, width), ffn[k]]) for k in range(2)
     ]
@@ -168,7 +193,7 @@
     swapped = [flip_sites(part, "vocab", 1) for part in got]
     pieces = (own, *got, *swapped)
     rows = 4 * attn.shape[1]
-    return (pieces, 0, 0), (pieces, 1, 0), (pieces, None, rows), swapped[-1][0]
+    return (pieces, 0, 0), (pieces, 1, 0), (pieces, None, rows), swapped[-1][0, 0]
 
 
 def attn_forward_kernel(causal, cross, pieces, part, first, *refs):
@@ -198,8 +223,8 @@
     bands = [slice(h * head_size, (h + 1) * head_size) for h in range(HEADS)]
 
     def step(qi, ki):
-        q_at, k_at = at_tile(qi), at_tile(ki)
-        allowed = tile_mask(segq_ref, segk_ref, qi, ki, causal)
+        q_at, k_at = at_tile(qi, 256), at_tile(ki, 256)
+        allowed = tile_mask(segq_ref, segk_ref, qi, ki, 256, 256, causal)
         scores = [dot_dims(kt_ref[band, k_at], qt_ref[band, q_at], 0, 0) * scale for band in bands]
         scores = [jnp.where(allowed, part, masked) for part in scores]
         top = top_ref[:, q_at]
@@ -222,7 +247,7 @@
             [acc[bands[h]] * fade[h : h + 1] + mixed[h] for h in range(HEADS)], axis=0
         )
 
-    for_tiles(length // TILE, edge_ref, causal, step)
+    for_tiles(length, 256, 256, edge_ref, causal, step)
     lse_ref[...] = top_ref[...] + jnp.log2(sum_ref[...])
     for h in range(HEADS):
         ot_ref[bands[h], :] = (acc_ref[bands[h], :] / sum_ref[h : h + 1, :]).astype(jnp.bfloat16)
@@ -250,18 +275,18 @@
             pltpu.VMEM((width, length), jnp.float32),
         ],
         smem_args=1,
+        microseconds=20,
     )
     whole = stored.pop() if len(weights) > 1 else weights[0]
-    return out, (x, ln, whole, segs, edges, causal, cross, normed, stored)
-
-
-def attn_backward_kernel(causal, cross, *refs):
-    (g_ref, x_ref, ln_ref, w_ref, segq_ref, segk_ref, qt_ref, kt_ref, vt_ref, ot_ref, lse_ref) = refs[:11]
-    refs = list(refs[11:])
-    edge_ref, out_ref, ln_grad_ref, low_ref, gq_ref, gk_ref, gv_ref = refs[:7]
-    refs = refs[7:]
-    key_grad_ref = refs.pop(0) if cross else None
-    got_ref, delta_ref, gqt_ref, gkt_ref, gvt_ref = refs
+    return out, (x, ln, whole, segs, edges, causal, key_in, normed, stored)
+
+
+def attn_backward_kernel(causal, cross, row_scale, *refs):
+    g_ref, x_ref, ln_ref, w_ref, pick_ref, segq_ref, segk_ref, a_ref = refs[:8]
+    refs = list(refs[8:])
+    key_ref = refs.pop(0) if cross else a_ref
+    qt_ref, kt_ref, vt_ref, ot_ref, lse_ref, edge_ref, out_ref, ln_grad_ref, block_ref, extra_ref = refs[:10]
+    low_ref, gq_ref, gk_ref, gv_ref, got_ref, delta_ref, gqt_ref, gkt_ref, gvt_ref = refs[10:]
     length, width = x_ref.shape
     head_size = width // HEADS
     low_ref[...] = g_ref[...].astype(jnp.bfloat16)
@@ -279,8 +304,8 @@
     back = 1.0 / math.sqrt(head_size)
 
     def step(qi, ki):
-        q_at, k_at = at_tile(qi), at_tile(ki)
-        allowed = tile_mask(segq_ref, segk_ref, qi, ki, causal)
+        q_at, k_at = at_tile(qi, 256), at_tile(ki, TILE)
+        allowed = tile_mask(segq_ref, segk_ref, qi, ki, 256, TILE, causal)
         scores = [dot_dims(kt_ref[band, k_at], qt_ref[band, q_at], 0, 0) for band in bands]
         grads = [dot_dims(vt_ref[band, k_at], got_ref[band, q_at], 0, 0) for band in bands]
         parts = [
@@ -298,40 +323,62 @@
         ):
             ref[:, place] += jnp.concatenate(terms, axis=0)
 
-    for_tiles(length // TILE, edge_ref, causal, step)
+    for_tiles(length, 256, TILE, edge_ref, causal, step)
     gq_ref[...] = (gqt_ref[...] * back).astype(jnp.bfloat16).T
     gk_ref[...] = (gkt_ref[...] * back).astype(jnp.bfloat16).T
     gv_ref[...] = gvt_ref[...].astype(jnp.bfloat16).T
     from_query = dot_dims(gq_ref[...], w_ref[0], 1, 1)
     from_keys = dot_dims(gk_ref[...], w_ref[1], 1, 1) + dot_dims(gv_ref[...], w_ref[2], 1, 1)
     if cross:
-        key_grad_ref[...] = from_keys
+        extra_ref[...] = from_keys
     else:
         from_query = from_query + from_keys
-    out_ref[...] = g_ref[...] + norm_backward(from_query, x_ref[...], ln_ref, ln_grad_ref)
-
-
-def attn_backward(grad, stored):
-    x, ln, weights, segs, edges, causal, cross, _, kept = stored
+    total = g_ref[...] + norm_backward(from_query, x_ref[...], ln_ref, ln_grad_ref)
+    out_ref[...] = total
+    owners = block_ref.shape[0]
+    if not cross:
+        columns = width // owners
+        for owner in range(owners):
+            band = slice(owner * columns, (owner + 1) * columns)
+            extra_ref[owner] = (total[:, band] * row_scale).astype(jnp.bfloat16)
+    own_a = dot_dims(pick_ref[...], a_ref[...], 1, 1).astype(jnp.bfloat16)
+    own_key = dot_dims(pick_ref[...], key_ref[...], 1, 1).astype(jnp.bfloat16) if cross else own_a
+    own_o = dot_dims(pick_ref[...], ot_ref[...], 1, 0).astype(jnp.bfloat16)
+    size = own_a.shape[0] // owners
+    products = ((own_a, gq_ref), (own_key, gk_ref), (own_key, gv_ref), (own_o, low_ref))
+    for m, (rows, right_ref) in enumerate(products):
+        product = dot_dims(rows, right_ref[...], 1, 0).astype(jnp.bfloat16)
+        for owner in range(owners):
+            block_ref[owner, m * size : (m + 1) * size, :] = product[owner * size : (owner + 1) * size]
+
+
+def attn_backward(grad, stored, picks, owners, row_scale, before=()):
+    x, ln, weights, segs, edges, causal, key_in, normed, kept = stored
     length, width = x.shape
-    outs = (full(length, width), full(2, width)) + (low(length, width),) * 4
-    if cross:
-        outs = outs + (full(length, width),)
-    out, ln_grad, *rest = call(
-        partial(attn_backward_kernel, causal, cross),
+    cross = key_in is not None
+    extra = full(length, width) if cross else low(owners, length, width // owners)
+    outs = (full(length, width), full(2, width), low(owners, 4 * picks.shape[0] // owners, width), extra)
+    keys = (key_in,) if cross else ()
+    return call(
+        partial(attn_backward_kernel, causal, cross, row_scale),
         outs,
         grad,
         x,
         ln,
         weights,
+        picks,
         *segs,
+        normed,
+        *keys,
         *kept,
         edges,
-        scratch=[pltpu.VMEM((width, length), jnp.bfloat16), pltpu.VMEM((HEADS, length), jnp.float32)]
+        scratch=[pltpu.VMEM((length, width), jnp.bfloat16)] * 4
+        + [pltpu.VMEM((width, length), jnp.bfloat16), pltpu.VMEM((HEADS, length), jnp.float32)]
         + [pltpu.VMEM((width, length), jnp.float32)] * 3,
         smem_args=1,
-    )
-    return out, ln_grad, rest[:4], rest[4] if cross else None
+        microseconds=25,
+        before=before,
+    )
 
 
 def gelu_parts(hidden):
@@ -371,39 +418,51 @@
     if len(weights) > 1:
         outs = outs + (low(2, 4 * (weights[0].shape[0] // 2 - first), width),)
     out, normed, after, *whole = call(
-        partial(ffn_forward_kernel, 512, len(weights), first), outs, x, ln, ln_next, *weights
+        partial(ffn_forward_kernel, 512, len(weights), first),
+        outs,
+        x,
+        ln,
+        ln_next,
+        *weights,
+        microseconds=12,
     )
     return out, after, (x, ln, whole[0] if whole else weights[0], normed, out, ln_next)
 
 
 def ffn_backward_kernel(
-    chunk, after_ref, y_ref, next_ref, x_ref, ln_ref, a_ref, w_ref,
-    out_ref, next_grad_ref, ln_grad_ref, low_ref, ut_ref, ht_ref, g_ref,
+    chunk, after_ref, y_ref, next_ref, x_ref, ln_ref, a_ref, w_ref, pick_ref,
+    out_ref, next_grad_ref, ln_grad_ref, in_ref, back_ref, low_ref, g_ref,
 ):
     w_in_ref, w_out_ref = w_ref.at[0], w_ref.at[1]
     g_ref[...] = norm_backward(after_ref[...], y_ref[...], next_ref, next_grad_ref)
     low_ref[...] = g_ref[...].astype(jnp.bfloat16)
     total = jnp.zeros(g_ref.shape, jnp.float32)
-    for start in range(0, w_in_ref.shape[0], chunk):
-        part = slice(start, start + chunk)
+    owners, size = in_ref.shape[:2]
+    blocks = pick_ref.shape[0] // size
+    for index in range(w_in_ref.shape[0] // chunk):
+        part = slice(index * chunk, (index + 1) * chunk)
         hidden = dot_dims(a_ref[...], w_in_ref[part, :], 1, 1)
         value, slope = gelu_parts(hidden)
-        ut_ref[part, :] = value.astype(jnp.bfloat16).T
         grad = (dot_dims(low_ref[...], w_out_ref[part, :], 1, 1) * slope).astype(jnp.bfloat16)
-        ht_ref[part, :] = grad.T
         total = total + dot_dims(grad, w_in_ref[part, :], 1, 0)
+        pairs = ((in_ref, grad, a_ref), (back_ref, value.astype(jnp.bfloat16), low_ref))
+        for ref, left, right_ref in pairs:
+            rows = dot_dims(pick_ref[...], left, 1, 1).astype(jnp.bfloat16)
+            product = dot_dims(rows, right_ref[...], 1, 0).astype(jnp.bfloat16)
+            for block in range(blocks):
+                ref[index * blocks + block] = product[block * size : (block + 1) * size]
     out_ref[...] = g_ref[...] + norm_backward(total, x_ref[...], ln_ref, ln_grad_ref)
 
 
-def ffn_backward(grad_after, stored):
+def ffn_backward(grad_after, stored, picks, owners, before=()):
     x, ln, weights, normed, out, ln_next = stored
     length, width = x.shape
-    hidden = weights.shape[1]
-    outs = (full(length, width), full(2, width), full(2, width))
-    outs = outs + (low(length, width), low(hidden, length), low(hidden, length))
-    out, next_grad, ln_grad, *rest = call(
-        partial(ffn_backward_kernel, 512),
-        outs,
+    chunk = picks.shape[1]
+    size = picks.shape[0] * weights.shape[1] // chunk // owners
+    block = low(owners, size, width)
+    return call(
+        partial(ffn_backward_kernel, chunk),
+        (full(length, width), full(2, width), full(2, width), block, block),
         grad_after,
         out,
         ln_next,
@@ -411,9 +470,49 @@
         ln,
         normed,
         weights,
-        scratch=[pltpu.VMEM((length, width), jnp.float32)],
-    )
-    return out, next_grad, ln_grad, rest
+        picks,
+        scratch=[
+            pltpu.VMEM((length, width), jnp.bfloat16),
+            pltpu.VMEM((length, width), jnp.float32),
+        ],
+        microseconds=17,
+        before=before,
+    )
+
+
+def update_kernel(factor_ref, g_ref, basis_ref, w_ref, m_ref, v_ref, new_w_ref, new_m_ref, new_v_ref):
+    high = basis_ref[0].astype(jnp.bfloat16)
+    rest = (basis_ref[0] - high.astype(jnp.float32)).astype(jnp.bfloat16)
+    grad = g_ref[0]
+    rotated = (dot_dims(grad, high, 1, 0) + dot_dims(grad, rest, 1, 0)) * factor_ref[0]
+    moment = beta_one * m_ref[0] + (1.0 - beta_one) * rotated
+    second = beta_two * v_ref[0] + (1.0 - beta_two) * rotated * rotated
+    new_m_ref[0] = moment
+    new_v_ref[0] = second
+    step = adam_direction(moment, second)
+    step_high = step.astype(jnp.bfloat16)
+    step_rest = (step - step_high.astype(jnp.float32)).astype(jnp.bfloat16)
+    back = (
+        dot_dims(step_high, high, 1, 1)
+        + dot_dims(step_high, rest, 1, 1)
+        + dot_dims(step_rest, high, 1, 1)
+    )
+    new_w_ref[0] = w_ref[0] - rate_matrix * (back + decay_rate * w_ref[0])
+
+
+def update_rotated(factor, grads, bases, weights, moments, seconds):
+    count, rows, width = weights.shape
+    block = pl.BlockSpec((1, rows, width), lambda k: (k, 0, 0))
+    square = pl.BlockSpec((1, width, width), lambda k: (k, 0, 0))
+    return pl.pallas_call(
+        update_kernel,
+        grid=(count,),
+        out_shape=(full(count, rows, width),) * 3,
+        in_specs=[smem, block, square, block, block, block],
+        out_specs=(block,) * 3,
+        compiler_params=pltpu.CompilerParams(vmem_limit_bytes=56 * 2**20),
+        cost_estimate=cost_of(10),
+    )(factor.reshape(1), grads, bases, weights, moments, seconds)
 
 
 def small_factor(block):
@@ -492,6 +591,7 @@
         statistic,
         basis,
         scratch=[pltpu.VMEM(shape, jnp.float32), pltpu.VMEM(shape, jnp.float32)],
+        microseconds=29,
     )
 
 
@@ -526,17 +626,21 @@
     return [pltpu.SemaphoreType.DMA((count,)), pltpu.SemaphoreType.DMA((count,))]
 
 
-def talk(kernel, outs, collective_id, *args, scratch=()):
+def talk(kernel, outs, collective_id, *args, scratch=(), microseconds=15, before=()):
+    def body(*refs):
+        kernel(*refs[: len(args)], *refs[len(args) + len(before) :])
+
     return pl.pallas_call(
-        kernel,
+        body,
         out_shape=outs,
-        in_specs=[vmem] * len(args),
+        in_specs=[vmem] * len(args) + [pl.BlockSpec(memory_space=pl.ANY)] * len(before),
         out_specs=jax.tree.map(lambda _: vmem, outs),
         scratch_shapes=list(scratch),
         compiler_params=pltpu.CompilerParams(
             collective_id=collective_id, has_side_effects=True, vmem_limit_bytes=56 * 2**20
         ),
-    )(*args)
+        cost_estimate=cost_of(microseconds),
+    )(*args, *before)
 
 
 def gather_kernel(axis, *refs):
@@ -691,15 +795,15 @@
     ]
 
 
-def gradient_kernel(
-    x_ref, rows_ref, out_ref, swapped_ref, parts_ref, s0, r0, s1, r1, s2, r2, s3, r3, s4, r4
-):
+def gradient_kernel(chunks, count, *refs):
+    x_refs, refs = refs[:chunks], refs[chunks:]
+    rows_refs, (out_ref, *refs) = refs[:count], refs[count:]
+    swapped_refs, (parts_ref, s0, r0, s1, r1, s2, r2, s3, r3, s4, r4) = refs[:count], refs[count:]
     owners = peers_of("dp")
     here, me = lax.axis_index("vocab"), lax.axis_index("dp")
     near = flip(here, 1)
     size = lax.axis_size("vocab")
     steps = range(2, size, 2)
-    chunks = x_ref.shape[1]
     greet(
         *[("dp", to) for _, to, _ in owners],
         *[("vocab", lax.rem(here + step, size)) for step in steps],
@@ -707,30 +811,44 @@
     )
 
     def spread(c, origin, sems, slot, to):
-        place = out_ref.at[origin, c]
+        place = out_ref.at[c, origin]
         return push(place, place, sems, slot, "vocab", to)
 
     arriving = [
         [
-            push(x_ref.at[to, c], parts_ref.at[me, c], (s0, r0), (step - 1) * chunks + c, "dp", to)
+            push(x_refs[c].at[to], parts_ref.at[c, me], (s0, r0), (step - 1) * chunks + c, "dp", to)
             for step, to, _ in owners
         ]
         for c in range(chunks)
     ]
-    half_rows = rows_ref.shape[1] // 2
-    half = pl.ds(pl.multiple_of(lax.rem(here, 2) * half_rows, half_rows), half_rows)
+
+    def half_of(ref):
+        rows = ref.shape[1] // 2
+        return pl.ds(pl.multiple_of(lax.rem(here, 2) * rows, rows), rows)
+
     swaps = [
-        push(rows_ref.at[to, half], swapped_ref.at[me, half], (s3, r3), step - 1, "dp", to)
-        for step, to, _ in owners
-    ]
-    swapped_ref[me] = rows_ref[me]
+        [
+            push(
+                rows_ref.at[to, half_of(rows_ref)],
+                swapped_ref.at[me, half_of(rows_ref)],
+                (s3, r3),
+                k * len(owners) + step - 1,
+                "dp",
+                to,
+            )
+            for step, to, _ in owners
+        ]
+        for k, (rows_ref, swapped_ref) in enumerate(zip(rows_refs, swapped_refs))
+    ]
+    for rows_ref, swapped_ref in zip(rows_refs, swapped_refs):
+        swapped_ref[me] = rows_ref[me]
     far, close = [], []
     for c in range(chunks):
-        parts_ref[me, c] = x_ref[me, c]
+        parts_ref[c, me] = x_refs[c][me]
         for copy in arriving[c]:
             copy.wait()
-        total = jnp.sum(parts_ref[:, c].astype(jnp.float32), axis=0)
-        out_ref[here, c] = total.astype(out_ref.dtype)
+        total = jnp.sum(parts_ref[c].astype(jnp.float32), axis=0)
+        out_ref[c, here] = total.astype(out_ref.dtype)
         far.append(
             [
                 spread(c, here, (s1, r1), k * chunks + c, lax.rem(here + step, size))
@@ -743,33 +861,37 @@
             far[c][k].wait()
             origin = lax.rem(here + size - step, size)
             close.append(spread(c, origin, (s2, r2), (k + 1) * chunks + c, near))
-    for copy, (step, _, origin) in zip(swaps, owners):
-        copy.wait()
-        place = swapped_ref.at[origin, half]
-        close.append(push(place, place, (s4, r4), step - 1, "vocab", near))
+    for k, swapped_ref in enumerate(swapped_refs):
+        for copy, (step, _, origin) in zip(swaps[k], owners):
+            copy.wait()
+            place = swapped_ref.at[origin, half_of(swapped_ref)]
+            close.append(push(place, place, (s4, r4), k * len(owners) + step - 1, "vocab", near))
     for copy in close:
         copy.wait()
 
 
-def share_gradients(x, rows, collective_id):
+def share_gradients(blocks, rows, collective_id, before):
     owners, replicas = lax.axis_size("dp"), lax.axis_size("vocab")
-    chunks = x.shape[1]
+    chunks = len(blocks)
     others = (replicas // 2 - 1) * chunks
+    shape, kind = blocks[0].shape, blocks[0].dtype
     return talk(
-        gradient_kernel,
+        partial(gradient_kernel, chunks, len(rows)),
         (
-            jax.ShapeDtypeStruct((replicas, *x.shape[1:]), x.dtype),
-            jax.ShapeDtypeStruct(rows.shape, rows.dtype),
+            jax.ShapeDtypeStruct((chunks, replicas, *shape[1:]), kind),
+            *[jax.ShapeDtypeStruct(part.shape, part.dtype) for part in rows],
         ),
         collective_id,
-        x,
-        rows,
-        scratch=[pltpu.VMEM(x.shape, x.dtype)]
+        *blocks,
+        *rows,
+        scratch=[pltpu.VMEM((chunks, *shape), kind)]
         + sem_pair((owners - 1) * chunks)
         + sem_pair(others)
         + sem_pair(others + chunks)
-        + sem_pair(owners - 1)
-        + sem_pair(owners - 1),
+        + sem_pair(len(rows) * (owners - 1))
+        + sem_pair(len(rows) * (owners - 1)),
+        microseconds=40,
+        before=before,
     )
 
 
@@ -925,6 +1047,7 @@
         + sem_pair(pairs)
         + sem_pair(2 * owners - 2)
         + sem_pair(2 * owners - 2),
+        microseconds=50,
     )
 
 
@@ -968,20 +1091,8 @@
     )
 
 
-def rotate(values, basis):
-    high = basis.astype(jnp.bfloat16)
-    rest = (basis - high.astype(jnp.float32)).astype(jnp.bfloat16)
-
-    def product(part):
-        return jnp.einsum("mfd,mde->mfe", values, part, preferred_element_type=jnp.float32)
-
-    return product(high) + product(rest)
-
-
-def share_rows(array, owners, shares, share):
-    rows, columns = array.shape
-    blocks = array.reshape(owners, shares, rows // (owners * shares), columns)
-    return lax.dynamic_index_in_dim(blocks, share, 1, keepdims=False)
+def after(array, number):
+    return array + jnp.where(jnp.isnan(number), 1, 0).astype(array.dtype)
 
 
 def body(
@@ -1019,13 +1130,19 @@
     pick_rows, labels = (pick_pos[0], pick_label[0])
     length = source.shape[0]
     embed_scale = math.sqrt(width)
-    halves = replica * (vocab_count // 2) + jnp.arange(vocab_count // 2)
-    paired = own_table.reshape(vocab_count // 2, -1)
+    half = vocab_count // 2
+    halves = jnp.arange(half)
+    paired = jnp.concatenate([own_table[:half], own_table[half:]], axis=1)
+
+    def paired_places(ids):
+        place = ids - replica * vocab_count
+        inside = (place >= 0) & (place < vocab_count)
+        return jnp.where(inside, place % half, -1), place < half
 
     def look_up(ids):
-        wide = lax.dot_general(one_hot(ids // 2, halves), paired, (((1,), (0,)), ((), ())))
-        left, right = jnp.split(wide, 2, axis=1)
-        return jnp.where((ids % 2 == 0)[:, None], left, right)
+        place, left = paired_places(ids)
+        wide = lax.dot_general(one_hot(place, halves), paired, (((1,), (0,)), ((), ())))
+        return jnp.where(left[:, None], wide[:, :paired.shape[1] // 2], wide[:, paired.shape[1] // 2 :])
 
     source_part, target_part = (look_up(all_ids[:, k].reshape(-1)) for k in (0, 1))
     positional = sinusoid(length, width)
@@ -1043,8 +1160,7 @@
         enc_in, norms[0], ((enc_attn_w,), 0, 0), source_seg, source_seg, None, False
     )
     self_w, cross_w, dec_ffn_w, ready = late_weights(attn_w[4:], ffn_w[2:], enc_in, enc_mid)
-    late_table, _ = lax.optimization_barrier((own_table, ready))
-    table_low = lax.all_gather(late_table, "dp", axis=1, tiled=True)
+    table_low = lax.all_gather(after(own_table, ready), "dp", axis=1, tiled=True)
     enc_out, encoded, enc_ffn = ffn_forward(enc_mid, norms[1], norms[2], ((enc_ffn_w,), 0, 0))
     target_rows = swap_owners(target_sum.reshape(owners, length, -1), 3)
     target_rows = jnp.swapaxes(target_rows, 0, 1).reshape(length, -1).astype(jnp.float32)
@@ -1075,86 +1191,64 @@
         weight[:, None] * (jnp.exp(logits - log_total[:, None]) - label_hit.astype(jnp.float32))
     ).astype(jnp.bfloat16)
     grad_picked = sum_vocab(dot_dims(grad_logits, table_low, 1, 0).astype(jnp.bfloat16), 5)
-    grad_table = lax.psum_scatter(
-        dot_dims(grad_logits, picked, 0, 0).astype(jnp.bfloat16),
-        "dp",
-        scatter_dimension=1,
-        tiled=True,
-    )
+    grad_table = [
+        dot_dims(grad_logits, part, 0, 0).astype(jnp.bfloat16)
+        for part in jnp.split(picked, owners, axis=1)
+    ]
+    table_parts = jnp.stack(grad_table)
+    grad_table = lax.psum_scatter(table_parts, "dp", scatter_dimension=0, tiled=False)
     grad_final = dot_dims(chosen_rows, grad_picked, 0, 0)
 
-    chosen_columns = share_rows(jnp.eye(width, dtype=jnp.bfloat16), owners, replicas, replica)
-    chosen_columns = chosen_columns.reshape(-1, width)
-
-    def weight_grads(stored, parts):
-        normed, kept, cross = stored[7], stored[8], stored[6]
-        grad_low, gq, gk, gv = parts
-        key_in = encoded if cross else normed
-        share = [dot_dims(chosen_columns, rows, 1, 1).astype(jnp.bfloat16) for rows in (normed, key_in)]
-        mixed = share_rows(kept[3], owners, replicas, replica).reshape(-1, length)
-        return [
-            dot_dims(share[0], gq, 1, 0),
-            dot_dims(share[1], gk, 1, 0),
-            dot_dims(share[1], gv, 1, 0),
-            dot_dims(mixed, grad_low, 1, 0),
-        ]
-
-    def hidden_grads(stored, parts):
-        grad_low, values, grads = parts
-        return [
-            dot_dims(share_rows(rows, owners, replicas, replica).reshape(-1, length), right, 1, 0)
-            for rows, right in ((grads, stored[3]), (values, grad_low))
-        ]
-
-    def gradient_blocks(pieces):
-        blocks = [piece.astype(jnp.bfloat16).reshape(owners, -1, width) for piece in pieces]
-        return blocks if len(blocks) == 2 else [jnp.concatenate(blocks, axis=1)]
-
+    picks = share_selector(width, owners, replicas, replica, width)
+    hidden = ffn_w.shape[1] * owners
+    hidden_picks = share_selector(hidden, owners, replicas, replica, 512)
     norm_grads = [None] * 7
-    grad, norm_grads[6], norm_grads[5], dec_ffn_parts = ffn_backward(grad_final, dec_ffn)
-    grad, norm_grads[4], cross_parts, grad_encoded = attn_backward(grad, dec_cross)
-    grad, norm_grads[3], self_parts, _ = attn_backward(grad, dec_self)
-    grad_target = (grad * embed_scale).astype(jnp.bfloat16)
-    early = (
-        gradient_blocks(weight_grads(dec_self, self_parts))
-        + gradient_blocks(weight_grads(dec_cross, cross_parts))
-        + gradient_blocks(hidden_grads(dec_ffn, dec_ffn_parts))
-    )
-    early = jnp.concatenate(early, axis=1)
-    early, grad_encoded = lax.optimization_barrier((early, grad_encoded))
-    early = lax.psum_scatter(early, "dp", scatter_dimension=0, tiled=False)
-    early = lax.all_gather(early, "vocab")
-    grad, norm_grads[2], norm_grads[1], enc_ffn_parts = ffn_backward(grad_encoded, enc_ffn)
-    grad, norm_grads[0], enc_parts, _ = attn_backward(grad, enc_attn)
-    grad_source = (grad * embed_scale).astype(jnp.bfloat16)
-    token_grads = jnp.concatenate([grad_source, grad_target]).reshape(2 * length, owners, -1)
-    late = gradient_blocks(weight_grads(enc_attn, enc_parts)) + gradient_blocks(
-        hidden_grads(enc_ffn, enc_ffn_parts)
-    )
-    late, token_grads = share_gradients(
-        jnp.stack(late, axis=1), jnp.swapaxes(token_grads, 0, 1), 7
-    )
-    token_grads = token_grads.reshape(owners * 2 * length, -1)
-    flat_ids = all_ids.reshape(-1)
-    even = (flat_ids % 2 == 0)[:, None]
+    grad, norm_grads[6], norm_grads[5], *ffn_blocks = ffn_backward(
+        grad_final, dec_ffn, hidden_picks, owners, before=(table_parts,)
+    )
+    grad, norm_grads[4], block, grad_encoded = attn_backward(grad, dec_cross, picks, owners, None)
+    early = lax.psum_scatter(
+        jnp.concatenate([block, *ffn_blocks], axis=1), "dp", scatter_dimension=0, tiled=False
+    )
+    grad, norm_grads[3], self_block, target_rows = attn_backward(
+        grad, dec_self, picks, owners, embed_scale
+    )
+    grad, norm_grads[2], norm_grads[1], *ffn_blocks = ffn_backward(
+        grad_encoded, enc_ffn, hidden_picks, owners, before=(grad_table, grad)
+    )
+    early_sum = after(early, grad[0, 0])
+    early = lax.all_gather(early_sum, "vocab")
+    grad, norm_grads[0], block, source_rows = attn_backward(
+        grad, enc_attn, picks, owners, embed_scale, before=(early_sum,)
+    )
+    norm_grad = jnp.stack([after(part, early[0, 0, 0]) for part in norm_grads])
+    norm_grad = jnp.concatenate([norm_grad[:, 0], norm_grad[:, 1], jnp.zeros((2, width))], axis=0)
+    norm_grad = jnp.swapaxes(norm_grad.reshape(16, owners, -1), 0, 1)
+    late, source_rows, target_rows, norm_grad = share_gradients(
+        [block, self_block, *ffn_blocks], [source_rows, target_rows, norm_grad], 7, (early,)
+    )
+    g_norm = jnp.sum(norm_grad, axis=0)[:14]
+    token_grads = jnp.concatenate([source_rows, target_rows], axis=1).reshape(
+        owners * 2 * length, -1
+    )
+    place, left = paired_places(all_ids.reshape(-1))
+    left = left[:, None]
     token_grads = jnp.concatenate(
-        [jnp.where(even, token_grads, 0), jnp.where(even, 0, token_grads)], axis=1
-    )
-    g_embed = grad_table.astype(jnp.float32) + dot_dims(
-        one_hot(flat_ids // 2, halves), token_grads, 0, 0
-    ).reshape(vocab_count, -1)
+        [jnp.where(left, token_grads, 0), jnp.where(left, 0, token_grads)], axis=1
+    )
+    g_paired = dot_dims(one_hot(place, halves), token_grads, 0, 0)
+    g_embed = grad_table.astype(jnp.float32) + jnp.concatenate(
+        jnp.split(g_paired, 2, axis=1), axis=0
+    )
 
     def by_matrix(shared, count):
         blocks = jnp.swapaxes(shared.reshape(replicas, count, -1, width), 0, 1)
         return blocks.reshape(count, -1, width)
 
-    early, late = by_matrix(early, 4), by_matrix(late, 3)
-    g_attn = [by_matrix(part, 4) for part in (late[0], early[0], early[1])]
+    early = by_matrix(early, 3)
+    g_attn = [by_matrix(part, 4) for part in (late[0], late[1], early[0])]
     g_attn = jnp.concatenate(g_attn).astype(jnp.float32)
-    g_ffn = jnp.concatenate([late[1:], early[2:]])
-    norm_grad = jnp.stack(norm_grads)
-    norm_grad = jnp.concatenate([norm_grad[:, 0], norm_grad[:, 1]], axis=0)
-    g_norm = lax.psum_scatter(norm_grad, "dp", scatter_dimension=1, tiled=True)
+    g_ffn = jnp.concatenate([late[2:].reshape(2, -1, width), early[1:]])
 
     matrix = replica // 2
     own_grad = lax.dynamic_index_in_dim(g_ffn, matrix, 0, keepdims=False)
@@ -1195,13 +1289,7 @@
     new_embed, m_embed, v_embed = adam_update(
         embedding, g_embed, embed_m, embed_v, rate_matrix, decay_rate
     )
-    rotated = factor * rotate(g_ffn_low, soap_basis)
-    m_ffn = beta_one * ffn_m + (1.0 - beta_one) * rotated
-    v_ffn = beta_two * ffn_v + (1.0 - beta_two) * rotated * rotated
-    back_rotated = jnp.einsum(
-        "mfe,mde->mfd", adam_direction(m_ffn, v_ffn), soap_basis, precision=lax.Precision.HIGH
-    )
-    new_ffn = ffn_w - rate_matrix * (back_rotated + decay_rate * ffn_w)
+    new_ffn, m_ffn, v_ffn = update_rotated(factor, g_ffn_low, soap_basis, ffn_w, ffn_m, ffn_v)
     return (
         loss_sum,
         sentences,

time: 708 us -> 649 us (0.917)
  matrix products: 93.3 us -> 49 us
  local copies, waits for them, and re-layouts: 62.2 us -> 37.1 us
  Pallas kernels: 416 us -> 406 us
  other arithmetic: 71.9 us -> 80.5 us
    dot_general x5 -> x2, matrix products: 44 us -> 16.4 us  [look_up(): lax.dot_general(one_hot(place, halves), paired, (((1,), (0,)), ((), ())))]
    ppermute x6, waiting for transfers between devices: 26.1 us -> 2.77 us  [flip_sites(): lax.ppermute(part, axis, [(s, s ^ bit) for s in range(lax.axis_size(axis))])]
    all_gather x2, waiting for transfers between devices: 0.01 us -> 21.1 us  [all_matrices(): lax.all_gather(half, 'vocab').reshape(4, 2 * rows, -1).astype(jnp.float32)]
    dot_general x26 -> x10, matrix products: 49.4 us -> 32.6 us  [dot_dims(): lax.dot_general(left, right, (((left_dim,), (right_dim,)), ((), ())), pre...]
    unnamed x152 -> x89, local copies, waits for them, and re-layouts: 20.6 us -> 5.86 us
    reshape x3 -> x0, local copies, waits for them, and re-layouts: 10.5 us -> none  [the longest x1 4.11 us: body(): jnp.concatenate([grad_source, grad_target]).reshape(2 * length, owners, -1)]
    pallas_call x18 -> x19, Pallas kernels: 416 us -> 406 us  [the longest x11 225 us: call(): pl.pallas_call(body, out_shape=outs, in_specs=[vmem] * (len(args) - smem_...]
    dynamic_slice x7 -> x0, local copies, waits for them, and re-layouts: 7.53 us -> none  [share_rows(): return lax.dynamic_index_in_dim(blocks, share, 1, keepdims=False)]
  transfers between devices with their start and end apart: 14 -> 13, of which waited for: 2 -> 3; matrix products, arithmetic and copies ran while one was open for 20% -> 11% of each run, Pallas kernels for 34% -> 39%
where the time goes in v5:
time: 649 us; the launch traced here: 636 us
  Pallas kernels  406 us (63%)
  other arithmetic  80.5 us (12%)
  matrix products  49 us (8%)
  local copies, waits for them, and re-layouts  37.1 us (6%)
  waiting for transfers between devices  31.4 us (5%)
  between operations  27.9 us (4%)
    pallas_call x11, Pallas kernels, call(): pl.pallas_call(body, out_shape=outs, in_specs=[vmem] * (len(args) - smem_...  225 us
    pallas_call x7, Pallas kernels, talk(): pl.pallas_call(body, out_shape=outs, in_specs=[vmem] * len(args) + [pl.Bl...  166 us
    dot_general x10, matrix products, dot_dims(): lax.dot_general(left, right, (((left_dim,), (right_dim,)), ((), ())), pre...  32.6 us
    all_gather x2, waiting for transfers between devices, all_matrices(): lax.all_gather(half, 'vocab').reshape(4, 2 * rows, -1).astype(jnp.float32)  21.1 us
    dot_general x2, matrix products, look_up(): lax.dot_general(one_hot(place, halves), paired, (((1,), (0,)), ((), ())))  16.4 us
    pallas_call x1, Pallas kernels, update_rotated(): pl.pallas_call(update_kernel, grid=(count,), out_shape=(full(count, rows,...  14.5 us
    sub x3, other arithmetic, adam_update(): weight - step_rate * (adam_direction(moment, second) + decay_weight * wei...  13.1 us
  transfers between devices with their start and end apart: 13, of which 3 were waited for; matrix products, arithmetic and copies ran while one was open for 11% of the time, Pallas kernels for 39%

profile of v5, /device:TPU:0, one launch (start us, length us, event | category | flops | bytes accessed | tf_op | source)
XLA Modules:
  0.0 636.2 jit_solution(10844753909130883571)
XLA Ops:
  10.7 7.9 %shard_map.332 = (s32[4,2,1024]{2,1,0:T(2,128)}, f32[4,16,128]{2,1,0:T(8,128)}) custom-call(s32[2,1024]{1,0:T(2,128)} %pad_add_fusion.refs_0_, f32[16,128]{1,0:T(8,128)} %pad_convert_fusion.refs_1_), custom_call_target="tpu_custom_call" | custom-call | flops 15000000512 | tf_op jit(solution)/shard_map/pallas_call | solution.py:633
  26.8 8.8 %fusion.2 = bf16[4096,256]{1,0:T(8,128)(2,1)S(1)} fusion(s32[4096]{0:T(1024)S(1)} %fusion.37, bf16[2368,128]{1,0:T(8,128)(2,1)} %get-tuple-element.189, bf16[2368,128]{1,0:T(8,128)(2,1)} %get-tuple-element.188), kind=kOutput, calls=%fused_computation.6 | convolution fusion | flops 4978180096 | bytes 3325952 | tf_op jit(solution)/shard_map/dot_general | solution.py:1144
  38.5 52.2 %shard_map.333 = (f32[1024,512]{1,0:T(8,128)}, bf16[4,512,512]{2,1,0:T(8,128)(2,1)}, bf16[2,2048,512]{2,1,0:T(8,128)(2,1)}) custom-call(bf16[4,1024,128]{2,1,0:T(8,128)(2,1)} %bitcast.207, f32[1024,512]{1,0:T(8,128)} %constant.226.clone.refs_1_, bf16[4,128,512]{2,1,0:T(8,128)(2,1)} %get-tuple-element.187.refs_2_, bf16[2,512,512]{2,1,0:T(8,128)(2,1)} %slice.295.refs_3_), custom_call_target="tpu_custom_call" | custom-call | flops 49999998976 | tf_op jit(solution)/shard_map/pallas_call | solution.py:633
  95.6 7.6 %fusion.1 = bf16[4096,256]{1,0:T(8,128)(2,1)S(1)} fusion(s32[4096]{0:T(1024)S(1)} %fusion.36, bf16[2368,128]{1,0:T(8,128)(2,1)S(1)} %copy-done.22, bf16[2368,128]{1,0:T(8,128)(2,1)S(1)} %copy-done.21), kind=kOutput, calls=%fused_computation.5 | convolution fusion | flops 4978180096 | bytes 3325952 | tf_op jit(solution)/shard_map/dot_general | solution.py:1144
  118.8 19.2 %shard_map.335 = (f32[1024,512]{1,0:T(8,128)}, bf16[1024,512]{1,0:T(8,128)(2,1)}, bf16[512,1024]{1,0:T(8,128)(2,1)}, bf16[512,1024]{1,0:T(8,128)(2,1)}, bf16[512...) custom-call(f32[1024,512]{1,0:T(8,128)} %get-tuple-element.88.refs_0_.refs_1_, ...), custom_call_target="tpu_custom_call" | custom-call | flops 20000000000 | tf_op jit(solution)/shard_map/pallas_call | solution.py:57
  140.7 11.0 %shard_map.337 = (f32[1024,512]{1,0:T(8,128)}, bf16[1024,512]{1,0:T(8,128)(2,1)}, bf16[1024,512]{1,0:T(8,128)(2,1)}) custom-call(f32[1024,512]{1,0:T(8,128)} %get-tuple-element.93.refs_0_.refs_3_, f32[2,512]{1,0:T(2,128)} %get-tuple-element.223.refs_1_.refs_4_, f32[2,512]{1,0:T(2,128)} %pad_maximum_fusion.13.refs_2_, ...), custom_call_target="tpu_custom_call" | custom-call | flops 12000000000 | tf_op jit(solution)/shard_map/pallas_call | solution.py:57
  158.6 7.4 %all-reduce.7.cloned.1.call-done.refs_0_ = bf16[4,1024,128]{2,1,0:T(8,128)(2,1)} async-done(((bf16[4,1024,128]{2,1,0:T(8,128)(2,1)}), bf16[4,1024,128]{2,1,0:T(8,128)(2,1)}) %all-reduce.7.cloned.1.call-update) | async-done | bytes 1048592 | tf_op jit(solution)/shard_map/psum | solution.py:1158
  166.0 18.5 %shard_map.334 = bf16[4,1024,128]{2,1,0:T(8,128)(2,1)} custom-call(bf16[4,1024,128]{2,1,0:T(8,128)(2,1)} %all-reduce.7.cloned.1.call-done.refs_0_), custom_call_target="tpu_custom_call" | custom-call | flops 15000000512 | tf_op jit(solution)/shard_map/pallas_call | solution.py:633
  188.6 19.0 %shard_map.336 = (f32[1024,512]{1,0:T(8,128)}, bf16[1024,512]{1,0:T(8,128)(2,1)}, bf16[512,1024]{1,0:T(8,128)(2,1)}, bf16[512,1024]{1,0:T(8,128)(2,1)}, bf16[512...) custom-call(f32[1024,512]{1,0:T(8,128)} %copy_bitcast_fusion.refs_0_.refs_1_, ...), custom_call_target="tpu_custom_call" | custom-call | flops 20000000000 | tf_op jit(solution)/shard_map/pallas_call | solution.py:57
  207.6 18.8 %shard_map.338 = (f32[1024,512]{1,0:T(8,128)}, bf16[1024,512]{1,0:T(8,128)(2,1)}, bf16[512,1024]{1,0:T(8,128)(2,1)}, bf16[512,1024]{1,0:T(8,128)(2,1)}, bf16[512...) custom-call(f32[1024,512]{1,0:T(8,128)} %get-tuple-element.97.refs_0_.refs_1_, ...), custom_call_target="tpu_custom_call" | custom-call | flops 20000000000 | tf_op jit(solution)/shard_map/pallas_call | solution.py:57
  226.4 13.9 %shard_map.339 = (f32[1024,512]{1,0:T(8,128)}, bf16[1024,512]{1,0:T(8,128)(2,1)}, bf16[1024,512]{1,0:T(8,128)(2,1)}, bf16[2,2048,512]{2,1,0:T(8,128)(2,1)}) custom-call(f32[1024,512]{1,0:T(8,128)} %get-tuple-element.100.refs_0_.refs_3_, f32[2,512]{1,0:T(2,128)} %get-tuple-element.224.refs_1_.refs_4_, f32[2,512]{1,0:T(2,128)} %get-tuple-element.225.refs_2_, ...), custom_call_target="tpu_custom_call" | custom-call | flops 12000000000 | tf_op jit(solution)/shard_map/pallas_call | solution.py:57
  242.1 3.9 fusion.64
  248.8 6.9 %shard_map.340 = f32[8,8,256]{2,1,0:T(8,128)} custom-call(f32[8,256]{1,0:T(8,128)} %select_maximum_fusion.refs_0_), custom_call_target="tpu_custom_call" | custom-call | flops 15000000512 | tf_op jit(solution)/shard_map/pallas_call | solution.py:633
  257.4 3.8 fusion.13
  270.2 4.5 convolution_convert_fusion.4.refs_0_
  274.7 16.1 %shard_map.341 = bf16[256,512]{1,0:T(8,128)(2,1)} custom-call(bf16[256,512]{1,0:T(8,128)(2,1)} %convolution_convert_fusion.4.refs_0_), custom_call_target="tpu_custom_call" | custom-call | flops 15000000512 | tf_op jit(solution)/shard_map/pallas_call | solution.py:633
  293.7 19.9 %shard_map.342 = (f32[1024,512]{1,0:T(8,128)}, f32[2,512]{1,0:T(2,128)}, f32[2,512]{1,0:T(2,128)}, bf16[4,64,512]{2,1,0:T(8,128)(2,1)}, bf16[4,64,512]{2,1,0:T(8,128)(2,1)}) custom-call(f32[1024,512]{1,0:T(8,128)} %fusion.22.refs_0_, f32[1024,512]{1,0:T(8,128)} %get-tuple-element.102.refs_1_, f32[2,512]{1,0:T(2,128)} %get-tuple-element.225.refs_2_, ...), custom_call_target="tpu_custom_call" | custom-call | flops 16999999488 | tf_op jit(solution)/shard_map/pallas_call | solution.py:57
  313.7 23.7 %shard_map.343 = (f32[1024,512]{1,0:T(8,128)}, f32[2,512]{1,0:T(2,128)}, bf16[4,64,512]{2,1,0:T(8,128)(2,1)}, f32[1024,512]{1,0:T(8,128)}) custom-call(f32[1024,512]{1,0:T(8,128)} %get-tuple-element.105.refs_0_, f32[1024,512]{1,0:T(8,128)} %get-tuple-element.97.refs_0_.refs_1_, f32[2,512]{1,0:T(2,128)} %get-tuple-element.221.refs_1_.refs_2_, ...), custom_call_target="tpu_custom_call" | custom-call | flops 24999999488 | tf_op jit(solution)/shard_map/pallas_call | solution.py:57
  339.3 24.3 %shard_map.344 = (f32[1024,512]{1,0:T(8,128)}, f32[2,512]{1,0:T(2,128)}, bf16[4,64,512]{2,1,0:T(8,128)(2,1)}, bf16[4,1024,128]{2,1,0:T(8,128)(2,1)}) custom-call(f32[1024,512]{1,0:T(8,128)} %get-tuple-element.116.refs_0_, f32[1024,512]{1,0:T(8,128)} %copy_bitcast_fusion.refs_0_.refs_1_, f32[2,512]{1,0:T(2,128)} %get-tuple-element.220.refs_1_.refs_2_, ...), custom_call_target="tpu_custom_call" | custom-call | flops 24999999488 | tf_op jit(solution)/shard_map/pallas_call | solution.py:57
  363.6 20.1 %shard_map.345 = (f32[1024,512]{1,0:T(8,128)}, f32[2,512]{1,0:T(2,128)}, f32[2,512]{1,0:T(2,128)}, bf16[4,64,512]{2,1,0:T(8,128)(2,1)}, bf16[4,64,512]{2,1,0:T(8,128)(2,1)}) custom-call(f32[1024,512]{1,0:T(8,128)} %get-tuple-element.113.refs_0_, f32[1024,512]{1,0:T(8,128)} %get-tuple-element.114.refs_1_, f32[2,512]{1,0:T(2,128)} %pad_maximum_fusion.13.refs_2_, ...), custom_call_target="tpu_custom_call" | custom-call | flops 16999999488 | tf_op jit(solution)/shard_map/pallas_call | solution.py:57
  393.6 26.2 %shard_map.346 = (f32[1024,512]{1,0:T(8,128)}, f32[2,512]{1,0:T(2,128)}, bf16[4,64,512]{2,1,0:T(8,128)(2,1)}, bf16[4,1024,128]{2,1,0:T(8,128)(2,1)}) custom-call(f32[1024,512]{1,0:T(8,128)} %get-tuple-element.125.refs_0_, f32[1024,512]{1,0:T(8,128)} %get-tuple-element.88.refs_0_.refs_1_, f32[2,512]{1,0:T(2,128)} %get-tuple-element.222.refs_1_.refs_2_, ...), custom_call_target="tpu_custom_call" | custom-call | flops 24999999488 | tf_op jit(solution)/shard_map/pallas_call | solution.py:57
  424.9 42.8 %shard_map.347 = (bf16[4,8,64,512]{3,2,1,0:T(8,128)(2,1)}, bf16[4,1024,128]{2,1,0:T(8,128)(2,1)}, bf16[4,1024,128]{2,1,0:T(8,128)(2,1)}, f32[4,16,128]{2,1,0:T(8,128)}) custom-call(bf16[4,64,512]{2,1,0:T(8,128)(2,1)} %get-tuple-element.135.refs_0_, bf16[4,64,512]{2,1,0:T(8,128)(2,1)} %get-tuple-element.136.refs_1_, ...), custom_call_target="tpu_custom_call" | custom-call | flops 40000000000 | tf_op jit(solution)/shard_map/pallas_call | solution.py:633
  473.2 4.3 bitcast_select_fusion.1
  477.5 14.2 %fusion = f32[2368,256]{1,0:T(8,128)S(1)} fusion(s32[8192]{0:T(1024)S(1)} %fusion.35, bf16[8192,128]{1,0:T(8,128)(2,1)S(1)} %get-tuple-element.180, bf16[8192,128]{1,0:T(8,128)(2,1)S(1)} %get-tuple-element.179), kind=kOutput, calls=%fused_computation.2 | convolution fusion | flops 9959899136 | bytes 6651904 | tf_op jit(solution)/shard_map/dot_general | solution.py:34
  504.9 21.9 %shard_map.348 = (f32[512,512]{1,0:T(8,128)}, f32[8,128]{1,0:T(8,128)}) custom-call(f32[512,512]{1,0:T(8,128)} %fusion.25.refs_0_, f32[8,128]{1,0:T(8,128)} %broadcast_in_dim.112.refs_1_), custom_call_target="tpu_custom_call" | custom-call | flops 15000000512 | tf_op jit(solution)/shard_map/pallas_call | solution.py:633
  533.0 29.1 %shard_map.350 = f32[512,512]{1,0:T(8,128)} custom-call(f32[512,512]{1,0:T(8,128)} %bitcast_add_fusion.refs_0_, f32[512,512]{1,0:T(8,128)} %dynamic-slice_bitcast_fusion.refs_1_), custom_call_target="tpu_custom_call" | custom-call | flops 28999999488 | tf_op jit(solution)/shard_map/pallas_call | solution.py:57
  567.9 14.5 %shard_map.349 = (f32[4,512,512]{2,1,0:T(8,128)}, f32[4,512,512]{2,1,0:T(8,128)}, f32[4,512,512]{2,1,0:T(8,128)}) custom-call(f32[1]{0:T(128)} %bitcast.81.factor_ref, bf16[4,512,512]{2,1,0:T(8,128)(2,1)} %pad_maximum_fusion.1.g_ref, f32[4,512,512]{2,1,0:T(8,128)} %basis_ref.1, f32[4,512,512]{2,1,0:T(8,128)} %w_ref.1, f32[4,512,512]{2,1,0:T(8,128)} %m_ref.1, ...), custom_call_target="tpu_custom_call" | custom-call | flops 10000000000 | tf_op jit(solution)/shard_map/pallas_call | solution.py:507
  582.5 8.1 %multiply_subtract_fusion = (f32[12,128,512]{2,1,0:T(8,128)}, f32[12,128,512]{2,1,0:T(8,128)}, f32[12,128,512]{2,1,0:T(8,128)}) fusion(f32[12,128,512]{2,1,0:T(8,128)S(1)} %copy-done.5, f32[]{:T(128)} %div.97, bf16[4,128,512]{2,1,0:T(8,128)(2,1)S(1)} %bitcast.192, bf16[4,128,512]{2,1,0:T(8,128)(2,1)S(1)} %bitcast.194, bf16[4,128,512]{2,1,0:T(8,128)(2,1)} %bitcast.196, ...), kind=kLoop, calls=%fused_computation.40 | loop fusion | flops 14942208 | bytes 20447236 | tf_op jit(solution)/shard_map/sub | solution.py:1088
  591.7 4.4 multiply_subtract_fusion.1
  596.1 4.2 convert.13
  600.3 21.1 %all-gather.13.cloned.1.call-done = bf16[2048,512]{1,0:T(8,128)(2,1)} async-done(((bf16[256,512]{1,0:T(8,128)(2,1)}), bf16[2048,512]{1,0:T(8,128)(2,1)}) %all-gather.13.cloned.1.call-update) | async-done | bytes 2097168 | tf_op jit(solution)/shard_map/all_gather | solution.py:1275
  624.2 3.0 multiply_add_fusion
  (226 shorter events, 107.1 us)
Async XLA Ops:
  8.0 157.9 %all-reduce.7.cloned.1.call-start = ((), (), s32[]{:S(2)}) async-start(), calls=%async_computation.2 | async-start | bytes 2097152 | tf_op jit(solution)/shard_map/psum | solution.py:1158
  10.7 10.0 %copy-start.13 = (f32[4,512,512]{2,1,0:T(8,128)S(1)}, f32[4,512,512]{2,1,0:T(8,128)}, u32[]{:S(2)}) copy-start(f32[4,512,512]{2,1,0:T(8,128)} %w_ref.1) | copy-start | bytes 12582916
  38.5 52.2 %copy-start.11 = (bf16[4,128,512]{2,1,0:T(8,128)(2,1)S(1)}, bf16[4,128,512]{2,1,0:T(8,128)(2,1)}, u32[]{:S(2)}) copy-start(bf16[4,128,512]{2,1,0:T(8,128)(2,1)} %get-tuple-element.185) | copy-start | bytes 1572868
  38.5 52.2 %copy-start.12 = (bf16[4,128,512]{2,1,0:T(8,128)(2,1)S(1)}, bf16[4,128,512]{2,1,0:T(8,128)(2,1)}, u32[]{:S(2)}) copy-start(bf16[4,128,512]{2,1,0:T(8,128)(2,1)} %get-tuple-element.186) | copy-start | bytes 1572868
  92.0 45.9 %collective-permute-start = (bf16[1024,512]{1,0:T(8,128)(2,1)}, bf16[1024,512]{1,0:T(8,128)(2,1)}, u32[]{:S(2)}, u32[]{:S(2)}) collective-permute-start(bf16[1024,512]{1,0:T(8,128)(2,1)} %maximum_select_fusion), channel_id=1, source_target_pairs={{0,8},{8,0},{16,24},{24,16},{1,9},{9,1},{17,25},{25,17},{2,10},{10... | collective-permute-start | bytes 3145736 | tf_op jit(solution)/shard_map/ppermute | solution.py:174
  92.8 47.9 %collective-permute-start.1 = (bf16[1024,512]{1,0:T(8,128)(2,1)}, bf16[1024,512]{1,0:T(8,128)(2,1)}, u32[]{:S(2)}, u32[]{:S(2)}) collective-permute-start(bf16[1024,512]{1,0:T(8,128)(2,1)} %maximum_select_fusion), channel_id=1, source_target_pairs={{0,16},{8,24},{16,0},{24,8},{1,17},{9,25},{17,1},{25,9},{2,18},{10... | collective-permute-start | bytes 3145736 | tf_op jit(solution)/shard_map/ppermute | solution.py:174
  93.5 47.2 %collective-permute-start.2 = (bf16[1024,512]{1,0:T(8,128)(2,1)}, bf16[1024,512]{1,0:T(8,128)(2,1)}, u32[]{:S(2)}, u32[]{:S(2)}) collective-permute-start(bf16[1024,512]{1,0:T(8,128)(2,1)} %maximum_select_fusion), channel_id=1, source_target_pairs={{0,24},{8,16},{16,8},{24,0},{1,25},{9,17},{17,9},{25,1},{2,26},{10... | collective-permute-start | bytes 3145736 | tf_op jit(solution)/shard_map/ppermute | solution.py:174
  103.2 6.8 %copy-start.28 = (f32[4,16,128]{2,1,0:T(8,128)S(1)}, f32[4,16,128]{2,1,0:T(8,128)}, u32[]{:S(2)}) copy-start(f32[4,16,128]{2,1,0:T(8,128)} %get-tuple-element.90) | copy-start | bytes 98308
  103.2 7.4 %copy-start.29 = (s32[1,256]{1,0:T(1,128)S(1)}, s32[1,256]{1,0:T(1,128)}, u32[]{:S(2)}) copy-start(s32[1,256]{1,0:T(1,128)} %param.25) | copy-start | bytes 3076
  106.1 135.9 %all-gather.7.cloned.1.call-start = ((), (), s32[]{:S(2)}) async-start(), calls=%async_computation.3 | async-start | bytes 6062080 | tf_op jit(solution)/shard_map/all_gather | solution.py:1163
  140.7 11.0 %collective-permute-start.5 = (bf16[1024,512]{1,0:T(8,128)(2,1)}, bf16[1024,512]{1,0:T(8,128)(2,1)S(1)}, u32[]{:S(2)}, u32[]{:S(2)}) collective-permute-start(bf16[1024,512]{1,0:T(8,128)(2,1)} %collective-permute-done.2.refs_7_.refs_8_.refs_6_), channel_id=1, source_target_pairs={{0,1},{1,0},{2,3},{3,2},{4,5},{5,4},{6,7},{7,6},{8,9},{9,8},{10,11... | collective-permute-start | bytes 3145736 | tf_op jit(solution)/shard_map/ppermute | solution.py:174
  154.7 208.9 %reduce-scatter.7.cloned.1.call-start = ((), (), s32[]{:S(2)}) async-start(), calls=%async_computation.7 | async-start | bytes 6062080
  158.0 26.4 %copy-start.16 = (f32[4,1024,128]{2,1,0:T(8,128)S(1)}, f32[4,1024,128]{2,1,0:T(8,128)}, u32[]{:S(2)}) copy-start(f32[4,1024,128]{2,1,0:T(8,128)} %constant.240) | copy-start | bytes 6291460
  158.0 29.3 %collective-permute-start.3 = (bf16[1024,512]{1,0:T(8,128)(2,1)}, bf16[1024,512]{1,0:T(8,128)(2,1)S(1)}, u32[]{:S(2)}, u32[]{:S(2)}) collective-permute-start(bf16[1024,512]{1,0:T(8,128)(2,1)} %collective-permute-done.refs_5_.refs_6_.refs_4_), channel_id=1, source_target_pairs={{0,1},{1,0},{2,3},{3,2},{4,5},{5,4},{6,7},{7,6},{8,9},{9,8},{10,11... | collective-permute-start | bytes 3145736 | tf_op jit(solution)/shard_map/ppermute | solution.py:174
  158.6 28.8 %collective-permute-start.4 = (bf16[1024,512]{1,0:T(8,128)(2,1)}, bf16[1024,512]{1,0:T(8,128)(2,1)}, u32[]{:S(2)}, u32[]{:S(2)}) collective-permute-start(bf16[1024,512]{1,0:T(8,128)(2,1)} %collective-permute-done.1.refs_6_.refs_7_.refs_5_), channel_id=1, source_target_pairs={{0,1},{1,0},{2,3},{3,2},{4,5},{5,4},{6,7},{7,6},{8,9},{9,8},{10,11... | collective-permute-start | bytes 3145736 | tf_op jit(solution)/shard_map/ppermute | solution.py:174
  267.9 118.3 %reduce-scatter.9.cloned.1.call-start = ((), (), s32[]{:S(2)}) async-start(), calls=%async_computation.8 | async-start | bytes 983040
  313.6 23.7 %copy-start.24 = (bf16[4,64,512]{2,1,0:T(8,128)(2,1)S(1)}, bf16[4,64,512]{2,1,0:T(8,128)(2,1)}, u32[]{:S(2)}) copy-start(bf16[4,64,512]{2,1,0:T(8,128)(2,1)} %get-tuple-element.133) | copy-start | bytes 786436
  313.6 23.7 %copy-start.25 = (bf16[4,64,512]{2,1,0:T(8,128)(2,1)S(1)}, bf16[4,64,512]{2,1,0:T(8,128)(2,1)}, u32[]{:S(2)}) copy-start(bf16[4,64,512]{2,1,0:T(8,128)(2,1)} %get-tuple-element.134) | copy-start | bytes 786436
  339.3 80.5 %all-gather.9.cloned.1.call-start = ((), (), s32[]{:S(2)}) async-start(), calls=%async_computation.4 | async-start | bytes 1769472 | tf_op jit(solution)/shard_map/all_gather | solution.py:1220
  387.9 208.2 %all-gather.11.cloned.1.call-start = ((), (), s32[]{:S(2)}) async-start(), calls=%async_computation.5 | async-start | bytes 2359296 | tf_op jit(solution)/shard_map/all_gather | solution.py:1275
  533.0 32.7 %copy-start.26 = (f32[14,128]{1,0:T(8,128)S(1)}, f32[14,128]{1,0:T(8,128)}, u32[]{:S(2)}) copy-start(f32[14,128]{1,0:T(8,128)} %param.35) | copy-start | bytes 21508
  533.0 32.7 %copy-start.30 = (f32[14,128]{1,0:T(8,128)S(1)}, f32[14,128]{1,0:T(8,128)}, u32[]{:S(2)}) copy-start(f32[14,128]{1,0:T(8,128)} %param.36) | copy-start | bytes 21508
  533.0 32.8 %copy-start.31 = (f32[14,128]{1,0:T(8,128)S(1)}, f32[14,128]{1,0:T(8,128)}, u32[]{:S(2)}) copy-start(f32[14,128]{1,0:T(8,128)} %param.37) | copy-start | bytes 21508
  563.9 57.5 %all-gather.13.cloned.1.call-start = ((), (), s32[]{:S(2)}) async-start(), calls=%async_computation.6 | async-start | bytes 2359296 | tf_op jit(solution)/shard_map/all_gather | solution.py:1275
  567.9 14.6 %copy-start.5 = (f32[12,128,512]{2,1,0:T(8,128)S(1)}, f32[12,128,512]{2,1,0:T(8,128)}, u32[]{:S(2)}) copy-start(f32[12,128,512]{2,1,0:T(8,128)} %param.27) | copy-start | bytes 9437188
  567.9 14.6 %copy-start.9 = (bf16[8,4,16,512]{3,2,0,1:T(8,128)(2,1)S(1)}, bf16[8,4,16,512]{3,2,0,1:T(8,128)(2,1)}, u32[]{:S(2)}) copy-start(bf16[8,4,16,512]{3,2,0,1:T(8,128)(2,1)} %copy.67) | copy-start | bytes 1572868
  567.9 14.6 %copy-start.10 = (bf16[4,8,16,512]{3,2,1,0:T(8,128)(2,1)S(1)}, bf16[4,8,16,512]{3,2,1,0:T(8,128)(2,1)}, u32[]{:S(2)}) copy-start(bf16[4,8,16,512]{3,2,1,0:T(8,128)(2,1)} %copy.66) | copy-start | bytes 1572868
  582.5 8.1 %copy-start.3 = (f32[4736,128]{1,0:T(8,128)S(1)}, f32[4736,128]{1,0:T(8,128)}, u32[]{:S(2)}) copy-start(f32[4736,128]{1,0:T(8,128)} %param.38) | copy-start | bytes 7274500
  582.5 8.1 %copy-start.6 = (f32[2368,128]{1,0:T(8,128)S(1)}, f32[2368,128]{1,0:T(8,128)}, u32[]{:S(2)}) copy-start(f32[2368,128]{1,0:T(8,128)} %get-tuple-element.178) | copy-start | bytes 3637252
  582.5 8.1 %copy-start.8 = (bf16[1,4736,128]{2,1,0:T(8,128)(2,1)S(1)}, bf16[1,4736,128]{2,1,0:T(8,128)(2,1)}, u32[]{:S(2)}) copy-start(bf16[1,4736,128]{2,1,0:T(8,128)(2,1)} %reduce-scatter.7.cloned.1.call-done) | copy-start | bytes 3637252
  582.5 8.1 %copy-start.14 = (f32[4736,128]{1,0:T(8,128)S(1)}, f32[4736,128]{1,0:T(8,128)}, u32[]{:S(2)}) copy-start(f32[4736,128]{1,0:T(8,128)} %param.39) | copy-start | bytes 7274500
  582.5 9.2 %copy-start.15 = (f32[4736,128]{1,0:T(8,128)S(1)}, f32[4736,128]{1,0:T(8,128)}, u32[]{:S(2)}) copy-start(f32[4736,128]{1,0:T(8,128)} %param.40) | copy-start | bytes 7274500
  (24 other events, 81.4 us)
Sparse Core Ops, SparseCore 0:
  106.2 59.6 all-reduce.6
  388.0 26.3 all-gather.8
  564.0 27.2 all-gather.10
  592.7 28.6 all-gather.12
Sparse Core Ops, SparseCore 1:
  154.8 65.0 all-gather.6
  267.9 57.6 reduce-scatter.6
  339.3 29.1 reduce-scatter.8

commit v6 on v5

--- a/solution.py
+++ b/solution.py
@@ -430,11 +430,24 @@
 
 
 def ffn_backward_kernel(
-    chunk, after_ref, y_ref, next_ref, x_ref, ln_ref, a_ref, w_ref, pick_ref,
+    chunk, picked, after_ref, *refs
+):
+    if picked:
+        place_ref, *refs = refs
+        shape = (refs[0].shape[0], place_ref.shape[1])
+        chosen = lax.broadcasted_iota(jnp.int32, shape, 0) == place_ref[...]
+        after = dot_dims(chosen.astype(jnp.bfloat16), after_ref[...], 1, 0)
+    else:
+        after = after_ref[...]
+    ffn_backward_rest(chunk, after, *refs)
+
+
+def ffn_backward_rest(
+    chunk, after, y_ref, next_ref, x_ref, ln_ref, a_ref, w_ref, pick_ref,
     out_ref, next_grad_ref, ln_grad_ref, in_ref, back_ref, low_ref, g_ref,
 ):
     w_in_ref, w_out_ref = w_ref.at[0], w_ref.at[1]
-    g_ref[...] = norm_backward(after_ref[...], y_ref[...], next_ref, next_grad_ref)
+    g_ref[...] = norm_backward(after, y_ref[...], next_ref, next_grad_ref)
     low_ref[...] = g_ref[...].astype(jnp.bfloat16)
     total = jnp.zeros(g_ref.shape, jnp.float32)
     owners, size = in_ref.shape[:2]
@@ -454,16 +467,17 @@
     out_ref[...] = g_ref[...] + norm_backward(total, x_ref[...], ln_ref, ln_grad_ref)
 
 
-def ffn_backward(grad_after, stored, picks, owners, before=()):
+def ffn_backward(grad_after, stored, picks, owners, before=(), places=None):
     x, ln, weights, normed, out, ln_next = stored
     length, width = x.shape
     chunk = picks.shape[1]
     size = picks.shape[0] * weights.shape[1] // chunk // owners
     block = low(owners, size, width)
     return call(
-        partial(ffn_backward_kernel, chunk),
+        partial(ffn_backward_kernel, chunk, places is not None),
         (full(length, width), full(2, width), full(2, width), block, block),
         grad_after,
+        *(() if places is None else (places[None, :],)),
         out,
         ln_next,
         x,
@@ -480,11 +494,105 @@
     )
 
 
-def update_kernel(factor_ref, g_ref, basis_ref, w_ref, m_ref, v_ref, new_w_ref, new_m_ref, new_v_ref):
+def loss_forward_kernel(chunks, final_ref, pick_ref, label_ref, table_ref, picked_ref, stat_ref, logit_ref):
+    count, length = pick_ref.shape[0], final_ref.shape[0]
+    places = lax.broadcasted_iota(jnp.int32, (count, length), 1)
+    chosen = (places == pick_ref[...]).astype(jnp.bfloat16)
+    picked_ref[...] = dot_dims(chosen, final_ref[...], 1, 0).astype(jnp.bfloat16)
+    rows = table_ref.shape[0] // chunks
+    top = jnp.full((1, count), masked, jnp.float32)
+    label = jnp.zeros((1, count), jnp.float32)
+    for index in range(chunks):
+        span = slice(index * rows, (index + 1) * rows)
+        logits = dot_dims(table_ref[span, :], picked_ref[...], 1, 1)
+        logit_ref[span, :] = logits
+        top = jnp.maximum(top, jnp.max(logits, axis=0, keepdims=True))
+        hit = lax.broadcasted_iota(jnp.int32, logits.shape, 0) + index * rows == label_ref[...]
+        label = label + jnp.sum(jnp.where(hit, logits, 0.0), axis=0, keepdims=True)
+    total = jnp.zeros((1, count), jnp.float32)
+    for index in range(chunks):
+        span = slice(index * rows, (index + 1) * rows)
+        total = total + jnp.sum(jnp.exp(logit_ref[span, :] - top), axis=0, keepdims=True)
+    stat_ref[...] = jnp.concatenate([top, total, label, jnp.zeros((5, count), jnp.float32)], axis=0)
+
+
+def loss_forward(final, pick_rows, labels, table):
+    count, width = pick_rows.shape[0], final.shape[1]
+    return call(
+        partial(loss_forward_kernel, 8),
+        (low(count, width), full(8, count)),
+        final,
+        pick_rows[:, None],
+        labels[None, :],
+        table,
+        scratch=[pltpu.VMEM((table.shape[0], count), jnp.float32)],
+        microseconds=6,
+    )
+
+
+def loss_backward_kernel(
+    chunks, picked_ref, seen_ref, weight_ref, label_ref, table_ref, grad_ref, parts_ref, loss_ref
+):
+    tops, totals, labels = (
+        jnp.concatenate([seen_ref[k, m : m + 1, :] for k in range(seen_ref.shape[0])], axis=0)
+        for m in range(3)
+    )
+    top = jnp.max(tops, axis=0, keepdims=True)
+    total = top + jnp.log(jnp.sum(totals * jnp.exp(tops - top), axis=0, keepdims=True))
+    loss_ref[...] = (total - jnp.sum(labels, axis=0, keepdims=True)) * weight_ref[...]
+    rows = table_ref.shape[0] // chunks
+    columns = parts_ref.shape[2]
+    grad = jnp.zeros(grad_ref.shape, jnp.float32)
+    for index in range(chunks):
+        span = slice(index * rows, (index + 1) * rows)
+        logits = dot_dims(table_ref[span, :], picked_ref[...], 1, 1)
+        hit = lax.broadcasted_iota(jnp.int32, logits.shape, 0) + index * rows == label_ref[...]
+        slopes = weight_ref[...] * (jnp.exp(logits - total) - jnp.where(hit, 1.0, 0.0))
+        slopes = slopes.astype(jnp.bfloat16)
+        product = dot_dims(slopes, picked_ref[...], 1, 0).astype(jnp.bfloat16)
+        for owner in range(parts_ref.shape[0]):
+            parts_ref[owner, span, :] = product[:, owner * columns : (owner + 1) * columns]
+        grad = grad + dot_dims(slopes, table_ref[span, :], 0, 0)
+    grad_ref[...] = grad.astype(jnp.bfloat16)
+
+
+def loss_backward(picked, seen, weight, labels, table, owners):
+    count, width = picked.shape
+    return call(
+        partial(loss_backward_kernel, 8),
+        (low(count, width), low(owners, table.shape[0], width // owners), full(1, count)),
+        picked,
+        seen,
+        weight[None, :],
+        labels[None, :],
+        table,
+        microseconds=8,
+    )
+
+
+def adam_parts(weight, grad, moment, second):
+    moment = beta_one * moment + (1.0 - beta_one) * grad
+    second = beta_two * second + (1.0 - beta_two) * grad * grad
+    step = adam_direction(moment, second) + decay_rate * weight
+    return weight - rate_matrix * step, moment, second
+
+
+def update_kernel(*refs):
+    factor_ref, basis_ref, *ins = refs[:14]
+    outs = refs[14:]
+    factor = factor_ref[0]
+    for k in (0, 1):
+        grad_ref, weight_ref, moment_ref, second_ref = ins[4 * k : 4 * k + 4]
+        grad = grad_ref[...].astype(jnp.float32) * factor
+        results = adam_parts(weight_ref[...], grad, moment_ref[...], second_ref[...])
+        for ref, result in zip(outs[3 * k : 3 * k + 3], results):
+            ref[...] = result
+    g_ref, w_ref, m_ref, v_ref = ins[8:]
+    new_w_ref, new_m_ref, new_v_ref = outs[6:]
     high = basis_ref[0].astype(jnp.bfloat16)
     rest = (basis_ref[0] - high.astype(jnp.float32)).astype(jnp.bfloat16)
     grad = g_ref[0]
-    rotated = (dot_dims(grad, high, 1, 0) + dot_dims(grad, rest, 1, 0)) * factor_ref[0]
+    rotated = (dot_dims(grad, high, 1, 0) + dot_dims(grad, rest, 1, 0)) * factor
     moment = beta_one * m_ref[0] + (1.0 - beta_one) * rotated
     second = beta_two * v_ref[0] + (1.0 - beta_two) * rotated * rotated
     new_m_ref[0] = moment
@@ -500,19 +608,22 @@
     new_w_ref[0] = w_ref[0] - rate_matrix * (back + decay_rate * w_ref[0])
 
 
-def update_rotated(factor, grads, bases, weights, moments, seconds):
-    count, rows, width = weights.shape
-    block = pl.BlockSpec((1, rows, width), lambda k: (k, 0, 0))
-    square = pl.BlockSpec((1, width, width), lambda k: (k, 0, 0))
+def update_matrices(factor, bases, attn, table, ffn):
+    def blocks(array):
+        shape = (array.shape[0] // 4, *array.shape[1:])
+        return pl.BlockSpec(shape, lambda k: (k,) + (0,) * (len(shape) - 1))
+
+    arrays = (*attn, *table, *ffn)
+    results = [part for group in (attn, table, ffn) for part in group[1:]]
     return pl.pallas_call(
         update_kernel,
-        grid=(count,),
-        out_shape=(full(count, rows, width),) * 3,
-        in_specs=[smem, block, square, block, block, block],
-        out_specs=(block,) * 3,
+        grid=(4,),
+        out_shape=tuple(full(*part.shape) for part in results),
+        in_specs=[smem, blocks(bases)] + [blocks(part) for part in arrays],
+        out_specs=tuple(blocks(part) for part in results),
         compiler_params=pltpu.CompilerParams(vmem_limit_bytes=56 * 2**20),
-        cost_estimate=cost_of(10),
-    )(factor.reshape(1), grads, bases, weights, moments, seconds)
+        cost_estimate=cost_of(20),
+    )(factor.reshape(1), bases, *arrays)
 
 
 def small_factor(block):
@@ -951,27 +1062,30 @@
     def place_of(index):
         return pl.ds(pl.multiple_of(side * half + index // 2 * share, share), share)
 
-    def weight_place(ref, own_ref, origin):
+    def send_weights(ref, own_ref, slot, span):
         count, rows = own_ref.shape[0] // 2, own_ref.shape[1]
-        return ref.at[pl.ds(side * count, count), pl.ds(pl.multiple_of(origin * rows, rows), rows)]
-
-    def send_weights(ref, own_ref, slot):
-        mine = own_ref.at[pl.ds(side * (own_ref.shape[0] // 2), own_ref.shape[0] // 2)]
-        return [
-            push(mine, weight_place(ref, own_ref, me), (s5, r5), slot + step - 1, "dp", to)
+        mine = pl.ds(side * count, count)
+
+        def place(origin):
+            return ref.at[mine, pl.ds(pl.multiple_of(origin * rows + span[0], span[1]), span[1])]
+
+        copies = [
+            push(own_ref.at[mine, pl.ds(*span)], place(me), (s5, r5), slot + step - 1, "dp", to)
             for step, to, _ in owners
         ]
-
-    def relay_weights(ref, own_ref, copies, slot):
+        return [(copy, place(origin), slot + step - 1) for copy, (step, _, origin) in zip(copies, owners)]
+
+    def relay_weights(sent):
         relays = []
-        for copy, (step, _, origin) in zip(copies, owners):
+        for copy, place, slot in sent:
             copy.wait()
-            place = weight_place(ref, own_ref, origin)
-            relays.append(push(place, place, (s6, r6), slot + step - 1, "vocab", near))
+            relays.append(push(place, place, (s6, r6), slot, "vocab", near))
         return relays
 
     first = push(x_ref.at[:, half_of(1 - side)], near_ref, (s0, r0), 0, "vocab", near)
-    attn_copies = send_weights(attn_out_ref, attn_ref, 0)
+    some = ffn_ref.shape[1] // 2
+    early = send_weights(attn_out_ref, attn_ref, 0, (0, attn_ref.shape[1]))
+    early += send_weights(ffn_out_ref, ffn_ref, len(owners), (0, some))
     for ref, own_ref in ((attn_out_ref, attn_ref), (ffn_out_ref, ffn_ref)):
         rows = own_ref.shape[1]
         ref[:, pl.ds(pl.multiple_of(me * rows, rows), rows), :] = own_ref[...]
@@ -1001,7 +1115,7 @@
     row_ref[me, place_of(here)] = blocks_ref[me]
     for copy in copies:
         copy.wait()
-    ffn_copies = send_weights(ffn_out_ref, ffn_ref, len(owners))
+    late = send_weights(ffn_out_ref, ffn_ref, 2 * len(owners), (some, some))
     mine = row_ref.at[:, place_of(here)]
     copies = [push(mine, mine, (s3, r3), slot, "vocab", to) for slot, to, _ in others]
     close = [push(mine, mine, (s4, r4), 0, "vocab", near)]
@@ -1009,13 +1123,13 @@
         copy.wait()
         theirs = row_ref.at[:, place_of(origin)]
         close.append(push(theirs, theirs, (s4, r4), slot + 1, "vocab", near))
-    close += relay_weights(attn_out_ref, attn_ref, attn_copies, 0)
+    close += relay_weights(early)
     for copy in close[: pairs]:
         copy.wait()
     for owner in range(count):
         band = slice(owner * columns, (owner + 1) * columns)
         out_ref[:, band] = row_ref[owner].astype(jnp.float32) * scale + place_ref[:, band]
-    close += relay_weights(ffn_out_ref, ffn_ref, ffn_copies, len(owners))
+    close += relay_weights(late)
     for copy in close[pairs:]:
         copy.wait()
 
@@ -1045,8 +1159,8 @@
         + sem_pair(owners - 1)
         + sem_pair(pairs - 1)
         + sem_pair(pairs)
-        + sem_pair(2 * owners - 2)
-        + sem_pair(2 * owners - 2),
+        + sem_pair(3 * owners - 3)
+        + sem_pair(3 * owners - 3),
         microseconds=50,
     )
 
@@ -1070,11 +1184,6 @@
 def pick_weights(target_seg, pick_rows):
     sentence = jnp.take(target_seg, pick_rows, axis=0)
     return jnp.sum((sentence[:, None] == sentence[None, :]).astype(jnp.float32), axis=1)
-
-
-def combine_stats(tops, totals, chosen):
-    top = jnp.max(tops, axis=0)
-    return top, jnp.sum(totals * jnp.exp(tops - top), axis=0), jnp.sum(chosen, axis=0)
 
 
 def adam_direction(moment, second):
@@ -1125,7 +1234,6 @@
     norm_rows = jnp.swapaxes(norm_rows, 0, 1).reshape(16, -1)
     norms = [jnp.stack([norm_rows[k], norm_rows[7 + k]]) for k in range(7)]
     vocab_count, width = embedding.shape[0], attn_w.shape[2]
-    columns = replica * vocab_count + jnp.arange(vocab_count)
     source, source_seg, target, target_seg = (src_ids[0], src_seg[0], tgt_ids[0], tgt_seg[0])
     pick_rows, labels = (pick_pos[0], pick_label[0])
     length = source.shape[0]
@@ -1160,9 +1268,10 @@
         enc_in, norms[0], ((enc_attn_w,), 0, 0), source_seg, source_seg, None, False
     )
     self_w, cross_w, dec_ffn_w, ready = late_weights(attn_w[4:], ffn_w[2:], enc_in, enc_mid)
-    table_low = lax.all_gather(after(own_table, ready), "dp", axis=1, tiled=True)
     enc_out, encoded, enc_ffn = ffn_forward(enc_mid, norms[1], norms[2], ((enc_ffn_w,), 0, 0))
     target_rows = swap_owners(target_sum.reshape(owners, length, -1), 3)
+    table_low = after(own_table, ready)
+    table_low = lax.all_gather(after(table_low, target_rows[0, 0, 0]), "dp", axis=1, tiled=True)
     target_rows = jnp.swapaxes(target_rows, 0, 1).reshape(length, -1).astype(jnp.float32)
     dec_in = target_rows * embed_scale + positional
     dec_mid, dec_self = attn_forward(
@@ -1173,38 +1282,24 @@
     )
     dec_out, final_low, dec_ffn = ffn_forward(dec_late, norms[5], norms[6], dec_ffn_w)
 
-    chosen_rows = one_hot(pick_rows, jnp.arange(length))
-    picked = dot_dims(chosen_rows, final_low, 1, 0).astype(jnp.bfloat16)
-    logits = dot_dims(picked, table_low, 1, 1)
-    row_top = jnp.max(logits, axis=-1)
-    row_total = jnp.sum(jnp.exp(logits - row_top[:, None]), axis=-1)
-    label_hit = labels[:, None] == columns[None, :]
-    chosen = jnp.sum(jnp.where(label_hit, logits, 0.0), axis=-1)
-    seen = jnp.pad(jnp.stack([row_top, row_total, chosen]), ((0, 5), (0, 0)))
-    (seen,) = gather_small("vocab", 4, seen)
-    row_top, row_total, chosen = combine_stats(seen[:, 0], seen[:, 1], seen[:, 2])
-    log_total = row_top + jnp.log(row_total)
+    own_labels = labels - replica * vocab_count
+    picked, own_stats = loss_forward(final_low, pick_rows, own_labels, table_low)
+    (seen,) = gather_small("vocab", 4, own_stats)
     weight = 1.0 / pick_weights(target_seg, pick_rows)
-    loss_part = jnp.sum((log_total - chosen) * weight)
+    grad_picked, table_parts, losses = loss_backward(
+        picked, seen, weight, own_labels, table_low, owners
+    )
+    grad_table = lax.psum_scatter(table_parts, "dp", scatter_dimension=0, tiled=False)
+    grad_picked = sum_vocab(grad_picked, 5)
+    loss_part = jnp.sum(losses)
     count_part = (target_seg[-1] + 1).astype(jnp.float32)
-    grad_logits = (
-        weight[:, None] * (jnp.exp(logits - log_total[:, None]) - label_hit.astype(jnp.float32))
-    ).astype(jnp.bfloat16)
-    grad_picked = sum_vocab(dot_dims(grad_logits, table_low, 1, 0).astype(jnp.bfloat16), 5)
-    grad_table = [
-        dot_dims(grad_logits, part, 0, 0).astype(jnp.bfloat16)
-        for part in jnp.split(picked, owners, axis=1)
-    ]
-    table_parts = jnp.stack(grad_table)
-    grad_table = lax.psum_scatter(table_parts, "dp", scatter_dimension=0, tiled=False)
-    grad_final = dot_dims(chosen_rows, grad_picked, 0, 0)
 
     picks = share_selector(width, owners, replicas, replica, width)
     hidden = ffn_w.shape[1] * owners
     hidden_picks = share_selector(hidden, owners, replicas, replica, 512)
     norm_grads = [None] * 7
     grad, norm_grads[6], norm_grads[5], *ffn_blocks = ffn_backward(
-        grad_final, dec_ffn, hidden_picks, owners, before=(table_parts,)
+        grad_picked, dec_ffn, hidden_picks, owners, places=pick_rows
     )
     grad, norm_grads[4], block, grad_encoded = attn_backward(grad, dec_cross, picks, owners, None)
     early = lax.psum_scatter(
@@ -1247,7 +1342,7 @@
 
     early = by_matrix(early, 3)
     g_attn = [by_matrix(part, 4) for part in (late[0], late[1], early[0])]
-    g_attn = jnp.concatenate(g_attn).astype(jnp.float32)
+    g_attn = jnp.concatenate(g_attn)
     g_ffn = jnp.concatenate([late[2:].reshape(2, -1, width), early[1:]])
 
     matrix = replica // 2
@@ -1255,7 +1350,7 @@
     own_products = dot_dims(own_grad, own_grad, 0, 0)
     g_ffn_low, g_ffn = g_ffn, g_ffn.astype(jnp.float32)
     first_copy = (replica == 0).astype(jnp.float32)
-    layer_sq = jnp.sum(g_attn * g_attn) + jnp.sum(g_ffn * g_ffn) + jnp.sum(g_norm * g_norm)
+    layer_sq = jnp.sum(jnp.square(g_attn.astype(jnp.float32))) + jnp.sum(g_ffn * g_ffn) + jnp.sum(g_norm * g_norm)
     raw_squares = jnp.sum(g_embed * g_embed) + first_copy * layer_sq
     few = jnp.stack([first_copy * loss_part, first_copy * count_part, raw_squares])
     few = jnp.broadcast_to(jnp.pad(few, (0, 5))[:, None], (8, 128))
@@ -1263,33 +1358,32 @@
     loss_sum, sentences, squares = few[0, 0], few[1, 0], few[2, 0]
     grad_norm = jnp.sqrt(squares) / sentences
     factor = jnp.minimum(1.0, clip_limit / (grad_norm + norm_eps)) / sentences
-    g_attn, g_norm, g_embed = (
-        g_attn * factor,
-        g_norm * factor,
-        g_embed * factor,
-    )
+    g_norm = g_norm * factor
 
     def all_matrices(own):
         rows = own.shape[0] // 2
         half = lax.dynamic_slice_in_dim(own.astype(jnp.bfloat16), replica % 2 * rows, rows, 0)
-        return lax.all_gather(half, "vocab").reshape(4, 2 * rows, -1).astype(jnp.float32)
+        return lax.all_gather(half, "vocab").reshape(4, 2 * rows, -1)
 
     all_products = all_matrices(own_products)
     new_stats = stat_decay * soap_stats + (1.0 - stat_decay) * (factor * factor) * (
-        all_products
+        all_products.astype(jnp.float32)
     )
     own_stat = stat_decay * lax.dynamic_index_in_dim(soap_stats, matrix, 0, keepdims=False) + (
         1.0 - stat_decay
     ) * (factor * factor) * own_products
     own_basis = renew_basis(own_stat, lax.dynamic_index_in_dim(soap_basis, matrix, 0, keepdims=False))
-    new_basis = all_matrices(own_basis)
-
-    new_attn, m_attn, v_attn = adam_update(attn_w, g_attn, attn_m, attn_v, rate_matrix, decay_rate)
+    new_basis = all_matrices(after(own_basis, new_stats[0, 0, 0])).astype(jnp.float32)
+
     new_norm, m_norm, v_norm = adam_update(norm_p, g_norm, norm_m, norm_v, rate_vector, 0.0)
-    new_embed, m_embed, v_embed = adam_update(
-        embedding, g_embed, embed_m, embed_v, rate_matrix, decay_rate
-    )
-    new_ffn, m_ffn, v_ffn = update_rotated(factor, g_ffn_low, soap_basis, ffn_w, ffn_m, ffn_v)
+    updated = update_matrices(
+        factor,
+        soap_basis,
+        (g_attn, attn_w, attn_m, attn_v),
+        (g_embed, embedding, embed_m, embed_v),
+        (g_ffn_low, ffn_w, ffn_m, ffn_v),
+    )
+    new_attn, m_attn, v_attn, new_embed, m_embed, v_embed, new_ffn, m_ffn, v_ffn = updated
     return (
         loss_sum,
         sentences,

time: 649 us -> 627 us (0.966)
  other arithmetic: 80.5 us -> 57.7 us
  Pallas kernels: 406 us -> 424 us
  matrix products: 49 us -> 32.2 us
    all_gather x3, waiting for transfers between devices: 21.1 us -> 0.02 us  [the longest x2 0.02 us: all_matrices(): return lax.all_gather(half, 'vocab').reshape(4, 2 * rows, -1)]
    pallas_call x11 -> x13, Pallas kernels: 225 us -> 242 us  [call(): pl.pallas_call(body, out_shape=outs, in_specs=[vmem] * (len(args) - smem_...]
    dot_general x10 -> x2, matrix products: 32.6 us -> 15.8 us  [dot_dims(): lax.dot_general(left, right, (((left_dim,), (right_dim,)), ((), ())), pre...]
    psum x1, waiting for transfers between devices: 7.39 us -> 23.6 us  [body(): target_sum = lax.psum(target_part, 'vocab')]
    pallas_call x1, Pallas kernels: 14.5 us -> 28.5 us  [update_matrices(): pl.pallas_call(update_kernel, grid=(4,), out_shape=tuple((full(*part.shap...]
    pallas_call x7, Pallas kernels: 166 us -> 154 us  [talk(): pl.pallas_call(body, out_shape=outs, in_specs=[vmem] * len(args) + [pl.Bl...]
    sub x3 -> x1, other arithmetic: 13.1 us -> 0.63 us  [adam_update(): weight - step_rate * (adam_direction(moment, second) + decay_weight * wei...]
  transfers between devices with their start and end apart: 13 -> 13, of which waited for: 3 -> 2; matrix products, arithmetic and copies ran while one was open for 11% -> 7% of each run, Pallas kernels for 39% -> 46%
where the time goes in v6:
time: 627 us; the launch traced here: 616 us
  Pallas kernels  424 us (68%)
  other arithmetic  57.7 us (9%)
  local copies, waits for them, and re-layouts  37.5 us (6%)
  matrix products  32.2 us (5%)
  waiting for transfers between devices  30.4 us (5%)
  between operations  29 us (5%)
    pallas_call x13, Pallas kernels, call(): pl.pallas_call(body, out_shape=outs, in_specs=[vmem] * (len(args) - smem_...  242 us
    pallas_call x7, Pallas kernels, talk(): pl.pallas_call(body, out_shape=outs, in_specs=[vmem] * len(args) + [pl.Bl...  154 us
    pallas_call x1, Pallas kernels, update_matrices(): pl.pallas_call(update_kernel, grid=(4,), out_shape=tuple((full(*part.shap...  28.5 us
    psum x1, waiting for transfers between devices, body(): target_sum = lax.psum(target_part, 'vocab')  23.6 us
    dot_general x2, matrix products, look_up(): lax.dot_general(one_hot(place, halves), paired, (((1,), (0,)), ((), ())))  16.4 us
    dot_general x2, matrix products, dot_dims(): lax.dot_general(left, right, (((left_dim,), (right_dim,)), ((), ())), pre...  15.8 us
  transfers between devices with their start and end apart: 13, of which 2 were waited for; matrix products, arithmetic and copies ran while one was open for 7% of the time, Pallas kernels for 46%

profile of v6, /device:TPU:0, one launch (start us, length us, event | category | flops | bytes accessed | tf_op | source)
XLA Modules:
  0.0 615.5 jit_solution(258414388599254237)
XLA Ops:
  9.9 7.9 %shard_map.332 = (s32[4,2,1024]{2,1,0:T(2,128)}, f32[4,16,128]{2,1,0:T(8,128)}) custom-call(s32[2,1024]{1,0:T(2,128)} %pad_add_fusion.refs_0_, f32[16,128]{1,0:T(8,128)} %pad_convert_fusion.refs_1_), custom_call_target="tpu_custom_call" | custom-call | flops 15000000512 | tf_op jit(solution)/shard_map/pallas_call | solution.py:744
  25.9 8.9 %fusion.2 = bf16[4096,256]{1,0:T(8,128)(2,1)S(1)} fusion(s32[4096]{0:T(1024)S(1)} %fusion.18, bf16[2368,128]{1,0:T(8,128)(2,1)} %get-tuple-element.202, bf16[2368,128]{1,0:T(8,128)(2,1)} %get-tuple-element.201), kind=kOutput, calls=%fused_computation.6 | convolution fusion | flops 4978180096 | bytes 3325952 | tf_op jit(solution)/shard_map/dot_general | solution.py:1252
  34.8 2.9 slice_select_fusion
  37.7 49.5 %shard_map.333 = (f32[1024,512]{1,0:T(8,128)}, bf16[4,512,512]{2,1,0:T(8,128)(2,1)}, bf16[2,2048,512]{2,1,0:T(8,128)(2,1)}) custom-call(bf16[4,1024,128]{2,1,0:T(8,128)(2,1)} %bitcast.170, f32[1024,512]{1,0:T(8,128)} %constant.204.clone.refs_1_, bf16[4,128,512]{2,1,0:T(8,128)(2,1)} %get-tuple-element.200.refs_2_, bf16[2,512,512]{2,1,0:T(8,128)(2,1)} %slice.291.refs_3_), custom_call_target="tpu_custom_call" | custom-call | flops 49999998976 | tf_op jit(solution)/shard_map/pallas_call | solution.py:744
  92.1 7.6 %fusion.1 = bf16[4096,256]{1,0:T(8,128)(2,1)S(1)} fusion(s32[4096]{0:T(1024)S(1)} %fusion.17, bf16[2368,128]{1,0:T(8,128)(2,1)S(1)} %copy-done.17, bf16[2368,128]{1,0:T(8,128)(2,1)S(1)} %copy-done.16), kind=kOutput, calls=%fused_computation.5 | convolution fusion | flops 4978180096 | bytes 3325952 | tf_op jit(solution)/shard_map/dot_general | solution.py:1252
  99.7 2.9 slice_select_fusion.1
  108.3 19.1 %shard_map.335 = (f32[1024,512]{1,0:T(8,128)}, bf16[1024,512]{1,0:T(8,128)(2,1)}, bf16[512,1024]{1,0:T(8,128)(2,1)}, bf16[512,1024]{1,0:T(8,128)(2,1)}, bf16[512...) custom-call(f32[1024,512]{1,0:T(8,128)} %get-tuple-element.99.refs_0_.refs_1_, ...), custom_call_target="tpu_custom_call" | custom-call | flops 20000000000 | tf_op jit(solution)/shard_map/pallas_call | solution.py:57
  130.9 6.6 %collective-permute-done.2.refs_7_.refs_8_.refs_6_ = bf16[1024,512]{1,0:T(8,128)(2,1)} collective-permute-done((bf16[1024,512]{1,0:T(8,128)(2,1)}, bf16[1024,512]{1,0:T(8,128)(2,1)}, u32[]{:S(2)}, u32[]{:S(2)}) %collective-permute-start.2) | collective-permute-done | bytes 1048608 | tf_op jit(solution)/shard_map/ppermute | solution.py:174
  137.5 23.6 %all-reduce.6.cloned.1.call-done.refs_0_ = bf16[4,1024,128]{2,1,0:T(8,128)(2,1)} async-done(((bf16[4,1024,128]{2,1,0:T(8,128)(2,1)}), bf16[4,1024,128]{2,1,0:T(8,128)(2,1)}) %all-reduce.6.cloned.1.call-update) | async-done | bytes 1048592 | tf_op jit(solution)/shard_map/psum | solution.py:1266
  161.1 12.0 %shard_map.334 = bf16[4,1024,128]{2,1,0:T(8,128)(2,1)} custom-call(bf16[4,1024,128]{2,1,0:T(8,128)(2,1)} %all-reduce.6.cloned.1.call-done.refs_0_), custom_call_target="tpu_custom_call" | custom-call | flops 15000000512 | tf_op jit(solution)/shard_map/pallas_call | solution.py:744
  180.1 11.0 %shard_map.337 = (f32[1024,512]{1,0:T(8,128)}, bf16[1024,512]{1,0:T(8,128)(2,1)}, bf16[1024,512]{1,0:T(8,128)(2,1)}) custom-call(f32[1024,512]{1,0:T(8,128)} %get-tuple-element.104.refs_0_.refs_3_, f32[2,512]{1,0:T(2,128)} %get-tuple-element.232.refs_1_.refs_4_, f32[2,512]{1,0:T(2,128)} %pad_maximum_fusion.12.refs_2_, ...), custom_call_target="tpu_custom_call" | custom-call | flops 12000000000 | tf_op jit(solution)/shard_map/pallas_call | solution.py:57
  198.5 18.9 %shard_map.336 = (f32[1024,512]{1,0:T(8,128)}, bf16[1024,512]{1,0:T(8,128)(2,1)}, bf16[512,1024]{1,0:T(8,128)(2,1)}, bf16[512,1024]{1,0:T(8,128)(2,1)}, bf16[512...) custom-call(f32[1024,512]{1,0:T(8,128)} %copy_bitcast_fusion.refs_0_.refs_1_, ...), custom_call_target="tpu_custom_call" | custom-call | flops 20000000000 | tf_op jit(solution)/shard_map/pallas_call | solution.py:57
  217.4 19.9 %shard_map.338 = (f32[1024,512]{1,0:T(8,128)}, bf16[1024,512]{1,0:T(8,128)(2,1)}, bf16[512,1024]{1,0:T(8,128)(2,1)}, bf16[512,1024]{1,0:T(8,128)(2,1)}, bf16[512...) custom-call(f32[1024,512]{1,0:T(8,128)} %get-tuple-element.108.refs_0_.refs_1_,, ...), custom_call_target="tpu_custom_call" | custom-call | flops 20000000000 | tf_op jit(solution)/shard_map/pallas_call | solution.py:57
  237.3 13.9 %shard_map.339 = (f32[1024,512]{1,0:T(8,128)}, bf16[1024,512]{1,0:T(8,128)(2,1)}, bf16[1024,512]{1,0:T(8,128)(2,1)}, bf16[2,2048,512]{2,1,0:T(8,128)(2,1)}) custom-call(f32[1024,512]{1,0:T(8,128)} %get-tuple-element.111.refs_0_.refs_4_, f32[2,512]{1,0:T(2,128)} %get-tuple-element.233.refs_1_.refs_5_, f32[2,512]{1,0:T(2,128)} %get-tuple-element.234.refs_2_.refs_3_, ...), custom_call_target="tpu_custom_call" | custom-call | flops 12000000000 | tf_op jit(solution)/shard_map/pallas_call | solution.py:57
  251.2 6.3 %shard_map.340 = (bf16[256,512]{1,0:T(8,128)(2,1)}, f32[8,256]{1,0:T(8,128)}) custom-call(bf16[1024,512]{1,0:T(8,128)(2,1)} %get-tuple-element.112.refs_0_, s32[256,1]{1,0:T(8,128)} %copy.60.refs_1_, s32[1,256]{1,0:T(1,128)} %broadcast_subtract_fusion.refs_2_.refs_3_, bf16[4736,512]{1,0:T(8,128)(2,1)} %all-gather.7.cloned.1.call-done.refs_3_.refs_4_), custom_call_target="tpu_custom_call" | custom-call | flops 6000000000 | tf_op jit(solution)/shard_map/pallas_call | solution.py:57
  257.5 6.9 %shard_map.341.refs_1_ = f32[8,8,256]{2,1,0:T(8,128)} custom-call(f32[8,256]{1,0:T(8,128)} %get-tuple-element.114.refs_0_), custom_call_target="tpu_custom_call" | custom-call | flops 15000000512 | tf_op jit(solution)/shard_map/pallas_call | solution.py:744
  264.5 10.3 %shard_map.342 = (bf16[256,512]{1,0:T(8,128)(2,1)}, bf16[4,4736,128]{2,1,0:T(8,128)(2,1)}, f32[1,256]{1,0:T(1,128)}) custom-call(bf16[256,512]{1,0:T(8,128)(2,1)} %get-tuple-element.113.refs_0_, f32[8,8,256]{2,1,0:T(8,128)} %shard_map.341.refs_1_, f32[1,256]{1,0:T(1,128)} %bitcast.191, s32[1,256]{1,0:T(1,128)} %broadcast_subtract_fusion.refs_2_.refs_3_, ...), custom_call_target="tpu_custom_call" | custom-call | flops 8000000000 | tf_op jit(solution)/shard_map/pallas_call | solution.py:57
  279.1 16.1 %shard_map.343.refs_0_ = bf16[256,512]{1,0:T(8,128)(2,1)} custom-call(bf16[256,512]{1,0:T(8,128)(2,1)} %get-tuple-element.115.refs_0_), custom_call_target="tpu_custom_call" | custom-call | flops 15000000512 | tf_op jit(solution)/shard_map/pallas_call | solution.py:744
  295.2 19.9 %shard_map.344 = (f32[1024,512]{1,0:T(8,128)}, f32[2,512]{1,0:T(2,128)}, f32[2,512]{1,0:T(2,128)}, bf16[4,64,512]{2,1,0:T(8,128)(2,1)}, bf16[4,64,512]{2,1,0:T(8,128)(2,1)}) custom-call(bf16[256,512]{1,0:T(8,128)(2,1)} %shard_map.343.refs_0_, s32[1,256]{1,0:T(1,128)} %refs_1_.3, f32[1024,512]{1,0:T(8,128)} %get-tuple-element.116.refs_2_, ...), custom_call_target="tpu_custom_call" | custom-call | flops 16999999488 | tf_op jit(solution)/shard_map/pallas_call | solution.py:57
  315.1 25.6 %shard_map.345 = (f32[1024,512]{1,0:T(8,128)}, f32[2,512]{1,0:T(2,128)}, bf16[4,64,512]{2,1,0:T(8,128)(2,1)}, f32[1024,512]{1,0:T(8,128)}) custom-call(f32[1024,512]{1,0:T(8,128)} %get-tuple-element.119.refs_0_, f32[1024,512]{1,0:T(8,128)} %get-tuple-element.108.refs_0_.refs_1_, f32[2,512]{1,0:T(2,128)} %get-tuple-element.230.refs_1_.refs_2_, ...), custom_call_target="tpu_custom_call" | custom-call | flops 24999999488 | tf_op jit(solution)/shard_map/pallas_call | solution.py:57
  342.6 23.3 %shard_map.346 = (f32[1024,512]{1,0:T(8,128)}, f32[2,512]{1,0:T(2,128)}, bf16[4,64,512]{2,1,0:T(8,128)(2,1)}, bf16[4,1024,128]{2,1,0:T(8,128)(2,1)}) custom-call(f32[1024,512]{1,0:T(8,128)} %get-tuple-element.131.refs_0_, f32[1024,512]{1,0:T(8,128)} %copy_bitcast_fusion.refs_0_.refs_1_, f32[2,512]{1,0:T(2,128)} %get-tuple-element.229.refs_1_.refs_2_, ...), custom_call_target="tpu_custom_call" | custom-call | flops 24999999488 | tf_op jit(solution)/shard_map/pallas_call | solution.py:57
  365.9 19.9 %shard_map.347 = (f32[1024,512]{1,0:T(8,128)}, f32[2,512]{1,0:T(2,128)}, f32[2,512]{1,0:T(2,128)}, bf16[4,64,512]{2,1,0:T(8,128)(2,1)}, bf16[4,64,512]{2,1,0:T(8,128)(2,1)}) custom-call(f32[1024,512]{1,0:T(8,128)} %get-tuple-element.127.refs_0_, f32[1024,512]{1,0:T(8,128)} %get-tuple-element.128.refs_1_, f32[2,512]{1,0:T(2,128)} %pad_maximum_fusion.12.refs_2_, ...), custom_call_target="tpu_custom_call" | custom-call | flops 16999999488 | tf_op jit(solution)/shard_map/pallas_call | solution.py:57
  393.0 25.0 %shard_map.348 = (f32[1024,512]{1,0:T(8,128)}, f32[2,512]{1,0:T(2,128)}, bf16[4,64,512]{2,1,0:T(8,128)(2,1)}, bf16[4,1024,128]{2,1,0:T(8,128)(2,1)}) custom-call(f32[1024,512]{1,0:T(8,128)} %get-tuple-element.140.refs_0_, f32[1024,512]{1,0:T(8,128)} %get-tuple-element.99.refs_0_.refs_1_, f32[2,512]{1,0:T(2,128)} %get-tuple-element.231.refs_1_.refs_2_, ...), custom_call_target="tpu_custom_call" | custom-call | flops 24999999488 | tf_op jit(solution)/shard_map/pallas_call | solution.py:57
  423.1 37.7 %shard_map.349 = (bf16[4,8,64,512]{3,2,1,0:T(8,128)(2,1)}, bf16[4,1024,128]{2,1,0:T(8,128)(2,1)}, bf16[4,1024,128]{2,1,0:T(8,128)(2,1)}, f32[4,16,128]{2,1,0:T(8,128)}) custom-call(bf16[4,64,512]{2,1,0:T(8,128)(2,1)} %get-tuple-element.150.refs_0_, bf16[4,64,512]{2,1,0:T(8,128)(2,1)} %get-tuple-element.151.refs_1_, ...), custom_call_target="tpu_custom_call" | custom-call | flops 40000000000 | tf_op jit(solution)/shard_map/pallas_call | solution.py:744
  466.8 4.3 bitcast_select_fusion.1
  471.1 14.2 %fusion = f32[2368,256]{1,0:T(8,128)S(1)} fusion(s32[8192]{0:T(1024)S(1)} %fusion.16, bf16[8192,128]{1,0:T(8,128)(2,1)S(1)} %get-tuple-element.193, bf16[8192,128]{1,0:T(8,128)(2,1)S(1)} %get-tuple-element.192), kind=kOutput, calls=%fused_computation.2 | convolution fusion | flops 9959899136 | bytes 6651904 | tf_op jit(solution)/shard_map/dot_general | solution.py:34
  489.6 3.9 multiply_reduce_fusion.1
  495.4 4.2 multiply_reduce_fusion.2
  501.1 23.3 %shard_map.350 = (f32[512,512]{1,0:T(8,128)}, f32[8,128]{1,0:T(8,128)}) custom-call(f32[512,512]{1,0:T(8,128)} %fusion.11.refs_0_, f32[8,128]{1,0:T(8,128)} %broadcast_in_dim.107.refs_1_), custom_call_target="tpu_custom_call" | custom-call | flops 15000000512 | tf_op jit(solution)/shard_map/pallas_call | solution.py:744
  534.8 29.0 %shard_map.352 = f32[512,512]{1,0:T(8,128)} custom-call(f32[512,512]{1,0:T(8,128)} %bitcast_add_fusion.refs_0_, f32[512,512]{1,0:T(8,128)} %dynamic-slice_bitcast_fusion.refs_1_), custom_call_target="tpu_custom_call" | custom-call | flops 28999999488 | tf_op jit(solution)/shard_map/pallas_call | solution.py:57
  574.5 28.5 %shard_map.351 = (f32[12,128,512]{2,1,0:T(8,128)}, f32[12,128,512]{2,1,0:T(8,128)}, f32[12,128,512]{2,1,0:T(8,128)}, f32[4736,128]{1,0:T(8,128)}, f32[4736,128]{...) custom-call(f32[1]{0:T(128)} %bitcast.74.refs_0_, ...), custom_call_target="tpu_custom_call" | custom-call | flops 20000000000 | tf_op jit(solution)/shard_map/pallas_call | solution.py:618
  603.0 4.2 convert.13
  (212 shorter events, 79.4 us)
Async XLA Ops:
  7.2 153.9 %all-reduce.6.cloned.1.call-start = ((), (), s32[]{:S(2)}) async-start(), calls=%async_computation.2 | async-start | bytes 2097152 | tf_op jit(solution)/shard_map/psum | solution.py:1266
  9.9 10.0 %copy-start.8 = (f32[4,512,512]{2,1,0:T(8,128)S(1)}, f32[4,512,512]{2,1,0:T(8,128)}, u32[]{:S(2)}) copy-start(f32[4,512,512]{2,1,0:T(8,128)} %refs_11_.1) | copy-start | bytes 12582916
  37.7 49.6 %copy-start.3 = (bf16[4,128,512]{2,1,0:T(8,128)(2,1)S(1)}, bf16[4,128,512]{2,1,0:T(8,128)(2,1)}, u32[]{:S(2)}) copy-start(bf16[4,128,512]{2,1,0:T(8,128)(2,1)} %get-tuple-element.198) | copy-start | bytes 1572868
  37.7 49.6 %copy-start.5 = (bf16[4,128,512]{2,1,0:T(8,128)(2,1)S(1)}, bf16[4,128,512]{2,1,0:T(8,128)(2,1)}, u32[]{:S(2)}) copy-start(bf16[4,128,512]{2,1,0:T(8,128)(2,1)} %get-tuple-element.199) | copy-start | bytes 1572868
  87.2 4.8 copy-start.16
  87.2 4.8 copy-start.17
  88.5 42.3 %collective-permute-start = (bf16[1024,512]{1,0:T(8,128)(2,1)}, bf16[1024,512]{1,0:T(8,128)(2,1)}, u32[]{:S(2)}, u32[]{:S(2)}) collective-permute-start(bf16[1024,512]{1,0:T(8,128)(2,1)} %maximum_select_fusion), channel_id=1, source_target_pairs={{0,8},{8,0},{16,24},{24,16},{1,9},{9,1},{17,25},{25,17},{2,10},{10... | collective-permute-start | bytes 3145736 | tf_op jit(solution)/shard_map/ppermute | solution.py:174
  89.5 41.3 %collective-permute-start.1 = (bf16[1024,512]{1,0:T(8,128)(2,1)}, bf16[1024,512]{1,0:T(8,128)(2,1)}, u32[]{:S(2)}, u32[]{:S(2)}) collective-permute-start(bf16[1024,512]{1,0:T(8,128)(2,1)} %maximum_select_fusion), channel_id=1, source_target_pairs={{0,16},{8,24},{16,0},{24,8},{1,17},{9,25},{17,1},{25,9},{2,18},{10... | collective-permute-start | bytes 3145736 | tf_op jit(solution)/shard_map/ppermute | solution.py:174
  90.1 47.4 %collective-permute-start.2 = (bf16[1024,512]{1,0:T(8,128)(2,1)}, bf16[1024,512]{1,0:T(8,128)(2,1)}, u32[]{:S(2)}, u32[]{:S(2)}) collective-permute-start(bf16[1024,512]{1,0:T(8,128)(2,1)} %maximum_select_fusion), channel_id=1, source_target_pairs={{0,24},{8,16},{16,8},{24,0},{1,25},{9,17},{17,9},{25,1},{2,26},{10... | collective-permute-start | bytes 3145736 | tf_op jit(solution)/shard_map/ppermute | solution.py:174
  99.7 3.2 copy-start.29
  99.7 4.4 copy-start
  99.7 5.6 copy-start.25
  102.6 148.6 %all-gather.7.cloned.1.call-start = ((), (), s32[]{:S(2)}) async-start(), calls=%async_computation.3 | async-start | bytes 6062080 | tf_op jit(solution)/shard_map/all_gather | solution.py:1274
  108.3 19.1 %copy-start.26 = (s32[1,256]{1,0:T(1,128)S(1)}, s32[1,256]{1,0:T(1,128)}, u32[]{:S(2)}) copy-start(s32[1,256]{1,0:T(1,128)} %refs_1_.3) | copy-start | bytes 3076
  137.5 38.1 %collective-permute-start.5 = (bf16[1024,512]{1,0:T(8,128)(2,1)}, bf16[1024,512]{1,0:T(8,128)(2,1)}, u32[]{:S(2)}, u32[]{:S(2)}) collective-permute-start(bf16[1024,512]{1,0:T(8,128)(2,1)} %collective-permute-done.2.refs_7_.refs_8_.refs_6_), channel_id=1, source_target_pairs={{0,1},{1,0},{2,3},{3,2},{4,5},{5,4},{6,7},{7,6},{8,9},{9,8},{10,11... | collective-permute-start | bytes 3145736 | tf_op jit(solution)/shard_map/ppermute | solution.py:174
  179.2 186.7 %reduce-scatter.7.cloned.1.call-start = ((), (), s32[]{:S(2)}) async-start(), calls=%async_computation.7 | async-start | bytes 6062080
  180.1 11.5 %copy-start.37 = (s32[1,256]{1,0:T(1,128)S(1)}, s32[1,256]{1,0:T(1,128)}, u32[]{:S(2)}) copy-start(s32[1,256]{1,0:T(1,128)} %param.26) | copy-start | bytes 3076
  180.1 12.7 %copy-start.4 = (bf16[4,128,512]{2,1,0:T(8,128)(2,1)S(1)}, bf16[4,128,512]{2,1,0:T(8,128)(2,1)}, u32[]{:S(2)}) copy-start(bf16[4,128,512]{2,1,0:T(8,128)(2,1)} %get-tuple-element.198) | copy-start | bytes 1572868
  180.1 12.7 %copy-start.6 = (bf16[4,128,512]{2,1,0:T(8,128)(2,1)S(1)}, bf16[4,128,512]{2,1,0:T(8,128)(2,1)}, u32[]{:S(2)}) copy-start(bf16[4,128,512]{2,1,0:T(8,128)(2,1)} %get-tuple-element.199) | copy-start | bytes 1572868
  191.1 5.9 collective-permute-start.3
  191.4 5.6 collective-permute-start.4
  274.8 113.6 %reduce-scatter.9.cloned.1.call-start = ((), (), s32[]{:S(2)}) async-start(), calls=%async_computation.8 | async-start | bytes 983040
  315.1 25.6 %copy-start.20 = (bf16[4,64,512]{2,1,0:T(8,128)(2,1)S(1)}, bf16[4,64,512]{2,1,0:T(8,128)(2,1)}, u32[]{:S(2)}) copy-start(bf16[4,64,512]{2,1,0:T(8,128)(2,1)} %get-tuple-element.148) | copy-start | bytes 786436
  315.1 25.6 %copy-start.21 = (bf16[4,64,512]{2,1,0:T(8,128)(2,1)S(1)}, bf16[4,64,512]{2,1,0:T(8,128)(2,1)}, u32[]{:S(2)}) copy-start(bf16[4,64,512]{2,1,0:T(8,128)(2,1)} %get-tuple-element.149) | copy-start | bytes 786436
  342.6 75.3 %all-gather.9.cloned.1.call-start = ((), (), s32[]{:S(2)}) async-start(), calls=%async_computation.4 | async-start | bytes 1769472 | tf_op jit(solution)/shard_map/all_gather | solution.py:1315
  365.9 24.2 %copy-start.38 = (f32[1,256]{1,0:T(1,128)S(1)}, f32[1,256]{1,0:T(1,128)}, u32[]{:S(2)}) copy-start(f32[1,256]{1,0:T(1,128)} %get-tuple-element.164) | copy-start | bytes 3076
  390.0 173.8 %all-gather.11.cloned.1.call-start = ((), (), s32[]{:S(2)}) async-start(), calls=%async_computation.5 | async-start | bytes 2359296 | tf_op jit(solution)/shard_map/all_gather | solution.py:1366
  419.6 2.8 copy-start.30
  524.4 7.8 %copy-start.12 = (f32[512,512]{1,0:T(8,128)S(1)}, f32[512,512]{1,0:T(8,128)}, u32[]{:S(2)}) copy-start(f32[512,512]{1,0:T(8,128)} %get-tuple-element.175) | copy-start | bytes 3145732
  526.3 76.6 %all-gather.13.cloned.1.call-start = ((), (), s32[]{:S(2)}) async-start(), calls=%async_computation.6 | async-start | bytes 2359296 | tf_op jit(solution)/shard_map/all_gather | solution.py:1366
  563.8 2.8 copy-start.2
  566.6 4.9 copy-start.19
  (22 other events, 45.0 us)
Sparse Core Ops, SparseCore 0:
  102.7 58.2 all-reduce.5
  179.4 56.4 all-gather.6
  274.9 55.8 reduce-scatter.6
  342.7 26.3 reduce-scatter.8
  390.1 25.2 all-gather.8
  526.4 27.6 all-gather.10
  572.4 27.5 all-gather.12

commit v7 on v6

--- a/solution.py
+++ b/solution.py
@@ -906,10 +906,48 @@
     ]
 
 
-def gradient_kernel(chunks, count, *refs):
+def sum_tokens(rows_refs, place_ref, left_ref, table_ref, wide_ref, embed_ref, square_ref):
+    owners, length, columns = rows_refs[0].shape
+    for owner in range(owners):
+        for k, rows_ref in enumerate(rows_refs):
+            start = (owner * len(rows_refs) + k) * length
+            span = slice(start, start + length)
+            left = rows_ref[owner] * left_ref[span, :]
+            wide_ref[span, :columns] = left
+            wide_ref[span, columns:] = rows_ref[owner] - left
+    tokens, half = wide_ref.shape[0], embed_ref.shape[0] // 2
+    tile, step = half // 4, 1024
+    square_ref[...] = jnp.zeros(square_ref.shape, jnp.float32)
+
+    def one(index, carry):
+        start = index * tile
+        places = lax.broadcasted_iota(jnp.int32, (tile, step), 0) + start
+        total = jnp.zeros((tile, 2 * columns), jnp.float32)
+        for first in range(0, tokens, step):
+            chosen = (places == place_ref[:, first : first + step]).astype(jnp.bfloat16)
+            total = total + dot_dims(chosen, wide_ref[first : first + step, :], 1, 0)
+        for side in range(2):
+            span = pl.ds(pl.multiple_of(side * half + start, 16), tile)
+            part = total[:, side * columns : (side + 1) * columns]
+            part = part + table_ref[span, :].astype(jnp.float32)
+            embed_ref[span, :] = part
+            square_ref[...] += jnp.sum(part * part, axis=0, keepdims=True)
+        return carry
+
+    lax.fori_loop(0, 4, one, 0)
+
+
+def gradient_kernel(chunks, count, inside, *refs):
     x_refs, refs = refs[:chunks], refs[chunks:]
-    rows_refs, (out_ref, *refs) = refs[:count], refs[count:]
-    swapped_refs, (parts_ref, s0, r0, s1, r1, s2, r2, s3, r3, s4, r4) = refs[:count], refs[count:]
+    rows_refs, refs = refs[:count], refs[count:]
+    if inside:
+        (place_ref, left_ref, table_ref), refs = refs[:3], refs[3:]
+    (out_ref, square_ref, *refs) = refs
+    swapped_refs, refs = refs[:count], refs[count:]
+    if inside:
+        (embed_ref, embed_square_ref), refs = refs[:2], refs[2:]
+        *refs, wide_ref = refs
+    parts_ref, s0, r0, s1, r1, s2, r2, s3, r3, s4, r4 = refs
     owners = peers_of("dp")
     here, me = lax.axis_index("vocab"), lax.axis_index("dp")
     near = flip(here, 1)
@@ -954,12 +992,14 @@
     for rows_ref, swapped_ref in zip(rows_refs, swapped_refs):
         swapped_ref[me] = rows_ref[me]
     far, close = [], []
+    square = jnp.zeros(square_ref.shape, jnp.float32)
     for c in range(chunks):
         parts_ref[c, me] = x_refs[c][me]
         for copy in arriving[c]:
             copy.wait()
         total = jnp.sum(parts_ref[c].astype(jnp.float32), axis=0)
         out_ref[c, here] = total.astype(out_ref.dtype)
+        square = square + jnp.sum(total * total, axis=0, keepdims=True)
         far.append(
             [
                 spread(c, here, (s1, r1), k * chunks + c, lax.rem(here + step, size))
@@ -967,40 +1007,52 @@
             ]
         )
         close.append(spread(c, here, (s2, r2), c, near))
+    square_ref[...] = square
+    moved = []
+    for k, swapped_ref in enumerate(swapped_refs):
+        for copy, (step, _, origin) in zip(swaps[k], owners):
+            copy.wait()
+            place = swapped_ref.at[origin, half_of(swapped_ref)]
+            moved.append(push(place, place, (s4, r4), k * len(owners) + step - 1, "vocab", near))
+    for copy in moved:
+        copy.wait()
+    if inside:
+        sum_tokens(
+            swapped_refs[:2], place_ref, left_ref, table_ref, wide_ref, embed_ref, embed_square_ref
+        )
     for c in range(chunks):
         for k, step in enumerate(steps):
             far[c][k].wait()
             origin = lax.rem(here + size - step, size)
             close.append(spread(c, origin, (s2, r2), (k + 1) * chunks + c, near))
-    for k, swapped_ref in enumerate(swapped_refs):
-        for copy, (step, _, origin) in zip(swaps[k], owners):
-            copy.wait()
-            place = swapped_ref.at[origin, half_of(swapped_ref)]
-            close.append(push(place, place, (s4, r4), k * len(owners) + step - 1, "vocab", near))
     for copy in close:
         copy.wait()
 
 
-def share_gradients(blocks, rows, collective_id, before):
+def share_gradients(blocks, rows, collective_id, before, tokens):
     owners, replicas = lax.axis_size("dp"), lax.axis_size("vocab")
     chunks = len(blocks)
     others = (replicas // 2 - 1) * chunks
     shape, kind = blocks[0].shape, blocks[0].dtype
     return talk(
-        partial(gradient_kernel, chunks, len(rows)),
+        partial(gradient_kernel, chunks, len(rows), bool(tokens)),
         (
             jax.ShapeDtypeStruct((chunks, replicas, *shape[1:]), kind),
+            full(1, shape[2]),
             *[jax.ShapeDtypeStruct(part.shape, part.dtype) for part in rows],
+            *[full(*size) for part in tokens[2:] for size in (part.shape, (1, part.shape[1]))],
         ),
         collective_id,
         *blocks,
         *rows,
+        *tokens,
         scratch=[pltpu.VMEM((chunks, *shape), kind)]
         + sem_pair((owners - 1) * chunks)
         + sem_pair(others)
         + sem_pair(others + chunks)
         + sem_pair(len(rows) * (owners - 1))
-        + sem_pair(len(rows) * (owners - 1)),
+        + sem_pair(len(rows) * (owners - 1))
+        + [pltpu.VMEM((part.shape[1], 2 * tokens[2].shape[1]), jnp.bfloat16) for part in tokens[:1]],
         microseconds=40,
         before=before,
     )
@@ -1027,7 +1079,7 @@
         copy.wait()
 
 
-def swap_owners(x, collective_id):
+def swap_owners(x, collective_id, before):
     owners = lax.axis_size("dp")
     return talk(
         swap_kernel,
@@ -1035,12 +1087,30 @@
         collective_id,
         x,
         scratch=sem_pair(owners - 1) + sem_pair(owners - 1),
-    )
+        before=before,
+    )
+
+
+def look_up_tokens(code_ref, paired_ref, found_ref):
+    step = 256
+    columns = found_ref.shape[1]
+
+    def one(index, carry):
+        span = pl.ds(pl.multiple_of(index * step, step), step)
+        code = code_ref[span, :]
+        places = lax.broadcasted_iota(jnp.int32, (step, paired_ref.shape[0]), 1)
+        chosen = (places == lax.shift_right_arithmetic(code, 1)).astype(jnp.bfloat16)
+        wide = dot_dims(chosen, paired_ref[...], 1, 0)
+        left = jnp.bitwise_and(code, 1) == 1
+        found_ref[span, :] = jnp.where(left, wide[:, :columns], wide[:, columns:]).astype(jnp.bfloat16)
+        return carry
+
+    lax.fori_loop(0, code_ref.shape[0] // step, one, 0)
 
 
 def token_kernel(
-    scale, x_ref, place_ref, attn_ref, ffn_ref, out_ref, attn_out_ref, ffn_out_ref,
-    near_ref, parts_ref, blocks_ref, row_ref,
+    scale, inside, x_ref, place_ref, attn_ref, ffn_ref, code_ref, paired_ref, out_ref, attn_out_ref, ffn_out_ref,
+    found_ref, near_ref, parts_ref, blocks_ref, row_ref,
     s0, r0, s1, r1, s2, r2, s3, r3, s4, r4, s5, r5, s6, r6,
 ):
     owners, others = peers_of("dp"), far_replicas()
@@ -1095,6 +1165,10 @@
         push(near_ref.at[:, share_of(to)], parts_ref.at[slot], (s1, r1), slot, "vocab", to)
         for slot, to, _ in others
     ]
+    if inside:
+        look_up_tokens(code_ref, paired_ref, found_ref)
+    else:
+        found_ref[...] = jnp.zeros(found_ref.shape, found_ref.dtype)
     for copy in copies:
         copy.wait()
     total = near_ref[:, share_of(here)]
@@ -1134,20 +1208,22 @@
         copy.wait()
 
 
-def gather_tokens(x, places, attn, ffn, scale, collective_id):
+def gather_tokens(x, places, attn, ffn, codes, paired, scale, collective_id):
     owners, pairs = lax.axis_size("dp"), lax.axis_size("vocab") // 2
     _, length, columns = x.shape
     half = length // 2
     width = owners * columns
     whole = [low(w.shape[0], owners * w.shape[1], width) for w in (attn, ffn)]
     return talk(
-        partial(token_kernel, scale),
-        (full(length, width), *whole),
+        partial(token_kernel, scale, paired is not None),
+        (full(length, width), *whole, low(codes.shape[0], columns)),
         collective_id,
         x,
         places,
         attn,
         ffn,
+        codes,
+        attn[0] if paired is None else paired,
         scratch=[
             pltpu.VMEM((owners, half, columns), x.dtype),
             pltpu.VMEM((pairs - 1, owners, half // pairs, columns), x.dtype),
@@ -1252,24 +1328,33 @@
         wide = lax.dot_general(one_hot(place, halves), paired, (((1,), (0,)), ((), ())))
         return jnp.where(left[:, None], wide[:, :paired.shape[1] // 2], wide[:, paired.shape[1] // 2 :])
 
-    source_part, target_part = (look_up(all_ids[:, k].reshape(-1)) for k in (0, 1))
+    source_part = look_up(all_ids[:, 0].reshape(-1))
+    if owners == 4:
+        place, left = paired_places(all_ids[:, 1].reshape(-1))
+        codes = jnp.where(place < 0, -1, 2 * place + left.astype(jnp.int32))[:, None]
+        whole_paired = jnp.pad(paired, ((0, -half % 128), (0, 0)))
+    else:
+        codes, whole_paired = jnp.zeros((16, 1), jnp.int32), None
     positional = sinusoid(length, width)
-    enc_in, enc_attn_w, enc_ffn_w = gather_tokens(
+    enc_in, enc_attn_w, enc_ffn_w, target_part = gather_tokens(
         source_part.reshape(owners, length, -1),
         positional,
         attn_w[0:4].astype(jnp.bfloat16),
         ffn_w[0:2].astype(jnp.bfloat16),
+        codes,
+        whole_paired,
         embed_scale,
         2,
     )
-    target_part, _ = lax.optimization_barrier((target_part, enc_in))
+    if owners != 4:
+        target_part = look_up(all_ids[:, 1].reshape(-1))
     target_sum = lax.psum(target_part, "vocab")
     enc_mid, enc_attn = attn_forward(
         enc_in, norms[0], ((enc_attn_w,), 0, 0), source_seg, source_seg, None, False
     )
     self_w, cross_w, dec_ffn_w, ready = late_weights(attn_w[4:], ffn_w[2:], enc_in, enc_mid)
     enc_out, encoded, enc_ffn = ffn_forward(enc_mid, norms[1], norms[2], ((enc_ffn_w,), 0, 0))
-    target_rows = swap_owners(target_sum.reshape(owners, length, -1), 3)
+    target_rows = swap_owners(target_sum.reshape(owners, length, -1), 3, (enc_out,))
     table_low = after(own_table, ready)
     table_low = lax.all_gather(after(table_low, target_rows[0, 0, 0]), "dp", axis=1, tiled=True)
     target_rows = jnp.swapaxes(target_rows, 0, 1).reshape(length, -1).astype(jnp.float32)
@@ -1319,22 +1404,30 @@
     norm_grad = jnp.stack([after(part, early[0, 0, 0]) for part in norm_grads])
     norm_grad = jnp.concatenate([norm_grad[:, 0], norm_grad[:, 1], jnp.zeros((2, width))], axis=0)
     norm_grad = jnp.swapaxes(norm_grad.reshape(16, owners, -1), 0, 1)
-    late, source_rows, target_rows, norm_grad = share_gradients(
-        [block, self_block, *ffn_blocks], [source_rows, target_rows, norm_grad], 7, (early,)
+    place, left = paired_places(all_ids.reshape(-1))
+    tokens = ()
+    if owners == 4:
+        ones = jnp.broadcast_to(left[:, None], (left.shape[0], width // owners))
+        tokens = (place[None, :], ones.astype(jnp.bfloat16), grad_table)
+    late, layer_squares, source_rows, target_rows, norm_grad, *found = share_gradients(
+        [block, self_block, *ffn_blocks], [source_rows, target_rows, norm_grad], 7, (early,), tokens
     )
     g_norm = jnp.sum(norm_grad, axis=0)[:14]
-    token_grads = jnp.concatenate([source_rows, target_rows], axis=1).reshape(
-        owners * 2 * length, -1
-    )
-    place, left = paired_places(all_ids.reshape(-1))
-    left = left[:, None]
-    token_grads = jnp.concatenate(
-        [jnp.where(left, token_grads, 0), jnp.where(left, 0, token_grads)], axis=1
-    )
-    g_paired = dot_dims(one_hot(place, halves), token_grads, 0, 0)
-    g_embed = grad_table.astype(jnp.float32) + jnp.concatenate(
-        jnp.split(g_paired, 2, axis=1), axis=0
-    )
+    if owners == 4:
+        g_embed, embed_squares = found
+    else:
+        token_grads = jnp.concatenate([source_rows, target_rows], axis=1).reshape(
+            owners * 2 * length, -1
+        )
+        left = left[:, None]
+        token_grads = jnp.concatenate(
+            [jnp.where(left, token_grads, 0), jnp.where(left, 0, token_grads)], axis=1
+        )
+        g_paired = dot_dims(one_hot(place, halves), token_grads, 0, 0)
+        g_embed = grad_table.astype(jnp.float32) + jnp.concatenate(
+            jnp.split(g_paired, 2, axis=1), axis=0
+        )
+        embed_squares = g_embed * g_embed
 
     def by_matrix(shared, count):
         blocks = jnp.swapaxes(shared.reshape(replicas, count, -1, width), 0, 1)
@@ -1348,10 +1441,13 @@
     matrix = replica // 2
     own_grad = lax.dynamic_index_in_dim(g_ffn, matrix, 0, keepdims=False)
     own_products = dot_dims(own_grad, own_grad, 0, 0)
-    g_ffn_low, g_ffn = g_ffn, g_ffn.astype(jnp.float32)
     first_copy = (replica == 0).astype(jnp.float32)
-    layer_sq = jnp.sum(jnp.square(g_attn.astype(jnp.float32))) + jnp.sum(g_ffn * g_ffn) + jnp.sum(g_norm * g_norm)
-    raw_squares = jnp.sum(g_embed * g_embed) + first_copy * layer_sq
+    raw_squares = (
+        jnp.sum(layer_squares)
+        + jnp.sum(jnp.square(early_sum.astype(jnp.float32)))
+        + jnp.sum(embed_squares)
+        + first_copy * jnp.sum(g_norm * g_norm)
+    )
     few = jnp.stack([first_copy * loss_part, first_copy * count_part, raw_squares])
     few = jnp.broadcast_to(jnp.pad(few, (0, 5))[:, None], (8, 128))
     own_products, few = sum_tail(own_products, few, 8)
@@ -1381,7 +1477,7 @@
         soap_basis,
         (g_attn, attn_w, attn_m, attn_v),
         (g_embed, embedding, embed_m, embed_v),
-        (g_ffn_low, ffn_w, ffn_m, ffn_v),
+        (g_ffn, ffn_w, ffn_m, ffn_v),
     )
     new_attn, m_attn, v_attn, new_embed, m_embed, v_embed, new_ffn, m_ffn, v_ffn = updated
     return (

time: 627 us -> 604 us (0.963)
  matrix products: 32.2 us -> 10.2 us
  Pallas kernels: 424 us -> 437 us
  other arithmetic: 57.7 us -> 49.4 us
  waiting for transfers between devices: 30.4 us -> 23.1 us
    dot_general x2 -> x1, matrix products: 15.8 us -> 1.64 us  [dot_dims(): lax.dot_general(left, right, (((left_dim,), (right_dim,)), ((), ())), pre...]
    pallas_call x7, Pallas kernels: 154 us -> 165 us  [talk(): pl.pallas_call(body, out_shape=outs, in_specs=[vmem] * len(args) + [pl.Bl...]
    psum x1, waiting for transfers between devices: 23.6 us -> 13.1 us  [body(): target_sum = lax.psum(target_part, 'vocab')]
    dot_general x2 -> x1, matrix products: 16.4 us -> 8.54 us  [look_up(): lax.dot_general(one_hot(place, halves), paired, (((1,), (0,)), ((), ())))]
    reduce_sum x3, other arithmetic: 9.81 us -> 3.46 us  [the longest x1 2.25 us: body(): jnp.sum(jnp.square(early_sum.astype(jnp.float32)))]
  transfers between devices with their start and end apart: 13 -> 13, of which waited for: 2 -> 2; matrix products, arithmetic and copies ran while one was open for 7% -> 6% of each run, Pallas kernels for 46% -> 48%
where the time goes in v7:
time: 604 us; the launch traced here: 594 us
  Pallas kernels  437 us (72%)
  other arithmetic  49.4 us (8%)
  local copies, waits for them, and re-layouts  40.5 us (7%)
  between operations  28.6 us (5%)
  waiting for transfers between devices  23.1 us (4%)
  matrix products  10.2 us (2%)
    pallas_call x13, Pallas kernels, call(): pl.pallas_call(body, out_shape=outs, in_specs=[vmem] * (len(args) - smem_...  243 us
    pallas_call x7, Pallas kernels, talk(): pl.pallas_call(body, out_shape=outs, in_specs=[vmem] * len(args) + [pl.Bl...  165 us
    pallas_call x1, Pallas kernels, update_matrices(): pl.pallas_call(update_kernel, grid=(4,), out_shape=tuple((full(*part.shap...  28.7 us
    psum x1, waiting for transfers between devices, body(): target_sum = lax.psum(target_part, 'vocab')  13.1 us
  transfers between devices with their start and end apart: 13, of which 2 were waited for; matrix products, arithmetic and copies ran while one was open for 6% of the time, Pallas kernels for 48%

profile of v7, /device:TPU:0, one launch (start us, length us, event | category | flops | bytes accessed | tf_op | source)
XLA Modules:
  0.0 593.9 jit_solution(17622516357869129830)
XLA Ops:
  9.9 7.9 %shard_map.332 = (s32[4,2,1024]{2,1,0:T(2,128)}, f32[4,16,128]{2,1,0:T(8,128)}) custom-call(s32[2,1024]{1,0:T(2,128)} %pad_add_fusion.refs_0_, f32[16,128]{1,0:T(8,128)} %pad_convert_fusion.refs_1_), custom_call_target="tpu_custom_call" | custom-call | flops 15000000512 | tf_op jit(solution)/shard_map/pallas_call | solution.py:744
  23.5 8.5 %fusion = bf16[4096,256]{1,0:T(8,128)(2,1)} fusion(s32[4096]{0:T(1024)S(1)} %fusion.11, bf16[2368,128]{1,0:T(8,128)(2,1)S(1)} %get-tuple-element.196, bf16[2368,128]{1,0:T(8,128)(2,1)S(1)} %get-tuple-element.195), kind=kOutput, calls=%fused_computation.2 | convolution fusion | flops 4978180096 | bytes 3325952 | tf_op jit(solution)/shard_map/dot_general | solution.py:1328
  38.9 4.7 slice_select_fusion
  44.7 3.3 add_select_fusion.1.refs_4_
  49.2 50.8 %shard_map.333 = (f32[1024,512]{1,0:T(8,128)}, bf16[4,512,512]{2,1,0:T(8,128)(2,1)}, bf16[2,2048,512]{2,1,0:T(8,128)(2,1)}, bf16[4096,128]{1,0:T(8,128)(2,1)}) custom-call(bf16[4,1024,128]{2,1,0:T(8,128)(2,1)} %bitcast.157, f32[1024,512]{1,0:T(8,128)} %constant.205.clone.refs_1_, bf16[4,128,512]{2,1,0:T(8,128)(2,1)} %get-tuple-element.194.refs_2_, ...), custom_call_target="tpu_custom_call" | custom-call | flops 49999998976 | tf_op jit(solution)/shard_map/pallas_call | solution.py:744
  109.1 19.1 %shard_map.334 = (f32[1024,512]{1,0:T(8,128)}, bf16[1024,512]{1,0:T(8,128)(2,1)}, bf16[512,1024]{1,0:T(8,128)(2,1)}, bf16[512,1024]{1,0:T(8,128)(2,1)}, bf16[512...) custom-call(f32[1024,512]{1,0:T(8,128)} %get-tuple-element.101.refs_0_.refs_1_, ...), custom_call_target="tpu_custom_call" | custom-call | flops 20000000000 | tf_op jit(solution)/shard_map/pallas_call | solution.py:57
  128.3 11.0 %shard_map.335 = (f32[1024,512]{1,0:T(8,128)}, bf16[1024,512]{1,0:T(8,128)(2,1)}, bf16[1024,512]{1,0:T(8,128)(2,1)}) custom-call(f32[1024,512]{1,0:T(8,128)} %get-tuple-element.104.refs_0_.refs_3_, f32[2,512]{1,0:T(2,128)} %get-tuple-element.228.refs_1_.refs_4_, f32[2,512]{1,0:T(2,128)} %pad_maximum_fusion.7.refs_2_, ...), custom_call_target="tpu_custom_call" | custom-call | flops 12000000000 | tf_op jit(solution)/shard_map/pallas_call | solution.py:57
  139.2 9.8 %collective-permute-done.2.refs_7_.refs_8_.refs_6_ = bf16[1024,512]{1,0:T(8,128)(2,1)} collective-permute-done((bf16[1024,512]{1,0:T(8,128)(2,1)}, bf16[1024,512]{1,0:T(8,128)(2,1)}, u32[]{:S(2)}, u32[]{:S(2)}) %collective-permute-start.2) | collective-permute-done | bytes 1048608 | tf_op jit(solution)/shard_map/ppermute | solution.py:174
  149.0 13.1 %all-reduce.7.cloned.1.call-done.refs_0_ = bf16[4,1024,128]{2,1,0:T(8,128)(2,1)} async-done(((bf16[4,1024,128]{2,1,0:T(8,128)(2,1)}), bf16[4,1024,128]{2,1,0:T(8,128)(2,1)}) %all-reduce.7.cloned.1.call-update) | async-done | bytes 1048592 | tf_op jit(solution)/shard_map/psum | solution.py:1351
  162.2 11.9 %shard_map.336 = bf16[4,1024,128]{2,1,0:T(8,128)(2,1)} custom-call(bf16[4,1024,128]{2,1,0:T(8,128)(2,1)} %all-reduce.7.cloned.1.call-done.refs_0_, f32[1024,512]{1,0:T(8,128)} %get-tuple-element.106.refs_1_), custom_call_target="tpu_custom_call" | custom-call | flops 15000000512 | tf_op jit(solution)/shard_map/pallas_call | solution.py:744
  191.6 18.6 %shard_map.337 = (f32[1024,512]{1,0:T(8,128)}, bf16[1024,512]{1,0:T(8,128)(2,1)}, bf16[512,1024]{1,0:T(8,128)(2,1)}, bf16[512,1024]{1,0:T(8,128)(2,1)}, bf16[512...) custom-call(f32[1024,512]{1,0:T(8,128)} %copy_bitcast_fusion.refs_0_.refs_1_, ...), custom_call_target="tpu_custom_call" | custom-call | flops 20000000000 | tf_op jit(solution)/shard_map/pallas_call | solution.py:57
  210.2 20.4 %shard_map.338 = (f32[1024,512]{1,0:T(8,128)}, bf16[1024,512]{1,0:T(8,128)(2,1)}, bf16[512,1024]{1,0:T(8,128)(2,1)}, bf16[512,1024]{1,0:T(8,128)(2,1)}, bf16[512...) custom-call(f32[1024,512]{1,0:T(8,128)} %get-tuple-element.111.refs_0_.refs_1_,, ...), custom_call_target="tpu_custom_call" | custom-call | flops 20000000000 | tf_op jit(solution)/shard_map/pallas_call | solution.py:57
  230.6 14.0 %shard_map.339 = (f32[1024,512]{1,0:T(8,128)}, bf16[1024,512]{1,0:T(8,128)(2,1)}, bf16[1024,512]{1,0:T(8,128)(2,1)}, bf16[2,2048,512]{2,1,0:T(8,128)(2,1)}) custom-call(f32[1024,512]{1,0:T(8,128)} %get-tuple-element.113.refs_0_.refs_4_, f32[2,512]{1,0:T(2,128)} %get-tuple-element.231.refs_1_.refs_5_, f32[2,512]{1,0:T(2,128)} %get-tuple-element.232.refs_2_.refs_3_, ...), custom_call_target="tpu_custom_call" | custom-call | flops 12000000000 | tf_op jit(solution)/shard_map/pallas_call | solution.py:57
  244.6 6.3 %shard_map.340 = (bf16[256,512]{1,0:T(8,128)(2,1)}, f32[8,256]{1,0:T(8,128)}) custom-call(bf16[1024,512]{1,0:T(8,128)(2,1)} %get-tuple-element.114.refs_0_, s32[256,1]{1,0:T(8,128)} %copy.78.refs_1_, s32[1,256]{1,0:T(1,128)} %broadcast_subtract_fusion.refs_2_.refs_3_, bf16[4736,512]{1,0:T(8,128)(2,1)} %all-gather.7.cloned.1.call-done.refs_3_.refs_4_), custom_call_target="tpu_custom_call" | custom-call | flops 6000000000 | tf_op jit(solution)/shard_map/pallas_call | solution.py:57
  250.9 6.9 %shard_map.341.refs_1_ = f32[8,8,256]{2,1,0:T(8,128)} custom-call(f32[8,256]{1,0:T(8,128)} %get-tuple-element.116.refs_0_), custom_call_target="tpu_custom_call" | custom-call | flops 15000000512 | tf_op jit(solution)/shard_map/pallas_call | solution.py:744
  257.8 10.5 %shard_map.342 = (bf16[256,512]{1,0:T(8,128)(2,1)}, bf16[4,4736,128]{2,1,0:T(8,128)(2,1)}, f32[1,256]{1,0:T(1,128)}) custom-call(bf16[256,512]{1,0:T(8,128)(2,1)} %get-tuple-element.115.refs_0_, f32[8,8,256]{2,1,0:T(8,128)} %shard_map.341.refs_1_, f32[1,256]{1,0:T(1,128)} %bitcast.178, s32[1,256]{1,0:T(1,128)} %broadcast_subtract_fusion.refs_2_.refs_3_, ...), custom_call_target="tpu_custom_call" | custom-call | flops 8000000000 | tf_op jit(solution)/shard_map/pallas_call | solution.py:57
  270.8 16.2 %shard_map.343.refs_0_ = bf16[256,512]{1,0:T(8,128)(2,1)} custom-call(bf16[256,512]{1,0:T(8,128)(2,1)} %get-tuple-element.117.refs_0_), custom_call_target="tpu_custom_call" | custom-call | flops 15000000512 | tf_op jit(solution)/shard_map/pallas_call | solution.py:744
  287.0 19.6 %shard_map.344 = (f32[1024,512]{1,0:T(8,128)}, f32[2,512]{1,0:T(2,128)}, f32[2,512]{1,0:T(2,128)}, bf16[4,64,512]{2,1,0:T(8,128)(2,1)}, bf16[4,64,512]{2,1,0:T(8,128)(2,1)}) custom-call(bf16[256,512]{1,0:T(8,128)(2,1)} %shard_map.343.refs_0_, s32[1,256]{1,0:T(1,128)} %refs_1_.3, f32[1024,512]{1,0:T(8,128)} %get-tuple-element.118.refs_2_, ...), custom_call_target="tpu_custom_call" | custom-call | flops 16999999488 | tf_op jit(solution)/shard_map/pallas_call | solution.py:57
  306.6 25.4 %shard_map.345 = (f32[1024,512]{1,0:T(8,128)}, f32[2,512]{1,0:T(2,128)}, bf16[4,64,512]{2,1,0:T(8,128)(2,1)}, f32[1024,512]{1,0:T(8,128)}) custom-call(f32[1024,512]{1,0:T(8,128)} %get-tuple-element.121.refs_0_, f32[1024,512]{1,0:T(8,128)} %get-tuple-element.111.refs_0_.refs_1_, f32[2,512]{1,0:T(2,128)} %get-tuple-element.230.refs_1_.refs_2_, ...), custom_call_target="tpu_custom_call" | custom-call | flops 24999999488 | tf_op jit(solution)/shard_map/pallas_call | solution.py:57
  333.9 23.5 %shard_map.346 = (f32[1024,512]{1,0:T(8,128)}, f32[2,512]{1,0:T(2,128)}, bf16[4,64,512]{2,1,0:T(8,128)(2,1)}, bf16[4,1024,128]{2,1,0:T(8,128)(2,1)}) custom-call(f32[1024,512]{1,0:T(8,128)} %get-tuple-element.132.refs_0_, f32[1024,512]{1,0:T(8,128)} %copy_bitcast_fusion.refs_0_.refs_1_, f32[2,512]{1,0:T(2,128)} %get-tuple-element.229.refs_1_.refs_2_, ...), custom_call_target="tpu_custom_call" | custom-call | flops 24999999488 | tf_op jit(solution)/shard_map/pallas_call | solution.py:57
  357.4 19.9 %shard_map.347 = (f32[1024,512]{1,0:T(8,128)}, f32[2,512]{1,0:T(2,128)}, f32[2,512]{1,0:T(2,128)}, bf16[4,64,512]{2,1,0:T(8,128)(2,1)}, bf16[4,64,512]{2,1,0:T(8,128)(2,1)}) custom-call(f32[1024,512]{1,0:T(8,128)} %get-tuple-element.129.refs_0_, f32[1024,512]{1,0:T(8,128)} %get-tuple-element.106.refs_1_, f32[2,512]{1,0:T(2,128)} %pad_maximum_fusion.7.refs_2_, ...), custom_call_target="tpu_custom_call" | custom-call | flops 16999999488 | tf_op jit(solution)/shard_map/pallas_call | solution.py:57
  379.9 2.3 multiply_reduce_fusion
  386.2 26.0 %shard_map.348 = (f32[1024,512]{1,0:T(8,128)}, f32[2,512]{1,0:T(2,128)}, bf16[4,64,512]{2,1,0:T(8,128)(2,1)}, bf16[4,1024,128]{2,1,0:T(8,128)(2,1)}) custom-call(f32[1024,512]{1,0:T(8,128)} %get-tuple-element.141.refs_0_, f32[1024,512]{1,0:T(8,128)} %get-tuple-element.101.refs_0_.refs_1_, f32[2,512]{1,0:T(2,128)} %get-tuple-element.227.refs_1_.refs_2_, ...), custom_call_target="tpu_custom_call" | custom-call | flops 24999999488 | tf_op jit(solution)/shard_map/pallas_call | solution.py:57
  416.3 2.2 broadcast_in_dim.86.refs_8_
  418.5 49.0 %shard_map.349 = (bf16[4,8,64,512]{3,2,1,0:T(8,128)(2,1)}, f32[1,512]{1,0:T(1,128)}, bf16[4,1024,128]{2,1,0:T(8,128)(2,1)}, bf16[4,1024,128]{2,1,0:T(8,128)(2,1)...) custom-call(bf16[4,64,512]{2,1,0:T(8,128)(2,1)} %get-tuple-element.151.refs_0_, ...), custom_call_target="tpu_custom_call" | custom-call | flops 40000000000 | tf_op jit(solution)/shard_map/pallas_call | solution.py:744
  477.4 22.1 %shard_map.350 = (f32[512,512]{1,0:T(8,128)}, f32[8,128]{1,0:T(8,128)}) custom-call(f32[512,512]{1,0:T(8,128)} %fusion.5.refs_0_, f32[8,128]{1,0:T(8,128)} %broadcast_in_dim.87.refs_1_), custom_call_target="tpu_custom_call" | custom-call | flops 15000000512 | tf_op jit(solution)/shard_map/pallas_call | solution.py:744
  501.9 2.3 dynamic-slice_bitcast_fusion.refs_1_
  507.6 2.4 bitcast_add_fusion.refs_0_
  510.0 28.9 %shard_map.352 = f32[512,512]{1,0:T(8,128)} custom-call(f32[512,512]{1,0:T(8,128)} %bitcast_add_fusion.refs_0_, f32[512,512]{1,0:T(8,128)} %dynamic-slice_bitcast_fusion.refs_1_), custom_call_target="tpu_custom_call" | custom-call | flops 28999999488 | tf_op jit(solution)/shard_map/pallas_call | solution.py:57
  539.0 2.3 convert_multiply_fusion
  552.8 28.7 %shard_map.351 = (f32[12,128,512]{2,1,0:T(8,128)}, f32[12,128,512]{2,1,0:T(8,128)}, f32[12,128,512]{2,1,0:T(8,128)}, f32[4736,128]{1,0:T(8,128)}, f32[4736,128]{...) custom-call(f32[1]{0:T(128)} %bitcast.66.refs_0_, ...), custom_call_target="tpu_custom_call" | custom-call | flops 20000000000 | tf_op jit(solution)/shard_map/pallas_call | solution.py:618
  581.6 4.2 convert.15
  (212 shorter events, 73.4 us)
Async XLA Ops:
  7.2 155.0 %all-reduce.7.cloned.1.call-start = ((), (), s32[]{:S(2)}) async-start(), calls=%async_computation.2 | async-start | bytes 2097152 | tf_op jit(solution)/shard_map/psum | solution.py:1351
  9.9 9.9 %copy-start.12 = (f32[4,512,512]{2,1,0:T(8,128)S(1)}, f32[4,512,512]{2,1,0:T(8,128)}, u32[]{:S(2)}) copy-start(f32[4,512,512]{2,1,0:T(8,128)} %refs_11_.1) | copy-start | bytes 12582916
  23.5 8.5 %copy-start.13 = (f32[12,128,512]{2,1,0:T(8,128)S(1)}, f32[12,128,512]{2,1,0:T(8,128)}, u32[]{:S(2)}) copy-start(f32[12,128,512]{2,1,0:T(8,128)} %refs_3_.1) | copy-start | bytes 9437188
  38.9 5.8 copy-start.2
  38.9 5.8 copy-start.3
  49.2 55.0 %copy-start.29 = (s32[1,1024]{1,0:T(1,128)S(1)}, s32[1,1024]{1,0:T(1,128)}, u32[]{:S(2)}) copy-start(s32[1,1024]{1,0:T(1,128)} %refs_5_.6) | copy-start | bytes 12292
  49.2 55.1 %copy-start = (s32[1,1024]{1,0:T(1,128)S(1)}, s32[1,1024]{1,0:T(1,128)}, u32[]{:S(2)}) copy-start(s32[1,1024]{1,0:T(1,128)} %refs_5_.5) | copy-start | bytes 12292
  49.2 56.3 %copy-start.25 = (f32[4,16,128]{2,1,0:T(8,128)S(1)}, f32[4,16,128]{2,1,0:T(8,128)}, u32[]{:S(2)}) copy-start(f32[4,16,128]{2,1,0:T(8,128)} %get-tuple-element.102) | copy-start | bytes 98308
  100.1 39.2 %collective-permute-start = (bf16[1024,512]{1,0:T(8,128)(2,1)}, bf16[1024,512]{1,0:T(8,128)(2,1)}, u32[]{:S(2)}, u32[]{:S(2)}) collective-permute-start(bf16[1024,512]{1,0:T(8,128)(2,1)} %maximum_select_fusion), channel_id=1, source_target_pairs={{0,8},{8,0},{16,24},{24,16},{1,9},{9,1},{17,25},{25,17},{2,10},{10... | collective-permute-start | bytes 3145736 | tf_op jit(solution)/shard_map/ppermute | solution.py:174
  101.1 38.1 %collective-permute-start.1 = (bf16[1024,512]{1,0:T(8,128)(2,1)}, bf16[1024,512]{1,0:T(8,128)(2,1)}, u32[]{:S(2)}, u32[]{:S(2)}) collective-permute-start(bf16[1024,512]{1,0:T(8,128)(2,1)} %maximum_select_fusion), channel_id=1, source_target_pairs={{0,16},{8,24},{16,0},{24,8},{1,17},{9,25},{17,1},{25,9},{2,18},{10... | collective-permute-start | bytes 3145736 | tf_op jit(solution)/shard_map/ppermute | solution.py:174
  101.6 47.4 %collective-permute-start.2 = (bf16[1024,512]{1,0:T(8,128)(2,1)}, bf16[1024,512]{1,0:T(8,128)(2,1)}, u32[]{:S(2)}, u32[]{:S(2)}) collective-permute-start(bf16[1024,512]{1,0:T(8,128)(2,1)} %maximum_select_fusion), channel_id=1, source_target_pairs={{0,24},{8,16},{16,8},{24,0},{1,25},{9,17},{17,9},{25,1},{2,26},{10... | collective-permute-start | bytes 3145736 | tf_op jit(solution)/shard_map/ppermute | solution.py:174
  103.6 140.9 %all-gather.7.cloned.1.call-start = ((), (), s32[]{:S(2)}) async-start(), calls=%async_computation.3 | async-start | bytes 6062080 | tf_op jit(solution)/shard_map/all_gather | solution.py:1359
  149.0 27.6 %collective-permute-start.5 = (bf16[1024,512]{1,0:T(8,128)(2,1)}, bf16[1024,512]{1,0:T(8,128)(2,1)}, u32[]{:S(2)}, u32[]{:S(2)}) collective-permute-start(bf16[1024,512]{1,0:T(8,128)(2,1)} %collective-permute-done.2.refs_7_.refs_8_.refs_6_), channel_id=1, source_target_pairs={{0,1},{1,0},{2,3},{3,2},{4,5},{5,4},{6,7},{7,6},{8,9},{9,8},{10,11... | collective-permute-start | bytes 3145736 | tf_op jit(solution)/shard_map/ppermute | solution.py:174
  180.3 5.4 copy-start.8
  180.3 5.4 copy-start.10
  180.3 177.1 %reduce-scatter.7.cloned.1.call-start = ((), (), s32[]{:S(2)}) async-start(), calls=%async_computation.7 | async-start | bytes 6062080
  183.9 6.2 %collective-permute-start.3 = (bf16[1024,512]{1,0:T(8,128)(2,1)}, bf16[1024,512]{1,0:T(8,128)(2,1)S(1)}, u32[]{:S(2)}, u32[]{:S(2)}) collective-permute-start(bf16[1024,512]{1,0:T(8,128)(2,1)} %collective-permute-done.refs_5_.refs_6_.refs_4_), channel_id=1, source_target_pairs={{0,1},{1,0},{2,3},{3,2},{4,5},{5,4},{6,7},{7,6},{8,9},{9,8},{10,11... | collective-permute-start | bytes 3145736 | tf_op jit(solution)/shard_map/ppermute | solution.py:174
  184.4 5.7 collective-permute-start.4
  268.3 111.5 %reduce-scatter.9.cloned.1.call-start = ((), (), s32[]{:S(2)}) async-start(), calls=%async_computation.8 | async-start | bytes 983040
  306.6 25.4 %copy-start.21 = (bf16[4,64,512]{2,1,0:T(8,128)(2,1)S(1)}, bf16[4,64,512]{2,1,0:T(8,128)(2,1)}, u32[]{:S(2)}) copy-start(bf16[4,64,512]{2,1,0:T(8,128)(2,1)} %get-tuple-element.149) | copy-start | bytes 786436
  306.6 25.4 %copy-start.22 = (bf16[4,64,512]{2,1,0:T(8,128)(2,1)S(1)}, bf16[4,64,512]{2,1,0:T(8,128)(2,1)}, u32[]{:S(2)}) copy-start(bf16[4,64,512]{2,1,0:T(8,128)(2,1)} %get-tuple-element.150) | copy-start | bytes 786436
  333.9 78.4 %all-gather.9.cloned.1.call-start = ((), (), s32[]{:S(2)}) async-start(), calls=%async_computation.4 | async-start | bytes 1769472 | tf_op jit(solution)/shard_map/all_gather | solution.py:1400
  357.4 27.4 %copy-start.38 = (f32[1,256]{1,0:T(1,128)S(1)}, f32[1,256]{1,0:T(1,128)}, u32[]{:S(2)}) copy-start(f32[1,256]{1,0:T(1,128)} %get-tuple-element.165) | copy-start | bytes 3076
  382.1 156.8 %all-gather.11.cloned.1.call-start = ((), (), s32[]{:S(2)}) async-start(), calls=%async_computation.5 | async-start | bytes 2359296 | tf_op jit(solution)/shard_map/all_gather | solution.py:1462
  386.1 29.3 %copy-start.35 = (f32[2,512]{1,0:T(2,128)S(1)}, f32[2,512]{1,0:T(2,128)}, u32[]{:S(2)}) copy-start(f32[2,512]{1,0:T(2,128)} %get-tuple-element.158) | copy-start | bytes 12292
  386.1 29.3 %copy-start.34 = (f32[2,512]{1,0:T(2,128)S(1)}, f32[2,512]{1,0:T(2,128)}, u32[]{:S(2)}) copy-start(f32[2,512]{1,0:T(2,128)} %get-tuple-element.159) | copy-start | bytes 12292
  386.2 29.3 %copy-start.33 = (f32[2,512]{1,0:T(2,128)S(1)}, f32[2,512]{1,0:T(2,128)}, u32[]{:S(2)}) copy-start(f32[2,512]{1,0:T(2,128)} %get-tuple-element.160) | copy-start | bytes 12292
  386.2 29.3 %copy-start.32 = (f32[2,512]{1,0:T(2,128)S(1)}, f32[2,512]{1,0:T(2,128)}, u32[]{:S(2)}) copy-start(f32[2,512]{1,0:T(2,128)} %get-tuple-element.161) | copy-start | bytes 12292
  386.2 29.3 %copy-start.31 = (f32[2,512]{1,0:T(2,128)S(1)}, f32[2,512]{1,0:T(2,128)}, u32[]{:S(2)}) copy-start(f32[2,512]{1,0:T(2,128)} %get-tuple-element.162) | copy-start | bytes 12292
  386.2 29.3 %copy-start.30 = (f32[2,512]{1,0:T(2,128)S(1)}, f32[2,512]{1,0:T(2,128)}, u32[]{:S(2)}) copy-start(f32[2,512]{1,0:T(2,128)} %get-tuple-element.163) | copy-start | bytes 12292
  499.5 8.1 %copy-start.16 = (f32[512,512]{1,0:T(8,128)S(1)}, f32[512,512]{1,0:T(8,128)}, u32[]{:S(2)}) copy-start(f32[512,512]{1,0:T(8,128)} %get-tuple-element.177) | copy-start | bytes 3145732
  501.4 80.2 %all-gather.13.cloned.1.call-start = ((), (), s32[]{:S(2)}) async-start(), calls=%async_computation.6 | async-start | bytes 2359296 | tf_op jit(solution)/shard_map/all_gather | solution.py:1462
  (23 other events, 52.5 us)
Sparse Core Ops, SparseCore 0:
  103.8 58.3 all-reduce.6
  180.4 56.4 all-gather.6
  268.5 56.5 reduce-scatter.6
  334.0 27.1 reduce-scatter.8
  382.3 25.2 all-gather.8
  501.5 28.0 all-gather.10
  547.5 28.2 all-gather.12

commit v8 on v7

--- a/solution.py
+++ b/solution.py
@@ -50,16 +50,19 @@
     return pl.CostEstimate(flops=microseconds * 10**9, bytes_accessed=0, transcendentals=0)
 
 
-def call(kernel, outs, *args, scratch=(), smem_args=0, microseconds=5, before=()):
+def call(kernel, outs, *args, scratch=(), smem_args=0, microseconds=5, before=(), far=()):
+    any_spec = pl.BlockSpec(memory_space=pl.ANY)
+    specs = [vmem] * (len(args) - smem_args) + [smem] * smem_args + [any_spec] * len(before)
+    for k in far:
+        specs[k] = any_spec
+
     def body(*refs):
         kernel(*refs[: len(args)], *refs[len(args) + len(before) :])
 
     return pl.pallas_call(
         body,
         out_shape=outs,
-        in_specs=[vmem] * (len(args) - smem_args)
-        + [smem] * smem_args
-        + [pl.BlockSpec(memory_space=pl.ANY)] * len(before),
+        in_specs=specs,
         out_specs=jax.tree.map(lambda _: vmem, outs),
         scratch_shapes=list(scratch),
         compiler_params=pltpu.CompilerParams(vmem_limit_bytes=56 * 2**20),
@@ -148,26 +151,41 @@
     return (picked[:, None] == jnp.arange(count)[None, :]).astype(jnp.bfloat16)
 
 
-def lay_weights(w_ref, piece_refs, part, first):
+def load_weights(w_ref, piece_refs, part, first, sems):
+    if len(piece_refs) == 1:
+        copies = [pltpu.make_async_copy(piece_refs[0], w_ref, sems.at[0])]
+        copies[0].start()
+        return copies
     own = piece_refs[0]
     matrices, rows = w_ref.shape[0], w_ref.shape[1] // 4
     half = own.shape[0] // 2
     me, side = lax.axis_index("dp"), lax.rem(lax.axis_index("vocab"), 2)
+    copies = []
     for m in range(matrices):
-        span = slice(first + m * rows, first + (m + 1) * rows)
-        w_ref[m, pl.ds(pl.multiple_of(me * rows, rows), rows), :] = own[
-            part * half + span.start : part * half + span.stop, :
-        ]
+        which = m if part is None else part
+        start = first if part is None else first + m * rows
+
+        def copy_from(ref, offset, owner, slot):
+            place = pl.ds(pl.multiple_of(owner * rows, rows), rows)
+            return pltpu.make_async_copy(
+                ref.at[pl.ds(offset + start, rows)], w_ref.at[m, place], sems.at[slot]
+            )
+
+        copies.append(copy_from(own, which * half, me, 4 * m))
+        copies[-1].start()
         for k in range(1, 4):
-            place = pl.ds(pl.multiple_of((me ^ k) * rows, rows), rows)
-
-            @pl.when(side == part)
+            mine, theirs = (copy_from(piece_refs[n], 0, me ^ k, 4 * m + k) for n in (k, k + 3))
+
+            @pl.when(side == which)
             def _():
-                w_ref[m, place, :] = piece_refs[k][span, :]
-
-            @pl.when(side != part)
+                mine.start()
+
+            @pl.when(side != which)
             def _():
-                w_ref[m, place, :] = piece_refs[k + 3][span, :]
+                theirs.start()
+
+            copies.append(mine)
+    return copies
 
 
 def flip_sites(part, axis, bit):
@@ -204,15 +222,14 @@
     piece_refs, refs = refs[:pieces], refs[pieces:]
     edge_ref, out_ref, a_ref, qt_ref, kt_ref, vt_ref, ot_ref, lse_ref = refs[:8]
     refs = refs[8:]
-    w_ref = piece_refs[0]
-    if pieces > 1:
-        w_ref = refs.pop(0)
-        lay_weights(w_ref, piece_refs, part, first)
-    top_ref, sum_ref, acc_ref = refs
+    w_ref, top_ref, sum_ref, acc_ref, sems = refs
+    weights = load_weights(w_ref, piece_refs, part, first, sems)
     length, width = x_ref.shape
     head_size = width // HEADS
     a_ref[...] = norm_forward(x_ref[...], ln_ref).astype(jnp.bfloat16)
     key_in = key_ref if cross else a_ref
+    for copy in weights:
+        copy.wait()
     qt_ref[...] = dot_dims(a_ref[...], w_ref[0], 1, 0).astype(jnp.bfloat16).T
     kt_ref[...] = dot_dims(key_in[...], w_ref[1], 1, 0).astype(jnp.bfloat16).T
     vt_ref[...] = dot_dims(key_in[...], w_ref[2], 1, 0).astype(jnp.bfloat16).T
@@ -269,13 +286,16 @@
         partial(attn_forward_kernel, causal, cross, len(weights), part, first),
         outs,
         *args,
-        scratch=[
+        scratch=[pltpu.VMEM((4, width, width), jnp.bfloat16)][: len(weights) == 1]
+        + [
             pltpu.VMEM((HEADS, length), jnp.float32),
             pltpu.VMEM((HEADS, length), jnp.float32),
             pltpu.VMEM((width, length), jnp.float32),
+            pltpu.SemaphoreType.DMA((16,)),
         ],
         smem_args=1,
         microseconds=20,
+        far=range(len(args) - 1 - len(weights), len(args) - 1),
     )
     whole = stored.pop() if len(weights) > 1 else weights[0]
     return out, (x, ln, whole, segs, edges, causal, key_in, normed, stored)
@@ -393,15 +413,13 @@
 
 
 def ffn_forward_kernel(chunk, pieces, first, x_ref, ln_ref, next_ref, *refs):
-    piece_refs, (out_ref, a_ref, after_ref, *refs) = refs[:pieces], refs[pieces:]
-    w_ref = piece_refs[0]
-    if pieces > 1:
-        (w_ref,) = refs
-        for part in range(2):
-            lay_weights(w_ref.at[part : part + 1], piece_refs, part, first)
+    piece_refs, (out_ref, a_ref, after_ref, w_ref, sems) = refs[:pieces], refs[pieces:]
+    weights = load_weights(w_ref, piece_refs, None, first, sems)
     w_in_ref, w_out_ref = w_ref.at[0], w_ref.at[1]
     a_ref[...] = norm_forward(x_ref[...], ln_ref).astype(jnp.bfloat16)
     total = x_ref[...]
+    for copy in weights:
+        copy.wait()
     for start in range(0, w_in_ref.shape[0], chunk):
         part = slice(start, start + chunk)
         hidden = dot_dims(a_ref[...], w_in_ref[part, :], 1, 1)
@@ -424,7 +442,10 @@
         ln,
         ln_next,
         *weights,
+        scratch=[pltpu.VMEM(w.shape, w.dtype) for w in weights if len(weights) == 1]
+        + [pltpu.SemaphoreType.DMA((8,))],
         microseconds=12,
+        far=range(3, 3 + len(weights)),
     )
     return out, after, (x, ln, whole[0] if whole else weights[0], normed, out, ln_next)
 
@@ -492,6 +513,23 @@
         microseconds=17,
         before=before,
     )
+
+
+def look_up_tokens(code_ref, paired_ref, found_ref):
+    step = 256
+    columns = found_ref.shape[1]
+
+    def one(index, carry):
+        span = pl.ds(pl.multiple_of(index * step, step), step)
+        code = code_ref[span, :]
+        places = lax.broadcasted_iota(jnp.int32, (step, paired_ref.shape[0]), 1)
+        chosen = (places == lax.shift_right_arithmetic(code, 1)).astype(jnp.bfloat16)
+        wide = dot_dims(chosen, paired_ref[...], 1, 0)
+        left = jnp.bitwise_and(code, 1) == 1
+        found_ref[span, :] = jnp.where(left, wide[:, :columns], wide[:, columns:]).astype(jnp.bfloat16)
+        return carry
+
+    lax.fori_loop(0, code_ref.shape[0] // step, one, 0)
 
 
 def loss_forward_kernel(chunks, final_ref, pick_ref, label_ref, table_ref, picked_ref, stat_ref, logit_ref):
@@ -667,9 +705,21 @@
     return jnp.concatenate(rows, axis=0)[:, size:]
 
 
-def renew_kernel(stat_ref, basis_ref, out_ref, gram_ref, rest_ref):
+def renew_kernel(
+    product_ref, stats_ref, bases_ref, factor_ref, half_ref, stat_ref, basis_ref, out_ref, gram_ref, rest_ref, sems
+):
     size = stat_ref.shape[0]
-    product = dot_exact(stat_ref[...], basis_ref[...], 1, 0)
+    here = lax.axis_index("vocab")
+    copies = [
+        pltpu.make_async_copy(ref.at[here // 2], place, sems.at[k])
+        for k, (ref, place) in enumerate(((stats_ref, stat_ref), (bases_ref, basis_ref)))
+    ]
+    for copy in copies:
+        copy.start()
+    for copy in copies:
+        copy.wait()
+    statistic = stat_decay * stat_ref[...] + factor_ref[0] * product_ref[...]
+    product = dot_exact(statistic, basis_ref[...], 1, 0)
     rest_ref[...] = product
     gram_ref[...] = dot_exact(product, product, 0, 0)
     for low in range(0, size, 128):
@@ -692,17 +742,24 @@
             panel = dot_exact(inverse, gram_ref[low:high, high:], 1, 0)
             gram_ref[high:, high:] -= dot_exact(panel, panel, 0, 0)
             rest_ref[:, high:] -= dot_exact(columns, panel, 1, 0)
-
-
-def renew_basis(statistic, basis):
-    shape = statistic.shape
+    rows = size // 2
+    half = pl.ds(pl.multiple_of(lax.rem(here, 2) * rows, rows), rows)
+    half_ref[...] = out_ref[half, :].astype(jnp.bfloat16)
+
+
+def renew_basis(products, stats, bases, factor):
+    size = products.shape[0]
     return call(
         renew_kernel,
-        full(*shape),
-        statistic,
-        basis,
-        scratch=[pltpu.VMEM(shape, jnp.float32), pltpu.VMEM(shape, jnp.float32)],
+        low(size // 2, size),
+        products,
+        stats,
+        bases,
+        factor.reshape(1),
+        scratch=[pltpu.VMEM((size, size), jnp.float32)] * 5 + [pltpu.SemaphoreType.DMA((2,))],
+        smem_args=1,
         microseconds=29,
+        far=(1, 2),
     )
 
 
@@ -777,55 +834,75 @@
     return talk(partial(gather_kernel, axis), outs, collective_id, *arrays, scratch=sems)
 
 
-def sum_kernel(x_ref, out_ref, parts_ref, mine_ref, s0, r0, s1, r1):
-    others = peers_of("vocab")
-    greet(*[("vocab", to) for _, to, _ in others])
-    size, me = lax.axis_size("vocab"), lax.axis_index("vocab")
-    rows = mine_ref.shape[0]
-
-    def rows_of(index):
-        return pl.ds(pl.multiple_of(index * rows, rows), rows)
-
+def flip(index, bit):
+    return index + bit - 2 * bit * lax.rem(index // bit, 2)
+
+
+def far_replicas():
+    here, size = lax.axis_index("vocab"), lax.axis_size("vocab")
+    return [
+        (step // 2 - 1, lax.rem(here + step, size), lax.rem(here + size - step, size))
+        for step in range(2, size, 2)
+    ]
+
+
+def sum_kernel(x_ref, out_ref, near_ref, send_ref, parts_ref, s0, r0, s1, r1, s2, r2, s3, r3):
+    here, others = lax.axis_index("vocab"), far_replicas()
+    near, side = flip(here, 1), lax.rem(here, 2)
+    greet(*[("vocab", to) for _, to, _ in others], ("vocab", near))
+    half = near_ref.shape[0]
+    share = parts_ref.shape[1]
+
+    def half_of(which):
+        return pl.ds(pl.multiple_of(which * half, half), half)
+
+    def share_of(index, start):
+        return pl.ds(pl.multiple_of(start + index // 2 * share, share), share)
+
+    push(x_ref.at[half_of(1 - side)], near_ref, (s0, r0), 0, "vocab", near).wait()
+    total = near_ref[...].astype(jnp.float32) + x_ref[half_of(side), :].astype(jnp.float32)
+    send_ref[...] = total.astype(send_ref.dtype)
     copies = [
-        push(x_ref.at[rows_of(to)], parts_ref.at[me], (s0, r0), step - 1, "vocab", to)
-        for step, to, _ in others
+        push(send_ref.at[share_of(to, 0)], parts_ref.at[slot], (s1, r1), slot, "vocab", to)
+        for slot, to, _ in others
     ]
-    parts_ref[me] = x_ref[rows_of(me), :]
-    for copy in copies:
-        copy.wait()
-    total = parts_ref[0].astype(jnp.float32)
-    for index in range(1, size):
-        total = total + parts_ref[index].astype(jnp.float32)
-    mine_ref[...] = total.astype(mine_ref.dtype)
+    total = send_ref[share_of(here, 0), :].astype(jnp.float32)
+    for copy, (slot, _, _) in zip(copies, others):
+        copy.wait()
+        total = total + parts_ref[slot].astype(jnp.float32)
+    mine = share_of(here, side * half)
+    out_ref[mine, :] = total.astype(out_ref.dtype)
     copies = [
-        push(mine_ref, out_ref.at[rows_of(me)], (s1, r1), step - 1, "vocab", to)
-        for step, to, _ in others
+        push(out_ref.at[mine], out_ref.at[mine], (s2, r2), slot, "vocab", to) for slot, to, _ in others
     ]
-    out_ref[rows_of(me), :] = mine_ref[...]
-    for copy in copies:
+    close = [push(out_ref.at[mine], out_ref.at[mine], (s3, r3), 0, "vocab", near)]
+    for copy, (slot, _, origin) in zip(copies, others):
+        copy.wait()
+        theirs = out_ref.at[share_of(origin, side * half)]
+        close.append(push(theirs, theirs, (s3, r3), slot + 1, "vocab", near))
+    for copy in close:
         copy.wait()
 
 
 def sum_vocab(x, collective_id):
-    replicas = lax.axis_size("vocab")
+    pairs = lax.axis_size("vocab") // 2
     rows, columns = x.shape
-    share = rows // replicas
+    half = rows // 2
     return talk(
         sum_kernel,
         jax.ShapeDtypeStruct(x.shape, x.dtype),
         collective_id,
         x,
         scratch=[
-            pltpu.VMEM((replicas, share, columns), x.dtype),
-            pltpu.VMEM((share, columns), x.dtype),
+            pltpu.VMEM((half, columns), x.dtype),
+            pltpu.VMEM((half, columns), x.dtype),
+            pltpu.VMEM((pairs - 1, half // pairs, columns), x.dtype),
         ]
-        + sem_pair(replicas - 1)
-        + sem_pair(replicas - 1),
-    )
-
-
-def flip(index, bit):
-    return index + bit - 2 * bit * lax.rem(index // bit, 2)
+        + sem_pair(1)
+        + sem_pair(pairs - 1)
+        + sem_pair(pairs - 1)
+        + sem_pair(pairs),
+    )
 
 
 def tail_kernel(
@@ -896,14 +973,6 @@
         + sem_pair(owners - 1)
         + sem_pair(owners),
     )
-
-
-def far_replicas():
-    here, size = lax.axis_index("vocab"), lax.axis_size("vocab")
-    return [
-        (step // 2 - 1, lax.rem(here + step, size), lax.rem(here + size - step, size))
-        for step in range(2, size, 2)
-    ]
 
 
 def sum_tokens(rows_refs, place_ref, left_ref, table_ref, wide_ref, embed_ref, square_ref):
@@ -1058,7 +1127,7 @@
     )
 
 
-def swap_kernel(x_ref, out_ref, s0, r0, s1, r1):
+def swap_kernel(scale, x_ref, place_ref, sum_ref, out_ref, s0, r0, s1, r1):
     others = peers_of("dp")
     me, here = lax.axis_index("dp"), lax.axis_index("vocab")
     near, side = flip(here, 1), lax.rem(here, 2)
@@ -1077,35 +1146,24 @@
         close.append(push(place, place, (s1, r1), step - 1, "vocab", near))
     for copy in close:
         copy.wait()
-
-
-def swap_owners(x, collective_id, before):
+    columns = out_ref.shape[2]
+    for owner in range(out_ref.shape[0]):
+        band = slice(owner * columns, (owner + 1) * columns)
+        sum_ref[:, band] = out_ref[owner].astype(jnp.float32) * scale + place_ref[:, band]
+
+
+def swap_owners(x, places, scale, collective_id, before):
     owners = lax.axis_size("dp")
     return talk(
-        swap_kernel,
-        jax.ShapeDtypeStruct(x.shape, x.dtype),
+        partial(swap_kernel, scale),
+        full(*places.shape),
         collective_id,
         x,
-        scratch=sem_pair(owners - 1) + sem_pair(owners - 1),
+        places,
+        scratch=[pltpu.VMEM(x.shape, x.dtype)]
+        + sem_pair(owners - 1) + sem_pair(owners - 1),
         before=before,
     )
-
-
-def look_up_tokens(code_ref, paired_ref, found_ref):
-    step = 256
-    columns = found_ref.shape[1]
-
-    def one(index, carry):
-        span = pl.ds(pl.multiple_of(index * step, step), step)
-        code = code_ref[span, :]
-        places = lax.broadcasted_iota(jnp.int32, (step, paired_ref.shape[0]), 1)
-        chosen = (places == lax.shift_right_arithmetic(code, 1)).astype(jnp.bfloat16)
-        wide = dot_dims(chosen, paired_ref[...], 1, 0)
-        left = jnp.bitwise_and(code, 1) == 1
-        found_ref[span, :] = jnp.where(left, wide[:, :columns], wide[:, columns:]).astype(jnp.bfloat16)
-        return carry
-
-    lax.fori_loop(0, code_ref.shape[0] // step, one, 0)
 
 
 def token_kernel(
@@ -1328,12 +1386,16 @@
         wide = lax.dot_general(one_hot(place, halves), paired, (((1,), (0,)), ((), ())))
         return jnp.where(left[:, None], wide[:, :paired.shape[1] // 2], wide[:, paired.shape[1] // 2 :])
 
-    source_part = look_up(all_ids[:, 0].reshape(-1))
     if owners == 4:
-        place, left = paired_places(all_ids[:, 1].reshape(-1))
-        codes = jnp.where(place < 0, -1, 2 * place + left.astype(jnp.int32))[:, None]
+        place, left = paired_places(jnp.swapaxes(all_ids, 0, 1).reshape(2, -1, 1))
+        all_codes = jnp.where(place < 0, -1, 2 * place + left.astype(jnp.int32))
+        codes = all_codes[1]
         whole_paired = jnp.pad(paired, ((0, -half % 128), (0, 0)))
+        source_part = call(
+            look_up_tokens, low(codes.shape[0], width // owners), all_codes[0], whole_paired
+        )
     else:
+        source_part = look_up(all_ids[:, 0].reshape(-1))
         codes, whole_paired = jnp.zeros((16, 1), jnp.int32), None
     positional = sinusoid(length, width)
     enc_in, enc_attn_w, enc_ffn_w, target_part = gather_tokens(
@@ -1354,11 +1416,11 @@
     )
     self_w, cross_w, dec_ffn_w, ready = late_weights(attn_w[4:], ffn_w[2:], enc_in, enc_mid)
     enc_out, encoded, enc_ffn = ffn_forward(enc_mid, norms[1], norms[2], ((enc_ffn_w,), 0, 0))
-    target_rows = swap_owners(target_sum.reshape(owners, length, -1), 3, (enc_out,))
-    table_low = after(own_table, ready)
-    table_low = lax.all_gather(after(table_low, target_rows[0, 0, 0]), "dp", axis=1, tiled=True)
-    target_rows = jnp.swapaxes(target_rows, 0, 1).reshape(length, -1).astype(jnp.float32)
-    dec_in = target_rows * embed_scale + positional
+    dec_in = swap_owners(
+        target_sum.reshape(owners, length, -1), positional, embed_scale, 3, (enc_out,)
+    )
+    late_table = after(own_table, ready.astype(jnp.float32) + dec_in[0, 0])
+    table_low = lax.all_gather(late_table, "dp", axis=1, tiled=True)
     dec_mid, dec_self = attn_forward(
         dec_in, norms[3], self_w, target_seg, target_seg, None, True
     )
@@ -1456,20 +1518,14 @@
     factor = jnp.minimum(1.0, clip_limit / (grad_norm + norm_eps)) / sentences
     g_norm = g_norm * factor
 
-    def all_matrices(own):
-        rows = own.shape[0] // 2
-        half = lax.dynamic_slice_in_dim(own.astype(jnp.bfloat16), replica % 2 * rows, rows, 0)
-        return lax.all_gather(half, "vocab").reshape(4, 2 * rows, -1)
-
-    all_products = all_matrices(own_products)
-    new_stats = stat_decay * soap_stats + (1.0 - stat_decay) * (factor * factor) * (
-        all_products.astype(jnp.float32)
-    )
-    own_stat = stat_decay * lax.dynamic_index_in_dim(soap_stats, matrix, 0, keepdims=False) + (
-        1.0 - stat_decay
-    ) * (factor * factor) * own_products
-    own_basis = renew_basis(own_stat, lax.dynamic_index_in_dim(soap_basis, matrix, 0, keepdims=False))
-    new_basis = all_matrices(after(own_basis, new_stats[0, 0, 0])).astype(jnp.float32)
+    rows = width // 2
+    own_half = lax.dynamic_slice_in_dim(own_products.astype(jnp.bfloat16), replica % 2 * rows, rows, 0)
+    all_products = lax.all_gather(own_half, "vocab").reshape(4, width, width)
+    weight_new = (1.0 - stat_decay) * (factor * factor)
+    own_basis = renew_basis(own_products, soap_stats, soap_basis, weight_new)
+    own_basis = after(own_basis, all_products[0, 0, 0])
+    new_basis = lax.all_gather(own_basis, "vocab").reshape(4, width, width).astype(jnp.float32)
+    new_stats = stat_decay * soap_stats + weight_new * all_products.astype(jnp.float32)
 
     new_norm, m_norm, v_norm = adam_update(norm_p, g_norm, norm_m, norm_v, rate_vector, 0.0)
     updated = update_matrices(

time: 604 us -> 590 us (0.977)
  Pallas kernels: 437 us -> 449 us
  other arithmetic: 49.4 us -> 40.8 us
  matrix products: 10.2 us -> 1.65 us
  local copies, waits for them, and re-layouts: 40.5 us -> 33.2 us
    pallas_call x13 -> x14, Pallas kernels: 243 us -> 257 us  [call(): pl.pallas_call(body, out_shape=outs, in_specs=specs, out_specs=jax.tree.m...]
    dot_general x1 -> x0, matrix products: 8.54 us -> none  [look_up(): lax.dot_general(one_hot(place, halves), paired, (((1,), (0,)), ((), ())))]
    select_n x2 -> x1, other arithmetic: 7.94 us -> 0.96 us  [body(): all_codes = jnp.where(place < 0, -1, 2 * place + left.astype(jnp.int32))]
  transfers between devices with their start and end apart: 13 -> 13, of which waited for: 2 -> 3; matrix products, arithmetic and copies ran while one was open for 6% -> 5% of each run, Pallas kernels for 48% -> 49%
where the time goes in v8:
time: 590 us; the launch traced here: 581 us
  Pallas kernels  449 us (76%)
  other arithmetic  40.8 us (7%)
  local copies, waits for them, and re-layouts  33.2 us (6%)
  between operations  27.4 us (5%)
  waiting for transfers between devices  23.7 us (4%)
    pallas_call x14, Pallas kernels, call(): pl.pallas_call(body, out_shape=outs, in_specs=specs, out_specs=jax.tree.m...  257 us
    pallas_call x7, Pallas kernels, talk(): pl.pallas_call(body, out_shape=outs, in_specs=[vmem] * len(args) + [pl.Bl...  163 us
    pallas_call x1, Pallas kernels, update_matrices(): pl.pallas_call(update_kernel, grid=(4,), out_shape=tuple((full(*part.shap...  28.7 us
    psum x1, waiting for transfers between devices, body(): target_sum = lax.psum(target_part, 'vocab')  13.6 us
  transfers between devices with their start and end apart: 13, of which 3 were waited for; matrix products, arithmetic and copies ran while one was open for 5% of the time, Pallas kernels for 49%

profile of v8, /device:TPU:0, one launch (start us, length us, event | category | flops | bytes accessed | tf_op | source)
XLA Modules:
  0.0 580.6 jit_solution(6635507861883296377)
XLA Ops:
  9.9 7.9 %shard_map.332 = (s32[4,2,1024]{2,1,0:T(2,128)}, f32[4,16,128]{2,1,0:T(8,128)}) custom-call(s32[2,1024]{1,0:T(2,128)} %pad_add_fusion.refs_0_, f32[16,128]{1,0:T(8,128)} %pad_convert_fusion.refs_1_), custom_call_target="tpu_custom_call" | custom-call | flops 15000000512 | tf_op jit(solution)/shard_map/pallas_call | solution.py:801
  22.5 2.0 copy.67.refs_0_
  28.2 2.0 copy.68.refs_4_
  30.2 2.4 fusion.2.refs_1_.refs_5_
  32.6 11.7 %shard_map.333 = bf16[4096,128]{1,0:T(8,128)(2,1)} custom-call(s32[4096,1]{1,0:T(8,128)} %copy.67.refs_0_, bf16[2432,256]{1,0:T(8,128)(2,1)} %fusion.2.refs_1_.refs_5_), custom_call_target="tpu_custom_call" | custom-call | flops 5000000000 | tf_op jit(solution)/shard_map/pallas_call | solution.py:62
  44.3 50.9 %shard_map.334 = (f32[1024,512]{1,0:T(8,128)}, bf16[4,512,512]{2,1,0:T(8,128)(2,1)}, bf16[2,2048,512]{2,1,0:T(8,128)(2,1)}, bf16[4096,128]{1,0:T(8,128)(2,1)}) custom-call(bf16[4,1024,128]{2,1,0:T(8,128)(2,1)} %bitcast.173, f32[1024,512]{1,0:T(8,128)} %constant.189.clone.refs_1_, bf16[4,128,512]{2,1,0:T(8,128)(2,1)} %get-tuple-element.192.refs_2_, ...), custom_call_target="tpu_custom_call" | custom-call | flops 49999998976 | tf_op jit(solution)/shard_map/pallas_call | solution.py:801
  98.0 2.0 collective-permute-start.2
  105.3 19.7 %shard_map.335 = (f32[1024,512]{1,0:T(8,128)}, bf16[1024,512]{1,0:T(8,128)(2,1)}, bf16[512,1024]{1,0:T(8,128)(2,1)}, bf16[512,1024]{1,0:T(8,128)(2,1)}, bf16[512...) custom-call(f32[1024,512]{1,0:T(8,128)} %get-tuple-element.101.refs_0_.refs_1_, ...), custom_call_target="tpu_custom_call" | custom-call | flops 20000000000 | tf_op jit(solution)/shard_map/pallas_call | solution.py:62
  125.0 11.5 %shard_map.336 = (f32[1024,512]{1,0:T(8,128)}, bf16[1024,512]{1,0:T(8,128)(2,1)}, bf16[1024,512]{1,0:T(8,128)(2,1)}) custom-call(f32[1024,512]{1,0:T(8,128)} %get-tuple-element.104.refs_0_.refs_3_, f32[2,512]{1,0:T(2,128)} %get-tuple-element.223.refs_1_.refs_4_, f32[2,512]{1,0:T(2,128)} %pad_maximum_fusion.6.refs_2_, ...), custom_call_target="tpu_custom_call" | custom-call | flops 12000000000 | tf_op jit(solution)/shard_map/pallas_call | solution.py:62
  136.6 8.8 %collective-permute-done.2.refs_7_.refs_8_.refs_6_ = bf16[1024,512]{1,0:T(8,128)(2,1)} collective-permute-done((bf16[1024,512]{1,0:T(8,128)(2,1)}, bf16[1024,512]{1,0:T(8,128)(2,1)}, u32[]{:S(2)}, u32[]{:S(2)}) %collective-permute-start.2) | collective-permute-done | bytes 1048608 | tf_op jit(solution)/shard_map/ppermute | solution.py:192
  145.4 13.6 %all-reduce.7.cloned.1.call-done.refs_0_ = bf16[4,1024,128]{2,1,0:T(8,128)(2,1)} async-done(((bf16[4,1024,128]{2,1,0:T(8,128)(2,1)}), bf16[4,1024,128]{2,1,0:T(8,128)(2,1)}) %all-reduce.7.cloned.1.call-update) | async-done | bytes 1048592 | tf_op jit(solution)/shard_map/psum | solution.py:1413
  159.0 13.0 %shard_map.337.refs_0_.refs_1_ = f32[1024,512]{1,0:T(8,128)} custom-call(bf16[4,1024,128]{2,1,0:T(8,128)(2,1)} %all-reduce.7.cloned.1.call-done.refs_0_, f32[1024,512]{1,0:T(8,128)} %constant.189.clone.refs_1_, f32[1024,512]{1,0:T(8,128)} %get-tuple-element.106.refs_2_.refs_1_), custom_call_target="tpu_custom_call" | custom-call | flops 15000000512 | tf_op jit(solution)/shard_map/pallas_call | solution.py:801
  187.0 18.2 %shard_map.338 = (f32[1024,512]{1,0:T(8,128)}, bf16[1024,512]{1,0:T(8,128)(2,1)}, bf16[512,1024]{1,0:T(8,128)(2,1)}, bf16[512,1024]{1,0:T(8,128)(2,1)}, bf16[512...) custom-call(f32[1024,512]{1,0:T(8,128)} %shard_map.337.refs_0_.refs_1_, ...), custom_call_target="tpu_custom_call" | custom-call | flops 20000000000 | tf_op jit(solution)/shard_map/pallas_call | solution.py:62
  205.2 20.0 %shard_map.339 = (f32[1024,512]{1,0:T(8,128)}, bf16[1024,512]{1,0:T(8,128)(2,1)}, bf16[512,1024]{1,0:T(8,128)(2,1)}, bf16[512,1024]{1,0:T(8,128)(2,1)}, bf16[512...) custom-call(f32[1024,512]{1,0:T(8,128)} %get-tuple-element.111.refs_0_.refs_1_,, ...), custom_call_target="tpu_custom_call" | custom-call | flops 20000000000 | tf_op jit(solution)/shard_map/pallas_call | solution.py:62
  225.2 12.9 %shard_map.340 = (f32[1024,512]{1,0:T(8,128)}, bf16[1024,512]{1,0:T(8,128)(2,1)}, bf16[1024,512]{1,0:T(8,128)(2,1)}, bf16[2,2048,512]{2,1,0:T(8,128)(2,1)}) custom-call(f32[1024,512]{1,0:T(8,128)} %get-tuple-element.113.refs_0_.refs_4_, f32[2,512]{1,0:T(2,128)} %get-tuple-element.225.refs_1_.refs_5_, f32[2,512]{1,0:T(2,128)} %pad_maximum_fusion.10.refs_2_.refs_3_, ...), custom_call_target="tpu_custom_call" | custom-call | flops 12000000000 | tf_op jit(solution)/shard_map/pallas_call | solution.py:62
  238.1 6.3 %shard_map.341 = (bf16[256,512]{1,0:T(8,128)(2,1)}, f32[8,256]{1,0:T(8,128)}) custom-call(bf16[1024,512]{1,0:T(8,128)(2,1)} %get-tuple-element.114.refs_0_, s32[256,1]{1,0:T(8,128)} %copy.69.refs_1_, s32[1,256]{1,0:T(1,128)} %broadcast_subtract_fusion.refs_2_.refs_3_, bf16[4736,512]{1,0:T(8,128)(2,1)} %all-gather.7.cloned.1.call-done.refs_3_.refs_4_), custom_call_target="tpu_custom_call" | custom-call | flops 6000000000 | tf_op jit(solution)/shard_map/pallas_call | solution.py:62
  244.4 6.9 %shard_map.342.refs_1_ = f32[8,8,256]{2,1,0:T(8,128)} custom-call(f32[8,256]{1,0:T(8,128)} %get-tuple-element.116.refs_0_), custom_call_target="tpu_custom_call" | custom-call | flops 15000000512 | tf_op jit(solution)/shard_map/pallas_call | solution.py:801
  251.4 10.3 %shard_map.343 = (bf16[256,512]{1,0:T(8,128)(2,1)}, bf16[4,4736,128]{2,1,0:T(8,128)(2,1)}, f32[1,256]{1,0:T(1,128)}) custom-call(bf16[256,512]{1,0:T(8,128)(2,1)} %get-tuple-element.115.refs_0_, f32[8,8,256]{2,1,0:T(8,128)} %shard_map.342.refs_1_, f32[1,256]{1,0:T(1,128)} %bitcast.166, s32[1,256]{1,0:T(1,128)} %broadcast_subtract_fusion.refs_2_.refs_3_, ...), custom_call_target="tpu_custom_call" | custom-call | flops 8000000000 | tf_op jit(solution)/shard_map/pallas_call | solution.py:62
  263.9 15.0 %shard_map.344.refs_0_ = bf16[256,512]{1,0:T(8,128)(2,1)} custom-call(bf16[256,512]{1,0:T(8,128)(2,1)} %get-tuple-element.117.refs_0_), custom_call_target="tpu_custom_call" | custom-call | flops 15000000512 | tf_op jit(solution)/shard_map/pallas_call | solution.py:801
  278.9 19.9 %shard_map.345 = (f32[1024,512]{1,0:T(8,128)}, f32[2,512]{1,0:T(2,128)}, f32[2,512]{1,0:T(2,128)}, bf16[4,64,512]{2,1,0:T(8,128)(2,1)}, bf16[4,64,512]{2,1,0:T(8,128)(2,1)}) custom-call(bf16[256,512]{1,0:T(8,128)(2,1)} %shard_map.344.refs_0_, s32[1,256]{1,0:T(1,128)} %refs_1_.5, f32[1024,512]{1,0:T(8,128)} %get-tuple-element.118.refs_2_, ...), custom_call_target="tpu_custom_call" | custom-call | flops 16999999488 | tf_op jit(solution)/shard_map/pallas_call | solution.py:62
  298.8 25.3 %shard_map.346 = (f32[1024,512]{1,0:T(8,128)}, f32[2,512]{1,0:T(2,128)}, bf16[4,64,512]{2,1,0:T(8,128)(2,1)}, f32[1024,512]{1,0:T(8,128)}) custom-call(f32[1024,512]{1,0:T(8,128)} %get-tuple-element.121.refs_0_, f32[1024,512]{1,0:T(8,128)} %get-tuple-element.111.refs_0_.refs_1_, f32[2,512]{1,0:T(2,128)} %get-tuple-element.224.refs_1_.refs_2_, ...), custom_call_target="tpu_custom_call" | custom-call | flops 24999999488 | tf_op jit(solution)/shard_map/pallas_call | solution.py:62
  326.1 24.3 %shard_map.347 = (f32[1024,512]{1,0:T(8,128)}, f32[2,512]{1,0:T(2,128)}, bf16[4,64,512]{2,1,0:T(8,128)(2,1)}, bf16[4,1024,128]{2,1,0:T(8,128)(2,1)}) custom-call(f32[1024,512]{1,0:T(8,128)} %get-tuple-element.132.refs_0_, f32[1024,512]{1,0:T(8,128)} %shard_map.337.refs_0_.refs_1_, f32[2,512]{1,0:T(2,128)} %pad_maximum_fusion.7.refs_1_.refs_2_, ...), custom_call_target="tpu_custom_call" | custom-call | flops 24999999488 | tf_op jit(solution)/shard_map/pallas_call | solution.py:62
  350.4 20.0 %shard_map.348 = (f32[1024,512]{1,0:T(8,128)}, f32[2,512]{1,0:T(2,128)}, f32[2,512]{1,0:T(2,128)}, bf16[4,64,512]{2,1,0:T(8,128)(2,1)}, bf16[4,64,512]{2,1,0:T(8,128)(2,1)}) custom-call(f32[1024,512]{1,0:T(8,128)} %get-tuple-element.129.refs_0_, f32[1024,512]{1,0:T(8,128)} %get-tuple-element.106.refs_2_.refs_1_, f32[2,512]{1,0:T(2,128)} %pad_maximum_fusion.6.refs_2_, ...), custom_call_target="tpu_custom_call" | custom-call | flops 16999999488 | tf_op jit(solution)/shard_map/pallas_call | solution.py:62
  373.0 2.3 multiply_reduce_fusion
  379.3 27.1 %shard_map.349 = (f32[1024,512]{1,0:T(8,128)}, f32[2,512]{1,0:T(2,128)}, bf16[4,64,512]{2,1,0:T(8,128)(2,1)}, bf16[4,1024,128]{2,1,0:T(8,128)(2,1)}) custom-call(f32[1024,512]{1,0:T(8,128)} %get-tuple-element.141.refs_0_, f32[1024,512]{1,0:T(8,128)} %get-tuple-element.101.refs_0_.refs_1_, f32[2,512]{1,0:T(2,128)} %get-tuple-element.222.refs_1_.refs_2_, ...), custom_call_target="tpu_custom_call" | custom-call | flops 24999999488 | tf_op jit(solution)/shard_map/pallas_call | solution.py:62
  410.5 2.2 broadcast_in_dim.69.refs_8_
  412.7 47.7 %shard_map.350 = (bf16[4,8,64,512]{3,2,1,0:T(8,128)(2,1)}, f32[1,512]{1,0:T(1,128)}, bf16[4,1024,128]{2,1,0:T(8,128)(2,1)}, bf16[4,1024,128]{2,1,0:T(8,128)(2,1)...) custom-call(bf16[4,64,512]{2,1,0:T(8,128)(2,1)} %get-tuple-element.151.refs_0_, ...), custom_call_target="tpu_custom_call" | custom-call | flops 40000000000 | tf_op jit(solution)/shard_map/pallas_call | solution.py:801
  470.3 21.1 %shard_map.351 = (f32[512,512]{1,0:T(8,128)}, f32[8,128]{1,0:T(8,128)}) custom-call(f32[512,512]{1,0:T(8,128)} %fusion.5.refs_0_, f32[8,128]{1,0:T(8,128)} %broadcast_in_dim.70.refs_1_), custom_call_target="tpu_custom_call" | custom-call | flops 15000000512 | tf_op jit(solution)/shard_map/pallas_call | solution.py:801
  496.9 30.1 %shard_map.353 = bf16[256,512]{1,0:T(8,128)(2,1)} custom-call(f32[512,512]{1,0:T(8,128)} %get-tuple-element.177.refs_0_, f32[4,512,512]{2,1,0:T(8,128)} %refs_1_.7, f32[4,512,512]{2,1,0:T(8,128)} %refs_2_.7, f32[1]{0:T(128)} %bitcast.79.refs_3_), custom_call_target="tpu_custom_call" | custom-call | flops 28999999488 | tf_op jit(solution)/shard_map/pallas_call | solution.py:62
  536.7 28.7 %shard_map.352 = (f32[12,128,512]{2,1,0:T(8,128)}, f32[12,128,512]{2,1,0:T(8,128)}, f32[12,128,512]{2,1,0:T(8,128)}, f32[4736,128]{1,0:T(8,128)}, f32[4736,128]{...) custom-call(f32[1]{0:T(128)} %bitcast.69.refs_0_, ...), custom_call_target="tpu_custom_call" | custom-call | flops 20000000000 | tf_op jit(solution)/shard_map/pallas_call | solution.py:656
  565.4 2.9 multiply_add_fusion
  568.2 4.2 convert.20
  (197 shorter events, 62.4 us)
Async XLA Ops:
  7.2 151.9 %all-reduce.7.cloned.1.call-start = ((), (), s32[]{:S(2)}) async-start(), calls=%async_computation.2 | async-start | bytes 2097152 | tf_op jit(solution)/shard_map/psum | solution.py:1413
  9.9 10.2 %copy-start.7 = (f32[4,512,512]{2,1,0:T(8,128)S(1)}, f32[4,512,512]{2,1,0:T(8,128)}, u32[]{:S(2)}) copy-start(f32[4,512,512]{2,1,0:T(8,128)} %refs_11_.1) | copy-start | bytes 12582916
  44.3 50.9 %copy-start.3 = (bf16[4,128,512]{2,1,0:T(8,128)(2,1)S(1)}, bf16[4,128,512]{2,1,0:T(8,128)(2,1)}, u32[]{:S(2)}) copy-start(bf16[4,128,512]{2,1,0:T(8,128)(2,1)} %get-tuple-element.190) | copy-start | bytes 1572868
  44.3 50.9 %copy-start.5 = (bf16[4,128,512]{2,1,0:T(8,128)(2,1)S(1)}, bf16[4,128,512]{2,1,0:T(8,128)(2,1)}, u32[]{:S(2)}) copy-start(bf16[4,128,512]{2,1,0:T(8,128)(2,1)} %get-tuple-element.191) | copy-start | bytes 1572868
  95.2 5.3 copy-start
  95.2 6.5 %copy-start.22 = (f32[4,16,128]{2,1,0:T(8,128)S(1)}, f32[4,16,128]{2,1,0:T(8,128)}, u32[]{:S(2)}) copy-start(f32[4,16,128]{2,1,0:T(8,128)} %get-tuple-element.102) | copy-start | bytes 98308
  96.5 40.1 %collective-permute-start = (bf16[1024,512]{1,0:T(8,128)(2,1)}, bf16[1024,512]{1,0:T(8,128)(2,1)}, u32[]{:S(2)}, u32[]{:S(2)}) collective-permute-start(bf16[1024,512]{1,0:T(8,128)(2,1)} %maximum_select_fusion), channel_id=1, source_target_pairs={{0,8},{8,0},{16,24},{24,16},{1,9},{9,1},{17,25},{25,17},{2,10},{10... | collective-permute-start | bytes 3145736 | tf_op jit(solution)/shard_map/ppermute | solution.py:192
  97.5 39.1 %collective-permute-start.1 = (bf16[1024,512]{1,0:T(8,128)(2,1)}, bf16[1024,512]{1,0:T(8,128)(2,1)}, u32[]{:S(2)}, u32[]{:S(2)}) collective-permute-start(bf16[1024,512]{1,0:T(8,128)(2,1)} %maximum_select_fusion), channel_id=1, source_target_pairs={{0,16},{8,24},{16,0},{24,8},{1,17},{9,25},{17,1},{25,9},{2,18},{10... | collective-permute-start | bytes 3145736 | tf_op jit(solution)/shard_map/ppermute | solution.py:192
  98.0 47.4 %collective-permute-start.2 = (bf16[1024,512]{1,0:T(8,128)(2,1)}, bf16[1024,512]{1,0:T(8,128)(2,1)}, u32[]{:S(2)}, u32[]{:S(2)}) collective-permute-start(bf16[1024,512]{1,0:T(8,128)(2,1)} %maximum_select_fusion), channel_id=1, source_target_pairs={{0,24},{8,16},{16,8},{24,0},{1,25},{9,17},{17,9},{25,1},{2,26},{10... | collective-permute-start | bytes 3145736 | tf_op jit(solution)/shard_map/ppermute | solution.py:192
  100.0 138.1 %all-gather.7.cloned.1.call-start = ((), (), s32[]{:S(2)}) async-start(), calls=%async_computation.3 | async-start | bytes 6062080 | tf_op jit(solution)/shard_map/all_gather | solution.py:1423
  145.4 27.8 %collective-permute-start.5 = (bf16[1024,512]{1,0:T(8,128)(2,1)}, bf16[1024,512]{1,0:T(8,128)(2,1)}, u32[]{:S(2)}, u32[]{:S(2)}) collective-permute-start(bf16[1024,512]{1,0:T(8,128)(2,1)} %collective-permute-done.2.refs_7_.refs_8_.refs_6_), channel_id=1, source_target_pairs={{0,1},{1,0},{2,3},{3,2},{4,5},{5,4},{6,7},{7,6},{8,9},{9,8},{10,11... | collective-permute-start | bytes 3145736 | tf_op jit(solution)/shard_map/ppermute | solution.py:192
  176.9 6.4 %copy-start.4 = (bf16[4,128,512]{2,1,0:T(8,128)(2,1)S(1)}, bf16[4,128,512]{2,1,0:T(8,128)(2,1)}, u32[]{:S(2)}) copy-start(bf16[4,128,512]{2,1,0:T(8,128)(2,1)} %get-tuple-element.190) | copy-start | bytes 1572868
  176.9 6.4 %copy-start.6 = (bf16[4,128,512]{2,1,0:T(8,128)(2,1)S(1)}, bf16[4,128,512]{2,1,0:T(8,128)(2,1)}, u32[]{:S(2)}) copy-start(bf16[4,128,512]{2,1,0:T(8,128)(2,1)} %get-tuple-element.191) | copy-start | bytes 1572868
  176.9 173.5 %reduce-scatter.7.cloned.1.call-start = ((), (), s32[]{:S(2)}) async-start(), calls=%async_computation.7 | async-start | bytes 6062080
  181.4 3.3 collective-permute-start.3
  181.8 4.0 collective-permute-start.4
  261.7 111.3 %reduce-scatter.9.cloned.1.call-start = ((), (), s32[]{:S(2)}) async-start(), calls=%async_computation.8 | async-start | bytes 983040
  298.8 25.3 %copy-start.15 = (bf16[4,64,512]{2,1,0:T(8,128)(2,1)S(1)}, bf16[4,64,512]{2,1,0:T(8,128)(2,1)}, u32[]{:S(2)}) copy-start(bf16[4,64,512]{2,1,0:T(8,128)(2,1)} %get-tuple-element.149) | copy-start | bytes 786436
  298.8 25.4 %copy-start.16 = (bf16[4,64,512]{2,1,0:T(8,128)(2,1)S(1)}, bf16[4,64,512]{2,1,0:T(8,128)(2,1)}, u32[]{:S(2)}) copy-start(bf16[4,64,512]{2,1,0:T(8,128)(2,1)} %get-tuple-element.150) | copy-start | bytes 786436
  326.1 80.4 %all-gather.9.cloned.1.call-start = ((), (), s32[]{:S(2)}) async-start(), calls=%async_computation.4 | async-start | bytes 1769472 | tf_op jit(solution)/shard_map/all_gather | solution.py:1462
  350.4 26.8 %copy-start.19 = (bf16[4,8,2,128]{3,2,1,0:T(2,128)(2,1)S(1)}, bf16[4,8,2,128]{3,2,1,0:T(2,128)(2,1)}, u32[]{:S(2)}) copy-start(bf16[4,8,2,128]{3,2,1,0:T(2,128)(2,1)} %get-tuple-element.195) | copy-start | bytes 49156
  350.4 27.6 %copy-start.35 = (f32[1,256]{1,0:T(1,128)S(1)}, f32[1,256]{1,0:T(1,128)}, u32[]{:S(2)}) copy-start(f32[1,256]{1,0:T(1,128)} %get-tuple-element.165) | copy-start | bytes 3076
  375.3 151.8 %all-gather.11.cloned.1.call-start = ((), (), s32[]{:S(2)}) async-start(), calls=%async_computation.5 | async-start | bytes 2359296 | tf_op jit(solution)/shard_map/all_gather | solution.py:1523
  379.3 30.3 %copy-start.32 = (f32[2,512]{1,0:T(2,128)S(1)}, f32[2,512]{1,0:T(2,128)}, u32[]{:S(2)}) copy-start(f32[2,512]{1,0:T(2,128)} %get-tuple-element.158) | copy-start | bytes 12292
  379.3 30.3 %copy-start.31 = (f32[2,512]{1,0:T(2,128)S(1)}, f32[2,512]{1,0:T(2,128)}, u32[]{:S(2)}) copy-start(f32[2,512]{1,0:T(2,128)} %get-tuple-element.159) | copy-start | bytes 12292
  379.3 30.4 %copy-start.30 = (f32[2,512]{1,0:T(2,128)S(1)}, f32[2,512]{1,0:T(2,128)}, u32[]{:S(2)}) copy-start(f32[2,512]{1,0:T(2,128)} %get-tuple-element.160) | copy-start | bytes 12292
  379.3 30.4 %copy-start.29 = (f32[2,512]{1,0:T(2,128)S(1)}, f32[2,512]{1,0:T(2,128)}, u32[]{:S(2)}) copy-start(f32[2,512]{1,0:T(2,128)} %get-tuple-element.161) | copy-start | bytes 12292
  379.3 30.4 %copy-start.28 = (f32[2,512]{1,0:T(2,128)S(1)}, f32[2,512]{1,0:T(2,128)}, u32[]{:S(2)}) copy-start(f32[2,512]{1,0:T(2,128)} %get-tuple-element.162) | copy-start | bytes 12292
  379.3 30.4 %copy-start.27 = (f32[2,512]{1,0:T(2,128)S(1)}, f32[2,512]{1,0:T(2,128)}, u32[]{:S(2)}) copy-start(f32[2,512]{1,0:T(2,128)} %get-tuple-element.163) | copy-start | bytes 12292
  493.3 75.0 %all-gather.13.cloned.1.call-start = ((), (), s32[]{:S(2)}) async-start(), calls=%async_computation.6 | async-start | bytes 2359296 | tf_op jit(solution)/shard_map/all_gather | solution.py:1527
  536.7 28.7 %copy-start.8 = (f32[4,512,512]{2,1,0:T(8,128)S(1)}, f32[4,512,512]{2,1,0:T(8,128)}, u32[]{:S(2)}) copy-start(f32[4,512,512]{2,1,0:T(8,128)} %refs_1_.7) | copy-start | bytes 12582916
  536.7 28.7 %copy-start.11 = (bf16[2048,512]{1,0:T(8,128)(2,1)S(1)}, bf16[2048,512]{1,0:T(8,128)(2,1)}, u32[]{:S(2)}) copy-start(bf16[2048,512]{1,0:T(8,128)(2,1)} %all-gather.11.cloned.1.call-done) | copy-start | bytes 6291460
  (20 other events, 41.3 us)
Sparse Core Ops, SparseCore 0:
  100.1 58.8 all-reduce.6
  177.0 56.5 all-gather.6
  261.8 55.9 reduce-scatter.6
  326.2 23.9 reduce-scatter.8
  375.4 22.9 all-gather.8
  493.4 27.6 all-gather.10
  531.4 27.5 all-gather.12

commit v9 on v8

--- a/solution.py
+++ b/solution.py
@@ -198,7 +198,7 @@
     attn, ffn = attn.astype(jnp.bfloat16), ffn.astype(jnp.bfloat16)
     if owners != 4:
         attn, ffn = (lax.all_gather(part, "dp", axis=1, tiled=True) for part in (attn, ffn))
-        return ((attn[:4],), 0, 0), ((attn[4:],), 0, 0), ((ffn,), 0, 0), ffn[0, 0, 0]
+        return ((attn[:4],), 0, 0), ((attn[4:],), 0, 0), ((ffn,), 0, 0), ffn
     halves = [
         jnp.concatenate([attn[4 * k : 4 * k + 4].reshape(-1, width), ffn[k]]) for k in range(2)
     ]
@@ -211,7 +211,7 @@
     swapped = [flip_sites(part, "vocab", 1) for part in got]
     pieces = (own, *got, *swapped)
     rows = 4 * attn.shape[1]
-    return (pieces, 0, 0), (pieces, 1, 0), (pieces, None, rows), swapped[-1][0, 0]
+    return (pieces, 0, 0), (pieces, 1, 0), (pieces, None, rows), swapped[-1]
 
 
 def attn_forward_kernel(causal, cross, pieces, part, first, *refs):
@@ -513,6 +513,43 @@
         microseconds=17,
         before=before,
     )
+
+
+def follow_kernel(x_ref, out_ref):
+    out_ref[...] = x_ref[...]
+
+
+def follow(x, *before):
+    out = jax.ShapeDtypeStruct(x.shape, x.dtype)
+    return call(follow_kernel, out, x, microseconds=1, before=before)
+
+
+def square_kernel(x_ref, out_ref, square_ref):
+    out_ref[...] = x_ref[...]
+    values = x_ref[...].astype(jnp.float32)
+    square_ref[...] = jnp.sum(values * values, axis=0, keepdims=True)
+
+
+def follow_with_squares(x, *before):
+    outs = (low(*x.shape), full(1, x.shape[1]))
+    return call(square_kernel, outs, x, microseconds=1, before=before)
+
+
+def norm_blocks_kernel(*refs):
+    refs, out_ref = refs[:-1], refs[-1]
+    owners, _, columns = out_ref.shape
+    out_ref[...] = jnp.zeros(out_ref.shape, jnp.float32)
+    for k, ref in enumerate(refs):
+        for owner in range(owners):
+            band = slice(owner * columns, (owner + 1) * columns)
+            out_ref[owner, k : k + 1, :] = ref[0:1, band]
+            out_ref[owner, len(refs) + k : len(refs) + k + 1, :] = ref[1:2, band]
+
+
+def norm_blocks(grads, owners, *before):
+    width = grads[0].shape[1]
+    outs = full(owners, 16, width // owners)
+    return call(norm_blocks_kernel, outs, *grads, microseconds=1, before=before)
 
 
 def look_up_tokens(code_ref, paired_ref, found_ref):
@@ -1334,10 +1371,6 @@
     )
 
 
-def after(array, number):
-    return array + jnp.where(jnp.isnan(number), 1, 0).astype(array.dtype)
-
-
 def body(
     src_ids,
     src_seg,
@@ -1416,11 +1449,23 @@
     )
     self_w, cross_w, dec_ffn_w, ready = late_weights(attn_w[4:], ffn_w[2:], enc_in, enc_mid)
     enc_out, encoded, enc_ffn = ffn_forward(enc_mid, norms[1], norms[2], ((enc_ffn_w,), 0, 0))
+    weight = 1.0 / pick_weights(target_seg, pick_rows)
+    picks = share_selector(width, owners, replicas, replica, width)
+    hidden = ffn_w.shape[1] * owners
+    hidden_picks = share_selector(hidden, owners, replicas, replica, 512)
+    place, left = paired_places(all_ids.reshape(-1))
+    tokens = ()
+    if owners == 4:
+        ones = jnp.broadcast_to(left[:, None], (left.shape[0], width // owners))
+        tokens = (place[None, :], ones.astype(jnp.bfloat16))
     dec_in = swap_owners(
-        target_sum.reshape(owners, length, -1), positional, embed_scale, 3, (enc_out,)
-    )
-    late_table = after(own_table, ready.astype(jnp.float32) + dec_in[0, 0])
-    table_low = lax.all_gather(late_table, "dp", axis=1, tiled=True)
+        target_sum.reshape(owners, length, -1),
+        positional,
+        embed_scale,
+        3,
+        (enc_out, weight, picks, hidden_picks, *tokens),
+    )
+    table_low = lax.all_gather(follow(own_table, ready, dec_in), "dp", axis=1, tiled=True)
     dec_mid, dec_self = attn_forward(
         dec_in, norms[3], self_w, target_seg, target_seg, None, True
     )
@@ -1432,7 +1477,6 @@
     own_labels = labels - replica * vocab_count
     picked, own_stats = loss_forward(final_low, pick_rows, own_labels, table_low)
     (seen,) = gather_small("vocab", 4, own_stats)
-    weight = 1.0 / pick_weights(target_seg, pick_rows)
     grad_picked, table_parts, losses = loss_backward(
         picked, seen, weight, own_labels, table_low, owners
     )
@@ -1441,9 +1485,6 @@
     loss_part = jnp.sum(losses)
     count_part = (target_seg[-1] + 1).astype(jnp.float32)
 
-    picks = share_selector(width, owners, replicas, replica, width)
-    hidden = ffn_w.shape[1] * owners
-    hidden_picks = share_selector(hidden, owners, replicas, replica, 512)
     norm_grads = [None] * 7
     grad, norm_grads[6], norm_grads[5], *ffn_blocks = ffn_backward(
         grad_picked, dec_ffn, hidden_picks, owners, places=pick_rows
@@ -1458,21 +1499,14 @@
     grad, norm_grads[2], norm_grads[1], *ffn_blocks = ffn_backward(
         grad_encoded, enc_ffn, hidden_picks, owners, before=(grad_table, grad)
     )
-    early_sum = after(early, grad[0, 0])
+    early_sum, early_squares = follow_with_squares(early, grad)
     early = lax.all_gather(early_sum, "vocab")
     grad, norm_grads[0], block, source_rows = attn_backward(
         grad, enc_attn, picks, owners, embed_scale, before=(early_sum,)
     )
-    norm_grad = jnp.stack([after(part, early[0, 0, 0]) for part in norm_grads])
-    norm_grad = jnp.concatenate([norm_grad[:, 0], norm_grad[:, 1], jnp.zeros((2, width))], axis=0)
-    norm_grad = jnp.swapaxes(norm_grad.reshape(16, owners, -1), 0, 1)
-    place, left = paired_places(all_ids.reshape(-1))
-    tokens = ()
-    if owners == 4:
-        ones = jnp.broadcast_to(left[:, None], (left.shape[0], width // owners))
-        tokens = (place[None, :], ones.astype(jnp.bfloat16), grad_table)
+    norm_grad = norm_blocks(norm_grads, owners, early)
     late, layer_squares, source_rows, target_rows, norm_grad, *found = share_gradients(
-        [block, self_block, *ffn_blocks], [source_rows, target_rows, norm_grad], 7, (early,), tokens
+        [block, self_block, *ffn_blocks], [source_rows, target_rows, norm_grad], 7, (early,), (*tokens, *[grad_table][: len(tokens)])
     )
     g_norm = jnp.sum(norm_grad, axis=0)[:14]
     if owners == 4:
@@ -1506,7 +1540,7 @@
     first_copy = (replica == 0).astype(jnp.float32)
     raw_squares = (
         jnp.sum(layer_squares)
-        + jnp.sum(jnp.square(early_sum.astype(jnp.float32)))
+        + jnp.sum(early_squares)
         + jnp.sum(embed_squares)
         + first_copy * jnp.sum(g_norm * g_norm)
     )
@@ -1523,7 +1557,7 @@
     all_products = lax.all_gather(own_half, "vocab").reshape(4, width, width)
     weight_new = (1.0 - stat_decay) * (factor * factor)
     own_basis = renew_basis(own_products, soap_stats, soap_basis, weight_new)
-    own_basis = after(own_basis, all_products[0, 0, 0])
+    own_basis = follow(own_basis, all_products)
     new_basis = lax.all_gather(own_basis, "vocab").reshape(4, width, width).astype(jnp.float32)
     new_stats = stat_decay * soap_stats + weight_new * all_products.astype(jnp.float32)
 

time: 590 us -> 570 us (0.966)
  other arithmetic: 40.8 us -> 32.7 us
    slice x6 -> x0, local copies, waits for them, and re-layouts: 5.98 us -> none  [the longest x1 1.2 us: body(): early_sum = after(early, grad[0, 0])]
    pallas_call x14 -> x18, Pallas kernels: 257 us -> 259 us  [call(): pl.pallas_call(body, out_shape=outs, in_specs=specs, out_specs=jax.tree.m...]
  transfers between devices with their start and end apart: 13 -> 13, of which waited for: 3 -> 3; matrix products, arithmetic and copies ran while one was open for 5% -> 5% of each run, Pallas kernels for 49% -> 50%
where the time goes in v9:
time: 570 us; the launch traced here: 563 us
  Pallas kernels  453 us (79%)
  other arithmetic  32.7 us (6%)
  local copies, waits for them, and re-layouts  27.7 us (5%)
  between operations  22.1 us (4%)
  waiting for transfers between devices  20.6 us (4%)
    pallas_call x18, Pallas kernels, call(): pl.pallas_call(body, out_shape=outs, in_specs=specs, out_specs=jax.tree.m...  259 us
    pallas_call x7, Pallas kernels, talk(): pl.pallas_call(body, out_shape=outs, in_specs=[vmem] * len(args) + [pl.Bl...  166 us
    pallas_call x1, Pallas kernels, update_matrices(): pl.pallas_call(update_kernel, grid=(4,), out_shape=tuple((full(*part.shap...  28.7 us
    psum x1, waiting for transfers between devices, body(): target_sum = lax.psum(target_part, 'vocab')  13.4 us
  transfers between devices with their start and end apart: 13, of which 3 were waited for; matrix products, arithmetic and copies ran while one was open for 5% of the time, Pallas kernels for 50%

profile of v9, /device:TPU:0, one launch (start us, length us, event | category | flops | bytes accessed | tf_op | source)
XLA Modules:
  0.0 563.0 jit_solution(16489421688558920785)
XLA Ops:
  9.9 7.9 %shard_map.332 = (s32[4,2,1024]{2,1,0:T(2,128)}, f32[4,16,128]{2,1,0:T(8,128)}) custom-call(s32[2,1024]{1,0:T(2,128)} %pad_add_fusion.refs_0_, f32[16,128]{1,0:T(8,128)} %pad_convert_fusion.refs_1_), custom_call_target="tpu_custom_call" | custom-call | flops 15000000512 | tf_op jit(solution)/shard_map/pallas_call | solution.py:838
  23.1 2.7 copy.61.refs_0_
  26.0 2.1 copy-done.5
  29.2 2.0 copy.62.refs_4_
  32.3 11.7 %shard_map.333 = bf16[4096,128]{1,0:T(8,128)(2,1)} custom-call(s32[4096,1]{1,0:T(8,128)} %copy.61.refs_0_, bf16[2432,256]{1,0:T(8,128)(2,1)} %fusion.2.refs_1_.refs_5_), custom_call_target="tpu_custom_call" | custom-call | flops 5000000000 | tf_op jit(solution)/shard_map/pallas_call | solution.py:62
  44.0 50.8 %shard_map.334 = (f32[1024,512]{1,0:T(8,128)}, bf16[4,512,512]{2,1,0:T(8,128)(2,1)}, bf16[2,2048,512]{2,1,0:T(8,128)(2,1)}, bf16[4096,128]{1,0:T(8,128)(2,1)}) custom-call(bf16[4,1024,128]{2,1,0:T(8,128)(2,1)} %bitcast.151, f32[1024,512]{1,0:T(8,128)} %constant.177.clone.refs_1_, bf16[4,128,512]{2,1,0:T(8,128)(2,1)} %get-tuple-element.194.refs_2_, ...), custom_call_target="tpu_custom_call" | custom-call | flops 49999998976 | tf_op jit(solution)/shard_map/pallas_call | solution.py:838
  96.8 2.0 collective-permute-start.2
  104.8 19.7 %shard_map.335 = (f32[1024,512]{1,0:T(8,128)}, bf16[1024,512]{1,0:T(8,128)(2,1)}, bf16[512,1024]{1,0:T(8,128)(2,1)}, bf16[512,1024]{1,0:T(8,128)(2,1)}, bf16[512...) custom-call(f32[1024,512]{1,0:T(8,128)} %get-tuple-element.103.refs_0_.refs_1_, ...), custom_call_target="tpu_custom_call" | custom-call | flops 20000000000 | tf_op jit(solution)/shard_map/pallas_call | solution.py:62
  124.5 11.5 %shard_map.336 = (f32[1024,512]{1,0:T(8,128)}, bf16[1024,512]{1,0:T(8,128)(2,1)}, bf16[1024,512]{1,0:T(8,128)(2,1)}) custom-call(f32[1024,512]{1,0:T(8,128)} %get-tuple-element.106.refs_0_.refs_3_, f32[2,512]{1,0:T(2,128)} %get-tuple-element.225.refs_1_.refs_4_, f32[2,512]{1,0:T(2,128)} %pad_maximum_fusion.6.refs_2_, ...), custom_call_target="tpu_custom_call" | custom-call | flops 12000000000 | tf_op jit(solution)/shard_map/pallas_call | solution.py:62
  138.2 5.7 %collective-permute-done.2.refs_7_.refs_8_.refs_6_ = bf16[1024,512]{1,0:T(8,128)(2,1)} collective-permute-done((bf16[1024,512]{1,0:T(8,128)(2,1)S(1)}, bf16[1024,512]{1,0:T(8,128)(2,1)}, u32[]{:S(2)}, u32[]{:S(2)}) %collective-permute-start.2) | collective-permute-done | bytes 1048608 | tf_op jit(solution)/shard_map/ppermute | solution.py:192
  143.9 13.4 %all-reduce.7.cloned.1.call-done.refs_0_ = bf16[4,1024,128]{2,1,0:T(8,128)(2,1)} async-done(((bf16[4,1024,128]{2,1,0:T(8,128)(2,1)}), bf16[4,1024,128]{2,1,0:T(8,128)(2,1)}) %all-reduce.7.cloned.1.call-update) | async-done | bytes 1048592 | tf_op jit(solution)/shard_map/psum | solution.py:1446
  157.3 2.3 broadcast_in_dim.34.refs_7_.refs_8_
  159.7 13.3 %shard_map.337.refs_0_.refs_2_.refs_1_ = f32[1024,512]{1,0:T(8,128)} custom-call(bf16[4,1024,128]{2,1,0:T(8,128)(2,1)} %all-reduce.7.cloned.1.call-done.refs_0_, f32[1024,512]{1,0:T(8,128)} %constant.177.clone.refs_1_, f32[1024,512]{1,0:T(8,128)} %get-tuple-element.108.refs_2_.refs_1_, f32[256]{0:T(256)} %broadcast_divide_fusion.refs_3_, ...), custom_call_target="tpu_custom_call" | custom-call | flops 15000000512 | tf_op jit(solution)/shard_map/pallas_call | solution.py:838
  174.0 2.4 shard_map.341
  182.8 17.4 %shard_map.338 = (f32[1024,512]{1,0:T(8,128)}, bf16[1024,512]{1,0:T(8,128)(2,1)}, bf16[512,1024]{1,0:T(8,128)(2,1)}, bf16[512,1024]{1,0:T(8,128)(2,1)}, bf16[512...) custom-call(f32[1024,512]{1,0:T(8,128)} %shard_map.337.refs_0_.refs_2_.refs_1_,, ...), custom_call_target="tpu_custom_call" | custom-call | flops 20000000000 | tf_op jit(solution)/shard_map/pallas_call | solution.py:62
  200.2 18.8 %shard_map.339 = (f32[1024,512]{1,0:T(8,128)}, bf16[1024,512]{1,0:T(8,128)(2,1)}, bf16[512,1024]{1,0:T(8,128)(2,1)}, bf16[512,1024]{1,0:T(8,128)(2,1)}, bf16[512...) custom-call(f32[1024,512]{1,0:T(8,128)} %get-tuple-element.113.refs_0_.refs_1_,, ...), custom_call_target="tpu_custom_call" | custom-call | flops 20000000000 | tf_op jit(solution)/shard_map/pallas_call | solution.py:62
  219.0 12.8 %shard_map.340 = (f32[1024,512]{1,0:T(8,128)}, bf16[1024,512]{1,0:T(8,128)(2,1)}, bf16[1024,512]{1,0:T(8,128)(2,1)}, bf16[2,2048,512]{2,1,0:T(8,128)(2,1)}) custom-call(f32[1024,512]{1,0:T(8,128)} %get-tuple-element.115.refs_0_.refs_4_, f32[2,512]{1,0:T(2,128)} %get-tuple-element.227.refs_1_.refs_5_, f32[2,512]{1,0:T(2,128)} %pad_maximum_fusion.10.refs_2_.refs_3_, ...), custom_call_target="tpu_custom_call" | custom-call | flops 12000000000 | tf_op jit(solution)/shard_map/pallas_call | solution.py:62
  233.1 6.3 %shard_map.342 = (bf16[256,512]{1,0:T(8,128)(2,1)}, f32[8,256]{1,0:T(8,128)}) custom-call(bf16[1024,512]{1,0:T(8,128)(2,1)} %get-tuple-element.116.refs_0_, s32[256,1]{1,0:T(8,128)} %copy.63.refs_1_, s32[1,256]{1,0:T(1,128)} %broadcast_subtract_fusion.refs_2_.refs_3_, bf16[4736,512]{1,0:T(8,128)(2,1)} %all-gather.8.cloned.1.call-done.refs_3_.refs_4_), custom_call_target="tpu_custom_call" | custom-call | flops 6000000000 | tf_op jit(solution)/shard_map/pallas_call | solution.py:62
  239.5 7.4 %shard_map.343.refs_1_ = f32[8,8,256]{2,1,0:T(8,128)} custom-call(f32[8,256]{1,0:T(8,128)} %get-tuple-element.118.refs_0_), custom_call_target="tpu_custom_call" | custom-call | flops 15000000512 | tf_op jit(solution)/shard_map/pallas_call | solution.py:838
  246.9 10.5 %shard_map.344 = (bf16[256,512]{1,0:T(8,128)(2,1)}, bf16[4,4736,128]{2,1,0:T(8,128)(2,1)}, f32[1,256]{1,0:T(1,128)}) custom-call(bf16[256,512]{1,0:T(8,128)(2,1)} %get-tuple-element.117.refs_0_, f32[8,8,256]{2,1,0:T(8,128)} %shard_map.343.refs_1_, f32[1,256]{1,0:T(1,128)} %bitcast.143, s32[1,256]{1,0:T(1,128)} %broadcast_subtract_fusion.refs_2_.refs_3_, ...), custom_call_target="tpu_custom_call" | custom-call | flops 8000000000 | tf_op jit(solution)/shard_map/pallas_call | solution.py:62
  257.4 16.2 %shard_map.345.refs_0_ = bf16[256,512]{1,0:T(8,128)(2,1)} custom-call(bf16[256,512]{1,0:T(8,128)(2,1)} %get-tuple-element.119.refs_0_), custom_call_target="tpu_custom_call" | custom-call | flops 15000000512 | tf_op jit(solution)/shard_map/pallas_call | solution.py:838
  273.6 19.6 %shard_map.346 = (f32[1024,512]{1,0:T(8,128)}, f32[2,512]{1,0:T(2,128)}, f32[2,512]{1,0:T(2,128)}, bf16[4,64,512]{2,1,0:T(8,128)(2,1)}, bf16[4,64,512]{2,1,0:T(8,128)(2,1)}) custom-call(bf16[256,512]{1,0:T(8,128)(2,1)} %shard_map.345.refs_0_, s32[1,256]{1,0:T(1,128)} %refs_1_.5, f32[1024,512]{1,0:T(8,128)} %get-tuple-element.120.refs_2_, ...), custom_call_target="tpu_custom_call" | custom-call | flops 16999999488 | tf_op jit(solution)/shard_map/pallas_call | solution.py:62
  293.3 23.6 %shard_map.347 = (f32[1024,512]{1,0:T(8,128)}, f32[2,512]{1,0:T(2,128)}, bf16[4,64,512]{2,1,0:T(8,128)(2,1)}, f32[1024,512]{1,0:T(8,128)}) custom-call(f32[1024,512]{1,0:T(8,128)} %get-tuple-element.123.refs_0_, f32[1024,512]{1,0:T(8,128)} %get-tuple-element.113.refs_0_.refs_1_, f32[2,512]{1,0:T(2,128)} %get-tuple-element.226.refs_1_.refs_2_, ...), custom_call_target="tpu_custom_call" | custom-call | flops 24999999488 | tf_op jit(solution)/shard_map/pallas_call | solution.py:62
  318.8 23.3 %shard_map.348 = (f32[1024,512]{1,0:T(8,128)}, f32[2,512]{1,0:T(2,128)}, bf16[4,64,512]{2,1,0:T(8,128)(2,1)}, bf16[4,1024,128]{2,1,0:T(8,128)(2,1)}) custom-call(f32[1024,512]{1,0:T(8,128)} %get-tuple-element.134.refs_0_, f32[1024,512]{1,0:T(8,128)} %shard_map.337.refs_0_.refs_2_.refs_1_, f32[2,512]{1,0:T(2,128)} %pad_maximum_fusion.7.refs_1_.refs_2_, ...), custom_call_target="tpu_custom_call" | custom-call | flops 24999999488 | tf_op jit(solution)/shard_map/pallas_call | solution.py:62
  342.1 20.2 %shard_map.349 = (f32[1024,512]{1,0:T(8,128)}, f32[2,512]{1,0:T(2,128)}, f32[2,512]{1,0:T(2,128)}, bf16[4,64,512]{2,1,0:T(8,128)(2,1)}, bf16[4,64,512]{2,1,0:T(8,128)(2,1)}) custom-call(f32[1024,512]{1,0:T(8,128)} %get-tuple-element.131.refs_0_, f32[1024,512]{1,0:T(8,128)} %get-tuple-element.108.refs_2_.refs_1_, f32[2,512]{1,0:T(2,128)} %pad_maximum_fusion.6.refs_2_, ...), custom_call_target="tpu_custom_call" | custom-call | flops 16999999488 | tf_op jit(solution)/shard_map/pallas_call | solution.py:62
  368.5 26.1 %shard_map.351 = (f32[1024,512]{1,0:T(8,128)}, f32[2,512]{1,0:T(2,128)}, bf16[4,64,512]{2,1,0:T(8,128)(2,1)}, bf16[4,1024,128]{2,1,0:T(8,128)(2,1)}) custom-call(f32[1024,512]{1,0:T(8,128)} %get-tuple-element.143.refs_1_.refs_0_, f32[1024,512]{1,0:T(8,128)} %get-tuple-element.103.refs_0_.refs_1_, f32[2,512]{1,0:T(2,128)} %get-tuple-element.224.refs_1_.refs_2_, ...), custom_call_target="tpu_custom_call" | custom-call | flops 24999999488 | tf_op jit(solution)/shard_map/pallas_call | solution.py:62
  396.0 49.5 %shard_map.353 = (bf16[4,8,64,512]{3,2,1,0:T(8,128)(2,1)}, f32[1,512]{1,0:T(1,128)}, bf16[4,1024,128]{2,1,0:T(8,128)(2,1)}, bf16[4,1024,128]{2,1,0:T(8,128)(2,1)...) custom-call(bf16[4,64,512]{2,1,0:T(8,128)(2,1)} %get-tuple-element.154.refs_0_, ...), custom_call_target="tpu_custom_call" | custom-call | flops 40000000000 | tf_op jit(solution)/shard_map/pallas_call | solution.py:838
  455.4 20.9 %shard_map.354 = (f32[512,512]{1,0:T(8,128)}, f32[8,128]{1,0:T(8,128)}) custom-call(f32[512,512]{1,0:T(8,128)} %fusion.5.refs_0_, f32[8,128]{1,0:T(8,128)} %broadcast_in_dim.36.refs_1_), custom_call_target="tpu_custom_call" | custom-call | flops 15000000512 | tf_op jit(solution)/shard_map/pallas_call | solution.py:838
  481.7 30.1 %shard_map.356.refs_0_ = bf16[256,512]{1,0:T(8,128)(2,1)} custom-call(f32[512,512]{1,0:T(8,128)} %get-tuple-element.181.refs_0_, f32[4,512,512]{2,1,0:T(8,128)} %refs_1_.7, f32[4,512,512]{2,1,0:T(8,128)} %refs_2_.7, f32[1]{0:T(128)} %bitcast.67.refs_3_), custom_call_target="tpu_custom_call" | custom-call | flops 28999999488 | tf_op jit(solution)/shard_map/pallas_call | solution.py:62
  519.0 28.7 %shard_map.355 = (f32[12,128,512]{2,1,0:T(8,128)}, f32[12,128,512]{2,1,0:T(8,128)}, f32[12,128,512]{2,1,0:T(8,128)}, f32[4736,128]{1,0:T(8,128)}, f32[4736,128]{...) custom-call(f32[1]{0:T(128)} %bitcast.57.refs_0_, ...), custom_call_target="tpu_custom_call" | custom-call | flops 20000000000 | tf_op jit(solution)/shard_map/pallas_call | solution.py:693
  547.7 2.9 multiply_add_fusion
  550.6 4.2 convert.16
  (154 shorter events, 55.1 us)
Async XLA Ops:
  7.2 150.1 %all-reduce.7.cloned.1.call-start = ((), (), s32[]{:S(2)}) async-start(), calls=%async_computation.2 | async-start | bytes 2097152 | tf_op jit(solution)/shard_map/psum | solution.py:1446
  9.9 10.2 %copy-start.3 = (f32[4,512,512]{2,1,0:T(8,128)S(1)}, f32[4,512,512]{2,1,0:T(8,128)}, u32[]{:S(2)}) copy-start(f32[4,512,512]{2,1,0:T(8,128)} %refs_11_.1) | copy-start | bytes 12582916
  21.4 4.4 copy-start.6
  25.7 2.3 copy-start.5
  25.9 2.4 copy-start.1
  94.8 4.5 copy-start.20
  94.8 4.7 copy-start
  94.8 5.0 copy-start.16
  94.8 5.0 copy-start.17
  94.8 6.4 %copy-start.13 = (bf16[4,8,2,128]{3,2,1,0:T(2,128)(2,1)S(1)}, bf16[4,8,2,128]{3,2,1,0:T(2,128)(2,1)}, u32[]{:S(2)}) copy-start(bf16[4,8,2,128]{3,2,1,0:T(2,128)(2,1)} %get-tuple-element.211) | copy-start | bytes 49156
  95.2 43.1 %collective-permute-start = (bf16[1024,512]{1,0:T(8,128)(2,1)S(1)}, bf16[1024,512]{1,0:T(8,128)(2,1)}, u32[]{:S(2)}, u32[]{:S(2)}) collective-permute-start(bf16[1024,512]{1,0:T(8,128)(2,1)S(1)} %maximum_select_fusion), channel_id=1, source_target_pairs={{0,8},{8,0},{16,24},{24,16},{1,9},{9,1},{17,25},{25,17},{2,10},{10... | collective-permute-start | bytes 3145736 | tf_op jit(solution)/shard_map/ppermute | solution.py:192
  96.2 42.0 %collective-permute-start.1 = (bf16[1024,512]{1,0:T(8,128)(2,1)S(1)}, bf16[1024,512]{1,0:T(8,128)(2,1)}, u32[]{:S(2)}, u32[]{:S(2)}) collective-permute-start(bf16[1024,512]{1,0:T(8,128)(2,1)S(1)} %maximum_select_fusion), channel_id=1, source_target_pairs={{0,16},{8,24},{16,0},{24,8},{1,17},{9,25},{17,1},{25,9},{2,18},{10... | collective-permute-start | bytes 3145736 | tf_op jit(solution)/shard_map/ppermute | solution.py:192
  96.8 47.2 %collective-permute-start.2 = (bf16[1024,512]{1,0:T(8,128)(2,1)S(1)}, bf16[1024,512]{1,0:T(8,128)(2,1)}, u32[]{:S(2)}, u32[]{:S(2)}) collective-permute-start(bf16[1024,512]{1,0:T(8,128)(2,1)S(1)} %maximum_select_fusion), channel_id=1, source_target_pairs={{0,24},{8,16},{16,8},{24,0},{1,25},{9,17},{17,9},{25,1},{2,26},{10... | collective-permute-start | bytes 3145736 | tf_op jit(solution)/shard_map/ppermute | solution.py:192
  98.7 134.4 %all-gather.8.cloned.1.call-start = ((), (), s32[]{:S(2)}) async-start(), calls=%async_computation.3 | async-start | bytes 6062080 | tf_op jit(solution)/shard_map/all_gather | solution.py:1468
  143.9 29.1 %collective-permute-start.5 = (bf16[1024,512]{1,0:T(8,128)(2,1)}, bf16[1024,512]{1,0:T(8,128)(2,1)S(1)}, u32[]{:S(2)}, u32[]{:S(2)}) collective-permute-start(bf16[1024,512]{1,0:T(8,128)(2,1)} %collective-permute-done.2.refs_7_.refs_8_.refs_6_), channel_id=1, source_target_pairs={{0,1},{1,0},{2,3},{3,2},{4,5},{5,4},{6,7},{7,6},{8,9},{9,8},{10,11... | collective-permute-start | bytes 3145736 | tf_op jit(solution)/shard_map/ppermute | solution.py:192
  173.0 6.6 %copy-start.22 = (s32[1,256]{1,0:T(1,128)S(1)}, s32[1,256]{1,0:T(1,128)}, u32[]{:S(2)}) copy-start(s32[1,256]{1,0:T(1,128)} %param.26) | copy-start | bytes 3076
  176.4 165.7 %reduce-scatter.7.cloned.1.call-start = ((), (), s32[]{:S(2)}) async-start(), calls=%async_computation.7 | async-start | bytes 6062080
  176.4 5.2 collective-permute-start.3
  176.9 4.8 collective-permute-start.4
  257.4 104.9 %reduce-scatter.9.cloned.1.call-start = ((), (), s32[]{:S(2)}) async-start(), calls=%async_computation.8 | async-start | bytes 983040
  293.3 23.6 %copy-start.11 = (bf16[4,64,512]{2,1,0:T(8,128)(2,1)S(1)}, bf16[4,64,512]{2,1,0:T(8,128)(2,1)}, u32[]{:S(2)}) copy-start(bf16[4,64,512]{2,1,0:T(8,128)(2,1)} %get-tuple-element.151) | copy-start | bytes 786436
  293.3 23.6 %copy-start.12 = (bf16[4,64,512]{2,1,0:T(8,128)(2,1)S(1)}, bf16[4,64,512]{2,1,0:T(8,128)(2,1)}, u32[]{:S(2)}) copy-start(bf16[4,64,512]{2,1,0:T(8,128)(2,1)} %get-tuple-element.152) | copy-start | bytes 786436
  318.8 75.8 %all-gather.10.cloned.1.call-start = ((), (), s32[]{:S(2)}) async-start(), calls=%async_computation.4 | async-start | bytes 1769472 | tf_op jit(solution)/shard_map/all_gather | solution.py:1503
  362.3 3.6 copy-start.23
  363.9 147.9 %all-gather.12.cloned.1.call-start = ((), (), s32[]{:S(2)}) async-start(), calls=%async_computation.5 | async-start | bytes 2359296 | tf_op jit(solution)/shard_map/all_gather | solution.py:1557
  445.5 1.7 copy-start.9
  447.2 2.0 copy-start.25
  447.2 2.6 copy-start.15
  478.1 72.5 %all-gather.14.cloned.1.call-start = ((), (), s32[]{:S(2)}) async-start(), calls=%async_computation.6 | async-start | bytes 2359296 | tf_op jit(solution)/shard_map/all_gather | solution.py:1561
  513.6 1.7 copy-start.7
  519.0 28.7 %copy-start.4 = (f32[4,512,512]{2,1,0:T(8,128)S(1)}, f32[4,512,512]{2,1,0:T(8,128)}, u32[]{:S(2)}) copy-start(f32[4,512,512]{2,1,0:T(8,128)} %refs_1_.7) | copy-start | bytes 12582916
  519.0 28.8 %copy-start.8 = (bf16[2048,512]{1,0:T(8,128)(2,1)S(1)}, bf16[2048,512]{1,0:T(8,128)(2,1)}, u32[]{:S(2)}) copy-start(bf16[2048,512]{1,0:T(8,128)(2,1)} %all-gather.12.cloned.1.call-done) | copy-start | bytes 6291460
  (7 other events, 9.2 us)
Sparse Core Ops, SparseCore 0:
  98.9 58.4 all-reduce.6
  176.5 56.5 all-gather.7
  257.5 58.0 reduce-scatter.6
  318.9 26.8 reduce-scatter.8
  364.1 24.8 all-gather.9
  478.2 27.9 all-gather.11
  513.7 27.8 all-gather.13

commit v10 on v9

--- a/solution.py
+++ b/solution.py
@@ -567,6 +567,25 @@
         return carry
 
     lax.fori_loop(0, code_ref.shape[0] // step, one, 0)
+
+
+def finish_kernel(weight_ref, stats_ref, products_ref, basis_ref, new_stats_ref, new_basis_ref):
+    products = products_ref[...].astype(jnp.float32)
+    new_stats_ref[...] = stat_decay * stats_ref[...] + weight_ref[0] * products
+    new_basis_ref[...] = basis_ref[...].astype(jnp.float32)
+
+
+def finish_matrices(weight, stats, products, bases):
+    block = pl.BlockSpec((1, *stats.shape[1:]), lambda k: (k, 0, 0))
+    return pl.pallas_call(
+        finish_kernel,
+        grid=stats.shape[:1],
+        out_shape=(full(*stats.shape),) * 2,
+        in_specs=[smem] + [block] * 3,
+        out_specs=(block,) * 2,
+        compiler_params=pltpu.CompilerParams(vmem_limit_bytes=56 * 2**20),
+        cost_estimate=cost_of(5),
+    )(weight.reshape(1), stats, products, bases)
 
 
 def loss_forward_kernel(chunks, final_ref, pick_ref, label_ref, table_ref, picked_ref, stat_ref, logit_ref):
@@ -1358,7 +1377,8 @@
 
 
 def adam_direction(moment, second):
-    return moment / (1.0 - beta_one**STEP) / (jnp.sqrt(second / (1.0 - beta_two**STEP)) + adam_eps)
+    first_scale, second_scale = 1.0 / (1.0 - beta_one**STEP), 1.0 / (1.0 - beta_two**STEP)
+    return (moment * first_scale) / (jnp.sqrt(second * second_scale) + adam_eps)
 
 
 def adam_update(weight, grad_item, moment, second, step_rate, decay_weight):
@@ -1558,8 +1578,8 @@
     weight_new = (1.0 - stat_decay) * (factor * factor)
     own_basis = renew_basis(own_products, soap_stats, soap_basis, weight_new)
     own_basis = follow(own_basis, all_products)
-    new_basis = lax.all_gather(own_basis, "vocab").reshape(4, width, width).astype(jnp.float32)
-    new_stats = stat_decay * soap_stats + weight_new * all_products.astype(jnp.float32)
+    new_basis = lax.all_gather(own_basis, "vocab").reshape(4, width, width)
+    new_stats, new_basis = finish_matrices(weight_new, soap_stats, all_products, new_basis)
 
     new_norm, m_norm, v_norm = adam_update(norm_p, g_norm, norm_m, norm_v, rate_vector, 0.0)
     updated = update_matrices(

time: 570 us -> 567 us (level)
  other arithmetic: 32.7 us -> 25.5 us
  Pallas kernels: 453 us -> 459 us
    pallas_call x0 -> x1, Pallas kernels: none -> 6.98 us  [finish_matrices(): pl.pallas_call(finish_kernel, grid=stats.shape[:1], out_shape=(full(*stat...]
where the time goes in v10:
time: 567 us; the launch traced here: 562 us
  Pallas kernels  459 us (81%)
  local copies, waits for them, and re-layouts  28 us (5%)
  other arithmetic  25.5 us (4%)
  between operations  22.1 us (4%)
  waiting for transfers between devices  20.9 us (4%)
    pallas_call x18, Pallas kernels, call(): pl.pallas_call(body, out_shape=outs, in_specs=specs, out_specs=jax.tree.m...  259 us
    pallas_call x7, Pallas kernels, talk(): pl.pallas_call(body, out_shape=outs, in_specs=[vmem] * len(args) + [pl.Bl...  164 us
    pallas_call x1, Pallas kernels, update_matrices(): pl.pallas_call(update_kernel, grid=(4,), out_shape=tuple((full(*part.shap...  28.6 us
    psum x1, waiting for transfers between devices, body(): target_sum = lax.psum(target_part, 'vocab')  13.4 us
  transfers between devices with their start and end apart: 13, of which 3 were waited for; matrix products, arithmetic and copies ran while one was open for 5% of the time, Pallas kernels for 50%

profile of v10, /device:TPU:0, one launch (start us, length us, event | category | flops | bytes accessed | tf_op | source)
XLA Modules:
  0.0 562.3 jit_solution(11462984603696100256)
XLA Ops:
  9.9 7.9 %shard_map.332 = (s32[4,2,1024]{2,1,0:T(2,128)}, f32[4,16,128]{2,1,0:T(8,128)}) custom-call(s32[2,1024]{1,0:T(2,128)} %pad_add_fusion.refs_0_, f32[16,128]{1,0:T(8,128)} %pad_convert_fusion.refs_1_), custom_call_target="tpu_custom_call" | custom-call | flops 15000000512 | tf_op jit(solution)/shard_map/pallas_call | solution.py:857
  23.1 2.7 copy.61.refs_0_
  26.0 2.1 copy-done.4
  29.2 2.0 copy.62.refs_4_
  32.3 11.7 %shard_map.333 = bf16[4096,128]{1,0:T(8,128)(2,1)} custom-call(s32[4096,1]{1,0:T(8,128)} %copy.61.refs_0_, bf16[2432,256]{1,0:T(8,128)(2,1)} %fusion.2.refs_1_.refs_5_), custom_call_target="tpu_custom_call" | custom-call | flops 5000000000 | tf_op jit(solution)/shard_map/pallas_call | solution.py:62
  44.0 50.7 %shard_map.334 = (f32[1024,512]{1,0:T(8,128)}, bf16[4,512,512]{2,1,0:T(8,128)(2,1)}, bf16[2,2048,512]{2,1,0:T(8,128)(2,1)}, bf16[4096,128]{1,0:T(8,128)(2,1)}) custom-call(bf16[4,1024,128]{2,1,0:T(8,128)(2,1)} %bitcast.150, f32[1024,512]{1,0:T(8,128)} %constant.173.clone.refs_1_, bf16[4,128,512]{2,1,0:T(8,128)(2,1)} %get-tuple-element.198.refs_2_, ...), custom_call_target="tpu_custom_call" | custom-call | flops 49999998976 | tf_op jit(solution)/shard_map/pallas_call | solution.py:857
  96.7 2.0 collective-permute-start.2
  104.5 19.7 %shard_map.335 = (f32[1024,512]{1,0:T(8,128)}, bf16[1024,512]{1,0:T(8,128)(2,1)}, bf16[512,1024]{1,0:T(8,128)(2,1)}, bf16[512,1024]{1,0:T(8,128)(2,1)}, bf16[512...) custom-call(f32[1024,512]{1,0:T(8,128)} %get-tuple-element.105.refs_0_.refs_1_, ...), custom_call_target="tpu_custom_call" | custom-call | flops 20000000000 | tf_op jit(solution)/shard_map/pallas_call | solution.py:62
  124.2 11.5 %shard_map.336 = (f32[1024,512]{1,0:T(8,128)}, bf16[1024,512]{1,0:T(8,128)(2,1)}, bf16[1024,512]{1,0:T(8,128)(2,1)}) custom-call(f32[1024,512]{1,0:T(8,128)} %get-tuple-element.108.refs_0_.refs_3_, f32[2,512]{1,0:T(2,128)} %get-tuple-element.229.refs_1_.refs_4_, f32[2,512]{1,0:T(2,128)} %pad_maximum_fusion.6.refs_2_, ...), custom_call_target="tpu_custom_call" | custom-call | flops 12000000000 | tf_op jit(solution)/shard_map/pallas_call | solution.py:62
  138.0 6.0 %collective-permute-done.2.refs_7_.refs_8_.refs_6_ = bf16[1024,512]{1,0:T(8,128)(2,1)} collective-permute-done((bf16[1024,512]{1,0:T(8,128)(2,1)S(1)}, bf16[1024,512]{1,0:T(8,128)(2,1)}, u32[]{:S(2)}, u32[]{:S(2)}) %collective-permute-start.2) | collective-permute-done | bytes 1048608 | tf_op jit(solution)/shard_map/ppermute | solution.py:192
  143.9 13.4 %all-reduce.7.cloned.1.call-done.refs_0_ = bf16[4,1024,128]{2,1,0:T(8,128)(2,1)} async-done(((bf16[4,1024,128]{2,1,0:T(8,128)(2,1)}), bf16[4,1024,128]{2,1,0:T(8,128)(2,1)}) %all-reduce.7.cloned.1.call-update) | async-done | bytes 1048592 | tf_op jit(solution)/shard_map/psum | solution.py:1466
  157.3 2.7 broadcast_in_dim.34.refs_7_.refs_8_
  160.0 13.3 %shard_map.337.refs_0_.refs_2_.refs_1_ = f32[1024,512]{1,0:T(8,128)} custom-call(bf16[4,1024,128]{2,1,0:T(8,128)(2,1)} %all-reduce.7.cloned.1.call-done.refs_0_, f32[1024,512]{1,0:T(8,128)} %constant.173.clone.refs_1_, f32[1024,512]{1,0:T(8,128)} %get-tuple-element.110.refs_2_.refs_1_, f32[256]{0:T(256)} %broadcast_divide_fusion.refs_3_, ...), custom_call_target="tpu_custom_call" | custom-call | flops 15000000512 | tf_op jit(solution)/shard_map/pallas_call | solution.py:857
  174.3 2.4 shard_map.341
  183.2 17.4 %shard_map.338 = (f32[1024,512]{1,0:T(8,128)}, bf16[1024,512]{1,0:T(8,128)(2,1)}, bf16[512,1024]{1,0:T(8,128)(2,1)}, bf16[512,1024]{1,0:T(8,128)(2,1)}, bf16[512...) custom-call(f32[1024,512]{1,0:T(8,128)} %shard_map.337.refs_0_.refs_2_.refs_1_,, ...), custom_call_target="tpu_custom_call" | custom-call | flops 20000000000 | tf_op jit(solution)/shard_map/pallas_call | solution.py:62
  200.6 18.7 %shard_map.339 = (f32[1024,512]{1,0:T(8,128)}, bf16[1024,512]{1,0:T(8,128)(2,1)}, bf16[512,1024]{1,0:T(8,128)(2,1)}, bf16[512,1024]{1,0:T(8,128)(2,1)}, bf16[512...) custom-call(f32[1024,512]{1,0:T(8,128)} %get-tuple-element.115.refs_0_.refs_1_,, ...), custom_call_target="tpu_custom_call" | custom-call | flops 20000000000 | tf_op jit(solution)/shard_map/pallas_call | solution.py:62
  219.3 12.8 %shard_map.340 = (f32[1024,512]{1,0:T(8,128)}, bf16[1024,512]{1,0:T(8,128)(2,1)}, bf16[1024,512]{1,0:T(8,128)(2,1)}, bf16[2,2048,512]{2,1,0:T(8,128)(2,1)}) custom-call(f32[1024,512]{1,0:T(8,128)} %get-tuple-element.117.refs_0_.refs_4_, f32[2,512]{1,0:T(2,128)} %get-tuple-element.231.refs_1_.refs_5_, f32[2,512]{1,0:T(2,128)} %pad_maximum_fusion.10.refs_2_.refs_3_, ...), custom_call_target="tpu_custom_call" | custom-call | flops 12000000000 | tf_op jit(solution)/shard_map/pallas_call | solution.py:62
  233.5 6.3 %shard_map.342 = (bf16[256,512]{1,0:T(8,128)(2,1)}, f32[8,256]{1,0:T(8,128)}) custom-call(bf16[1024,512]{1,0:T(8,128)(2,1)} %get-tuple-element.118.refs_0_, s32[256,1]{1,0:T(8,128)} %copy.63.refs_1_, s32[1,256]{1,0:T(1,128)} %broadcast_subtract_fusion.refs_2_.refs_3_, bf16[4736,512]{1,0:T(8,128)(2,1)} %all-gather.8.cloned.1.call-done.refs_3_.refs_4_), custom_call_target="tpu_custom_call" | custom-call | flops 6000000000 | tf_op jit(solution)/shard_map/pallas_call | solution.py:62
  239.8 7.4 %shard_map.343.refs_1_ = f32[8,8,256]{2,1,0:T(8,128)} custom-call(f32[8,256]{1,0:T(8,128)} %get-tuple-element.120.refs_0_), custom_call_target="tpu_custom_call" | custom-call | flops 15000000512 | tf_op jit(solution)/shard_map/pallas_call | solution.py:857
  247.2 10.3 %shard_map.344 = (bf16[256,512]{1,0:T(8,128)(2,1)}, bf16[4,4736,128]{2,1,0:T(8,128)(2,1)}, f32[1,256]{1,0:T(1,128)}) custom-call(bf16[256,512]{1,0:T(8,128)(2,1)} %get-tuple-element.119.refs_0_, f32[8,8,256]{2,1,0:T(8,128)} %shard_map.343.refs_1_, f32[1,256]{1,0:T(1,128)} %bitcast.139, s32[1,256]{1,0:T(1,128)} %broadcast_subtract_fusion.refs_2_.refs_3_, ...), custom_call_target="tpu_custom_call" | custom-call | flops 8000000000 | tf_op jit(solution)/shard_map/pallas_call | solution.py:62
  257.5 16.2 %shard_map.345.refs_0_ = bf16[256,512]{1,0:T(8,128)(2,1)} custom-call(bf16[256,512]{1,0:T(8,128)(2,1)} %get-tuple-element.121.refs_0_), custom_call_target="tpu_custom_call" | custom-call | flops 15000000512 | tf_op jit(solution)/shard_map/pallas_call | solution.py:857
  273.8 19.9 %shard_map.346 = (f32[1024,512]{1,0:T(8,128)}, f32[2,512]{1,0:T(2,128)}, f32[2,512]{1,0:T(2,128)}, bf16[4,64,512]{2,1,0:T(8,128)(2,1)}, bf16[4,64,512]{2,1,0:T(8,128)(2,1)}) custom-call(bf16[256,512]{1,0:T(8,128)(2,1)} %shard_map.345.refs_0_, s32[1,256]{1,0:T(1,128)} %refs_1_.5, f32[1024,512]{1,0:T(8,128)} %get-tuple-element.122.refs_2_, ...), custom_call_target="tpu_custom_call" | custom-call | flops 16999999488 | tf_op jit(solution)/shard_map/pallas_call | solution.py:62
  293.7 23.6 %shard_map.347 = (f32[1024,512]{1,0:T(8,128)}, f32[2,512]{1,0:T(2,128)}, bf16[4,64,512]{2,1,0:T(8,128)(2,1)}, f32[1024,512]{1,0:T(8,128)}) custom-call(f32[1024,512]{1,0:T(8,128)} %get-tuple-element.125.refs_0_, f32[1024,512]{1,0:T(8,128)} %get-tuple-element.115.refs_0_.refs_1_, f32[2,512]{1,0:T(2,128)} %get-tuple-element.230.refs_1_.refs_2_, ...), custom_call_target="tpu_custom_call" | custom-call | flops 24999999488 | tf_op jit(solution)/shard_map/pallas_call | solution.py:62
  317.3 1.9 pad_maximum_fusion.3
  319.2 24.3 %shard_map.348 = (f32[1024,512]{1,0:T(8,128)}, f32[2,512]{1,0:T(2,128)}, bf16[4,64,512]{2,1,0:T(8,128)(2,1)}, bf16[4,1024,128]{2,1,0:T(8,128)(2,1)}) custom-call(f32[1024,512]{1,0:T(8,128)} %get-tuple-element.136.refs_0_, f32[1024,512]{1,0:T(8,128)} %shard_map.337.refs_0_.refs_2_.refs_1_, f32[2,512]{1,0:T(2,128)} %pad_maximum_fusion.7.refs_1_.refs_2_, ...), custom_call_target="tpu_custom_call" | custom-call | flops 24999999488 | tf_op jit(solution)/shard_map/pallas_call | solution.py:62
  343.5 20.1 %shard_map.349 = (f32[1024,512]{1,0:T(8,128)}, f32[2,512]{1,0:T(2,128)}, f32[2,512]{1,0:T(2,128)}, bf16[4,64,512]{2,1,0:T(8,128)(2,1)}, bf16[4,64,512]{2,1,0:T(8,128)(2,1)}) custom-call(f32[1024,512]{1,0:T(8,128)} %get-tuple-element.133.refs_0_, f32[1024,512]{1,0:T(8,128)} %get-tuple-element.110.refs_2_.refs_1_, f32[2,512]{1,0:T(2,128)} %pad_maximum_fusion.6.refs_2_, ...), custom_call_target="tpu_custom_call" | custom-call | flops 16999999488 | tf_op jit(solution)/shard_map/pallas_call | solution.py:62
  369.8 26.1 %shard_map.351 = (f32[1024,512]{1,0:T(8,128)}, f32[2,512]{1,0:T(2,128)}, bf16[4,64,512]{2,1,0:T(8,128)(2,1)}, bf16[4,1024,128]{2,1,0:T(8,128)(2,1)}) custom-call(f32[1024,512]{1,0:T(8,128)} %get-tuple-element.145.refs_1_.refs_0_, f32[1024,512]{1,0:T(8,128)} %get-tuple-element.105.refs_0_.refs_1_, f32[2,512]{1,0:T(2,128)} %get-tuple-element.228.refs_1_.refs_2_, ...), custom_call_target="tpu_custom_call" | custom-call | flops 24999999488 | tf_op jit(solution)/shard_map/pallas_call | solution.py:62
  397.2 47.6 %shard_map.353 = (bf16[4,8,64,512]{3,2,1,0:T(8,128)(2,1)}, f32[1,512]{1,0:T(1,128)}, bf16[4,1024,128]{2,1,0:T(8,128)(2,1)}, bf16[4,1024,128]{2,1,0:T(8,128)(2,1)...) custom-call(bf16[4,64,512]{2,1,0:T(8,128)(2,1)} %get-tuple-element.156.refs_0_, ...), custom_call_target="tpu_custom_call" | custom-call | flops 40000000000 | tf_op jit(solution)/shard_map/pallas_call | solution.py:857
  454.7 21.1 %shard_map.354 = (f32[512,512]{1,0:T(8,128)}, f32[8,128]{1,0:T(8,128)}) custom-call(f32[512,512]{1,0:T(8,128)} %fusion.5.refs_0_, f32[8,128]{1,0:T(8,128)} %broadcast_in_dim.36.refs_1_), custom_call_target="tpu_custom_call" | custom-call | flops 15000000512 | tf_op jit(solution)/shard_map/pallas_call | solution.py:857
  481.2 30.1 %shard_map.356.refs_0_ = bf16[256,512]{1,0:T(8,128)(2,1)} custom-call(f32[512,512]{1,0:T(8,128)} %get-tuple-element.183.refs_0_, f32[4,512,512]{2,1,0:T(8,128)} %stats_ref.1, f32[4,512,512]{2,1,0:T(8,128)} %refs_2_.7, f32[1]{0:T(128)} %bitcast.67.refs_3_.weight_ref), custom_call_target="tpu_custom_call" | custom-call | flops 28999999488 | tf_op jit(solution)/shard_map/pallas_call | solution.py:62
  518.5 28.6 %shard_map.355 = (f32[12,128,512]{2,1,0:T(8,128)}, f32[12,128,512]{2,1,0:T(8,128)}, f32[12,128,512]{2,1,0:T(8,128)}, f32[4736,128]{1,0:T(8,128)}, f32[4736,128]{...) custom-call(f32[1]{0:T(128)} %bitcast.57.refs_0_, ...), custom_call_target="tpu_custom_call" | custom-call | flops 20000000000 | tf_op jit(solution)/shard_map/pallas_call | solution.py:712
  547.1 7.0 %shard_map.358 = (f32[4,512,512]{2,1,0:T(8,128)}, f32[4,512,512]{2,1,0:T(8,128)}) custom-call(f32[1]{0:T(128)} %bitcast.67.refs_3_.weight_ref, f32[4,512,512]{2,1,0:T(8,128)} %stats_ref.1, bf16[4,512,512]{2,1,0:T(8,128)(2,1)} %bitcast.145, bf16[4,512,512]{2,1,0:T(8,128)(2,1)} %bitcast.146), custom_call_target="tpu_custom_call" | custom-call | flops 5000000000 | tf_op jit(solution)/shard_map/pallas_call | solution.py:580
  (149 shorter events, 53.0 us)
Async XLA Ops:
  7.2 150.1 %all-reduce.7.cloned.1.call-start = ((), (), s32[]{:S(2)}) async-start(), calls=%async_computation.2 | async-start | bytes 2097152 | tf_op jit(solution)/shard_map/psum | solution.py:1466
  9.9 10.2 %copy-start.3 = (f32[4,512,512]{2,1,0:T(8,128)S(1)}, f32[4,512,512]{2,1,0:T(8,128)}, u32[]{:S(2)}) copy-start(f32[4,512,512]{2,1,0:T(8,128)} %refs_11_.1) | copy-start | bytes 12582916
  21.4 4.4 copy-start.5
  25.7 2.3 copy-start.4
  25.9 2.4 copy-start.1
  94.8 4.3 copy-start.18
  94.8 4.5 copy-start
  94.8 4.8 copy-start.14
  94.8 4.8 copy-start.15
  94.8 6.2 %copy-start.11 = (bf16[4,8,2,128]{3,2,1,0:T(2,128)(2,1)S(1)}, bf16[4,8,2,128]{3,2,1,0:T(2,128)(2,1)}, u32[]{:S(2)}) copy-start(bf16[4,8,2,128]{3,2,1,0:T(2,128)(2,1)} %get-tuple-element.215) | copy-start | bytes 49156
  95.1 42.8 %collective-permute-start = (bf16[1024,512]{1,0:T(8,128)(2,1)S(1)}, bf16[1024,512]{1,0:T(8,128)(2,1)}, u32[]{:S(2)}, u32[]{:S(2)}) collective-permute-start(bf16[1024,512]{1,0:T(8,128)(2,1)S(1)} %maximum_select_fusion), channel_id=1, source_target_pairs={{0,8},{8,0},{16,24},{24,16},{1,9},{9,1},{17,25},{25,17},{2,10},{10... | collective-permute-start | bytes 3145736 | tf_op jit(solution)/shard_map/ppermute | solution.py:192
  96.2 41.8 %collective-permute-start.1 = (bf16[1024,512]{1,0:T(8,128)(2,1)S(1)}, bf16[1024,512]{1,0:T(8,128)(2,1)}, u32[]{:S(2)}, u32[]{:S(2)}) collective-permute-start(bf16[1024,512]{1,0:T(8,128)(2,1)S(1)} %maximum_select_fusion), channel_id=1, source_target_pairs={{0,16},{8,24},{16,0},{24,8},{1,17},{9,25},{17,1},{25,9},{2,18},{10... | collective-permute-start | bytes 3145736 | tf_op jit(solution)/shard_map/ppermute | solution.py:192
  96.7 47.2 %collective-permute-start.2 = (bf16[1024,512]{1,0:T(8,128)(2,1)S(1)}, bf16[1024,512]{1,0:T(8,128)(2,1)}, u32[]{:S(2)}, u32[]{:S(2)}) collective-permute-start(bf16[1024,512]{1,0:T(8,128)(2,1)S(1)} %maximum_select_fusion), channel_id=1, source_target_pairs={{0,24},{8,16},{16,8},{24,0},{1,25},{9,17},{17,9},{25,1},{2,26},{10... | collective-permute-start | bytes 3145736 | tf_op jit(solution)/shard_map/ppermute | solution.py:192
  98.7 134.8 %all-gather.8.cloned.1.call-start = ((), (), s32[]{:S(2)}) async-start(), calls=%async_computation.3 | async-start | bytes 6062080 | tf_op jit(solution)/shard_map/all_gather | solution.py:1488
  143.9 29.4 %collective-permute-start.5 = (bf16[1024,512]{1,0:T(8,128)(2,1)}, bf16[1024,512]{1,0:T(8,128)(2,1)S(1)}, u32[]{:S(2)}, u32[]{:S(2)}) collective-permute-start(bf16[1024,512]{1,0:T(8,128)(2,1)} %collective-permute-done.2.refs_7_.refs_8_.refs_6_), channel_id=1, source_target_pairs={{0,1},{1,0},{2,3},{3,2},{4,5},{5,4},{6,7},{7,6},{8,9},{9,8},{10,11... | collective-permute-start | bytes 3145736 | tf_op jit(solution)/shard_map/ppermute | solution.py:192
  173.3 6.6 %copy-start.20 = (s32[1,256]{1,0:T(1,128)S(1)}, s32[1,256]{1,0:T(1,128)}, u32[]{:S(2)}) copy-start(s32[1,256]{1,0:T(1,128)} %param.26) | copy-start | bytes 3076
  176.7 166.8 %reduce-scatter.7.cloned.1.call-start = ((), (), s32[]{:S(2)}) async-start(), calls=%async_computation.7 | async-start | bytes 6062080
  176.8 5.2 collective-permute-start.3
  177.2 4.8 collective-permute-start.4
  257.5 106.1 %reduce-scatter.9.cloned.1.call-start = ((), (), s32[]{:S(2)}) async-start(), calls=%async_computation.8 | async-start | bytes 983040
  293.7 23.6 %copy-start.9 = (bf16[4,64,512]{2,1,0:T(8,128)(2,1)S(1)}, bf16[4,64,512]{2,1,0:T(8,128)(2,1)}, u32[]{:S(2)}) copy-start(bf16[4,64,512]{2,1,0:T(8,128)(2,1)} %get-tuple-element.153) | copy-start | bytes 786436
  293.7 23.6 %copy-start.10 = (bf16[4,64,512]{2,1,0:T(8,128)(2,1)S(1)}, bf16[4,64,512]{2,1,0:T(8,128)(2,1)}, u32[]{:S(2)}) copy-start(bf16[4,64,512]{2,1,0:T(8,128)(2,1)} %get-tuple-element.154) | copy-start | bytes 786436
  319.2 76.6 %all-gather.10.cloned.1.call-start = ((), (), s32[]{:S(2)}) async-start(), calls=%async_computation.4 | async-start | bytes 1769472 | tf_op jit(solution)/shard_map/all_gather | solution.py:1523
  363.6 3.6 copy-start.21
  365.2 146.1 %all-gather.12.cloned.1.call-start = ((), (), s32[]{:S(2)}) async-start(), calls=%async_computation.5 | async-start | bytes 2359296 | tf_op jit(solution)/shard_map/all_gather | solution.py:1577
  444.8 1.7 copy-start.7
  446.5 2.0 copy-start.23
  446.5 2.6 copy-start.13
  477.6 69.5 %all-gather.14.cloned.1.call-start = ((), (), s32[]{:S(2)}) async-start(), calls=%async_computation.6 | async-start | bytes 2359296 | tf_op jit(solution)/shard_map/all_gather | solution.py:1581
  513.1 1.7 copy-start.6
  516.3 1.5 copy-start.16
  516.3 1.5 copy-start.17
  (5 other events, 6.2 us)
Sparse Core Ops, SparseCore 0:
  98.8 58.4 all-reduce.6
  176.8 56.5 all-gather.7
  257.6 58.0 reduce-scatter.6
  319.3 25.8 reduce-scatter.8
  365.4 22.8 all-gather.9
  477.7 27.8 all-gather.11
  513.2 27.6 all-gather.13
